TPU v7x, 256 devices: a whole 4x4x8 slice. The times are simulated.
256 devices in a mesh: ep: 64 (over z, x, core), grp: 4 (over y).
Axes of the slice: x: 4, y: 4, z: 8, core: 2. Of those that a mesh axis runs over, the one named last changes fastest.
Arguments:
- hidden: bfloat16 [4096, 3584], P(('ep', 'grp')), may hold values from -6 to 6
- expert_ids: int32 [4096, 8], P(('ep', 'grp')), may hold values from 0 to 63, all different within a row; in each aligned block of 16 rows (0 to 15, 16 to 31, ...) at most 4 rows name the same one
- gate_weights: float32 [4096, 8], P(('ep', 'grp')), may hold values from 0.05 to 0.5
- w_up: bfloat16 [64, 3584, 1024], P('ep', None, 'grp'), may hold values from -0.09375 to 0.09375
- w_down: bfloat16 [64, 3584, 1024], P('ep', None, 'grp'), may hold values from -0.1875 to 0.1875
- query_first: bfloat16 [4096, 64, 576], P(('ep', 'grp')), may hold values from -17 to 17
- kv_first: bfloat16 [4096, 576], P(('ep', 'grp')), may hold values from -6 to 6
- query_second: bfloat16 [4096, 64, 576], P(('ep', 'grp')), may hold values from -17 to 17
- kv_second: bfloat16 [4096, 576], P(('ep', 'grp')), may hold values from -6 to 6
- cache_pool: bfloat16 [8192, 64, 576], P(('ep', 'grp')), may hold values from -6 to 6
- cache_len: int32 [256, 16], P(('ep', 'grp')), may hold values from 1 to 512, 1024 in all within a row
- page_perm: int32 [256, 32], P(('ep', 'grp')), may hold values from 0 to 31, each once within a row
- mig_slot: int32 [64, 4], P('ep', 'grp'), may hold values from 0 to 15
- mig_dest: int32 [64, 4], P('ep', 'grp'), may hold values from 0 to 3, each once within a row
Outputs:
- attn_first: bfloat16 [4096, 64, 512], P(('ep', 'grp'))
- attn_second: bfloat16 [4096, 64, 512], P(('ep', 'grp'))
- moe_out: bfloat16 [4096, 3584], P(('ep', 'grp'))
Inputs may be any that keep to these rules, and one draw needn't show every extreme that they name: `expert_ids`: the entries of the rows of one device name each expert at most 4 times. `cache_len`: each row's lengths sum to 1024. `page_perm`: each row is a permutation of the 32 page numbers. `mig_dest`: each row is a permutation of the 4 grp indices.
All inputs are finite; a program needn't handle non-finite values.
Results may differ from a plain program's by a relative error of at most 0.0058.
Values may be sent and summed in bfloat16 or wider, within the bound.
No kernel may reach another device: no remote copies, remote signals or barrier semaphores. Data moves between devices by JAX's collectives and lax.ppermute only.
A program may use at most 128 MiB of HBM per device.

v0:
```python
import math

import jax
import jax.numpy as jnp
from jax import lax
from jax.sharding import PartitionSpec as P

LAT = 512
MAXP = 8


def attend(query_rows, key_rows, key_valid):
    score_scale = 1.0 / math.sqrt(query_rows.shape[-1] / 3.0)
    scores = (
        jnp.einsum("bhk,blk->bhl", query_rows, key_rows, preferred_element_type=jnp.float32)
        * score_scale
    )
    scores = jnp.where(key_valid[:, None, :], scores, -jnp.inf)
    row_max = jnp.max(scores, axis=2, keepdims=True)
    weights = jnp.exp(scores - row_max)
    probability = (weights / jnp.sum(weights, axis=2, keepdims=True)).astype(jnp.bfloat16)
    return jnp.einsum(
        "bhl,blk->bhk", probability, key_rows[:, :, :LAT], preferred_element_type=jnp.float32
    ).astype(jnp.bfloat16)


def local_cache(cache_pool, cache_len, page_perm):
    lengths = cache_len[0]
    page_order = page_perm[0]
    pool_pages, page_rows, key_width = cache_pool.shape
    pages_used = (lengths + page_rows - 1) // page_rows
    page_offset = jnp.cumsum(pages_used) - pages_used
    page_slots = jnp.minimum(
        page_offset[:, None] + jnp.arange(MAXP, dtype=jnp.int32)[None, :], pool_pages - 1
    )
    page_index = page_order[page_slots]
    key_rows = cache_pool[page_index.reshape(-1)].reshape(
        lengths.shape[0], MAXP * page_rows, key_width
    )
    key_valid = jnp.arange(MAXP * page_rows, dtype=jnp.int32)[None, :] < lengths[:, None]
    return (key_rows, key_valid)


def shards(
    hidden,
    expert_ids,
    gate_weights,
    w_up,
    w_down,
    query_first,
    kv_first,
    query_second,
    kv_second,
    cache_pool,
    cache_len,
    page_perm,
    mig_slot,
    mig_dest,
):
    samples, picks_per = expert_ids.shape
    ep_size = lax.axis_size("ep")
    grp_size = lax.axis_size("grp")
    local_experts = w_up.shape[0]
    experts_all = local_experts * ep_size
    capacity = min(samples, max(2, 2 * samples * picks_per // experts_all))
    slots_all = experts_all * capacity
    flat_ids = expert_ids.reshape(-1)
    expert_hits = (flat_ids[:, None] == jnp.arange(experts_all, dtype=jnp.int32)[None, :]).astype(
        jnp.int32
    )
    earlier = jnp.sum((jnp.cumsum(expert_hits, axis=0) - expert_hits) * expert_hits, axis=1)
    slot_index = flat_ids * capacity + earlier
    slot_hits = (slot_index[:, None] == jnp.arange(slots_all, dtype=jnp.int32)[None, :]).astype(
        jnp.float32
    )
    token_hits = (
        jnp.arange(samples * picks_per, dtype=jnp.int32)[:, None] // picks_per
        == jnp.arange(samples, dtype=jnp.int32)[None, :]
    ).astype(jnp.float32)
    placing = jnp.dot(slot_hits.T, token_hits, precision=lax.Precision.HIGHEST).astype(jnp.bfloat16)
    outgoing = jnp.dot(placing, hidden, preferred_element_type=jnp.float32).astype(jnp.bfloat16)
    outgoing = outgoing.reshape(ep_size, local_experts, capacity, hidden.shape[1])
    arrived = lax.all_to_all(outgoing, "ep", split_axis=0, concat_axis=0, tiled=True)
    hidden_units = jnp.einsum(
        "gsjcd,jdf->gsjcf",
        lax.all_gather(arrived[None], "grp", axis=0, tiled=True),
        w_up,
        preferred_element_type=jnp.float32,
    )
    hidden_units = jax.nn.silu(hidden_units).astype(jnp.bfloat16)
    partial_value = jnp.einsum(
        "gsjcf,jdf->gsjcd", hidden_units, w_down, preferred_element_type=jnp.float32
    )
    produced = lax.psum_scatter(partial_value, "grp", scatter_dimension=0, tiled=True)[0].astype(
        jnp.bfloat16
    )
    returned = lax.all_to_all(produced, "ep", split_axis=0, concat_axis=0, tiled=True).reshape(
        slots_all, hidden.shape[1]
    )
    mixing = jnp.dot(
        token_hits.T, slot_hits * gate_weights.reshape(-1)[:, None], precision=lax.Precision.HIGHEST
    )
    moe_out = jnp.dot(
        mixing, returned, preferred_element_type=jnp.float32, precision=lax.Precision.HIGHEST
    ).astype(jnp.bfloat16)
    cache_keys, cache_valid = local_cache(cache_pool, cache_len, page_perm)
    always_one = jnp.ones((samples, 1), dtype=bool)
    always_two = jnp.ones((samples, 2), dtype=bool)
    attn_first = attend(
        query_first,
        jnp.concatenate([cache_keys, kv_first[:, None, :]], axis=1),
        jnp.concatenate([cache_valid, always_one], axis=1),
    )
    moved_slot = mig_slot[0, 0]
    moved_target = mig_dest[0, 0]
    to_target = jnp.arange(grp_size, dtype=jnp.int32) == moved_target
    zero_bf = jnp.zeros((), jnp.bfloat16)
    sent_keys = jnp.where(to_target[:, None, None], cache_keys[moved_slot][None], zero_bf)
    sent_valid = jnp.where(
        to_target[:, None], cache_valid[moved_slot].astype(jnp.bfloat16)[None], zero_bf
    )
    sent_fresh = jnp.where(to_target[:, None], kv_first[moved_slot][None], zero_bf)
    got_keys, got_valid, got_fresh = (
        lax.all_to_all(sent_keys, "grp", split_axis=0, concat_axis=0, tiled=True),
        lax.all_to_all(sent_valid, "grp", split_axis=0, concat_axis=0, tiled=True),
        lax.all_to_all(sent_fresh, "grp", split_axis=0, concat_axis=0, tiled=True),
    )
    in_keys = jnp.sum(got_keys.astype(jnp.float32), axis=0).astype(jnp.bfloat16)
    in_valid = jnp.sum(got_valid.astype(jnp.float32), axis=0) > 0.5
    in_fresh = jnp.sum(got_fresh.astype(jnp.float32), axis=0).astype(jnp.bfloat16)
    keys_next = cache_keys.at[moved_slot].set(in_keys)
    valid_next = cache_valid.at[moved_slot].set(in_valid)
    fresh_next = kv_first.at[moved_slot].set(in_fresh)
    all_keys = jnp.concatenate([keys_next, fresh_next[:, None, :], kv_second[:, None, :]], axis=1)
    all_valid = jnp.concatenate([valid_next, always_two], axis=1)
    attn_second = attend(query_second, all_keys, all_valid)
    return (attn_first, attn_second, moe_out)


def solution(mesh):
    return jax.shard_map(
        shards,
        mesh=mesh,
        in_specs=(
            P(("ep", "grp"), None),
            P(("ep", "grp"), None),
            P(("ep", "grp"), None),
            P("ep", None, "grp"),
            P("ep", None, "grp"),
            P(("ep", "grp"), None, None),
            P(("ep", "grp"), None),
            P(("ep", "grp"), None, None),
            P(("ep", "grp"), None),
            P(("ep", "grp"), None, None),
            P(("ep", "grp"), None),
            P(("ep", "grp"), None),
            P("ep", "grp"),
            P("ep", "grp"),
        ),
        out_specs=(
            P(("ep", "grp"), None, None),
            P(("ep", "grp"), None, None),
            P(("ep", "grp"), None),
        ),
        check_vma=False,
    )
```

profile of v0, /device:TPU:1, one launch (start us, length us, event | category | flops | bytes accessed | tf_op | source)
XLA Modules:
  0.0 400.5 jit_solution(4703498623927363379)
XLA Ops:
  7.2 0.0 copy-start
  7.2 0.0 all-gather.3.cloned.1.call-start
  7.2 0.9 copy.96
  8.1 0.1 reshape.451
  8.2 0.1 fusion.74
  8.3 0.2 reduce_window_sum.18
  8.5 0.2 select_reduce_fusion
  8.7 0.3 convolution_convert_fusion.2
  8.9 2.8 convolution_convert_fusion
  11.8 4.1 %reshape.452 = bf16[64,1,4,3584]{3,2,0,1:T(4,128)(2,1)} reshape(bf16[256,3584]{1,0:T(8,128)(2,1)} %convolution_convert_fusion) | data formatting | bytes 3670016 | tf_op jit(solution)/shard_map/reshape | solution.py:82
  15.8 57.3 %all_to_all.27 = bf16[64,1,4,3584]{3,2,1,0:T(4,128)(2,1)S(1)} all-to-all(bf16[64,1,4,3584]{3,2,1,0:T(4,128)(2,1)} %bitcast.117), channel_id=1, replica_groups=mesh['ep'=64,'grp'=4] {'ep'}, dimensions={0} | all-to-all | bytes 3670016 | tf_op jit(solution)/shard_map/all_to_all | solution.py:83
  73.1 1.6 copy.99
  74.6 0.0 all-gather.3.cloned.1.call-update
  74.6 0.0 reduce-scatter.2.cloned.1.call-start
  74.7 74.7 %all-gather.3.cloned.1.call-done = bf16[256,1,4,3584]{3,0,2,1:T(8,128)(2,1)} async-done(((bf16[64,1,4,3584]{3,0,2,1:T(8,128)(2,1)}), bf16[256,1,4,3584]{3,0,2,1:T(8,128)(2,1)}) %all-gather.3.cloned.1.call-update) | async-done | bytes 7340048 | tf_op jit(solution)/shard_map/all_gather | solution.py:86
  149.4 17.0 %convolution_bitcast_fusion = f32[4,64,1,4,3584]{4,1,3,0,2:T(8,128)} fusion(bf16[1,3584,256]{2,1,0:T(8,128)(2,1)} %param.24, bf16[1,3584,256]{2,1,0:T(8,128)(2,1)} %param.23, bf16[4,64,4,3584]{3,1,0,2:T(8,128)(2,1)} %bitcast.118), kind=kOutput, calls=%fused_computation.14 | convolution fusion | flops 3759407104 | bytes 25690112 | tf_op jit(solution)/shard_map/gsjcf,jdf->gsjcd/dot_general | solution.py:91
  166.4 0.0 reduce-scatter.2.cloned.1.call-update
  167.7 0.1 iota_compare_fusion.7
  167.8 0.1 broadcast_select_fusion.2
  167.9 0.5 broadcast.417
  168.4 0.7 reduce.28
  169.1 0.6 reshape.487
  169.7 3.6 all-to-all-start
  173.3 0.1 copy.88
  173.4 0.1 reduce.20
  173.5 0.1 compare_select_fusion
  173.6 0.1 reshape.461
  173.7 1.2 gather_fusion
  175.0 8.0 %gather_fusion.1 = bf16[128,64,576]{2,1,0:T(8,128)(2,1)} fusion(bf16[32,64,576]{2,1,0:T(8,128)(2,1)S(1)} %copy-done, s32[1024]{0:T(1024)S(1)} %pad_clamp_fusion), kind=kCustom, calls=%fused_computation.1 | custom fusion | bytes 18874880 | tf_op jit(solution)/shard_map/gather | solution.py:37
  183.0 0.1 broadcast_select_fusion.1
  183.1 1.2 constant_dynamic-slice_fusion.1
  184.3 0.7 reduce.27
  185.0 0.7 reshape.485
  185.6 0.2 copy.91
  185.9 4.2 %all-to-all-start.2 = ((bf16[4,2,288]{2,1,0:T(2,128)(2,1)}), bf16[4,2,288]{2,1,0:T(2,128)(2,1)S(1)}, u32[]{:S(2)}, u32[]{:S(2)}) async-start(bf16[4,2,288]{2,1,0:T(2,128)(2,1)} %reshape.485), calls=%async_computation.2 | async-start | bytes 12288 | tf_op jit(solution)/shard_map/all_to_all | solution.py:126
  190.1 1.6 broadcast_select_fusion
  191.8 2.6 all-to-all-done.2
  194.4 3.8 all-to-all-start.1
  198.2 7.9 %fusion.2 = f32[16,513,64]{1,2,0:T(8,128)S(1)} fusion(bf16[16,64,576]{2,1,0:T(8,128)(2,1)} %param.25, bf16[16,1,576]{2,1,0:T(2,128)(2,1)S(1)} %copy.89, bf16[16,512,576]{2,1,0:T(8,128)(2,1)} %bitcast.114), kind=kOutput, calls=%fused_computation.4 | convolution fusion | flops 624070656 | bytes 12736512 | tf_op jit(solution)/shard_map/bhk,blk->bhl/dot_general | solution.py:15
  206.2 2.4 fusion.93
  208.6 118.3 %reduce-scatter.2.cloned.1.call-done = f32[1,64,1,4,3584]{4,1,3,0,2:T(8,128)} async-done(((f32[4,64,1,4,3584]{4,1,3,0,2:T(8,128)}), f32[1,64,1,4,3584]{4,1,3,0,2:T(8,128)}) %reduce-scatter.2.cloned.1.call-update) | async-done | bytes 3670032 | tf_op jit(solution)/shard_map/reduce_scatter | solution.py:94
  326.8 2.2 convert_bitcast_fusion
  329.1 2.6 copy.101
  331.7 10.8 %all-to-all-start.4 = ((bf16[64,1,4,3584]{3,2,1,0:T(4,128)(2,1)}), bf16[64,1,4,3584]{3,2,1,0:T(4,128)(2,1)}, u32[]{:S(2)}, u32[]{:S(2)}) async-start(bf16[64,1,4,3584]{3,2,1,0:T(4,128)(2,1)} %copy.101), calls=%async_computation.5 | async-start | bytes 3670016 | tf_op jit(solution)/shard_map/all_to_all | solution.py:97
  342.5 0.0 copy-start.8
  342.5 0.0 copy-start.7
  342.6 7.2 %fusion.34 = bf16[16,64,512]{2,1,0:T(8,128)(2,1)} fusion(bf16[16,1,576]{2,1,0:T(2,128)(2,1)S(1)} %copy.89, bf16[16,512,576]{2,1,0:T(8,128)(2,1)} %bitcast.115, f32[16,64,513]{2,1,0:T(8,128)} %get-tuple-element.40, f32[16,64]{1,0:T(8,128)S(1)} %get-tuple-element.39), kind=kOutput, calls=%fused_computation.45 | convolution fusion | flops 556304384 | bytes 12609536 | tf_op jit(solution)/shard_map/bhl,blk->bhk/dot_general | solution.py:22
  349.7 0.1 copy.97
  349.8 0.1 mul.48
  350.0 0.7 and_reduce_fusion.1
  350.7 0.7 and_reduce_fusion
  351.4 0.3 fusion.68
  351.7 0.7 reshape_select_fusion
  352.4 0.1 reshape.486
  352.6 0.7 fusion.78
  353.2 0.7 reduce_sum.62
  354.0 0.3 copy.92
  354.3 2.8 fusion.66
  357.1 6.7 %fusion.6 = f32[16,514,64]{1,2,0:T(8,128)S(1)} fusion(bf16[16,64,576]{2,1,0:T(8,128)(2,1)S(1)} %copy-done.9, bf16[16,1,576]{2,1,0:T(2,128)(2,1)S(1)} %copy.95, bf16[16,1,576]{2,1,0:T(2,128)(2,1)S(1)} %fusion.78, bf16[16,512,576]{2,1,0:T(8,128)(2,1)} %fusion.66), kind=kOutput, calls=%fused_computation.8 | convolution fusion | flops 634761216 | bytes 12759040 | tf_op jit(solution)/shard_map/bhk,blk->bhl/dot_general | solution.py:15
  363.8 3.2 fusion.94
  367.0 5.7 %fusion.37 = bf16[16,64,512]{2,1,0:T(8,128)(2,1)} fusion(bf16[16,1,576]{2,1,0:T(2,128)(2,1)S(1)} %copy.95, bf16[16,1,576]{2,1,0:T(2,128)(2,1)S(1)} %fusion.78, bf16[16,512,576]{2,1,0:T(8,128)(2,1)} %fusion.66, f32[16,64,514]{2,1,0:T(8,128)S(1)} %get-tuple-element.42, f32[16,64]{1,0:T(8,128)S(1)} %get-tuple-element.41), kind=kOutput, calls=%fused_computation.46 | convolution fusion | flops 565809152 | bytes 12632064 | tf_op jit(solution)/shard_map/bhl,blk->bhk/dot_general | solution.py:22
  372.7 14.0 %all-to-all-done.4 = bf16[64,1,4,3584]{3,2,1,0:T(4,128)(2,1)} async-done(((bf16[64,1,4,3584]{3,2,1,0:T(4,128)(2,1)}), bf16[64,1,4,3584]{3,2,1,0:T(4,128)(2,1)}, u32[]{:S(2)}, u32[]{:S(2)}) %all-to-all-start.4) | async-done | bytes 1835040 | tf_op jit(solution)/shard_map/all_to_all | solution.py:97
  386.7 4.0 reshape.457
  390.7 3.0 convolution_convert_fusion.1
  (38 shorter events, 0.4 us)
Async XLA Ops:
  7.2 167.8 %copy-start = (bf16[32,64,576]{2,1,0:T(8,128)(2,1)S(1)}, bf16[32,64,576]{2,1,0:T(8,128)(2,1)}, u32[]{:S(2)}) copy-start(bf16[32,64,576]{2,1,0:T(8,128)(2,1)} %param.29) | copy-start | bytes 7077892
  7.2 142.2 %all-gather.3.cloned.1.call-start = ((), (), s32[]{:S(2)}) async-start(), calls=%async_computation.7 | async-start | bytes 9175040 | tf_op jit(solution)/shard_map/all_gather | solution.py:86
  74.6 252.2 %reduce-scatter.2.cloned.1.call-start = ((), (), s32[]{:S(2)}) async-start(), calls=%async_computation.6 | async-start | bytes 18350080 | tf_op jit(solution)/shard_map/reduce_scatter | solution.py:94
  166.4 1.4 copy-start.6
  166.4 7.3 %copy-start.2 = (s32[1,32]{1,0:T(1,128)S(1)}, s32[1,32]{1,0:T(1,128)}, u32[]{:S(2)}) copy-start(s32[1,32]{1,0:T(1,128)} %param.31) | copy-start | bytes 388
  169.7 16.2 %all-to-all-start = ((bf16[4,2,256]{2,1,0:T(2,128)(2,1)}), bf16[4,2,256]{2,1,0:T(2,128)(2,1)S(1)}, u32[]{:S(2)}, u32[]{:S(2)}) async-start(bf16[4,2,256]{2,1,0:T(2,128)(2,1)} %reshape.487), calls=%async_computation | async-start | bytes 8192 | tf_op jit(solution)/shard_map/all_to_all | solution.py:125
  175.0 8.0 %copy-start.3 = (bf16[16,576]{1,0:T(8,128)(2,1)S(1)}, bf16[16,576]{1,0:T(8,128)(2,1)}, u32[]{:S(2)}) copy-start(bf16[16,576]{1,0:T(8,128)(2,1)} %param.26) | copy-start | bytes 55300
  185.9 8.5 %all-to-all-start.2 = ((bf16[4,2,288]{2,1,0:T(2,128)(2,1)}), bf16[4,2,288]{2,1,0:T(2,128)(2,1)S(1)}, u32[]{:S(2)}, u32[]{:S(2)}) async-start(bf16[4,2,288]{2,1,0:T(2,128)(2,1)} %reshape.485), calls=%async_computation.2 | async-start | bytes 12288 | tf_op jit(solution)/shard_map/all_to_all | solution.py:126
  194.4 137.3 %all-to-all-start.1 = ((bf16[4,512,576]{1,2,0:T(8,128)(2,1)}), bf16[4,512,576]{1,2,0:T(8,128)(2,1)S(1)}, u32[]{:S(2)}, u32[]{:S(2)}) async-start(bf16[4,512,576]{1,2,0:T(8,128)(2,1)} %broadcast_select_fusion), calls=%async_computation.1 | async-start | bytes 4718592 | tf_op jit(solution)/shard_map/all_to_all | solution.py:124
  331.7 55.0 %all-to-all-start.4 = ((bf16[64,1,4,3584]{3,2,1,0:T(4,128)(2,1)}), bf16[64,1,4,3584]{3,2,1,0:T(4,128)(2,1)}, u32[]{:S(2)}, u32[]{:S(2)}) async-start(bf16[64,1,4,3584]{3,2,1,0:T(4,128)(2,1)} %copy.101), calls=%async_computation.5 | async-start | bytes 3670016 | tf_op jit(solution)/shard_map/all_to_all | solution.py:97
  342.5 7.2 %copy-start.5 = (f32[16,8]{0,1:T(8,128)S(1)}, f32[16,8]{0,1:T(8,128)}, u32[]{:S(2)}) copy-start(f32[16,8]{0,1:T(8,128)} %param.22) | copy-start | bytes 1540
  342.5 7.4 %copy-start.4 = (bf16[16,576]{1,0:T(8,128)(2,1)S(1)}, bf16[16,576]{1,0:T(8,128)(2,1)}, u32[]{:S(2)}) copy-start(bf16[16,576]{1,0:T(8,128)(2,1)} %param.28) | copy-start | bytes 55300
  342.5 7.4 %copy-start.8 = (s32[2]{0:T(128)S(1)}, s32[2]{0:T(128)}, u32[]{:S(2)}) copy-start(s32[2]{0:T(128)} %constant.130.clone.1) | copy-start | bytes 28
  342.5 8.1 %copy-start.7 = (s32[3]{0:T(128)S(1)}, s32[3]{0:T(128)}, u32[]{:S(2)}) copy-start(s32[3]{0:T(128)} %constant.133.clone.1) | copy-start | bytes 40
  354.0 3.1 copy-start.9
  367.0 26.7 %copy-start.1 = (bf16[32,64,576]{2,1,0:T(8,128)(2,1)S(1)}, bf16[32,64,576]{2,1,0:T(8,128)(2,1)}, u32[]{:S(2)}) copy-start(bf16[32,64,576]{2,1,0:T(8,128)(2,1)} %param.29) | copy-start | bytes 7077892
Sparse Core Ops, SparseCore 0:
  74.8 74.5 all-gather.2
  166.5 160.2 reduce-scatter.1
where the time goes:
time: 402 us; the launch traced here: 400 us
  waiting for transfers between devices  210 us (52%)
  blocking collectives  57.3 us (14%)
  matrix products  50.7 us (13%)
  local copies, waits for them, and re-layouts  26.5 us (7%)
  starting transfers between devices  22.5 us (6%)
  other arithmetic  18.2 us (5%)
  between operations  15.7 us (4%)
    reduce_scatter x1, waiting for transfers between devices, shards(): lax.psum_scatter(partial_value, 'grp', scatter_dimension=0, tiled=True)[0]  118 us
    all_gather x1, waiting for transfers between devices, shards(): lax.all_gather(arrived[None], 'grp', axis=0, tiled=True)  74.7 us
    all_to_all x1, blocking collectives, shards(): lax.all_to_all(outgoing, 'ep', split_axis=0, concat_axis=0, tiled=True)  57.3 us
    dot_general x1, matrix products, shards(): jnp.einsum('gsjcf,jdf->gsjcd', hidden_units, w_down, preferred_element_ty...  17 us
    dot_general x2, matrix products, attend(): jnp.einsum('bhk,blk->bhl', query_rows, key_rows, preferred_element_type=j...  14.6 us
    all_to_all x1, waiting for transfers between devices, shards(): lax.all_to_all(produced, 'ep', split_axis=0, concat_axis=0, tiled=True)  14 us
    dot_general x2, matrix products, attend(): jnp.einsum('bhl,blk->bhk', probability, key_rows[:, :, :LAT], preferred_e...  12.8 us
    all_to_all x1, starting transfers between devices, shards(): lax.all_to_all(produced, 'ep', split_axis=0, concat_axis=0, tiled=True)  10.8 us
  transfers between devices with their start and end apart: 6, of which 4 were waited for; matrix products, arithmetic and copies ran while one was open for 15% of the time, Pallas kernels for 0%

commit v1 on v0

v1 whole, which is shorter than its diff:
```python
import functools
import math

import jax
import jax.numpy as jnp
from jax import lax
from jax.experimental import pallas as pl
from jax.experimental.pallas import tpu as pltpu
from jax.sharding import PartitionSpec as P

LAT = 512
MAXP = 8
CHUNKS = 4
NEG = -1e30


def hop(value, axis, step):
    size = lax.axis_size(axis)
    return lax.ppermute(value, axis, [(i, (i + step) % size) for i in range(size)])


def attention_kernel(
    lens, pages, moved, q_one, q_two, q_in, kv_one, kv_two, kv_in, pool, out_one, out_two, out_moved, acc
):
    slot = pl.program_id(0)
    heads = q_one.shape[1]
    rows = 2 * heads
    key_width = q_one.shape[2]
    page_rows = pool.shape[1]
    block = 2 * page_rows
    scale = 1.0 / math.sqrt(key_width / 3.0)
    is_moved = slot == moved[0]
    second = jnp.where(is_moved, q_in[...], q_two[0])
    queries = jnp.concatenate([q_one[0], second], axis=0)
    fresh_one = kv_one[0]
    fresh_two = jnp.where(is_moved, kv_in[...], kv_two[0])
    fresh = jnp.concatenate(
        [fresh_one, fresh_two, jnp.zeros((14, key_width), jnp.bfloat16)], axis=0
    )
    contract = (((1,), (1,)), ((), ()))
    scores = lax.dot_general(queries, fresh, contract, preferred_element_type=jnp.float32) * scale
    row = lax.broadcasted_iota(jnp.int32, scores.shape, 0)
    col = lax.broadcasted_iota(jnp.int32, scores.shape, 1)
    scores = jnp.where((col == 0) | ((col == 1) & (row >= heads)), scores, NEG)
    top = jnp.max(scores, axis=1, keepdims=True)
    weights = jnp.exp(scores - top)
    total = jnp.sum(weights, axis=1, keepdims=True)
    acc[...] = jnp.dot(
        weights.astype(jnp.bfloat16), fresh[:, :LAT], preferred_element_type=jnp.float32
    )
    live = lens[slot]

    def step(b, carry):
        top, total = carry
        keys = jnp.concatenate(
            [pool[pages[slot * MAXP + 2 * b]], pool[pages[slot * MAXP + 2 * b + 1]]], axis=0
        )
        scores = (
            lax.dot_general(queries, keys, contract, preferred_element_type=jnp.float32) * scale
        )
        col = lax.broadcasted_iota(jnp.int32, scores.shape, 1) + b * block
        scores = jnp.where(col < live, scores, NEG)
        new_top = jnp.maximum(top, jnp.max(scores, axis=1, keepdims=True))
        shrink = jnp.exp(top - new_top)
        weights = jnp.exp(scores - new_top)
        total = total * shrink + jnp.sum(weights, axis=1, keepdims=True)
        acc[...] = acc[...] * shrink + jnp.dot(
            weights.astype(jnp.bfloat16), keys[:, :LAT], preferred_element_type=jnp.float32
        )
        return new_top, total

    top, total = lax.fori_loop(0, (live + block - 1) // block, step, (top, total))
    result = (acc[...] / total).astype(jnp.bfloat16)
    out_one[0] = result[:heads]
    out_two[0] = result[heads:]

    @pl.when(is_moved)
    def _():
        out_moved[...] = result[heads:]


def attention(lens, pages, moved, q_one, q_two, q_in, kv_one, kv_two, kv_in, pool):
    samples, heads, key_width = q_one.shape
    one = lambda *shape: pl.BlockSpec((1,) + shape, lambda i, *_: (i,) + (0,) * len(shape))
    whole = lambda *shape: pl.BlockSpec(shape, lambda i, *_: (0,) * len(shape))
    return pl.pallas_call(
        attention_kernel,
        grid_spec=pltpu.PrefetchScalarGridSpec(
            num_scalar_prefetch=3,
            grid=(samples,),
            in_specs=[
                one(heads, key_width),
                one(heads, key_width),
                whole(heads, key_width),
                one(1, key_width),
                one(1, key_width),
                whole(1, key_width),
                whole(*pool.shape),
            ],
            out_specs=[one(heads, LAT), one(heads, LAT), whole(heads, LAT)],
            scratch_shapes=[pltpu.VMEM((2 * heads, LAT), jnp.float32)],
        ),
        out_shape=[
            jax.ShapeDtypeStruct((samples, heads, LAT), jnp.bfloat16),
            jax.ShapeDtypeStruct((samples, heads, LAT), jnp.bfloat16),
            jax.ShapeDtypeStruct((heads, LAT), jnp.bfloat16),
        ],
        compiler_params=pltpu.CompilerParams(vmem_limit_bytes=24 * 1024 * 1024),
        cost_estimate=pl.CostEstimate(
            flops=12_000_000_000, bytes_accessed=8_000_000, transcendentals=1_000_000
        ),
        name="attention",
    )(lens, pages, moved, q_one, q_two, q_in, kv_one, kv_two, kv_in, pool)


def page_table(cache_len, page_perm, page_rows, pool_pages):
    used = (cache_len + page_rows - 1) // page_rows
    slots = used.shape[0]
    before = jnp.arange(slots)[None, :] < jnp.arange(slots)[:, None]
    offset = jnp.sum(jnp.where(before, used[None, :], 0), axis=1)
    place = jnp.minimum(
        offset[:, None] + jnp.arange(MAXP, dtype=jnp.int32)[None, :], pool_pages - 1
    ).reshape(-1)
    hit = place[:, None] == jnp.arange(pool_pages, dtype=jnp.int32)[None, :]
    return jnp.sum(jnp.where(hit, page_perm[None, :], 0), axis=1)


def shards(
    hidden,
    expert_ids,
    gate_weights,
    w_up,
    w_down,
    query_first,
    kv_first,
    query_second,
    kv_second,
    cache_pool,
    cache_len,
    page_perm,
    mig_slot,
    mig_dest,
):
    samples, picks = expert_ids.shape
    width = hidden.shape[1]
    ep_size = lax.axis_size("ep")
    grp_size = lax.axis_size("grp")
    capacity = min(samples, max(2, 2 * samples * picks // ep_size))
    slots_all = ep_size * capacity
    me = lax.axis_index("grp")

    up, down = w_up[0], w_down[0]
    half = width // 2
    piece = width // CHUNKS
    up_parts = [up[:half], up[half:]]
    up_prev = [hop(p, "grp", 1) for p in up_parts]
    up_next = [hop(p, "grp", -1) for p in reversed(up_parts)][::-1]
    up_far = [hop(up_prev[0], "grp", 1), hop(up_next[1], "grp", -1)]
    down_all = []
    for c in range(CHUNKS):
        mid = piece // 2
        own = down[c * piece : (c + 1) * piece]
        parts = [own[:mid], own[mid:]]
        prev = [hop(p, "grp", 1) for p in parts]
        nxt = [hop(p, "grp", -1) for p in reversed(parts)][::-1]
        far = [hop(prev[0], "grp", 1), hop(nxt[1], "grp", -1)]
        down_all.append((parts, prev, nxt, far))

    moved_slot = mig_slot[0, 0]
    moved_target = mig_dest[0, 0]
    q_here = lax.dynamic_index_in_dim(query_second, moved_slot, 0, keepdims=False)
    kv_here = lax.dynamic_index_in_dim(kv_second, moved_slot, 0, keepdims=True)
    packet = jnp.concatenate(
        [q_here, kv_here, jnp.zeros((15, q_here.shape[1]), jnp.bfloat16)], axis=0
    )
    offset = (moved_target - me) % grp_size
    got = packet
    for step in range(1, grp_size):
        got = jnp.where(offset == step, hop(packet, "grp", -step), got)
    heads = q_here.shape[0]
    q_in, kv_in = got[:heads], got[heads : heads + 1]

    lens = cache_len[0]
    pages = page_table(lens, page_perm[0], cache_pool.shape[1], cache_pool.shape[0])
    attn_first, attn_second, out_moved = attention(
        lens,
        pages,
        moved_slot[None],
        query_first,
        query_second,
        q_in,
        kv_first[:, None, :],
        kv_second[:, None, :],
        kv_in,
        cache_pool,
    )
    zero = jnp.zeros((), jnp.bfloat16)
    arrived_out = jnp.where(offset == 0, out_moved, zero)
    for step in range(1, grp_size):
        arrived_out = arrived_out + hop(jnp.where(offset == step, out_moved, zero), "grp", step)
    attn_second = lax.dynamic_update_index_in_dim(attn_second, arrived_out, moved_slot, 0)

    flat_ids = expert_ids.reshape(-1)
    entries = flat_ids.shape[0]
    hits = flat_ids[:, None] == jnp.arange(ep_size, dtype=jnp.int32)[None, :]
    order = jnp.arange(entries, dtype=jnp.int32)
    lower = (order[None, :] < order[:, None]).astype(jnp.bfloat16)
    ahead = jnp.dot(lower, hits.astype(jnp.bfloat16), preferred_element_type=jnp.float32)
    earlier = jnp.sum(jnp.where(hits, ahead, 0.0), axis=1).astype(jnp.int32)
    slot_index = (flat_ids * capacity + earlier).reshape(samples, picks)
    slot_range = jnp.arange(slots_all, dtype=jnp.int32)
    match = slot_index[:, :, None] == slot_range[None, None, :]
    placing = jnp.sum(match.astype(jnp.float32), axis=1).astype(jnp.bfloat16)
    mixing = jnp.sum(jnp.where(match, gate_weights[:, :, None], 0.0), axis=1)
    outgoing = lax.dot_general(
        placing, hidden, (((0,), (0,)), ((), ())), preferred_element_type=jnp.float32
    ).astype(jnp.bfloat16)
    arrived = lax.all_to_all(
        outgoing.reshape(ep_size, capacity, width), "ep", split_axis=0, concat_axis=0, tiled=True
    ).reshape(slots_all, width)

    f32dot = functools.partial(jnp.dot, preferred_element_type=jnp.float32)

    def act(v):
        return jax.nn.silu(v).astype(jnp.bfloat16)

    def up_of(parts):
        return act(f32dot(arrived[:, :half], parts[0]) + f32dot(arrived[:, half:], parts[1]))

    h_all = [up_of(p) for p in (up_parts, up_prev, up_next, up_far)]
    contract = (((1,), (1,)), ((), ()))
    results = []
    for c in range(CHUNKS):
        cols = []
        for s in range(2):
            total = 0.0
            for h, parts in zip(h_all, down_all[c]):
                total = total + lax.dot_general(
                    h, parts[s], contract, preferred_element_type=jnp.float32
                )
            cols.append(total.astype(jnp.bfloat16))
        produced = jnp.concatenate(cols, axis=1)
        returned = lax.all_to_all(
            produced.reshape(ep_size, capacity, piece), "ep", split_axis=0, concat_axis=0, tiled=True
        ).reshape(slots_all, piece)
        results.append(
            jnp.dot(
                mixing,
                returned.astype(jnp.float32),
                preferred_element_type=jnp.float32,
                precision=lax.Precision.HIGHEST,
            ).astype(jnp.bfloat16)
        )
    moe_out = jnp.concatenate(results, axis=1)
    return (attn_first, attn_second, moe_out)


def solution(mesh):
    return jax.shard_map(
        shards,
        mesh=mesh,
        in_specs=(
            P(("ep", "grp"), None),
            P(("ep", "grp"), None),
            P(("ep", "grp"), None),
            P("ep", None, "grp"),
            P("ep", None, "grp"),
            P(("ep", "grp"), None, None),
            P(("ep", "grp"), None),
            P(("ep", "grp"), None, None),
            P(("ep", "grp"), None),
            P(("ep", "grp"), None, None),
            P(("ep", "grp"), None),
            P(("ep", "grp"), None),
            P("ep", "grp"),
            P("ep", "grp"),
        ),
        out_specs=(
            P(("ep", "grp"), None, None),
            P(("ep", "grp"), None, None),
            P(("ep", "grp"), None),
        ),
        check_vma=False,
    )
```

time: 402 us -> 295 us (0.73)
  waiting for transfers between devices: 210 us -> 103 us
  starting transfers between devices: 22.5 us -> 106 us
  blocking collectives: 57.3 us -> 0 us
  Pallas kernels: 0 us -> 18.5 us
  matrix products: 50.7 us -> 34.8 us
  other arithmetic: 18.2 us -> 5.24 us
  between operations: 15.7 us -> 3.05 us
  local copies, waits for them, and re-layouts: 26.5 us -> 19.6 us
    reduce_scatter x1 -> x0, waiting for transfers between devices: 118 us -> none  [shards(): lax.psum_scatter(partial_value, 'grp', scatter_dimension=0, tiled=True)[0]]
    ppermute x0 -> x36, waiting for transfers between devices: none -> 75.1 us  [hop(): lax.ppermute(value, axis, [(i, (i + step) % size) for i in range(size)])]
    all_gather x1 -> x0, waiting for transfers between devices: 74.7 us -> none  [shards(): lax.all_gather(arrived[None], 'grp', axis=0, tiled=True)]
    all_to_all x1 -> x0, blocking collectives: 57.3 us -> none  [shards(): lax.all_to_all(outgoing, 'ep', split_axis=0, concat_axis=0, tiled=True)]
    ppermute x0 -> x36, starting transfers between devices: none -> 46.3 us  [hop(): lax.ppermute(value, axis, [(i, (i + step) % size) for i in range(size)])]
    all_to_all x4 -> x5, starting transfers between devices: 22.4 us -> 59.4 us  [the longest x4 46.4 us: shards(): lax.all_to_all(produced.reshape(ep_size, capacity, piece), 'ep', split_ax...]
    pallas_call x0 -> x1, Pallas kernels: none -> 18.5 us  [attention(): pl.pallas_call(attention_kernel, grid_spec=pltpu.PrefetchScalarGridSpec(n...]
    dot_general x9 -> x46, matrix products: 50.7 us -> 34.8 us  [the longest x32 21.8 us: shards(): lax.dot_general(h, parts[s], contract, preferred_element_type=jnp.float32)]
  transfers between devices with their start and end apart: 6 -> 41, of which waited for: 4 -> 14; matrix products, arithmetic and copies ran while one was open for 15% -> 19% of each run, Pallas kernels for 0% -> 6%
where the time goes in v1:
time: 295 us; the launch traced here: 290 us
  starting transfers between devices  106 us (36%)
  waiting for transfers between devices  103 us (35%)
  matrix products  34.8 us (12%)
  local copies, waits for them, and re-layouts  19.6 us (7%)
  Pallas kernels  18.5 us (6%)
  other arithmetic  5.24 us (2%)
  between operations  3.05 us (1%)
    ppermute x36, waiting for transfers between devices, hop(): lax.ppermute(value, axis, [(i, (i + step) % size) for i in range(size)])  75.1 us
    all_to_all x4, starting transfers between devices, shards(): lax.all_to_all(produced.reshape(ep_size, capacity, piece), 'ep', split_ax...  46.4 us
    ppermute x36, starting transfers between devices, hop(): lax.ppermute(value, axis, [(i, (i + step) % size) for i in range(size)])  46.3 us
    all_to_all x4, waiting for transfers between devices, shards(): lax.all_to_all(produced.reshape(ep_size, capacity, piece), 'ep', split_ax...  27.9 us
    dot_general x32, matrix products, shards(): lax.dot_general(h, parts[s], contract, preferred_element_type=jnp.float32)  21.8 us
    pallas_call x1, Pallas kernels, attention(): pl.pallas_call(attention_kernel, grid_spec=pltpu.PrefetchScalarGridSpec(n...  18.5 us
    all_to_all x1, starting transfers between devices, shards(): lax.all_to_all(outgoing.reshape(ep_size, capacity, width), 'ep', split_ax...  13 us
  transfers between devices with their start and end apart: 41, of which 14 were waited for; matrix products, arithmetic and copies ran while one was open for 19% of the time, Pallas kernels for 6%

profile of v1, /device:TPU:1, one launch (start us, length us, event | category | flops | bytes accessed | tf_op | source)
XLA Modules:
  0.0 289.9 jit_solution(15175049693729782655)
XLA Ops:
  3.4 1.5 reshape.79
  4.9 13.0 %all-to-all-start = ((bf16[64,4,3584]{2,1,0:T(4,128)(2,1)}), bf16[64,4,3584]{2,1,0:T(4,128)(2,1)S(1)}, u32[]{:S(2)}, u32[]{:S(2)}) async-start(bf16[64,4,3584]{2,1,0:T(4,128)(2,1)} %reshape.79), calls=%async_computation | async-start | bytes 3670016 | tf_op jit(solution)/shard_map/all_to_all | solution.py:218
  17.9 2.9 %slice_bitcast_fusion.1 = (bf16[1792,256]{1,0:T(8,128)(2,1)}, bf16[1792,256]{1,0:T(8,128)(2,1)}) fusion(bf16[1,3584,256]{2,1,0:T(8,128)(2,1)} %param.17), kind=kLoop, calls=%fused_computation.44 | loop fusion | bytes 3670016 | tf_op jit(solution)/shard_map/slice | solution.py:155
  20.9 1.3 collective-permute-start.7
  22.2 1.4 collective-permute-start.10
  25.1 2.6 collective-permute-start.1
  27.8 1.1 collective-permute-start.2
  29.9 3.0 %slice_bitcast_fusion.9 = (bf16[448,256]{1,0:T(8,128)(2,1)}, bf16[448,256]{1,0:T(8,128)(2,1)}, bf16[448,256]{1,0:T(8,128)(2,1)}, bf16[448,256]{1,0:T(8,128)(2,1)...) fusion(bf16[1,3584,256]{2,1,0:T(8,128)(2,1)} %param.18), kind=kLoop, calls=%fused_computation.72 | loop fusion | bytes 3670016 | tf_op jit(solution)/shard_map/slice | solution.py:163
  33.0 13.1 %collective-permute-done = bf16[80,576]{1,0:T(8,128)(2,1)} collective-permute-done((bf16[80,576]{1,0:T(8,128)(2,1)}, bf16[80,576]{1,0:T(8,128)(2,1)}, u32[]{:S(2)}, u32[]{:S(2)}) %collective-permute-start) | collective-permute-done | bytes 92192 | tf_op jit(solution)/shard_map/ppermute | solution.py:19
  46.2 3.3 %collective-permute-done.1 = bf16[80,576]{1,0:T(8,128)(2,1)} collective-permute-done((bf16[80,576]{1,0:T(8,128)(2,1)}, bf16[80,576]{1,0:T(8,128)(2,1)}, u32[]{:S(2)}, u32[]{:S(2)}) %collective-permute-start.1) | collective-permute-done | bytes 92192 | tf_op jit(solution)/shard_map/ppermute | solution.py:19
  49.5 1.5 collective-permute-start.8
  52.0 18.5 %attention.1 = (bf16[16,64,512]{2,1,0:T(8,128)(2,1)}, bf16[16,64,512]{2,1,0:T(8,128)(2,1)}, bf16[64,512]{1,0:T(8,128)(2,1)S(1)}) custom-call(s32[16]{0:T(128)S(1)} %bitcast.120, s32[128]{0:T(128)S(1)} %select_reduce_fusion.1.pages, s32[1]{0:T(128)} %bitcast.115.moved, bf16[16,64,576]{2,1,0:T(8,128)(2,1)S(1)} %copy-done.3, ...), custom_call_target="tpu_custom_call" | custom-call | flops 12000000000 | bytes 8000000 | tf_op jit(solution)/shard_map/attention/pallas_call | solution.py:86
  70.5 1.2 collective-permute-start.13
  72.4 1.5 reshape.80
  73.9 2.0 fusion.19
  75.9 1.6 fusion.11
  77.7 1.7 fusion.13
  79.4 1.7 collective-permute-start.15
  81.1 9.3 %collective-permute-done.13 = bf16[1792,256]{1,0:T(8,128)(2,1)} collective-permute-done((bf16[1792,256]{1,0:T(8,128)(2,1)}, bf16[1792,256]{1,0:T(8,128)(2,1)}, u32[]{:S(2)}, u32[]{:S(2)}) %collective-permute-start.13) | collective-permute-done | bytes 917536 | tf_op jit(solution)/shard_map/ppermute | solution.py:19
  90.4 1.6 fusion.9
  92.4 1.6 multiply_convert_fusion.2
  94.1 2.7 collective-permute-start.16
  96.8 1.6 multiply_convert_fusion.1
  98.4 9.5 %collective-permute-done.12 = bf16[1792,256]{1,0:T(8,128)(2,1)S(1)} collective-permute-done((bf16[1792,256]{1,0:T(8,128)(2,1)}, bf16[1792,256]{1,0:T(8,128)(2,1)S(1)}, u32[]{:S(2)}, u32[]{:S(2)}) %collective-permute-start.12) | collective-permute-done | bytes 917536 | tf_op jit(solution)/shard_map/ppermute | solution.py:19
  108.6 2.8 collective-permute-start.19
  111.4 1.2 convolution_add_fusion.23
  113.2 2.7 collective-permute-start.22
  116.6 8.2 %collective-permute-done.14 = bf16[448,256]{1,0:T(8,128)(2,1)S(1)} collective-permute-done((bf16[448,256]{1,0:T(8,128)(2,1)}, bf16[448,256]{1,0:T(8,128)(2,1)S(1)}, u32[]{:S(2)}, u32[]{:S(2)}) %collective-permute-start.14) | collective-permute-done | bytes 229408 | tf_op jit(solution)/shard_map/ppermute | solution.py:19
  125.0 5.8 %collective-permute-done.17 = bf16[448,256]{1,0:T(8,128)(2,1)S(1)} collective-permute-done((bf16[448,256]{1,0:T(8,128)(2,1)S(1)}, bf16[448,256]{1,0:T(8,128)(2,1)S(1)}, u32[]{:S(2)}, u32[]{:S(2)}) %collective-permute-start.17) | collective-permute-done | bytes 229408 | tf_op jit(solution)/shard_map/ppermute | solution.py:19
  132.9 18.9 %all-to-all-start.1 = ((bf16[64,4,896]{2,1,0:T(4,128)(2,1)}), bf16[64,4,896]{2,1,0:T(4,128)(2,1)S(1)}, u32[]{:S(2)}, u32[]{:S(2)}) async-start(bf16[64,4,896]{2,1,0:T(4,128)(2,1)} %reshape.81), calls=%async_computation.1 | async-start | bytes 917504 | tf_op jit(solution)/shard_map/all_to_all | solution.py:243
  152.0 3.0 %collective-permute-start.25 = (bf16[448,256]{1,0:T(8,128)(2,1)}, bf16[448,256]{1,0:T(8,128)(2,1)S(1)}, u32[]{:S(2)}, u32[]{:S(2)}) collective-permute-start(bf16[448,256]{1,0:T(8,128)(2,1)} %get-tuple-element.13), channel_id=1, source_target_pairs={{0,3},{1,0},{2,1},{3,2},{4,7},{5,4},{6,5},{7,6},{8,11},{9,8},{10,9... | collective-permute-start | bytes 688136 | tf_op jit(solution)/shard_map/ppermute | solution.py:19
  155.1 1.2 convolution_add_fusion.17
  156.3 8.9 %collective-permute-start.27 = (bf16[448,256]{1,0:T(8,128)(2,1)}, bf16[448,256]{1,0:T(8,128)(2,1)S(1)}, u32[]{:S(2)}, u32[]{:S(2)}) collective-permute-start(bf16[448,256]{1,0:T(8,128)(2,1)} %get-tuple-element.12), channel_id=1, source_target_pairs={{0,1},{1,2},{2,3},{3,0},{4,5},{5,6},{6,7},{7,4},{8,9},{9,10},{10,1... | collective-permute-start | bytes 688136 | tf_op jit(solution)/shard_map/ppermute | solution.py:19
  165.2 1.2 convolution_add_fusion.16
  166.6 2.7 collective-permute-start.28
  169.4 1.2 convolution_add_fusion.14
  170.7 1.2 convolution_add_fusion.13
  172.1 2.7 collective-permute-start.31
  174.9 1.2 convolution_add_fusion.11
  176.2 1.0 convolution_add_fusion.10
  177.6 1.0 convolution_add_fusion.8
  178.6 9.1 %collective-permute-done.20 = bf16[448,256]{1,0:T(8,128)(2,1)S(1)} collective-permute-done((bf16[448,256]{1,0:T(8,128)(2,1)}, bf16[448,256]{1,0:T(8,128)(2,1)S(1)}, u32[]{:S(2)}, u32[]{:S(2)}) %collective-permute-start.20) | collective-permute-done | bytes 229408 | tf_op jit(solution)/shard_map/ppermute | solution.py:19
  188.0 4.8 %collective-permute-done.23 = bf16[448,256]{1,0:T(8,128)(2,1)S(1)} collective-permute-done((bf16[448,256]{1,0:T(8,128)(2,1)}, bf16[448,256]{1,0:T(8,128)(2,1)S(1)}, u32[]{:S(2)}, u32[]{:S(2)}) %collective-permute-start.23) | collective-permute-done | bytes 229408 | tf_op jit(solution)/shard_map/ppermute | solution.py:19
  192.8 1.2 collective-permute-start.34
  195.3 2.0 reshape.83
  197.6 1.4 convolution_add_fusion.7
  199.0 4.6 %collective-permute-done.26 = bf16[448,256]{1,0:T(8,128)(2,1)S(1)} collective-permute-done((bf16[448,256]{1,0:T(8,128)(2,1)}, bf16[448,256]{1,0:T(8,128)(2,1)S(1)}, u32[]{:S(2)}, u32[]{:S(2)}) %collective-permute-start.26) | collective-permute-done | bytes 229408 | tf_op jit(solution)/shard_map/ppermute | solution.py:19
  203.9 4.8 %collective-permute-done.29 = bf16[448,256]{1,0:T(8,128)(2,1)S(1)} collective-permute-done((bf16[448,256]{1,0:T(8,128)(2,1)}, bf16[448,256]{1,0:T(8,128)(2,1)S(1)}, u32[]{:S(2)}, u32[]{:S(2)}) %collective-permute-start.29) | collective-permute-done | bytes 229408 | tf_op jit(solution)/shard_map/ppermute | solution.py:19
  210.0 1.9 reshape.85
  211.9 16.2 %all-to-all-start.2 = ((bf16[64,4,896]{2,1,0:T(4,128)(2,1)}), bf16[64,4,896]{2,1,0:T(4,128)(2,1)S(1)}, u32[]{:S(2)}, u32[]{:S(2)}) async-start(bf16[64,4,896]{2,1,0:T(4,128)(2,1)} %reshape.83), calls=%async_computation.2 | async-start | bytes 917504 | tf_op jit(solution)/shard_map/all_to_all | solution.py:243
  228.4 2.4 collective-permute-start.4
  230.8 2.0 convolution_add_fusion.5
  233.9 1.2 convolution_add_fusion.2
  236.1 8.4 %all-to-all-done.2 = bf16[64,4,896]{2,1,0:T(4,128)(2,1)S(1)} async-done(((bf16[64,4,896]{2,1,0:T(4,128)(2,1)}), bf16[64,4,896]{2,1,0:T(4,128)(2,1)S(1)}, u32[]{:S(2)}, u32[]{:S(2)}) %all-to-all-start.2) | async-done | bytes 458784 | tf_op jit(solution)/shard_map/all_to_all | solution.py:243
  244.5 5.7 %all-to-all-start.3 = ((bf16[64,4,896]{2,1,0:T(4,128)(2,1)}), bf16[64,4,896]{2,1,0:T(4,128)(2,1)S(1)}, u32[]{:S(2)}, u32[]{:S(2)}) async-start(bf16[64,4,896]{2,1,0:T(4,128)(2,1)} %reshape.85), calls=%async_computation.3 | async-start | bytes 917504 | tf_op jit(solution)/shard_map/all_to_all | solution.py:243
  250.2 1.2 convolution_add_fusion.1
  251.4 2.9 %collective-permute-start.35 = (bf16[448,256]{1,0:T(8,128)(2,1)}, bf16[448,256]{1,0:T(8,128)(2,1)S(1)}, u32[]{:S(2)}, u32[]{:S(2)}) collective-permute-start(bf16[448,256]{1,0:T(8,128)(2,1)} %collective-permute-done.34), channel_id=1, source_target_pairs={{0,3},{1,0},{2,1},{3,2},{4,7},{5,4},{6,5},{7,6},{8,11},{9,8},{10,9... | collective-permute-start | bytes 688136 | tf_op jit(solution)/shard_map/ppermute | solution.py:19
  254.3 1.2 convolution_add_fusion.4
  255.5 1.2 fusion.6
  256.7 2.4 collective-permute-done.35
  260.6 6.0 %all-to-all-done.3 = bf16[64,4,896]{2,1,0:T(4,128)(2,1)S(1)} async-done(((bf16[64,4,896]{2,1,0:T(4,128)(2,1)}), bf16[64,4,896]{2,1,0:T(4,128)(2,1)S(1)}, u32[]{:S(2)}, u32[]{:S(2)}) %all-to-all-start.3) | async-done | bytes 458784 | tf_op jit(solution)/shard_map/all_to_all | solution.py:243
  266.6 5.7 %all-to-all-start.4 = ((bf16[64,4,896]{2,1,0:T(4,128)(2,1)}), bf16[64,4,896]{2,1,0:T(4,128)(2,1)S(1)}, u32[]{:S(2)}, u32[]{:S(2)}) async-start(bf16[64,4,896]{2,1,0:T(4,128)(2,1)} %reshape.87), calls=%async_computation.4 | async-start | bytes 917504 | tf_op jit(solution)/shard_map/all_to_all | solution.py:243
  272.2 1.6 bitcast_dynamic-update-slice_fusion
  275.1 13.5 %all-to-all-done.4 = bf16[64,4,896]{2,1,0:T(4,128)(2,1)S(1)} async-done(((bf16[64,4,896]{2,1,0:T(4,128)(2,1)}), bf16[64,4,896]{2,1,0:T(4,128)(2,1)S(1)}, u32[]{:S(2)}, u32[]{:S(2)}) %all-to-all-start.4) | async-done | bytes 458784 | tf_op jit(solution)/shard_map/all_to_all | solution.py:243
  (138 shorter events, 21.3 us)
Async XLA Ops:
  0.6 2.1 copy-start
  4.9 67.5 %all-to-all-start = ((bf16[64,4,3584]{2,1,0:T(4,128)(2,1)}), bf16[64,4,3584]{2,1,0:T(4,128)(2,1)S(1)}, u32[]{:S(2)}, u32[]{:S(2)}) async-start(bf16[64,4,3584]{2,1,0:T(4,128)(2,1)} %reshape.79), calls=%async_computation | async-start | bytes 3670016 | tf_op jit(solution)/shard_map/all_to_all | solution.py:218
  17.9 6.4 %copy-start.11 = (bf16[16,576]{1,0:T(8,128)(2,1)S(1)}, bf16[16,576]{1,0:T(8,128)(2,1)}, u32[]{:S(2)}) copy-start(bf16[16,576]{1,0:T(8,128)(2,1)} %param.22) | copy-start | bytes 55300
  17.9 6.5 %copy-start.1 = (bf16[16,64,576]{2,1,0:T(8,128)(2,1)S(1)}, bf16[16,64,576]{2,1,0:T(8,128)(2,1)}, u32[]{:S(2)}) copy-start(bf16[16,64,576]{2,1,0:T(8,128)(2,1)} %q_two.1) | copy-start | bytes 3538948
  17.9 11.6 %copy-start.12 = (bf16[16,576]{1,0:T(8,128)(2,1)S(1)}, bf16[16,576]{1,0:T(8,128)(2,1)}, u32[]{:S(2)}) copy-start(bf16[16,576]{1,0:T(8,128)(2,1)} %param.20) | copy-start | bytes 55300
  17.9 11.7 %copy-start.4 = (s32[1,16]{1,0:T(1,128)S(1)}, s32[1,16]{1,0:T(1,128)}, u32[]{:S(2)}) copy-start(s32[1,16]{1,0:T(1,128)} %param.24) | copy-start | bytes 196
  20.9 56.7 %collective-permute-start.7 = (bf16[1792,256]{1,0:T(8,128)(2,1)}, bf16[1792,256]{1,0:T(8,128)(2,1)}, u32[]{:S(2)}, u32[]{:S(2)}) collective-permute-start(bf16[1792,256]{1,0:T(8,128)(2,1)} %get-tuple-element.20), channel_id=1, source_target_pairs={{0,1},{1,2},{2,3},{3,0},{4,5},{5,6},{6,7},{7,4},{8,9},{9,10},{10,1... | collective-permute-start | bytes 2752520 | tf_op jit(solution)/shard_map/ppermute | solution.py:19
  22.2 48.4 %collective-permute-start.10 = (bf16[1792,256]{1,0:T(8,128)(2,1)}, bf16[1792,256]{1,0:T(8,128)(2,1)}, u32[]{:S(2)}, u32[]{:S(2)}) collective-permute-start(bf16[1792,256]{1,0:T(8,128)(2,1)} %get-tuple-element.20), channel_id=1, source_target_pairs={{0,3},{1,0},{2,1},{3,2},{4,7},{5,4},{6,5},{7,6},{8,11},{9,8},{10,9... | collective-permute-start | bytes 2752520 | tf_op jit(solution)/shard_map/ppermute | solution.py:19
  25.1 21.1 %collective-permute-start = (bf16[80,576]{1,0:T(8,128)(2,1)}, bf16[80,576]{1,0:T(8,128)(2,1)}, u32[]{:S(2)}, u32[]{:S(2)}) collective-permute-start(bf16[80,576]{1,0:T(8,128)(2,1)} %maximum_maximum_fusion), channel_id=1, source_target_pairs={{0,1},{1,2},{2,3},{3,0},{4,5},{5,6},{6,7},{7,4},{8,9},{9,10},{10,1... | collective-permute-start | bytes 276488 | tf_op jit(solution)/shard_map/ppermute | solution.py:19
  25.1 24.3 %collective-permute-start.1 = (bf16[80,576]{1,0:T(8,128)(2,1)}, bf16[80,576]{1,0:T(8,128)(2,1)}, u32[]{:S(2)}, u32[]{:S(2)}) collective-permute-start(bf16[80,576]{1,0:T(8,128)(2,1)} %maximum_maximum_fusion), channel_id=1, source_target_pairs={{0,2},{1,3},{2,0},{3,1},{4,6},{5,7},{6,4},{7,5},{8,10},{9,11},{10,... | collective-permute-start | bytes 276488 | tf_op jit(solution)/shard_map/ppermute | solution.py:19
  27.8 21.7 %collective-permute-start.2 = (bf16[80,576]{1,0:T(8,128)(2,1)}, bf16[80,576]{1,0:T(8,128)(2,1)}, u32[]{:S(2)}, u32[]{:S(2)}) collective-permute-start(bf16[80,576]{1,0:T(8,128)(2,1)} %maximum_maximum_fusion), channel_id=1, source_target_pairs={{0,3},{1,0},{2,1},{3,2},{4,7},{5,4},{6,5},{7,6},{8,11},{9,8},{10,9... | collective-permute-start | bytes 276488 | tf_op jit(solution)/shard_map/ppermute | solution.py:19
  29.5 3.5 %copy-start.13 = (s32[1,32]{1,0:T(1,128)S(1)}, s32[1,32]{1,0:T(1,128)}, u32[]{:S(2)}) copy-start(s32[1,32]{1,0:T(1,128)} %param.25) | copy-start | bytes 388
  29.9 22.1 %copy-start.2 = (bf16[32,64,576]{2,1,0:T(8,128)(2,1)S(1)}, bf16[32,64,576]{2,1,0:T(8,128)(2,1)}, u32[]{:S(2)}) copy-start(bf16[32,64,576]{2,1,0:T(8,128)(2,1)} %pool.1) | copy-start | bytes 7077892
  29.9 22.1 %copy-start.3 = (bf16[16,64,576]{2,1,0:T(8,128)(2,1)S(1)}, bf16[16,64,576]{2,1,0:T(8,128)(2,1)}, u32[]{:S(2)}) copy-start(bf16[16,64,576]{2,1,0:T(8,128)(2,1)} %q_one.1) | copy-start | bytes 3538948
  46.2 33.2 %collective-permute-start.6 = (bf16[1792,256]{1,0:T(8,128)(2,1)}, bf16[1792,256]{1,0:T(8,128)(2,1)}, u32[]{:S(2)}, u32[]{:S(2)}) collective-permute-start(bf16[1792,256]{1,0:T(8,128)(2,1)} %get-tuple-element.19), channel_id=1, source_target_pairs={{0,1},{1,2},{2,3},{3,0},{4,5},{5,6},{6,7},{7,4},{8,9},{9,10},{10,1... | collective-permute-start | bytes 2752520 | tf_op jit(solution)/shard_map/ppermute | solution.py:19
  49.5 44.6 %collective-permute-start.9 = (bf16[1792,256]{1,0:T(8,128)(2,1)}, bf16[1792,256]{1,0:T(8,128)(2,1)}, u32[]{:S(2)}, u32[]{:S(2)}) collective-permute-start(bf16[1792,256]{1,0:T(8,128)(2,1)} %get-tuple-element.19), channel_id=1, source_target_pairs={{0,3},{1,0},{2,1},{3,2},{4,7},{5,4},{6,5},{7,6},{8,11},{9,8},{10,9... | collective-permute-start | bytes 2752520 | tf_op jit(solution)/shard_map/ppermute | solution.py:19
  49.5 59.1 %collective-permute-start.8 = (bf16[448,256]{1,0:T(8,128)(2,1)}, bf16[448,256]{1,0:T(8,128)(2,1)}, u32[]{:S(2)}, u32[]{:S(2)}) collective-permute-start(bf16[448,256]{1,0:T(8,128)(2,1)} %get-tuple-element.11), channel_id=1, source_target_pairs={{0,1},{1,2},{2,3},{3,0},{4,5},{5,6},{6,7},{7,4},{8,9},{9,10},{10,1... | collective-permute-start | bytes 688136 | tf_op jit(solution)/shard_map/ppermute | solution.py:19
  70.5 19.8 %collective-permute-start.13 = (bf16[1792,256]{1,0:T(8,128)(2,1)}, bf16[1792,256]{1,0:T(8,128)(2,1)}, u32[]{:S(2)}, u32[]{:S(2)}) collective-permute-start(bf16[1792,256]{1,0:T(8,128)(2,1)} %collective-permute-done.10), channel_id=1, source_target_pairs={{0,3},{1,0},{2,1},{3,2},{4,7},{5,4},{6,5},{7,6},{8,11},{9,8},{10,9... | collective-permute-start | bytes 2752520 | tf_op jit(solution)/shard_map/ppermute | solution.py:19
  73.9 2.1 copy-start.7
  75.9 3.5 %copy-start.10 = (bf16[448,256]{1,0:T(8,128)(2,1)S(1)}, bf16[448,256]{1,0:T(8,128)(2,1)}, u32[]{:S(2)}) copy-start(bf16[448,256]{1,0:T(8,128)(2,1)} %get-tuple-element.16) | copy-start | bytes 688132
  77.6 14.4 %copy-start.6 = (bf16[1,3584,256]{2,1,0:T(8,128)(2,1)S(1)}, bf16[1,3584,256]{2,1,0:T(8,128)(2,1)}, u32[]{:S(2)}) copy-start(bf16[1,3584,256]{2,1,0:T(8,128)(2,1)} %param.17) | copy-start | bytes 5505028
  77.6 35.6 %collective-permute-start.11 = (bf16[448,256]{1,0:T(8,128)(2,1)}, bf16[448,256]{1,0:T(8,128)(2,1)S(1)}, u32[]{:S(2)}, u32[]{:S(2)}) collective-permute-start(bf16[448,256]{1,0:T(8,128)(2,1)} %get-tuple-element.11), channel_id=1, source_target_pairs={{0,3},{1,0},{2,1},{3,2},{4,7},{5,4},{6,5},{7,6},{8,11},{9,8},{10,9... | collective-permute-start | bytes 688136 | tf_op jit(solution)/shard_map/ppermute | solution.py:19
  79.4 33.4 %collective-permute-start.15 = (bf16[448,256]{1,0:T(8,128)(2,1)S(1)}, bf16[448,256]{1,0:T(8,128)(2,1)S(1)}, u32[]{:S(2)}, u32[]{:S(2)}) collective-permute-start(bf16[448,256]{1,0:T(8,128)(2,1)S(1)} %copy-done.10), channel_id=1, source_target_pairs={{0,1},{1,2},{2,3},{3,0},{4,5},{5,6},{6,7},{7,4},{8,9},{9,10},{10,1... | collective-permute-start | bytes 688136 | tf_op jit(solution)/shard_map/ppermute | solution.py:19
  90.3 17.6 %collective-permute-start.12 = (bf16[1792,256]{1,0:T(8,128)(2,1)}, bf16[1792,256]{1,0:T(8,128)(2,1)S(1)}, u32[]{:S(2)}, u32[]{:S(2)}) collective-permute-start(bf16[1792,256]{1,0:T(8,128)(2,1)} %collective-permute-done.6), channel_id=1, source_target_pairs={{0,1},{1,2},{2,3},{3,0},{4,5},{5,6},{6,7},{7,4},{8,9},{9,10},{10,1... | collective-permute-start | bytes 2752520 | tf_op jit(solution)/shard_map/ppermute | solution.py:19
  94.1 22.1 %collective-permute-start.16 = (bf16[448,256]{1,0:T(8,128)(2,1)S(1)}, bf16[448,256]{1,0:T(8,128)(2,1)S(1)}, u32[]{:S(2)}, u32[]{:S(2)}) collective-permute-start(bf16[448,256]{1,0:T(8,128)(2,1)S(1)} %copy-done.10), channel_id=1, source_target_pairs={{0,3},{1,0},{2,1},{3,2},{4,7},{5,4},{6,5},{7,6},{8,11},{9,8},{10,9... | collective-permute-start | bytes 688136 | tf_op jit(solution)/shard_map/ppermute | solution.py:19
  98.4 10.0 %copy-start.5 = (bf16[1,3584,256]{2,1,0:T(8,128)(2,1)S(1)}, bf16[1,3584,256]{2,1,0:T(8,128)(2,1)}, u32[]{:S(2)}) copy-start(bf16[1,3584,256]{2,1,0:T(8,128)(2,1)} %param.18) | copy-start | bytes 5505028
  107.9 44.1 %collective-permute-start.18 = (bf16[448,256]{1,0:T(8,128)(2,1)}, bf16[448,256]{1,0:T(8,128)(2,1)}, u32[]{:S(2)}, u32[]{:S(2)}) collective-permute-start(bf16[448,256]{1,0:T(8,128)(2,1)} %get-tuple-element.15), channel_id=1, source_target_pairs={{0,1},{1,2},{2,3},{3,0},{4,5},{5,6},{6,7},{7,4},{8,9},{9,10},{10,1... | collective-permute-start | bytes 688136 | tf_op jit(solution)/shard_map/ppermute | solution.py:19
  108.6 47.6 %collective-permute-start.19 = (bf16[448,256]{1,0:T(8,128)(2,1)}, bf16[448,256]{1,0:T(8,128)(2,1)}, u32[]{:S(2)}, u32[]{:S(2)}) collective-permute-start(bf16[448,256]{1,0:T(8,128)(2,1)} %get-tuple-element.15), channel_id=1, source_target_pairs={{0,3},{1,0},{2,1},{3,2},{4,7},{5,4},{6,5},{7,6},{8,11},{9,8},{10,9... | collective-permute-start | bytes 688136 | tf_op jit(solution)/shard_map/ppermute | solution.py:19
  112.8 53.8 %collective-permute-start.21 = (bf16[448,256]{1,0:T(8,128)(2,1)}, bf16[448,256]{1,0:T(8,128)(2,1)}, u32[]{:S(2)}, u32[]{:S(2)}) collective-permute-start(bf16[448,256]{1,0:T(8,128)(2,1)} %get-tuple-element.14), channel_id=1, source_target_pairs={{0,1},{1,2},{2,3},{3,0},{4,5},{5,6},{6,7},{7,4},{8,9},{9,10},{10,1... | collective-permute-start | bytes 688136 | tf_op jit(solution)/shard_map/ppermute | solution.py:19
  113.2 57.4 %collective-permute-start.22 = (bf16[448,256]{1,0:T(8,128)(2,1)}, bf16[448,256]{1,0:T(8,128)(2,1)}, u32[]{:S(2)}, u32[]{:S(2)}) collective-permute-start(bf16[448,256]{1,0:T(8,128)(2,1)} %get-tuple-element.14), channel_id=1, source_target_pairs={{0,3},{1,0},{2,1},{3,2},{4,7},{5,4},{6,5},{7,6},{8,11},{9,8},{10,9... | collective-permute-start | bytes 688136 | tf_op jit(solution)/shard_map/ppermute | solution.py:19
  116.2 8.5 %collective-permute-start.14 = (bf16[448,256]{1,0:T(8,128)(2,1)}, bf16[448,256]{1,0:T(8,128)(2,1)S(1)}, u32[]{:S(2)}, u32[]{:S(2)}) collective-permute-start(bf16[448,256]{1,0:T(8,128)(2,1)} %collective-permute-done.8), channel_id=1, source_target_pairs={{0,1},{1,2},{2,3},{3,0},{4,5},{5,6},{6,7},{7,4},{8,9},{9,10},{10,1... | collective-permute-start | bytes 688136 | tf_op jit(solution)/shard_map/ppermute | solution.py:19
  124.7 6.1 %collective-permute-start.17 = (bf16[448,256]{1,0:T(8,128)(2,1)S(1)}, bf16[448,256]{1,0:T(8,128)(2,1)S(1)}, u32[]{:S(2)}, u32[]{:S(2)}) collective-permute-start(bf16[448,256]{1,0:T(8,128)(2,1)S(1)} %collective-permute-done.16), channel_id=1, source_target_pairs={{0,3},{1,0},{2,1},{3,2},{4,7},{5,4},{6,5},{7,6},{8,11},{9,8},{10,9... | collective-permute-start | bytes 688136 | tf_op jit(solution)/shard_map/ppermute | solution.py:19
  130.8 41.3 %collective-permute-start.24 = (bf16[448,256]{1,0:T(8,128)(2,1)}, bf16[448,256]{1,0:T(8,128)(2,1)}, u32[]{:S(2)}, u32[]{:S(2)}) collective-permute-start(bf16[448,256]{1,0:T(8,128)(2,1)} %get-tuple-element.13), channel_id=1, source_target_pairs={{0,1},{1,2},{2,3},{3,0},{4,5},{5,6},{6,7},{7,4},{8,9},{9,10},{10,1... | collective-permute-start | bytes 688136 | tf_op jit(solution)/shard_map/ppermute | solution.py:19
  132.9 79.0 %all-to-all-start.1 = ((bf16[64,4,896]{2,1,0:T(4,128)(2,1)}), bf16[64,4,896]{2,1,0:T(4,128)(2,1)S(1)}, u32[]{:S(2)}, u32[]{:S(2)}) async-start(bf16[64,4,896]{2,1,0:T(4,128)(2,1)} %reshape.81), calls=%async_computation.1 | async-start | bytes 917504 | tf_op jit(solution)/shard_map/all_to_all | solution.py:243
  152.0 24.0 %collective-permute-start.25 = (bf16[448,256]{1,0:T(8,128)(2,1)}, bf16[448,256]{1,0:T(8,128)(2,1)S(1)}, u32[]{:S(2)}, u32[]{:S(2)}) collective-permute-start(bf16[448,256]{1,0:T(8,128)(2,1)} %get-tuple-element.13), channel_id=1, source_target_pairs={{0,3},{1,0},{2,1},{3,2},{4,7},{5,4},{6,5},{7,6},{8,11},{9,8},{10,9... | collective-permute-start | bytes 688136 | tf_op jit(solution)/shard_map/ppermute | solution.py:19
  156.3 21.2 %collective-permute-start.27 = (bf16[448,256]{1,0:T(8,128)(2,1)}, bf16[448,256]{1,0:T(8,128)(2,1)S(1)}, u32[]{:S(2)}, u32[]{:S(2)}) collective-permute-start(bf16[448,256]{1,0:T(8,128)(2,1)} %get-tuple-element.12), channel_id=1, source_target_pairs={{0,1},{1,2},{2,3},{3,0},{4,5},{5,6},{6,7},{7,4},{8,9},{9,10},{10,1... | collective-permute-start | bytes 688136 | tf_op jit(solution)/shard_map/ppermute | solution.py:19
  166.6 30.7 %collective-permute-start.28 = (bf16[448,256]{1,0:T(8,128)(2,1)}, bf16[448,256]{1,0:T(8,128)(2,1)}, u32[]{:S(2)}, u32[]{:S(2)}) collective-permute-start(bf16[448,256]{1,0:T(8,128)(2,1)} %get-tuple-element.12), channel_id=1, source_target_pairs={{0,3},{1,0},{2,1},{3,2},{4,7},{5,4},{6,5},{7,6},{8,11},{9,8},{10,9... | collective-permute-start | bytes 688136 | tf_op jit(solution)/shard_map/ppermute | solution.py:19
  170.6 57.8 %collective-permute-start.30 = (bf16[448,256]{1,0:T(8,128)(2,1)}, bf16[448,256]{1,0:T(8,128)(2,1)}, u32[]{:S(2)}, u32[]{:S(2)}) collective-permute-start(bf16[448,256]{1,0:T(8,128)(2,1)} %get-tuple-element.18), channel_id=1, source_target_pairs={{0,1},{1,2},{2,3},{3,0},{4,5},{5,6},{6,7},{7,4},{8,9},{9,10},{10,1... | collective-permute-start | bytes 688136 | tf_op jit(solution)/shard_map/ppermute | solution.py:19
  172.1 79.2 %collective-permute-start.31 = (bf16[448,256]{1,0:T(8,128)(2,1)}, bf16[448,256]{1,0:T(8,128)(2,1)}, u32[]{:S(2)}, u32[]{:S(2)}) collective-permute-start(bf16[448,256]{1,0:T(8,128)(2,1)} %get-tuple-element.18), channel_id=1, source_target_pairs={{0,3},{1,0},{2,1},{3,2},{4,7},{5,4},{6,5},{7,6},{8,11},{9,8},{10,9... | collective-permute-start | bytes 688136 | tf_op jit(solution)/shard_map/ppermute | solution.py:19
  176.1 56.9 %collective-permute-start.33 = (bf16[448,256]{1,0:T(8,128)(2,1)}, bf16[448,256]{1,0:T(8,128)(2,1)}, u32[]{:S(2)}, u32[]{:S(2)}) collective-permute-start(bf16[448,256]{1,0:T(8,128)(2,1)} %get-tuple-element.17), channel_id=1, source_target_pairs={{0,1},{1,2},{2,3},{3,0},{4,5},{5,6},{6,7},{7,4},{8,9},{9,10},{10,1... | collective-permute-start | bytes 688136 | tf_op jit(solution)/shard_map/ppermute | solution.py:19
  177.5 10.3 %collective-permute-start.20 = (bf16[448,256]{1,0:T(8,128)(2,1)}, bf16[448,256]{1,0:T(8,128)(2,1)S(1)}, u32[]{:S(2)}, u32[]{:S(2)}) collective-permute-start(bf16[448,256]{1,0:T(8,128)(2,1)} %collective-permute-done.18), channel_id=1, source_target_pairs={{0,1},{1,2},{2,3},{3,0},{4,5},{5,6},{6,7},{7,4},{8,9},{9,10},{10,1... | collective-permute-start | bytes 688136 | tf_op jit(solution)/shard_map/ppermute | solution.py:19
  187.7 5.1 %collective-permute-start.23 = (bf16[448,256]{1,0:T(8,128)(2,1)}, bf16[448,256]{1,0:T(8,128)(2,1)S(1)}, u32[]{:S(2)}, u32[]{:S(2)}) collective-permute-start(bf16[448,256]{1,0:T(8,128)(2,1)} %collective-permute-done.22), channel_id=1, source_target_pairs={{0,3},{1,0},{2,1},{3,2},{4,7},{5,4},{6,5},{7,6},{8,11},{9,8},{10,9... | collective-permute-start | bytes 688136 | tf_op jit(solution)/shard_map/ppermute | solution.py:19
  192.8 42.3 %collective-permute-start.34 = (bf16[448,256]{1,0:T(8,128)(2,1)}, bf16[448,256]{1,0:T(8,128)(2,1)}, u32[]{:S(2)}, u32[]{:S(2)}) collective-permute-start(bf16[448,256]{1,0:T(8,128)(2,1)} %get-tuple-element.17), channel_id=1, source_target_pairs={{0,3},{1,0},{2,1},{3,2},{4,7},{5,4},{6,5},{7,6},{8,11},{9,8},{10,9... | collective-permute-start | bytes 688136 | tf_op jit(solution)/shard_map/ppermute | solution.py:19
  195.3 8.3 %copy-start.8 = (f32[256,448]{0,1:T(8,128)S(1)}, f32[256,448]{0,1:T(8,128)}, u32[]{:S(2)}) copy-start(f32[256,448]{0,1:T(8,128)} %convolution_add_fusion.10) | copy-start | bytes 1376260
  197.3 6.3 %collective-permute-start.26 = (bf16[448,256]{1,0:T(8,128)(2,1)}, bf16[448,256]{1,0:T(8,128)(2,1)S(1)}, u32[]{:S(2)}, u32[]{:S(2)}) collective-permute-start(bf16[448,256]{1,0:T(8,128)(2,1)} %collective-permute-done.24), channel_id=1, source_target_pairs={{0,1},{1,2},{2,3},{3,0},{4,5},{5,6},{6,7},{7,4},{8,9},{9,10},{10,1... | collective-permute-start | bytes 688136 | tf_op jit(solution)/shard_map/ppermute | solution.py:19
  203.6 5.1 %collective-permute-start.29 = (bf16[448,256]{1,0:T(8,128)(2,1)}, bf16[448,256]{1,0:T(8,128)(2,1)S(1)}, u32[]{:S(2)}, u32[]{:S(2)}) collective-permute-start(bf16[448,256]{1,0:T(8,128)(2,1)} %collective-permute-done.28), channel_id=1, source_target_pairs={{0,3},{1,0},{2,1},{3,2},{4,7},{5,4},{6,5},{7,6},{8,11},{9,8},{10,9... | collective-permute-start | bytes 688136 | tf_op jit(solution)/shard_map/ppermute | solution.py:19
  208.7 63.5 %collective-permute-start.3 = (bf16[64,512]{1,0:T(8,128)(2,1)}, bf16[64,512]{1,0:T(8,128)(2,1)}, u32[]{:S(2)}, u32[]{:S(2)}) collective-permute-start(bf16[64,512]{1,0:T(8,128)(2,1)} %get-tuple-element.21), channel_id=1, source_target_pairs={{0,1},{1,2},{2,3},{3,0},{4,5},{5,6},{6,7},{7,4},{8,9},{9,10},{10,1... | collective-permute-start | bytes 196616 | tf_op jit(solution)/shard_map/ppermute | solution.py:19
  211.9 32.6 %all-to-all-start.2 = ((bf16[64,4,896]{2,1,0:T(4,128)(2,1)}), bf16[64,4,896]{2,1,0:T(4,128)(2,1)S(1)}, u32[]{:S(2)}, u32[]{:S(2)}) async-start(bf16[64,4,896]{2,1,0:T(4,128)(2,1)} %reshape.83), calls=%async_computation.2 | async-start | bytes 917504 | tf_op jit(solution)/shard_map/all_to_all | solution.py:243
  228.4 43.9 %collective-permute-start.4 = (bf16[64,512]{1,0:T(8,128)(2,1)}, bf16[64,512]{1,0:T(8,128)(2,1)}, u32[]{:S(2)}, u32[]{:S(2)}) collective-permute-start(bf16[64,512]{1,0:T(8,128)(2,1)} %get-tuple-element.23), channel_id=1, source_target_pairs={{0,2},{1,3},{2,0},{3,1},{4,6},{5,7},{6,4},{7,5},{8,10},{9,11},{10,... | collective-permute-start | bytes 196616 | tf_op jit(solution)/shard_map/ppermute | solution.py:19
  233.0 21.3 %copy-start.9 = (f32[256,448]{0,1:T(8,128)S(1)}, f32[256,448]{0,1:T(8,128)}, u32[]{:S(2)}) copy-start(f32[256,448]{0,1:T(8,128)} %convolution_add_fusion.5) | copy-start | bytes 1376260
  233.0 39.2 %collective-permute-start.5 = (bf16[64,512]{1,0:T(8,128)(2,1)}, bf16[64,512]{1,0:T(8,128)(2,1)}, u32[]{:S(2)}, u32[]{:S(2)}) collective-permute-start(bf16[64,512]{1,0:T(8,128)(2,1)} %get-tuple-element.22), channel_id=1, source_target_pairs={{0,3},{1,0},{2,1},{3,2},{4,7},{5,4},{6,5},{7,6},{8,11},{9,8},{10,9... | collective-permute-start | bytes 196616 | tf_op jit(solution)/shard_map/ppermute | solution.py:19
  235.1 20.4 %collective-permute-start.32 = (bf16[448,256]{1,0:T(8,128)(2,1)}, bf16[448,256]{1,0:T(8,128)(2,1)}, u32[]{:S(2)}, u32[]{:S(2)}) collective-permute-start(bf16[448,256]{1,0:T(8,128)(2,1)} %collective-permute-done.30), channel_id=1, source_target_pairs={{0,1},{1,2},{2,3},{3,0},{4,5},{5,6},{6,7},{7,4},{8,9},{9,10},{10,1... | collective-permute-start | bytes 688136 | tf_op jit(solution)/shard_map/ppermute | solution.py:19
  244.5 22.1 %all-to-all-start.3 = ((bf16[64,4,896]{2,1,0:T(4,128)(2,1)}), bf16[64,4,896]{2,1,0:T(4,128)(2,1)S(1)}, u32[]{:S(2)}, u32[]{:S(2)}) async-start(bf16[64,4,896]{2,1,0:T(4,128)(2,1)} %reshape.85), calls=%async_computation.3 | async-start | bytes 917504 | tf_op jit(solution)/shard_map/all_to_all | solution.py:243
  251.4 7.8 %collective-permute-start.35 = (bf16[448,256]{1,0:T(8,128)(2,1)}, bf16[448,256]{1,0:T(8,128)(2,1)S(1)}, u32[]{:S(2)}, u32[]{:S(2)}) collective-permute-start(bf16[448,256]{1,0:T(8,128)(2,1)} %collective-permute-done.34), channel_id=1, source_target_pairs={{0,3},{1,0},{2,1},{3,2},{4,7},{5,4},{6,5},{7,6},{8,11},{9,8},{10,9... | collective-permute-start | bytes 688136 | tf_op jit(solution)/shard_map/ppermute | solution.py:19
  266.6 22.1 %all-to-all-start.4 = ((bf16[64,4,896]{2,1,0:T(4,128)(2,1)}), bf16[64,4,896]{2,1,0:T(4,128)(2,1)S(1)}, u32[]{:S(2)}, u32[]{:S(2)}) async-start(bf16[64,4,896]{2,1,0:T(4,128)(2,1)} %reshape.87), calls=%async_computation.4 | async-start | bytes 917504 | tf_op jit(solution)/shard_map/all_to_all | solution.py:243

commit v2 on v1

--- a/solution.py
+++ b/solution.py
@@ -10,13 +10,17 @@
 
 LAT = 512
 MAXP = 8
-CHUNKS = 4
+CHUNKS = 2
 NEG = -1e30
 
 
 def hop(value, axis, step):
     size = lax.axis_size(axis)
     return lax.ppermute(value, axis, [(i, (i + step) % size) for i in range(size)])
+
+
+def after(first, *values):
+    return lax.optimization_barrier((first,) + values)[1:]
 
 
 def attention_kernel(
@@ -147,24 +151,26 @@
     grp_size = lax.axis_size("grp")
     capacity = min(samples, max(2, 2 * samples * picks // ep_size))
     slots_all = ep_size * capacity
-    me = lax.axis_index("grp")
 
     up, down = w_up[0], w_down[0]
     half = width // 2
     piece = width // CHUNKS
-    up_parts = [up[:half], up[half:]]
-    up_prev = [hop(p, "grp", 1) for p in up_parts]
-    up_next = [hop(p, "grp", -1) for p in reversed(up_parts)][::-1]
-    up_far = [hop(up_prev[0], "grp", 1), hop(up_next[1], "grp", -1)]
-    down_all = []
+    mid = piece // 2
+    own = [down[c * piece : (c + 1) * piece] for c in range(CHUNKS)]
+    up_prev, up_next = hop(up, "grp", 1), hop(up, "grp", -1)
+    prev, nxt, far = [], [], []
+    ahead_of = (up_prev, up_next)
+    far_from = (up_prev[:half], up_next[half:])
+    far_all = []
     for c in range(CHUNKS):
-        mid = piece // 2
-        own = down[c * piece : (c + 1) * piece]
-        parts = [own[:mid], own[mid:]]
-        prev = [hop(p, "grp", 1) for p in parts]
-        nxt = [hop(p, "grp", -1) for p in reversed(parts)][::-1]
-        far = [hop(prev[0], "grp", 1), hop(nxt[1], "grp", -1)]
-        down_all.append((parts, prev, nxt, far))
+        out, top, low = after(ahead_of, own[c], far_from[0], far_from[1])
+        far_all.append((hop(top, "grp", 1), hop(low, "grp", -1)))
+        prev.append(hop(out, "grp", 1))
+        nxt.append(hop(out, "grp", -1))
+        ahead_of = (prev[c], nxt[c])
+        far_from = (prev[c][:mid], nxt[c][mid:])
+    far_all.append((hop(far_from[0], "grp", 1), hop(far_from[1], "grp", -1)))
+    up_far, down_far = far_all[0], far_all[1:]
 
     moved_slot = mig_slot[0, 0]
     moved_target = mig_dest[0, 0]
@@ -173,10 +179,14 @@
     packet = jnp.concatenate(
         [q_here, kv_here, jnp.zeros((15, q_here.shape[1]), jnp.bfloat16)], axis=0
     )
-    offset = (moved_target - me) % grp_size
-    got = packet
-    for step in range(1, grp_size):
-        got = jnp.where(offset == step, hop(packet, "grp", -step), got)
+    offered = lax.all_to_all(
+        jnp.broadcast_to(packet[None], (grp_size,) + packet.shape),
+        "grp",
+        split_axis=0,
+        concat_axis=0,
+        tiled=True,
+    )
+    got = lax.dynamic_index_in_dim(offered, moved_target, 0, keepdims=False)
     heads = q_here.shape[0]
     q_in, kv_in = got[:heads], got[heads : heads + 1]
 
@@ -194,10 +204,10 @@
         kv_in,
         cache_pool,
     )
-    zero = jnp.zeros((), jnp.bfloat16)
-    arrived_out = jnp.where(offset == 0, out_moved, zero)
-    for step in range(1, grp_size):
-        arrived_out = arrived_out + hop(jnp.where(offset == step, out_moved, zero), "grp", step)
+    to_target = jnp.arange(grp_size, dtype=jnp.int32) == moved_target
+    sent_out = jnp.where(to_target[:, None, None], out_moved[None], jnp.zeros((), jnp.bfloat16))
+    got_out = lax.all_to_all(sent_out, "grp", split_axis=0, concat_axis=0, tiled=True)
+    arrived_out = got_out[0] + got_out[1] + got_out[2] + got_out[3]
     attn_second = lax.dynamic_update_index_in_dim(attn_second, arrived_out, moved_slot, 0)
 
     flat_ids = expert_ids.reshape(-1)
@@ -224,21 +234,24 @@
     def act(v):
         return jax.nn.silu(v).astype(jnp.bfloat16)
 
-    def up_of(parts):
-        return act(f32dot(arrived[:, :half], parts[0]) + f32dot(arrived[:, half:], parts[1]))
-
-    h_all = [up_of(p) for p in (up_parts, up_prev, up_next, up_far)]
+    def up_of(weight):
+        return act(f32dot(arrived, weight))
+
+    far_up = act(f32dot(arrived[:, :half], up_far[0]) + f32dot(arrived[:, half:], up_far[1]))
+    h_own, h_prev, h_next = up_of(up), up_of(up_prev), up_of(up_next)
     contract = (((1,), (1,)), ((), ()))
+
+    def down_of(h, weight):
+        return lax.dot_general(h, weight, contract, preferred_element_type=jnp.float32)
+
     results = []
     for c in range(CHUNKS):
-        cols = []
-        for s in range(2):
-            total = 0.0
-            for h, parts in zip(h_all, down_all[c]):
-                total = total + lax.dot_general(
-                    h, parts[s], contract, preferred_element_type=jnp.float32
-                )
-            cols.append(total.astype(jnp.bfloat16))
+        near = down_of(h_own, own[c]) + down_of(h_prev, prev[c]) + down_of(h_next, nxt[c])
+        top, low = down_of(far_up, down_far[c][0]), down_of(far_up, down_far[c][1])
+        cols = [
+            (near[:, :mid] + top).astype(jnp.bfloat16),
+            (near[:, mid:] + low).astype(jnp.bfloat16),
+        ]
         produced = jnp.concatenate(cols, axis=1)
         returned = lax.all_to_all(
             produced.reshape(ep_size, capacity, piece), "ep", split_axis=0, concat_axis=0, tiled=True

time: 295 us -> 227 us (0.77); the launches traced: 290 us -> 226 us
  starting transfers between devices: 106 us -> 55.9 us
  matrix products: 34.8 us -> 20 us
  local copies, waits for them, and re-layouts: 19.6 us -> 24.4 us
    ppermute x36 -> x12, starting transfers between devices: 46.3 us -> 12.6 us  [hop(): lax.ppermute(value, axis, [(i, (i + step) % size) for i in range(size)])]
    all_to_all x4 -> x2, starting transfers between devices: 46.4 us -> 19.7 us  [shards(): lax.all_to_all(produced.reshape(ep_size, capacity, piece), 'ep', split_ax...]
    dot_general x40 -> x15, matrix products: 32.8 us -> 18.2 us  [the longest x10 8.3 us: down_of(): lax.dot_general(h, weight, contract, preferred_element_type=jnp.float32)]
    all_to_all x0 -> x2, starting transfers between devices: none -> 9.23 us  [the longest x1 5.01 us: shards(): lax.all_to_all(jnp.broadcast_to(packet[None], (grp_size,) + packet.shape)...]
    ppermute x36 -> x12, waiting for transfers between devices: 75.1 us -> 68.3 us  [hop(): lax.ppermute(value, axis, [(i, (i + step) % size) for i in range(size)])]
    slice x2 -> x7, local copies, waits for them, and re-layouts: 5.91 us -> 10.8 us  [the longest x2 4.33 us: shards(): far_from = (up_prev[:half], up_next[half:])]
    reshape x4 -> x2, local copies, waits for them, and re-layouts: 5.68 us -> 2.27 us  [shards(): produced.reshape(ep_size, capacity, piece)]
    all_to_all x4 -> x2, waiting for transfers between devices: 27.9 us -> 30.3 us  [shards(): lax.all_to_all(produced.reshape(ep_size, capacity, piece), 'ep', split_ax...]
  transfers between devices with their start and end apart: 41 -> 17, of which waited for: 14 -> 8; matrix products, arithmetic and copies ran while one was open for 19% -> 19% of each run, Pallas kernels for 6% -> 8%
where the time goes in v2:
time: 227 us; the launch traced here: 226 us
  waiting for transfers between devices  101 us (44%)
  starting transfers between devices  55.9 us (25%)
  local copies, waits for them, and re-layouts  24.4 us (11%)
  matrix products  20 us (9%)
  Pallas kernels  18.4 us (8%)
  other arithmetic  3.75 us (2%)
  between operations  2.43 us (1%)
    ppermute x12, waiting for transfers between devices, hop(): lax.ppermute(value, axis, [(i, (i + step) % size) for i in range(size)])  68.3 us
    all_to_all x2, waiting for transfers between devices, shards(): lax.all_to_all(produced.reshape(ep_size, capacity, piece), 'ep', split_ax...  30.3 us
    all_to_all x2, starting transfers between devices, shards(): lax.all_to_all(produced.reshape(ep_size, capacity, piece), 'ep', split_ax...  19.7 us
    pallas_call x1, Pallas kernels, attention(): pl.pallas_call(attention_kernel, grid_spec=pltpu.PrefetchScalarGridSpec(n...  18.4 us
    all_to_all x1, starting transfers between devices, shards(): lax.all_to_all(outgoing.reshape(ep_size, capacity, width), 'ep', split_ax...  14.3 us
    ppermute x12, starting transfers between devices, hop(): lax.ppermute(value, axis, [(i, (i + step) % size) for i in range(size)])  12.6 us
    dot_general x10, matrix products, down_of(): lax.dot_general(h, weight, contract, preferred_element_type=jnp.float32)  8.3 us
    dot_general x3, matrix products, up_of(): return act(f32dot(arrived, weight))  6.72 us
  transfers between devices with their start and end apart: 17, of which 8 were waited for; matrix products, arithmetic and copies ran while one was open for 19% of the time, Pallas kernels for 8%

profile of v2, /device:TPU:1, one launch (start us, length us, event | category | flops | bytes accessed | tf_op | source)
XLA Modules:
  0.0 225.6 jit_solution(1997753258460934191)
XLA Ops:
  1.3 0.9 dynamic-slice_bitcast_fusion.1
  2.2 0.7 constant_dynamic-slice_fusion
  3.1 0.8 broadcast_in_dim.101
  3.9 5.0 %all-to-all-start = ((bf16[4,80,576]{2,1,0:T(8,128)(2,1)}), bf16[4,80,576]{2,1,0:T(8,128)(2,1)S(1)}, u32[]{:S(2)}, u32[]{:S(2)}) async-start(bf16[4,80,576]{2,1,0:T(8,128)(2,1)} %broadcast_in_dim.101), calls=%async_computation | async-start | bytes 819200 | tf_op jit(solution)/shard_map/all_to_all | solution.py:182
  8.9 0.8 copy.27
  9.8 0.2 fusion
  10.0 0.8 copy.29
  11.0 0.7 convolution_convert_fusion
  11.6 1.5 reshape.63
  13.1 2.1 all-to-all-done
  15.3 14.3 %all-to-all-start.2 = ((bf16[64,4,3584]{2,1,0:T(4,128)(2,1)}), bf16[64,4,3584]{2,1,0:T(4,128)(2,1)S(1)}, u32[]{:S(2)}, u32[]{:S(2)}) async-start(bf16[64,4,3584]{2,1,0:T(4,128)(2,1)} %reshape.63), calls=%async_computation.2 | async-start | bytes 3670016 | tf_op jit(solution)/shard_map/all_to_all | solution.py:228
  29.6 0.4 collective-permute-start
  30.0 2.4 %collective-permute-start.1 = (bf16[3584,256]{1,0:T(8,128)(2,1)}, bf16[3584,256]{1,0:T(8,128)(2,1)}, u32[]{:S(2)}, u32[]{:S(2)}) collective-permute-start(bf16[3584,256]{1,0:T(8,128)(2,1)} %bitcast.65), channel_id=1, source_target_pairs={{0,3},{1,0},{2,1},{3,2},{4,7},{5,4},{6,5},{7,6},{8,11},{9,8},{10,9... | collective-permute-start | bytes 5505032 | tf_op jit(solution)/shard_map/ppermute | solution.py:19
  33.5 2.7 %slice_bitcast_fusion = (bf16[1792,256]{1,0:T(8,128)(2,1)}, bf16[1792,256]{1,0:T(8,128)(2,1)S(1)}) fusion(bf16[1,3584,256]{2,1,0:T(8,128)(2,1)} %param.18), kind=kLoop, calls=%fused_computation.23 | loop fusion | bytes 3670016 | tf_op jit(solution)/shard_map/slice | solution.py:159
  36.3 36.1 %collective-permute-done = bf16[3584,256]{1,0:T(8,128)(2,1)} collective-permute-done((bf16[3584,256]{1,0:T(8,128)(2,1)}, bf16[3584,256]{1,0:T(8,128)(2,1)}, u32[]{:S(2)}, u32[]{:S(2)}) %collective-permute-start) | collective-permute-done | bytes 1835040 | tf_op jit(solution)/shard_map/ppermute | solution.py:19
  72.3 2.2 slice.100
  74.5 2.2 slice.101
  76.7 2.7 %collective-permute-start.3 = (bf16[1792,256]{1,0:T(8,128)(2,1)S(1)}, bf16[1792,256]{1,0:T(8,128)(2,1)S(1)}, u32[]{:S(2)}, u32[]{:S(2)}) collective-permute-start(bf16[1792,256]{1,0:T(8,128)(2,1)S(1)} %get-tuple-element.15), channel_id=1, source_target_pairs={{0,3},{1,0},{2,1},{3,2},{4,7},{5,4},{6,5},{7,6},{8,11},{9,8},{10,9... | collective-permute-start | bytes 2752520 | tf_op jit(solution)/shard_map/ppermute | solution.py:19
  79.4 18.4 %attention.1 = (bf16[16,64,512]{2,1,0:T(8,128)(2,1)}, bf16[16,64,512]{2,1,0:T(8,128)(2,1)}, bf16[64,512]{1,0:T(8,128)(2,1)S(1)}) custom-call(s32[16]{0:T(128)S(1)} %bitcast.61, s32[128]{0:T(128)S(1)} %select_reduce_fusion.1.pages, s32[1]{0:T(128)} %bitcast.53.moved, bf16[16,64,576]{2,1,0:T(8,128)(2,1)S(1)} %copy-done.3, bf16[16,64,576]{2,1,0:T(8,128)(2,1)S(1)} %copy-done.1, ...), custom_call_target="tpu_custom_call" | custom-call | flops 12000000000 | bytes 8000000 | tf_op jit(solution)/shard_map/attention/pallas_call | solution.py:90
  97.8 0.8 broadcast_select_fusion
  98.6 1.4 collective-permute-start.4
  100.1 0.9 slice.105
  100.9 0.9 slice.106
  101.8 2.7 %collective-permute-start.9 = (bf16[1792,256]{1,0:T(8,128)(2,1)}, bf16[1792,256]{1,0:T(8,128)(2,1)}, u32[]{:S(2)}, u32[]{:S(2)}) collective-permute-start(bf16[1792,256]{1,0:T(8,128)(2,1)} %get-tuple-element.20), channel_id=1, source_target_pairs={{0,3},{1,0},{2,1},{3,2},{4,7},{5,4},{6,5},{7,6},{8,11},{9,8},{10,9... | collective-permute-start | bytes 2752520 | tf_op jit(solution)/shard_map/ppermute | solution.py:19
  104.6 1.3 copy-done.5
  105.8 4.2 %all-to-all-start.1 = ((bf16[4,64,512]{2,1,0:T(8,128)(2,1)}), bf16[4,64,512]{2,1,0:T(8,128)(2,1)}, u32[]{:S(2)}, u32[]{:S(2)}) async-start(bf16[4,64,512]{2,1,0:T(8,128)(2,1)} %broadcast_select_fusion), calls=%async_computation.1 | async-start | bytes 524288 | tf_op jit(solution)/shard_map/all_to_all | solution.py:209
  110.0 2.9 %reshape.64 = bf16[256,3584]{1,0:T(8,128)(2,1)S(1)} reshape(bf16[64,4,3584]{2,1,0:T(4,128)(2,1)} %copy-done.5) | data formatting | bytes 3670016 | tf_op jit(solution)/shard_map/reshape | solution.py:230
  113.0 2.3 %multiply_convert_fusion.3 = bf16[256,256]{1,0:T(8,128)(2,1)S(1)} fusion(bf16[256,3584]{1,0:T(8,128)(2,1)S(1)} %reshape.64, bf16[1,3584,256]{2,1,0:T(8,128)(2,1)} %param.17), kind=kOutput, calls=%fused_computation.28 | convolution fusion | flops 470089728 | bytes 3801088 | tf_op jit(solution)/shard_map/dot_general | solution.py:238
  115.3 0.4 fusion.18
  115.7 0.2 copy-done.12
  116.0 2.2 fusion.20
  118.2 0.4 convolution_add_fusion.3
  118.7 2.2 fusion.21
  120.9 0.4 convolution_add_fusion.2
  121.4 0.5 copy-done.13
  121.9 1.4 collective-permute-start.6
  123.3 1.6 fusion.4
  124.9 1.6 multiply_convert_fusion
  126.5 21.9 %collective-permute-done.7 = bf16[896,256]{1,0:T(8,128)(2,1)} collective-permute-done((bf16[896,256]{1,0:T(8,128)(2,1)}, bf16[896,256]{1,0:T(8,128)(2,1)}, u32[]{:S(2)}, u32[]{:S(2)}) %collective-permute-start.7) | collective-permute-done | bytes 458784 | tf_op jit(solution)/shard_map/ppermute | solution.py:19
  148.4 1.3 fusion.22
  149.7 2.6 %collective-permute-done.6 = bf16[896,256]{1,0:T(8,128)(2,1)S(1)} collective-permute-done((bf16[896,256]{1,0:T(8,128)(2,1)S(1)}, bf16[896,256]{1,0:T(8,128)(2,1)S(1)}, u32[]{:S(2)}, u32[]{:S(2)}) %collective-permute-start.6) | collective-permute-done | bytes 458784 | tf_op jit(solution)/shard_map/ppermute | solution.py:19
  152.3 0.4 fusion.7
  152.8 1.1 reshape.65
  153.9 13.3 %all-to-all-start.3 = ((bf16[64,4,1792]{2,1,0:T(4,128)(2,1)}), bf16[64,4,1792]{2,1,0:T(4,128)(2,1)S(1)}, u32[]{:S(2)}, u32[]{:S(2)}) async-start(bf16[64,4,1792]{2,1,0:T(4,128)(2,1)} %reshape.65), calls=%async_computation.3 | async-start | bytes 1835008 | tf_op jit(solution)/shard_map/all_to_all | solution.py:256
  167.2 1.3 fusion.19
  168.6 1.1 slice.111
  169.7 1.0 slice.109
  170.8 1.5 collective-permute-start.10
  172.3 1.6 convolution_add_fusion.1
  173.9 1.6 convolution_add_fusion
  175.6 5.8 %collective-permute-done.11 = bf16[896,256]{1,0:T(8,128)(2,1)S(1)} collective-permute-done((bf16[896,256]{1,0:T(8,128)(2,1)S(1)}, bf16[896,256]{1,0:T(8,128)(2,1)S(1)}, u32[]{:S(2)}, u32[]{:S(2)}) %collective-permute-start.11) | collective-permute-done | bytes 458784 | tf_op jit(solution)/shard_map/ppermute | solution.py:19
  181.3 0.3 fusion.23
  181.7 2.0 collective-permute-done.10
  183.7 0.4 fusion.2
  184.1 1.1 reshape.67
  185.2 7.3 %all-to-all-done.3 = bf16[64,4,1792]{2,1,0:T(4,128)(2,1)S(1)} async-done(((bf16[64,4,1792]{2,1,0:T(4,128)(2,1)}), bf16[64,4,1792]{2,1,0:T(4,128)(2,1)S(1)}, u32[]{:S(2)}, u32[]{:S(2)}) %all-to-all-start.3) | async-done | bytes 917536 | tf_op jit(solution)/shard_map/all_to_all | solution.py:256
  192.5 6.5 %all-to-all-start.4 = ((bf16[64,4,1792]{2,1,0:T(4,128)(2,1)}), bf16[64,4,1792]{2,1,0:T(4,128)(2,1)S(1)}, u32[]{:S(2)}, u32[]{:S(2)}) async-start(bf16[64,4,1792]{2,1,0:T(4,128)(2,1)} %reshape.67), calls=%async_computation.4 | async-start | bytes 1835008 | tf_op jit(solution)/shard_map/all_to_all | solution.py:256
  199.0 1.6 fusion.10
  200.6 0.2 reshape.66
  200.8 0.5 convolution_convert_fusion.2
  201.3 23.0 %all-to-all-done.4 = bf16[64,4,1792]{2,1,0:T(4,128)(2,1)S(1)} async-done(((bf16[64,4,1792]{2,1,0:T(4,128)(2,1)}), bf16[64,4,1792]{2,1,0:T(4,128)(2,1)S(1)}, u32[]{:S(2)}, u32[]{:S(2)}) %all-to-all-start.4) | async-done | bytes 917536 | tf_op jit(solution)/shard_map/all_to_all | solution.py:256
  224.3 0.2 reshape.68
  224.5 0.5 convolution_convert_fusion.1
  225.0 0.7 pad_maximum_fusion.2
  (65 shorter events, 1.4 us)
Async XLA Ops:
  0.6 10.3 %copy-start = (bf16[16,3584]{1,0:T(8,128)(2,1)S(1)}, bf16[16,3584]{1,0:T(8,128)(2,1)}, u32[]{:S(2)}) copy-start(bf16[16,3584]{1,0:T(8,128)(2,1)} %param.14) | copy-start | bytes 344068
  3.9 11.4 %all-to-all-start = ((bf16[4,80,576]{2,1,0:T(8,128)(2,1)}), bf16[4,80,576]{2,1,0:T(8,128)(2,1)S(1)}, u32[]{:S(2)}, u32[]{:S(2)}) async-start(bf16[4,80,576]{2,1,0:T(8,128)(2,1)} %broadcast_in_dim.101), calls=%async_computation | async-start | bytes 819200 | tf_op jit(solution)/shard_map/all_to_all | solution.py:182
  13.1 19.9 %copy-start.15 = (bf16[16,576]{1,0:T(8,128)(2,1)S(1)}, bf16[16,576]{1,0:T(8,128)(2,1)}, u32[]{:S(2)}) copy-start(bf16[16,576]{1,0:T(8,128)(2,1)} %param.20) | copy-start | bytes 55300
  13.1 19.9 %copy-start.14 = (bf16[16,576]{1,0:T(8,128)(2,1)S(1)}, bf16[16,576]{1,0:T(8,128)(2,1)}, u32[]{:S(2)}) copy-start(bf16[16,576]{1,0:T(8,128)(2,1)} %param.22) | copy-start | bytes 55300
  13.1 20.0 %copy-start.4 = (s32[1,16]{1,0:T(1,128)S(1)}, s32[1,16]{1,0:T(1,128)}, u32[]{:S(2)}) copy-start(s32[1,16]{1,0:T(1,128)} %param.24) | copy-start | bytes 196
  13.1 20.3 %copy-start.16 = (s32[1,32]{1,0:T(1,128)S(1)}, s32[1,32]{1,0:T(1,128)}, u32[]{:S(2)}) copy-start(s32[1,32]{1,0:T(1,128)} %param.25) | copy-start | bytes 388
  15.3 89.3 %all-to-all-start.2 = ((bf16[64,4,3584]{2,1,0:T(4,128)(2,1)}), bf16[64,4,3584]{2,1,0:T(4,128)(2,1)S(1)}, u32[]{:S(2)}, u32[]{:S(2)}) async-start(bf16[64,4,3584]{2,1,0:T(4,128)(2,1)} %reshape.63), calls=%async_computation.2 | async-start | bytes 3670016 | tf_op jit(solution)/shard_map/all_to_all | solution.py:228
  29.6 42.7 %collective-permute-start = (bf16[3584,256]{1,0:T(8,128)(2,1)}, bf16[3584,256]{1,0:T(8,128)(2,1)}, u32[]{:S(2)}, u32[]{:S(2)}) collective-permute-start(bf16[3584,256]{1,0:T(8,128)(2,1)} %bitcast.64), channel_id=1, source_target_pairs={{0,1},{1,2},{2,3},{3,0},{4,5},{5,6},{6,7},{7,4},{8,9},{9,10},{10,1... | collective-permute-start | bytes 5505032 | tf_op jit(solution)/shard_map/ppermute | solution.py:19
  30.0 44.5 %collective-permute-start.1 = (bf16[3584,256]{1,0:T(8,128)(2,1)}, bf16[3584,256]{1,0:T(8,128)(2,1)}, u32[]{:S(2)}, u32[]{:S(2)}) collective-permute-start(bf16[3584,256]{1,0:T(8,128)(2,1)} %bitcast.65), channel_id=1, source_target_pairs={{0,3},{1,0},{2,1},{3,2},{4,7},{5,4},{6,5},{7,6},{8,11},{9,8},{10,9... | collective-permute-start | bytes 5505032 | tf_op jit(solution)/shard_map/ppermute | solution.py:19
  33.5 45.8 %copy-start.2 = (bf16[32,64,576]{2,1,0:T(8,128)(2,1)S(1)}, bf16[32,64,576]{2,1,0:T(8,128)(2,1)}, u32[]{:S(2)}) copy-start(bf16[32,64,576]{2,1,0:T(8,128)(2,1)} %pool.1) | copy-start | bytes 7077892
  36.2 43.1 %copy-start.1 = (bf16[16,64,576]{2,1,0:T(8,128)(2,1)S(1)}, bf16[16,64,576]{2,1,0:T(8,128)(2,1)}, u32[]{:S(2)}) copy-start(bf16[16,64,576]{2,1,0:T(8,128)(2,1)} %q_two.1) | copy-start | bytes 3538948
  36.2 43.1 %copy-start.3 = (bf16[16,64,576]{2,1,0:T(8,128)(2,1)S(1)}, bf16[16,64,576]{2,1,0:T(8,128)(2,1)}, u32[]{:S(2)}) copy-start(bf16[16,64,576]{2,1,0:T(8,128)(2,1)} %q_one.1) | copy-start | bytes 3538948
  76.7 23.4 %collective-permute-start.2 = (bf16[1792,256]{1,0:T(8,128)(2,1)S(1)}, bf16[1792,256]{1,0:T(8,128)(2,1)S(1)}, u32[]{:S(2)}, u32[]{:S(2)}) collective-permute-start(bf16[1792,256]{1,0:T(8,128)(2,1)S(1)} %get-tuple-element.15), channel_id=1, source_target_pairs={{0,1},{1,2},{2,3},{3,0},{4,5},{5,6},{6,7},{7,4},{8,9},{9,10},{10,1... | collective-permute-start | bytes 2752520 | tf_op jit(solution)/shard_map/ppermute | solution.py:19
  76.7 24.2 %collective-permute-start.3 = (bf16[1792,256]{1,0:T(8,128)(2,1)S(1)}, bf16[1792,256]{1,0:T(8,128)(2,1)S(1)}, u32[]{:S(2)}, u32[]{:S(2)}) collective-permute-start(bf16[1792,256]{1,0:T(8,128)(2,1)S(1)} %get-tuple-element.15), channel_id=1, source_target_pairs={{0,3},{1,0},{2,1},{3,2},{4,7},{5,4},{6,5},{7,6},{8,11},{9,8},{10,9... | collective-permute-start | bytes 2752520 | tf_op jit(solution)/shard_map/ppermute | solution.py:19
  98.6 22.8 %collective-permute-start.5 = (bf16[1792,256]{1,0:T(8,128)(2,1)}, bf16[1792,256]{1,0:T(8,128)(2,1)}, u32[]{:S(2)}, u32[]{:S(2)}) collective-permute-start(bf16[1792,256]{1,0:T(8,128)(2,1)} %slice.101), channel_id=1, source_target_pairs={{0,3},{1,0},{2,1},{3,2},{4,7},{5,4},{6,5},{7,6},{8,11},{9,8},{10,9... | collective-permute-start | bytes 2752520 | tf_op jit(solution)/shard_map/ppermute | solution.py:19
  98.6 26.3 %collective-permute-start.4 = (bf16[1792,256]{1,0:T(8,128)(2,1)}, bf16[1792,256]{1,0:T(8,128)(2,1)}, u32[]{:S(2)}, u32[]{:S(2)}) collective-permute-start(bf16[1792,256]{1,0:T(8,128)(2,1)} %slice.100), channel_id=1, source_target_pairs={{0,1},{1,2},{2,3},{3,0},{4,5},{5,6},{6,7},{7,4},{8,9},{9,10},{10,1... | collective-permute-start | bytes 2752520 | tf_op jit(solution)/shard_map/ppermute | solution.py:19
  100.1 4.4 %copy-start.10 = (bf16[1792,256]{1,0:T(8,128)(2,1)}, bf16[1792,256]{1,0:T(8,128)(2,1)S(1)}, u32[]{:S(2)}) copy-start(bf16[1792,256]{1,0:T(8,128)(2,1)S(1)} %collective-permute-done.2) | copy-start | bytes 2752516
  100.9 3.5 %copy-start.8 = (bf16[1792,256]{1,0:T(8,128)(2,1)}, bf16[1792,256]{1,0:T(8,128)(2,1)S(1)}, u32[]{:S(2)}) copy-start(bf16[1792,256]{1,0:T(8,128)(2,1)S(1)} %collective-permute-done.3) | copy-start | bytes 2752516
  101.8 67.9 %collective-permute-start.8 = (bf16[1792,256]{1,0:T(8,128)(2,1)}, bf16[1792,256]{1,0:T(8,128)(2,1)}, u32[]{:S(2)}, u32[]{:S(2)}) collective-permute-start(bf16[1792,256]{1,0:T(8,128)(2,1)} %get-tuple-element.20), channel_id=1, source_target_pairs={{0,1},{1,2},{2,3},{3,0},{4,5},{5,6},{6,7},{7,4},{8,9},{9,10},{10,1... | collective-permute-start | bytes 2752520 | tf_op jit(solution)/shard_map/ppermute | solution.py:19
  101.8 66.8 %collective-permute-start.9 = (bf16[1792,256]{1,0:T(8,128)(2,1)}, bf16[1792,256]{1,0:T(8,128)(2,1)}, u32[]{:S(2)}, u32[]{:S(2)}) collective-permute-start(bf16[1792,256]{1,0:T(8,128)(2,1)} %get-tuple-element.20), channel_id=1, source_target_pairs={{0,3},{1,0},{2,1},{3,2},{4,7},{5,4},{6,5},{7,6},{8,11},{9,8},{10,9... | collective-permute-start | bytes 2752520 | tf_op jit(solution)/shard_map/ppermute | solution.py:19
  104.5 43.9 %collective-permute-start.7 = (bf16[896,256]{1,0:T(8,128)(2,1)}, bf16[896,256]{1,0:T(8,128)(2,1)}, u32[]{:S(2)}, u32[]{:S(2)}) collective-permute-start(bf16[896,256]{1,0:T(8,128)(2,1)} %slice.106), channel_id=1, source_target_pairs={{0,3},{1,0},{2,1},{3,2},{4,7},{5,4},{6,5},{7,6},{8,11},{9,8},{10,9... | collective-permute-start | bytes 1376264 | tf_op jit(solution)/shard_map/ppermute | solution.py:19
  104.5 1.3 copy-start.5
  105.8 48.1 %all-to-all-start.1 = ((bf16[4,64,512]{2,1,0:T(8,128)(2,1)}), bf16[4,64,512]{2,1,0:T(8,128)(2,1)}, u32[]{:S(2)}, u32[]{:S(2)}) async-start(bf16[4,64,512]{2,1,0:T(8,128)(2,1)} %broadcast_select_fusion), calls=%async_computation.1 | async-start | bytes 524288 | tf_op jit(solution)/shard_map/all_to_all | solution.py:209
  113.0 2.3 %copy-start.6 = (bf16[1,3584,256]{2,1,0:T(8,128)(2,1)S(1)}, bf16[1,3584,256]{2,1,0:T(8,128)(2,1)}, u32[]{:S(2)}) copy-start(bf16[1,3584,256]{2,1,0:T(8,128)(2,1)} %param.18) | copy-start | bytes 5505028
  115.3 0.7 copy-start.12
  116.0 2.2 copy-start.11
  118.6 2.2 copy-start.9
  120.9 1.0 copy-start.13
  121.9 30.4 %collective-permute-start.6 = (bf16[896,256]{1,0:T(8,128)(2,1)S(1)}, bf16[896,256]{1,0:T(8,128)(2,1)S(1)}, u32[]{:S(2)}, u32[]{:S(2)}) collective-permute-start(bf16[896,256]{1,0:T(8,128)(2,1)S(1)} %copy-done.13), channel_id=1, source_target_pairs={{0,1},{1,2},{2,3},{3,0},{4,5},{5,6},{6,7},{7,4},{8,9},{9,10},{10,1... | collective-permute-start | bytes 1376264 | tf_op jit(solution)/shard_map/ppermute | solution.py:19
  152.8 14.4 %copy-start.7 = (bf16[1,3584,256]{2,1,0:T(8,128)(2,1)S(1)}, bf16[1,3584,256]{2,1,0:T(8,128)(2,1)}, u32[]{:S(2)}) copy-start(bf16[1,3584,256]{2,1,0:T(8,128)(2,1)} %param.18) | copy-start | bytes 5505028
  153.9 38.6 %all-to-all-start.3 = ((bf16[64,4,1792]{2,1,0:T(4,128)(2,1)}), bf16[64,4,1792]{2,1,0:T(4,128)(2,1)S(1)}, u32[]{:S(2)}, u32[]{:S(2)}) async-start(bf16[64,4,1792]{2,1,0:T(4,128)(2,1)} %reshape.65), calls=%async_computation.3 | async-start | bytes 1835008 | tf_op jit(solution)/shard_map/all_to_all | solution.py:256
  169.6 11.7 %collective-permute-start.11 = (bf16[896,256]{1,0:T(8,128)(2,1)S(1)}, bf16[896,256]{1,0:T(8,128)(2,1)S(1)}, u32[]{:S(2)}, u32[]{:S(2)}) collective-permute-start(bf16[896,256]{1,0:T(8,128)(2,1)S(1)} %slice.111), channel_id=1, source_target_pairs={{0,3},{1,0},{2,1},{3,2},{4,7},{5,4},{6,5},{7,6},{8,11},{9,8},{10,9... | collective-permute-start | bytes 1376264 | tf_op jit(solution)/shard_map/ppermute | solution.py:19
  170.8 12.9 %collective-permute-start.10 = (bf16[896,256]{1,0:T(8,128)(2,1)S(1)}, bf16[896,256]{1,0:T(8,128)(2,1)S(1)}, u32[]{:S(2)}, u32[]{:S(2)}) collective-permute-start(bf16[896,256]{1,0:T(8,128)(2,1)S(1)} %slice.109), channel_id=1, source_target_pairs={{0,1},{1,2},{2,3},{3,0},{4,5},{5,6},{6,7},{7,4},{8,9},{9,10},{10,1... | collective-permute-start | bytes 1376264 | tf_op jit(solution)/shard_map/ppermute | solution.py:19
  192.5 31.8 %all-to-all-start.4 = ((bf16[64,4,1792]{2,1,0:T(4,128)(2,1)}), bf16[64,4,1792]{2,1,0:T(4,128)(2,1)S(1)}, u32[]{:S(2)}, u32[]{:S(2)}) async-start(bf16[64,4,1792]{2,1,0:T(4,128)(2,1)} %reshape.67), calls=%async_computation.4 | async-start | bytes 1835008 | tf_op jit(solution)/shard_map/all_to_all | solution.py:256

commit v3 on v1

--- a/solution.py
+++ b/solution.py
@@ -10,13 +10,16 @@
 
 LAT = 512
 MAXP = 8
-CHUNKS = 4
 NEG = -1e30
 
 
 def hop(value, axis, step):
     size = lax.axis_size(axis)
     return lax.ppermute(value, axis, [(i, (i + step) % size) for i in range(size)])
+
+
+def after(first, *values):
+    return lax.optimization_barrier((first,) + values)[1:]
 
 
 def attention_kernel(
@@ -148,26 +151,51 @@
     capacity = min(samples, max(2, 2 * samples * picks // ep_size))
     slots_all = ep_size * capacity
     me = lax.axis_index("grp")
-
-    up, down = w_up[0], w_down[0]
-    half = width // 2
-    piece = width // CHUNKS
-    up_parts = [up[:half], up[half:]]
-    up_prev = [hop(p, "grp", 1) for p in up_parts]
-    up_next = [hop(p, "grp", -1) for p in reversed(up_parts)][::-1]
-    up_far = [hop(up_prev[0], "grp", 1), hop(up_next[1], "grp", -1)]
-    down_all = []
-    for c in range(CHUNKS):
-        mid = piece // 2
-        own = down[c * piece : (c + 1) * piece]
-        parts = [own[:mid], own[mid:]]
-        prev = [hop(p, "grp", 1) for p in parts]
-        nxt = [hop(p, "grp", -1) for p in reversed(parts)][::-1]
-        far = [hop(prev[0], "grp", 1), hop(nxt[1], "grp", -1)]
-        down_all.append((parts, prev, nxt, far))
+    steps = range(grp_size)
+
+    flat_ids = expert_ids.reshape(-1)
+    entries = flat_ids.shape[0]
+    hits = flat_ids[:, None] == jnp.arange(ep_size, dtype=jnp.int32)[None, :]
+    order = jnp.arange(entries, dtype=jnp.int32)
+    lower = (order[None, :] < order[:, None]).astype(jnp.bfloat16)
+    ahead = jnp.dot(lower, hits.astype(jnp.bfloat16), preferred_element_type=jnp.float32)
+    earlier = jnp.sum(jnp.where(hits, ahead, 0.0), axis=1).astype(jnp.int32)
+    slot_index = (flat_ids * capacity + earlier).reshape(samples, picks)
+    match = slot_index[:, :, None] == jnp.arange(slots_all, dtype=jnp.int32)[None, None, :]
+    placing = jnp.sum(match.astype(jnp.float32), axis=1).astype(jnp.bfloat16)
+    outgoing = lax.dot_general(
+        placing, hidden, (((0,), (0,)), ((), ())), preferred_element_type=jnp.float32
+    ).astype(jnp.bfloat16)
+    arrived = lax.all_to_all(
+        outgoing.reshape(ep_size, capacity, width), "ep", split_axis=0, concat_axis=0, tiled=True
+    ).reshape(slots_all, width)
+
+    up_all = lax.all_gather(w_up[0], "grp", axis=0, tiled=False)
+    quarter = width // grp_size
+    blocks = w_down[0].reshape(grp_size, quarter, w_down.shape[2])
+    down_own = lax.dynamic_index_in_dim(blocks, me, 0, keepdims=False)
+    down_all = [down_own] + [
+        hop(lax.dynamic_index_in_dim(blocks, (me + r) % grp_size, 0, keepdims=False), "grp", r)
+        for r in steps[1:]
+    ]
+
+    note = jnp.concatenate([slot_index.astype(jnp.float32), gate_weights], axis=1)
+    notes = jnp.concatenate([note] + [hop(note, "grp", r) for r in steps[1:]], axis=0)
+    went = notes[:, :picks].astype(jnp.int32)
+    plane = (me - jnp.arange(grp_size * samples, dtype=jnp.int32) // samples) % grp_size
+    place = (went // capacity) * grp_size + plane[:, None]
+    place = place * capacity + went % capacity
+    lanes = jnp.arange(grp_size * slots_all, dtype=jnp.int32)
+    mixing = jnp.sum(
+        jnp.where(place[:, :, None] == lanes[None, None, :], notes[:, picks:][:, :, None], 0.0),
+        axis=1,
+    )
+    high = lax.reduce_precision(mixing, 8, 7)
+    mixing = jnp.concatenate([high, mixing - high], axis=0).astype(jnp.bfloat16)
 
     moved_slot = mig_slot[0, 0]
     moved_target = mig_dest[0, 0]
+    query_second, kv_second = after(outgoing, query_second, kv_second)
     q_here = lax.dynamic_index_in_dim(query_second, moved_slot, 0, keepdims=False)
     kv_here = lax.dynamic_index_in_dim(kv_second, moved_slot, 0, keepdims=True)
     packet = jnp.concatenate(
@@ -175,8 +203,8 @@
     )
     offset = (moved_target - me) % grp_size
     got = packet
-    for step in range(1, grp_size):
-        got = jnp.where(offset == step, hop(packet, "grp", -step), got)
+    for r in steps[1:]:
+        got = jnp.where(offset == r, hop(packet, "grp", -r), got)
     heads = q_here.shape[0]
     q_in, kv_in = got[:heads], got[heads : heads + 1]
 
@@ -196,62 +224,49 @@
     )
     zero = jnp.zeros((), jnp.bfloat16)
     arrived_out = jnp.where(offset == 0, out_moved, zero)
-    for step in range(1, grp_size):
-        arrived_out = arrived_out + hop(jnp.where(offset == step, out_moved, zero), "grp", step)
+    for r in steps[1:]:
+        arrived_out = arrived_out + hop(jnp.where(offset == r, out_moved, zero), "grp", r)
     attn_second = lax.dynamic_update_index_in_dim(attn_second, arrived_out, moved_slot, 0)
 
-    flat_ids = expert_ids.reshape(-1)
-    entries = flat_ids.shape[0]
-    hits = flat_ids[:, None] == jnp.arange(ep_size, dtype=jnp.int32)[None, :]
-    order = jnp.arange(entries, dtype=jnp.int32)
-    lower = (order[None, :] < order[:, None]).astype(jnp.bfloat16)
-    ahead = jnp.dot(lower, hits.astype(jnp.bfloat16), preferred_element_type=jnp.float32)
-    earlier = jnp.sum(jnp.where(hits, ahead, 0.0), axis=1).astype(jnp.int32)
-    slot_index = (flat_ids * capacity + earlier).reshape(samples, picks)
-    slot_range = jnp.arange(slots_all, dtype=jnp.int32)
-    match = slot_index[:, :, None] == slot_range[None, None, :]
-    placing = jnp.sum(match.astype(jnp.float32), axis=1).astype(jnp.bfloat16)
-    mixing = jnp.sum(jnp.where(match, gate_weights[:, :, None], 0.0), axis=1)
-    outgoing = lax.dot_general(
-        placing, hidden, (((0,), (0,)), ((), ())), preferred_element_type=jnp.float32
-    ).astype(jnp.bfloat16)
-    arrived = lax.all_to_all(
-        outgoing.reshape(ep_size, capacity, width), "ep", split_axis=0, concat_axis=0, tiled=True
-    ).reshape(slots_all, width)
-
     f32dot = functools.partial(jnp.dot, preferred_element_type=jnp.float32)
-
-    def act(v):
-        return jax.nn.silu(v).astype(jnp.bfloat16)
-
-    def up_of(parts):
-        return act(f32dot(arrived[:, :half], parts[0]) + f32dot(arrived[:, half:], parts[1]))
-
-    h_all = [up_of(p) for p in (up_parts, up_prev, up_next, up_far)]
-    contract = (((1,), (1,)), ((), ()))
-    results = []
-    for c in range(CHUNKS):
-        cols = []
-        for s in range(2):
-            total = 0.0
-            for h, parts in zip(h_all, down_all[c]):
-                total = total + lax.dot_general(
-                    h, parts[s], contract, preferred_element_type=jnp.float32
-                )
-            cols.append(total.astype(jnp.bfloat16))
-        produced = jnp.concatenate(cols, axis=1)
-        returned = lax.all_to_all(
-            produced.reshape(ep_size, capacity, piece), "ep", split_axis=0, concat_axis=0, tiled=True
-        ).reshape(slots_all, piece)
-        results.append(
-            jnp.dot(
-                mixing,
-                returned.astype(jnp.float32),
-                preferred_element_type=jnp.float32,
-                precision=lax.Precision.HIGHEST,
-            ).astype(jnp.bfloat16)
-        )
-    moe_out = jnp.concatenate(results, axis=1)
+    arrived, *down_all = lax.optimization_barrier((arrived, *down_all))
+    held = jnp.concatenate(
+        [jax.nn.silu(f32dot(arrived, up_all[q])).astype(jnp.bfloat16) for q in range(grp_size)],
+        axis=1,
+    )
+    held_all = lax.all_gather(held, "grp", axis=0, tiled=False)
+    units = w_down.shape[2]
+    rows = (
+        held_all.reshape(grp_size, ep_size, capacity, grp_size * units)
+        .transpose(1, 0, 2, 3)
+        .reshape(grp_size * slots_all, grp_size * units)
+    )
+    produced = 0.0
+    for r in steps:
+        source = (me - r) % grp_size
+        part = lax.dynamic_slice_in_dim(rows, source * units, units, 1)
+        produced = produced + lax.dot_general(
+            part, down_all[r], (((1,), (1,)), ((), ())), preferred_element_type=jnp.float32
+        )
+    returned = lax.all_to_all(
+        produced.astype(jnp.bfloat16).reshape(ep_size, grp_size * capacity, quarter),
+        "ep",
+        split_axis=0,
+        concat_axis=0,
+        tiled=True,
+    ).reshape(grp_size * slots_all, quarter)
+    mixed = f32dot(mixing, returned)
+    tokens = grp_size * samples
+    summed = (mixed[:tokens] + mixed[tokens:]).astype(jnp.bfloat16)
+    summed = summed.reshape(grp_size, samples, quarter)
+    own = jnp.stack([summed[0]] + [hop(summed[r], "grp", -r) for r in steps[1:]])
+    moe_out = jnp.concatenate(
+        [
+            lax.dynamic_index_in_dim(own, (q - me) % grp_size, 0, keepdims=False)
+            for q in steps
+        ],
+        axis=1,
+    )
     return (attn_first, attn_second, moe_out)
 
 

time: 295 us -> 247 us (0.84)
  starting transfers between devices: 106 us -> 44.3 us
  waiting for transfers between devices: 103 us -> 125 us
  matrix products: 34.8 us -> 16.7 us
  between operations: 3.05 us -> 15.9 us
    all_gather x0 -> x2, waiting for transfers between devices: none -> 76.4 us  [the longest x1 39.7 us: shards(): up_all = lax.all_gather(w_up[0], 'grp', axis=0, tiled=False)]
    ppermute x36 -> x15, waiting for transfers between devices: 75.1 us -> 5.02 us  [hop(): lax.ppermute(value, axis, [(i, (i + step) % size) for i in range(size)])]
    all_to_all x1, waiting for transfers between devices: 0.01 us -> 37 us  [shards(): lax.all_to_all(outgoing.reshape(ep_size, capacity, width), 'ep', split_ax...]
    all_to_all x4 -> x1, starting transfers between devices: 46.4 us -> 11.8 us  [shards(): lax.all_to_all(produced.astype(jnp.bfloat16).reshape(ep_size, grp_size *...]
    ppermute x36 -> x15, starting transfers between devices: 46.3 us -> 19.4 us  [hop(): lax.ppermute(value, axis, [(i, (i + step) % size) for i in range(size)])]
    all_to_all x4 -> x1, waiting for transfers between devices: 27.9 us -> 5.67 us  [shards(): lax.all_to_all(produced.astype(jnp.bfloat16).reshape(ep_size, grp_size *...]
    dot_general x44 -> x9, matrix products: 34 us -> 15.8 us  [the longest x4 7.22 us: shards(): f32dot(arrived, up_all[q])]
    slice x2 -> x3, local copies, waits for them, and re-layouts: 5.91 us -> 0.1 us  [the longest x2 0.09 us: shards(): notes[:, picks:][:, :, None]]
  transfers between devices with their start and end apart: 41 -> 19, of which waited for: 14 -> 10; matrix products, arithmetic and copies ran while one was open for 19% -> 6% of each run, Pallas kernels for 6% -> 8%
where the time goes in v3:
time: 247 us; the launch traced here: 244 us
  waiting for transfers between devices  125 us (51%)
  starting transfers between devices  44.3 us (18%)
  local copies, waits for them, and re-layouts  19.4 us (8%)
  Pallas kernels  18.5 us (7%)
  matrix products  16.7 us (7%)
  between operations  15.9 us (6%)
  other arithmetic  4.69 us (2%)
    all_gather x1, waiting for transfers between devices, shards(): up_all = lax.all_gather(w_up[0], 'grp', axis=0, tiled=False)  39.7 us
    all_to_all x1, waiting for transfers between devices, shards(): lax.all_to_all(outgoing.reshape(ep_size, capacity, width), 'ep', split_ax...  37 us
    all_gather x1, waiting for transfers between devices, shards(): held_all = lax.all_gather(held, 'grp', axis=0, tiled=False)  36.6 us
    ppermute x15, starting transfers between devices, hop(): lax.ppermute(value, axis, [(i, (i + step) % size) for i in range(size)])  19.4 us
    pallas_call x1, Pallas kernels, attention(): pl.pallas_call(attention_kernel, grid_spec=pltpu.PrefetchScalarGridSpec(n...  18.5 us
    all_to_all x1, starting transfers between devices, shards(): lax.all_to_all(outgoing.reshape(ep_size, capacity, width), 'ep', split_ax...  13 us
    all_to_all x1, starting transfers between devices, shards(): lax.all_to_all(produced.astype(jnp.bfloat16).reshape(ep_size, grp_size *...  11.8 us
    dot_general x4, matrix products, shards(): f32dot(arrived, up_all[q])  7.22 us
  transfers between devices with their start and end apart: 19, of which 10 were waited for; matrix products, arithmetic and copies ran while one was open for 6% of the time, Pallas kernels for 8%

profile of v3, /device:TPU:1, one launch (start us, length us, event | category | flops | bytes accessed | tf_op | source)
XLA Modules:
  0.0 244.2 jit_solution(872367720402732563)
XLA Ops:
  7.2 0.7 all-gather.4.cloned.1.call-update
  7.9 0.8 copy.40
  8.7 0.1 eq.89
  8.8 0.2 fusion.4
  8.9 0.1 convert_element_type.46
  9.0 0.1 convert_reduce_fusion
  9.2 0.7 convolution_convert_fusion
  9.8 1.6 reshape.89
  11.4 13.0 %all-to-all-start = ((bf16[64,4,3584]{2,1,0:T(4,128)(2,1)}), bf16[64,4,3584]{2,1,0:T(4,128)(2,1)S(1)}, u32[]{:S(2)}, u32[]{:S(2)}) async-start(bf16[64,4,3584]{2,1,0:T(4,128)(2,1)} %reshape.89), calls=%async_computation | async-start | bytes 3670016 | tf_op jit(solution)/shard_map/all_to_all | solution.py:169
  24.5 2.8 %dynamic-slice_bitcast_fusion = (bf16[896,256]{1,0:T(8,128)(2,1)}, bf16[896,256]{1,0:T(8,128)(2,1)}, bf16[896,256]{1,0:T(8,128)(2,1)}, bf16[896,256]{1,0:T(8,128)(2,1)S(1)}) fusion(bf16[4,896,256]{2,1,0:T(8,128)(2,1)} %bitcast.76, s32[]{:T(128)S(6)} %select_n.226, s32[]{:T(128)S(6)} %select_n.224, s32[]{:T(128)S(6)} %select_n.222, s32[]{:T(128)S(6)} %select_n.220), kind=kLoop, calls=%fused_computation.23 | loop fusion | bytes 3670032 | tf_op jit(solution)/shard_map/jit(dynamic_index_in_dim)/squeeze | solution.py:178
  27.3 2.9 %collective-permute-start.10 = (bf16[896,256]{1,0:T(8,128)(2,1)}, bf16[896,256]{1,0:T(8,128)(2,1)S(1)}, u32[]{:S(2)}, u32[]{:S(2)}) collective-permute-start(bf16[896,256]{1,0:T(8,128)(2,1)} %get-tuple-element.26), channel_id=1, source_target_pairs={{0,2},{1,3},{2,0},{3,1},{4,6},{5,7},{6,4},{7,5},{8,10},{9,11},{10,... | collective-permute-start | bytes 1376264 | tf_op jit(solution)/shard_map/ppermute | solution.py:18
  30.2 0.8 collective-permute-start.11
  31.0 0.7 collective-permute-start.9
  31.7 37.0 %all-to-all-done = bf16[64,4,3584]{2,1,0:T(4,128)(2,1)S(1)} async-done(((bf16[64,4,3584]{2,1,0:T(4,128)(2,1)}), bf16[64,4,3584]{2,1,0:T(4,128)(2,1)S(1)}, u32[]{:S(2)}, u32[]{:S(2)}) %all-to-all-start) | async-done | bytes 1835040 | tf_op jit(solution)/shard_map/all_to_all | solution.py:169
  68.7 1.5 reshape.90
  70.2 0.5 collective-permute-done.11
  70.7 39.7 %all-gather.4.cloned.1.call-done = bf16[4,3584,256]{2,1,0:T(8,128)(2,1)} async-done(((bf16[1,3584,256]{2,1,0:T(8,128)(2,1)}), bf16[4,3584,256]{2,1,0:T(8,128)(2,1)}) %all-gather.4.cloned.1.call-update) | async-done | bytes 7340048 | tf_op jit(solution)/shard_map/all_gather | solution.py:173
  110.4 3.0 %multiply_convert_fusion = bf16[256,256]{0,1:T(8,128)(2,1)S(1)} fusion(bf16[256,3584]{1,0:T(8,128)(2,1)} %reshape.90, bf16[4,3584,256]{2,1,0:T(8,128)(2,1)} %all-gather.4.cloned.1.call-done), kind=kOutput, calls=%fused_computation.34 | convolution fusion | flops 470089728 | bytes 3801088 | tf_op jit(solution)/shard_map/dot_general | solution.py:234
  113.5 2.5 %multiply_convert_fusion.1 = bf16[256,256]{0,1:T(8,128)(2,1)S(1)} fusion(bf16[256,3584]{1,0:T(8,128)(2,1)S(1)} %copy-done.6, bf16[4,3584,256]{2,1,0:T(8,128)(2,1)} %all-gather.4.cloned.1.call-done), kind=kOutput, calls=%fused_computation.35 | convolution fusion | flops 470089728 | bytes 3801088 | tf_op jit(solution)/shard_map/dot_general | solution.py:234
  116.0 0.9 multiply_convert_fusion.2
  116.9 0.9 multiply_convert_fusion.3
  117.7 0.8 pad_maximum_fusion
  118.7 36.6 %all-gather.6.cloned.1.call-done = bf16[1024,1024]{0,1:T(8,128)(2,1)} async-done(((bf16[256,1024]{0,1:T(8,128)(2,1)}), bf16[1024,1024]{0,1:T(8,128)(2,1)}) %all-gather.6.cloned.1.call-update) | async-done | bytes 2097168 | tf_op jit(solution)/shard_map/all_gather | solution.py:237
  155.4 2.9 %copy.51 = bf16[1024,1024]{1,0:T(8,128)(2,1)S(1)} copy(bf16[1024,1024]{0,1:T(8,128)(2,1)} %all-gather.6.cloned.1.call-done) | data formatting | bytes 4194304 | tf_op jit(solution)/shard_map/all_gather | solution.py:237
  158.2 2.2 reshape.91
  160.4 2.8 %copy.52 = bf16[64,4,4,1024]{3,2,1,0:T(4,128)(2,1)S(1)} copy(bf16[64,4,4,1024]{3,2,0,1:T(4,128)(2,1)} %bitcast.75) | data formatting | bytes 4194304 | tf_op jit(solution)/shard_map/transpose | solution.py:241
  163.3 2.0 reshape.92
  165.3 2.1 fusion.11
  167.4 0.7 fusion.13
  168.1 0.7 fusion.9
  168.9 3.1 %add_convert_fusion = bf16[1024,896]{1,0:T(8,128)(2,1)} fusion(f32[1024,896]{1,0:T(8,128)S(1)} %fusion.9, f32[1024,896]{1,0:T(8,128)S(1)} %fusion.13, f32[1024,896]{1,0:T(8,128)S(1)} %fusion.11, bf16[896,256]{1,0:T(8,128)(2,1)} %collective-permute-done.11, bf16[1024,1024]{1,0:T(8,128)(2,1)S(1)} %copy-done.5, s32[]{:T(128)S(6)} %select_n.234), kind=kOutput, calls=%fused_computation.1 | convolution fusion | flops 473432064 | bytes 13828100 | tf_op jit(solution)/shard_map/dot_general | solution.py:248
  172.0 11.8 %all-to-all-start.1 = ((bf16[64,16,896]{2,1,0:T(8,128)(2,1)}), bf16[64,16,896]{2,1,0:T(8,128)(2,1)}, u32[]{:S(2)}, u32[]{:S(2)}) async-start(bf16[64,16,896]{2,1,0:T(8,128)(2,1)} %bitcast.20), calls=%async_computation.1 | async-start | bytes 3670016 | tf_op jit(solution)/shard_map/all_to_all | solution.py:251
  183.9 0.5 collective-permute-start.6
  184.5 2.4 collective-permute-start.7
  186.9 1.6 collective-permute-start.8
  189.3 0.1 maximum_maximum_fusion
  189.4 0.1 collective-permute-start
  189.4 1.2 collective-permute-start.1
  191.4 0.1 select_reduce_fusion.2
  191.6 0.1 min.15
  191.7 0.1 select_reduce_fusion.1.pages
  191.9 1.6 collective-permute-start.2
  193.7 0.1 pad_maximum_fusion.4
  193.8 0.1 copy.49
  193.9 0.1 copy.50
  194.0 0.7 select_reduce_fusion
  194.7 0.4 collective-permute-done
  195.1 0.6 collective-permute-done.1
  195.7 1.1 collective-permute-done.2
  196.8 1.0 select_select_fusion
  197.9 1.7 copy-done.2
  199.6 18.5 %attention.1 = (bf16[16,64,512]{2,1,0:T(8,128)(2,1)}, bf16[16,64,512]{2,1,0:T(8,128)(2,1)}, bf16[64,512]{1,0:T(8,128)(2,1)S(1)}) custom-call(s32[16]{0:T(128)S(1)} %bitcast.74, s32[128]{0:T(128)S(1)} %select_reduce_fusion.1.pages, s32[1]{0:T(128)} %bitcast.69.moved, bf16[16,64,576]{2,1,0:T(8,128)(2,1)S(1)} %copy-done.3, bf16[16,64,576]{2,1,0:T(8,128)(2,1)S(1)} %copy-done.1, ...), custom_call_target="tpu_custom_call" | custom-call | flops 12000000000 | bytes 8000000 | tf_op jit(solution)/shard_map/attention/pallas_call | solution.py:89
  218.1 1.8 collective-permute-start.3
  219.9 0.9 collective-permute-start.4
  220.8 1.6 collective-permute-start.5
  222.4 5.7 %all-to-all-done.1 = bf16[64,16,896]{2,1,0:T(8,128)(2,1)} async-done(((bf16[64,16,896]{2,1,0:T(8,128)(2,1)}), bf16[64,16,896]{2,1,0:T(8,128)(2,1)}, u32[]{:S(2)}, u32[]{:S(2)}) %all-to-all-start.1) | async-done | bytes 1835040 | tf_op jit(solution)/shard_map/all_to_all | solution.py:251
  228.1 2.0 fusion.16
  230.1 1.8 collective-permute-start.12
  231.9 0.8 collective-permute-start.13
  232.7 0.8 collective-permute-start.14
  233.5 0.7 bitcast_dynamic-update-slice_fusion
  234.1 2.0 collective-permute-done.13
  236.1 0.5 collective-permute-done.14
  236.7 0.7 pad_maximum_fusion.2
  (62 shorter events, 1.1 us)
Async XLA Ops:
  7.2 2.0 copy-start
  7.2 103.3 %all-gather.4.cloned.1.call-start = ((), (), s32[]{:S(2)}) async-start(), calls=%async_computation.2 | async-start | bytes 9175040 | tf_op jit(solution)/shard_map/all_gather | solution.py:173
  11.4 57.3 %all-to-all-start = ((bf16[64,4,3584]{2,1,0:T(4,128)(2,1)}), bf16[64,4,3584]{2,1,0:T(4,128)(2,1)S(1)}, u32[]{:S(2)}, u32[]{:S(2)}) async-start(bf16[64,4,3584]{2,1,0:T(4,128)(2,1)} %reshape.89), calls=%async_computation | async-start | bytes 3670016 | tf_op jit(solution)/shard_map/all_to_all | solution.py:169
  24.4 130.9 %all-gather.6.cloned.1.call-start = ((), (), s32[]{:S(2)}) async-start(), calls=%async_computation.3 | async-start | bytes 2621440 | tf_op jit(solution)/shard_map/all_gather | solution.py:237
  27.3 42.9 %collective-permute-start.10 = (bf16[896,256]{1,0:T(8,128)(2,1)}, bf16[896,256]{1,0:T(8,128)(2,1)S(1)}, u32[]{:S(2)}, u32[]{:S(2)}) collective-permute-start(bf16[896,256]{1,0:T(8,128)(2,1)} %get-tuple-element.26), channel_id=1, source_target_pairs={{0,2},{1,3},{2,0},{3,1},{4,6},{5,7},{6,4},{7,5},{8,10},{9,11},{10,... | collective-permute-start | bytes 1376264 | tf_op jit(solution)/shard_map/ppermute | solution.py:18
  30.2 40.5 %collective-permute-start.11 = (bf16[896,256]{1,0:T(8,128)(2,1)}, bf16[896,256]{1,0:T(8,128)(2,1)}, u32[]{:S(2)}, u32[]{:S(2)}) collective-permute-start(bf16[896,256]{1,0:T(8,128)(2,1)} %get-tuple-element.25), channel_id=1, source_target_pairs={{0,3},{1,0},{2,1},{3,2},{4,7},{5,4},{6,5},{7,6},{8,11},{9,8},{10,9... | collective-permute-start | bytes 1376264 | tf_op jit(solution)/shard_map/ppermute | solution.py:18
  31.0 39.7 %collective-permute-start.9 = (bf16[896,256]{1,0:T(8,128)(2,1)}, bf16[896,256]{1,0:T(8,128)(2,1)}, u32[]{:S(2)}, u32[]{:S(2)}) collective-permute-start(bf16[896,256]{1,0:T(8,128)(2,1)} %get-tuple-element.27), channel_id=1, source_target_pairs={{0,1},{1,2},{2,3},{3,0},{4,5},{5,6},{6,7},{7,4},{8,9},{9,10},{10,1... | collective-permute-start | bytes 1376264 | tf_op jit(solution)/shard_map/ppermute | solution.py:18
  70.7 42.8 %copy-start.6 = (bf16[256,3584]{1,0:T(8,128)(2,1)S(1)}, bf16[256,3584]{1,0:T(8,128)(2,1)}, u32[]{:S(2)}) copy-start(bf16[256,3584]{1,0:T(8,128)(2,1)} %reshape.90) | copy-start | bytes 5505028
  110.4 5.5 %copy-start.10 = (bf16[4,3584,256]{2,1,0:T(8,128)(2,1)S(1)}, bf16[4,3584,256]{2,1,0:T(8,128)(2,1)}, u32[]{:S(2)}) copy-start(bf16[4,3584,256]{2,1,0:T(8,128)(2,1)} %all-gather.4.cloned.1.call-done) | copy-start | bytes 22020100
  116.8 1.8 copy-start.9
  165.3 2.1 copy-start.5
  172.0 17.2 %copy-start.7 = (bf16[16,576]{1,0:T(8,128)(2,1)S(1)}, bf16[16,576]{1,0:T(8,128)(2,1)}, u32[]{:S(2)}) copy-start(bf16[16,576]{1,0:T(8,128)(2,1)} %param.22) | copy-start | bytes 55300
  172.0 17.2 %copy-start.1 = (bf16[16,64,576]{2,1,0:T(8,128)(2,1)S(1)}, bf16[16,64,576]{2,1,0:T(8,128)(2,1)}, u32[]{:S(2)}) copy-start(bf16[16,64,576]{2,1,0:T(8,128)(2,1)} %q_two) | copy-start | bytes 3538948
  172.0 19.4 %copy-start.4 = (s32[1,16]{1,0:T(1,128)S(1)}, s32[1,16]{1,0:T(1,128)}, u32[]{:S(2)}) copy-start(s32[1,16]{1,0:T(1,128)} %param.24) | copy-start | bytes 196
  172.0 19.7 %copy-start.11 = (s32[1,32]{1,0:T(1,128)S(1)}, s32[1,32]{1,0:T(1,128)}, u32[]{:S(2)}) copy-start(s32[1,32]{1,0:T(1,128)} %param.25) | copy-start | bytes 388
  172.0 19.8 %copy-start.8 = (bf16[16,576]{1,0:T(8,128)(2,1)S(1)}, bf16[16,576]{1,0:T(8,128)(2,1)}, u32[]{:S(2)}) copy-start(bf16[16,576]{1,0:T(8,128)(2,1)} %param.20) | copy-start | bytes 55300
  172.0 56.1 %all-to-all-start.1 = ((bf16[64,16,896]{2,1,0:T(8,128)(2,1)}), bf16[64,16,896]{2,1,0:T(8,128)(2,1)}, u32[]{:S(2)}, u32[]{:S(2)}) async-start(bf16[64,16,896]{2,1,0:T(8,128)(2,1)} %bitcast.20), calls=%async_computation.1 | async-start | bytes 3670016 | tf_op jit(solution)/shard_map/all_to_all | solution.py:251
  183.8 14.0 %copy-start.3 = (bf16[16,64,576]{2,1,0:T(8,128)(2,1)S(1)}, bf16[16,64,576]{2,1,0:T(8,128)(2,1)}, u32[]{:S(2)}) copy-start(bf16[16,64,576]{2,1,0:T(8,128)(2,1)} %q_one.1) | copy-start | bytes 3538948
  183.9 8.0 %collective-permute-start.6 = (f32[16,16]{1,0:T(8,128)S(1)}, f32[16,16]{1,0:T(8,128)S(1)}, u32[]{:S(2)}, u32[]{:S(2)}) collective-permute-start(f32[16,16]{1,0:T(8,128)S(1)} %pad_maximum_fusion.3), channel_id=1, source_target_pairs={{0,1},{1,2},{2,3},{3,0},{4,5},{5,6},{6,7},{7,4},{8,9},{9,10},{10,1... | collective-permute-start | bytes 3080 | tf_op jit(solution)/shard_map/ppermute | solution.py:18
  184.5 9.1 %collective-permute-start.7 = (f32[16,16]{1,0:T(8,128)S(1)}, f32[16,16]{1,0:T(8,128)S(1)}, u32[]{:S(2)}, u32[]{:S(2)}) collective-permute-start(f32[16,16]{1,0:T(8,128)S(1)} %pad_maximum_fusion.3), channel_id=1, source_target_pairs={{0,2},{1,3},{2,0},{3,1},{4,6},{5,7},{6,4},{7,5},{8,10},{9,11},{10,... | collective-permute-start | bytes 3080 | tf_op jit(solution)/shard_map/ppermute | solution.py:18
  186.9 6.8 %collective-permute-start.8 = (f32[16,16]{1,0:T(8,128)S(1)}, f32[16,16]{1,0:T(8,128)S(1)}, u32[]{:S(2)}, u32[]{:S(2)}) collective-permute-start(f32[16,16]{1,0:T(8,128)S(1)} %pad_maximum_fusion.3), channel_id=1, source_target_pairs={{0,3},{1,0},{2,1},{3,2},{4,7},{5,4},{6,5},{7,6},{8,11},{9,8},{10,9... | collective-permute-start | bytes 3080 | tf_op jit(solution)/shard_map/ppermute | solution.py:18
  189.4 5.7 %collective-permute-start = (bf16[80,576]{1,0:T(8,128)(2,1)S(1)}, bf16[80,576]{1,0:T(8,128)(2,1)S(1)}, u32[]{:S(2)}, u32[]{:S(2)}) collective-permute-start(bf16[80,576]{1,0:T(8,128)(2,1)S(1)} %maximum_maximum_fusion), channel_id=1, source_target_pairs={{0,1},{1,2},{2,3},{3,0},{4,5},{5,6},{6,7},{7,4},{8,9},{9,10},{10,1... | collective-permute-start | bytes 276488 | tf_op jit(solution)/shard_map/ppermute | solution.py:18
  189.4 6.3 %collective-permute-start.1 = (bf16[80,576]{1,0:T(8,128)(2,1)S(1)}, bf16[80,576]{1,0:T(8,128)(2,1)S(1)}, u32[]{:S(2)}, u32[]{:S(2)}) collective-permute-start(bf16[80,576]{1,0:T(8,128)(2,1)S(1)} %maximum_maximum_fusion), channel_id=1, source_target_pairs={{0,2},{1,3},{2,0},{3,1},{4,6},{5,7},{6,4},{7,5},{8,10},{9,11},{10,... | collective-permute-start | bytes 276488 | tf_op jit(solution)/shard_map/ppermute | solution.py:18
  191.9 4.9 %collective-permute-start.2 = (bf16[80,576]{1,0:T(8,128)(2,1)S(1)}, bf16[80,576]{1,0:T(8,128)(2,1)}, u32[]{:S(2)}, u32[]{:S(2)}) collective-permute-start(bf16[80,576]{1,0:T(8,128)(2,1)S(1)} %maximum_maximum_fusion), channel_id=1, source_target_pairs={{0,3},{1,0},{2,1},{3,2},{4,7},{5,4},{6,5},{7,6},{8,11},{9,8},{10,9... | collective-permute-start | bytes 276488 | tf_op jit(solution)/shard_map/ppermute | solution.py:18
  197.8 1.7 copy-start.2
  218.1 14.6 %collective-permute-start.3 = (bf16[64,512]{1,0:T(8,128)(2,1)S(1)}, bf16[64,512]{1,0:T(8,128)(2,1)S(1)}, u32[]{:S(2)}, u32[]{:S(2)}) collective-permute-start(bf16[64,512]{1,0:T(8,128)(2,1)S(1)} %get-tuple-element.39), channel_id=1, source_target_pairs={{0,1},{1,2},{2,3},{3,0},{4,5},{5,6},{6,7},{7,4},{8,9},{9,10},{10,1... | collective-permute-start | bytes 196616 | tf_op jit(solution)/shard_map/ppermute | solution.py:18
  219.9 13.6 %collective-permute-start.4 = (bf16[64,512]{1,0:T(8,128)(2,1)S(1)}, bf16[64,512]{1,0:T(8,128)(2,1)S(1)}, u32[]{:S(2)}, u32[]{:S(2)}) collective-permute-start(bf16[64,512]{1,0:T(8,128)(2,1)S(1)} %get-tuple-element.41), channel_id=1, source_target_pairs={{0,2},{1,3},{2,0},{3,1},{4,6},{5,7},{6,4},{7,5},{8,10},{9,11},{10,... | collective-permute-start | bytes 196616 | tf_op jit(solution)/shard_map/ppermute | solution.py:18
  220.8 12.7 %collective-permute-start.5 = (bf16[64,512]{1,0:T(8,128)(2,1)S(1)}, bf16[64,512]{1,0:T(8,128)(2,1)S(1)}, u32[]{:S(2)}, u32[]{:S(2)}) collective-permute-start(bf16[64,512]{1,0:T(8,128)(2,1)S(1)} %get-tuple-element.40), channel_id=1, source_target_pairs={{0,3},{1,0},{2,1},{3,2},{4,7},{5,4},{6,5},{7,6},{8,11},{9,8},{10,9... | collective-permute-start | bytes 196616 | tf_op jit(solution)/shard_map/ppermute | solution.py:18
  230.1 4.1 %collective-permute-start.12 = (bf16[16,896]{1,0:T(8,128)(2,1)S(1)}, bf16[16,896]{1,0:T(8,128)(2,1)S(1)}, u32[]{:S(2)}, u32[]{:S(2)}) collective-permute-start(bf16[16,896]{1,0:T(8,128)(2,1)S(1)} %get-tuple-element.38), channel_id=1, source_target_pairs={{0,3},{1,0},{2,1},{3,2},{4,7},{5,4},{6,5},{7,6},{8,11},{9,8},{10,9... | collective-permute-start | bytes 86024 | tf_op jit(solution)/shard_map/ppermute | solution.py:18
  231.9 4.2 %collective-permute-start.13 = (bf16[16,896]{1,0:T(8,128)(2,1)S(1)}, bf16[16,896]{1,0:T(8,128)(2,1)S(1)}, u32[]{:S(2)}, u32[]{:S(2)}) collective-permute-start(bf16[16,896]{1,0:T(8,128)(2,1)S(1)} %get-tuple-element.37), channel_id=1, source_target_pairs={{0,2},{1,3},{2,0},{3,1},{4,6},{5,7},{6,4},{7,5},{8,10},{9,11},{10,... | collective-permute-start | bytes 86024 | tf_op jit(solution)/shard_map/ppermute | solution.py:18
  232.7 3.9 %collective-permute-start.14 = (bf16[16,896]{1,0:T(8,128)(2,1)S(1)}, bf16[16,896]{1,0:T(8,128)(2,1)S(1)}, u32[]{:S(2)}, u32[]{:S(2)}) collective-permute-start(bf16[16,896]{1,0:T(8,128)(2,1)S(1)} %get-tuple-element.36), channel_id=1, source_target_pairs={{0,1},{1,2},{2,3},{3,0},{4,5},{5,6},{6,7},{7,4},{8,9},{9,10},{10,1... | collective-permute-start | bytes 86024 | tf_op jit(solution)/shard_map/ppermute | solution.py:18
Sparse Core Ops, SparseCore 0:
  9.8 100.5 all-gather.3
  118.7 36.6 all-gather.5

commit v4 on v3

--- a/solution.py
+++ b/solution.py
@@ -149,49 +149,66 @@
     ep_size = lax.axis_size("ep")
     grp_size = lax.axis_size("grp")
     capacity = min(samples, max(2, 2 * samples * picks // ep_size))
-    slots_all = ep_size * capacity
     me = lax.axis_index("grp")
     steps = range(grp_size)
 
-    flat_ids = expert_ids.reshape(-1)
+    half = width // 2
+    side = me // 2
+    partner = [(1, 2), (2, 1), (3, 0), (0, 3)]
+    relay = [(0, 1), (1, 0), (2, 3), (3, 2)]
+
+    def in_order(own, other, axis):
+        first = jnp.where(side == 0, own, other)
+        second = jnp.where(side == 0, other, own)
+        return jnp.concatenate([first, second], axis=axis)
+
+    def part(value, which, axis):
+        return lax.dynamic_slice_in_dim(value, which * half, half, axis)
+
+    ids = in_order(expert_ids, lax.ppermute(expert_ids, "grp", partner), 0)
+    rows = in_order(
+        part(hidden, side, 1), lax.ppermute(part(hidden, 1 - side, 1), "grp", partner), 0
+    )
+    pair_gates = lax.ppermute(gate_weights, "grp", partner)
+
+    def spread(weight):
+        ahead = jnp.where((me == 0) | (me == 3), 0, 1)
+        prev = hop(part(weight, ahead, 0), "grp", 1)
+        nxt = hop(part(weight, 1 - ahead, 0), "grp", -1)
+        return part(weight, side, 0), prev, nxt
+
+    def pass_on(prev, nxt):
+        return lax.ppermute(jnp.where(me % 2 == 0, prev, nxt), "grp", relay)
+
+    up_own, up_prev, up_next = spread(w_up[0])
+    up_prev, up_next, down = lax.optimization_barrier((up_prev, up_next, w_down[0]))
+    up_far = pass_on(up_prev, up_next)
+    down_own, down_prev, down_next = spread(down)
+    down_far = pass_on(down_prev, down_next)
+    up_all = [up_own, up_next, up_far, up_prev]
+    down_all = [down_own, down_next, down_far, down_prev]
+
+    rank = 2 * capacity
+    lanes_all = ep_size * rank
+    flat_ids = ids.reshape(-1)
     entries = flat_ids.shape[0]
     hits = flat_ids[:, None] == jnp.arange(ep_size, dtype=jnp.int32)[None, :]
     order = jnp.arange(entries, dtype=jnp.int32)
-    lower = (order[None, :] < order[:, None]).astype(jnp.bfloat16)
-    ahead = jnp.dot(lower, hits.astype(jnp.bfloat16), preferred_element_type=jnp.float32)
+    per = samples * picks
+    lower = (order[None, :] < order[:, None]) & (order[None, :] // per == order[:, None] // per)
+    ahead = jnp.dot(
+        lower.astype(jnp.bfloat16), hits.astype(jnp.bfloat16), preferred_element_type=jnp.float32
+    )
     earlier = jnp.sum(jnp.where(hits, ahead, 0.0), axis=1).astype(jnp.int32)
-    slot_index = (flat_ids * capacity + earlier).reshape(samples, picks)
-    match = slot_index[:, :, None] == jnp.arange(slots_all, dtype=jnp.int32)[None, None, :]
+    place = (flat_ids * rank + (order // per) * capacity + earlier).reshape(2 * samples, picks)
+    match = place[:, :, None] == jnp.arange(lanes_all, dtype=jnp.int32)[None, None, :]
     placing = jnp.sum(match.astype(jnp.float32), axis=1).astype(jnp.bfloat16)
     outgoing = lax.dot_general(
-        placing, hidden, (((0,), (0,)), ((), ())), preferred_element_type=jnp.float32
+        placing, rows, (((0,), (0,)), ((), ())), preferred_element_type=jnp.float32
     ).astype(jnp.bfloat16)
     arrived = lax.all_to_all(
-        outgoing.reshape(ep_size, capacity, width), "ep", split_axis=0, concat_axis=0, tiled=True
-    ).reshape(slots_all, width)
-
-    up_all = lax.all_gather(w_up[0], "grp", axis=0, tiled=False)
-    quarter = width // grp_size
-    blocks = w_down[0].reshape(grp_size, quarter, w_down.shape[2])
-    down_own = lax.dynamic_index_in_dim(blocks, me, 0, keepdims=False)
-    down_all = [down_own] + [
-        hop(lax.dynamic_index_in_dim(blocks, (me + r) % grp_size, 0, keepdims=False), "grp", r)
-        for r in steps[1:]
-    ]
-
-    note = jnp.concatenate([slot_index.astype(jnp.float32), gate_weights], axis=1)
-    notes = jnp.concatenate([note] + [hop(note, "grp", r) for r in steps[1:]], axis=0)
-    went = notes[:, :picks].astype(jnp.int32)
-    plane = (me - jnp.arange(grp_size * samples, dtype=jnp.int32) // samples) % grp_size
-    place = (went // capacity) * grp_size + plane[:, None]
-    place = place * capacity + went % capacity
-    lanes = jnp.arange(grp_size * slots_all, dtype=jnp.int32)
-    mixing = jnp.sum(
-        jnp.where(place[:, :, None] == lanes[None, None, :], notes[:, picks:][:, :, None], 0.0),
-        axis=1,
-    )
-    high = lax.reduce_precision(mixing, 8, 7)
-    mixing = jnp.concatenate([high, mixing - high], axis=0).astype(jnp.bfloat16)
+        outgoing.reshape(ep_size, rank, half), "ep", split_axis=0, concat_axis=0, tiled=True
+    ).reshape(lanes_all, half)
 
     moved_slot = mig_slot[0, 0]
     moved_target = mig_dest[0, 0]
@@ -229,44 +246,35 @@
     attn_second = lax.dynamic_update_index_in_dim(attn_second, arrived_out, moved_slot, 0)
 
     f32dot = functools.partial(jnp.dot, preferred_element_type=jnp.float32)
-    arrived, *down_all = lax.optimization_barrier((arrived, *down_all))
-    held = jnp.concatenate(
-        [jax.nn.silu(f32dot(arrived, up_all[q])).astype(jnp.bfloat16) for q in range(grp_size)],
-        axis=1,
-    )
-    held_all = lax.all_gather(held, "grp", axis=0, tiled=False)
-    units = w_down.shape[2]
-    rows = (
-        held_all.reshape(grp_size, ep_size, capacity, grp_size * units)
-        .transpose(1, 0, 2, 3)
-        .reshape(grp_size * slots_all, grp_size * units)
-    )
+    mine = [f32dot(arrived, weight) for weight in up_all]
+    theirs = lax.ppermute(jnp.stack([m.astype(jnp.bfloat16) for m in mine]), "grp", partner)
+    odd = me % 2 == 1
+    held = []
+    for i in range(grp_size):
+        other = jnp.where(odd, theirs[(i - 1) % grp_size], theirs[(i + 1) % grp_size])
+        held.append(jax.nn.silu(mine[i] + other.astype(jnp.float32)).astype(jnp.bfloat16))
     produced = 0.0
-    for r in steps:
-        source = (me - r) % grp_size
-        part = lax.dynamic_slice_in_dim(rows, source * units, units, 1)
+    for h, weight in zip(held, down_all):
         produced = produced + lax.dot_general(
-            part, down_all[r], (((1,), (1,)), ((), ())), preferred_element_type=jnp.float32
+            h, weight, (((1,), (1,)), ((), ())), preferred_element_type=jnp.float32
         )
     returned = lax.all_to_all(
-        produced.astype(jnp.bfloat16).reshape(ep_size, grp_size * capacity, quarter),
+        produced.astype(jnp.bfloat16).reshape(ep_size, rank, half),
         "ep",
         split_axis=0,
         concat_axis=0,
         tiled=True,
-    ).reshape(grp_size * slots_all, quarter)
+    ).reshape(lanes_all, half)
+    gates = in_order(gate_weights, pair_gates, 0)
+    mixing = jnp.sum(jnp.where(match, gates[:, :, None], 0.0), axis=1)
+    high = lax.reduce_precision(mixing, 8, 7)
+    mixing = jnp.concatenate([high, mixing - high], axis=0).astype(jnp.bfloat16)
     mixed = f32dot(mixing, returned)
-    tokens = grp_size * samples
-    summed = (mixed[:tokens] + mixed[tokens:]).astype(jnp.bfloat16)
-    summed = summed.reshape(grp_size, samples, quarter)
-    own = jnp.stack([summed[0]] + [hop(summed[r], "grp", -r) for r in steps[1:]])
-    moe_out = jnp.concatenate(
-        [
-            lax.dynamic_index_in_dim(own, (q - me) % grp_size, 0, keepdims=False)
-            for q in steps
-        ],
-        axis=1,
-    )
+    summed = (mixed[: 2 * samples] + mixed[2 * samples :]).astype(jnp.bfloat16)
+    first, second = summed[:samples], summed[samples:]
+    own = jnp.where(side == 0, first, second)
+    other = lax.ppermute(jnp.where(side == 0, second, first), "grp", partner)
+    moe_out = in_order(own, other, 1)
     return (attn_first, attn_second, moe_out)
 
 

time: 247 us -> 188 us (0.76)
  waiting for transfers between devices: 125 us -> 77.9 us
  between operations: 15.9 us -> 2.42 us
  local copies, waits for them, and re-layouts: 19.4 us -> 6.77 us
  matrix products: 16.7 us -> 22.7 us
  starting transfers between devices: 44.3 us -> 48.6 us
  other arithmetic: 4.69 us -> 8.24 us
    all_gather x2 -> x0, waiting for transfers between devices: 76.4 us -> none  [the longest x1 39.7 us: shards(): up_all = lax.all_gather(w_up[0], 'grp', axis=0, tiled=False)]
    ppermute x0 -> x7, waiting for transfers between devices: none -> 34.4 us  [the longest x2 20.6 us: pass_on(): return lax.ppermute(jnp.where(me % 2 == 0, prev, nxt), 'grp', relay)]
    all_to_all x2, waiting for transfers between devices: 42.7 us -> 9.15 us  [the longest x1 9.15 us: shards(): lax.all_to_all(produced.astype(jnp.bfloat16).reshape(ep_size, rank, half)...]
    ppermute x15 -> x10, waiting for transfers between devices: 5.02 us -> 34.3 us  [hop(): lax.ppermute(value, axis, [(i, (i + step) % size) for i in range(size)])]
    ppermute x0 -> x7, starting transfers between devices: none -> 8.61 us  [the longest x1 3.65 us: shards(): ids = in_order(expert_ids, lax.ppermute(expert_ids, 'grp', partner), 0)]
    reshape x4 -> x0, local copies, waits for them, and re-layouts: 7.37 us -> none  [the longest x1 2.23 us: shards(): held_all.reshape(grp_size, ep_size, capacity, grp_size * units)]
    ppermute x15 -> x10, starting transfers between devices: 19.4 us -> 12.4 us  [hop(): lax.ppermute(value, axis, [(i, (i + step) % size) for i in range(size)])]
    dot_general x10, matrix products: 14.7 us -> 20.8 us  [the longest x4 9.52 us: shards(): mine = [f32dot(arrived, weight) for weight in up_all]]
  transfers between devices with their start and end apart: 19 -> 19, of which waited for: 10 -> 11; matrix products, arithmetic and copies ran while one was open for 6% -> 14% of each run, Pallas kernels for 8% -> 10%
where the time goes in v4:
time: 188 us; the launch traced here: 186 us
  waiting for transfers between devices  77.9 us (41%)
  starting transfers between devices  48.6 us (26%)
  matrix products  22.7 us (12%)
  Pallas kernels  18.9 us (10%)
  other arithmetic  8.24 us (4%)
  local copies, waits for them, and re-layouts  6.77 us (4%)
  between operations  2.42 us (1%)
    ppermute x10, waiting for transfers between devices, hop(): lax.ppermute(value, axis, [(i, (i + step) % size) for i in range(size)])  34.3 us
    ppermute x2, waiting for transfers between devices, pass_on(): return lax.ppermute(jnp.where(me % 2 == 0, prev, nxt), 'grp', relay)  20.6 us
    pallas_call x1, Pallas kernels, attention(): pl.pallas_call(attention_kernel, grid_spec=pltpu.PrefetchScalarGridSpec(n...  18.9 us
    all_to_all x1, starting transfers between devices, shards(): lax.all_to_all(produced.astype(jnp.bfloat16).reshape(ep_size, rank, half)...  14.3 us
    all_to_all x1, starting transfers between devices, shards(): lax.all_to_all(outgoing.reshape(ep_size, rank, half), 'ep', split_axis=0,...  13.3 us
    ppermute x10, starting transfers between devices, hop(): lax.ppermute(value, axis, [(i, (i + step) % size) for i in range(size)])  12.4 us
    ppermute x1, waiting for transfers between devices, shards(): lax.ppermute(jnp.stack([m.astype(jnp.bfloat16) for m in mine]), 'grp', pa...  10.9 us
    dot_general x4, matrix products, shards(): mine = [f32dot(arrived, weight) for weight in up_all]  9.52 us
  transfers between devices with their start and end apart: 19, of which 11 were waited for; matrix products, arithmetic and copies ran while one was open for 14% of the time, Pallas kernels for 10%

profile of v4, /device:TPU:1, one launch (start us, length us, event | category | flops | bytes accessed | tf_op | source)
XLA Modules:
  0.0 185.5 jit_solution(715906140205098654)
XLA Ops:
  0.6 3.7 %collective-permute-start = (s32[16,8]{0,1:T(8,128)}, s32[16,8]{0,1:T(8,128)S(1)}, u32[]{:S(2)}, u32[]{:S(2)}) collective-permute-start(s32[16,8]{0,1:T(8,128)} %param.15), channel_id=1, source_target_pairs={{1,2},{2,1},{3,0},{0,3},{5,6},{6,5},{7,4},{4,7},{9,10},{10,9},{11,... | collective-permute-start | bytes 1544 | tf_op jit(solution)/shard_map/ppermute | solution.py:168
  4.3 0.1 collective-permute-start.8
  4.4 0.8 constant_dynamic-slice_fusion.3
  5.2 2.6 %collective-permute-start.1 = (bf16[16,1792]{1,0:T(8,128)(2,1)S(1)}, bf16[16,1792]{1,0:T(8,128)(2,1)S(1)}, u32[]{:S(2)}, u32[]{:S(2)}) collective-permute-start(bf16[16,1792]{1,0:T(8,128)(2,1)S(1)} %constant_dynamic-slice_fusion.3), channel_id=1, source_target_pairs={{1,2},{2,1},{3,0},{0,3},{5,6},{6,5},{7,4},{4,7},{9,10},{10,9},{11,... | collective-permute-start | bytes 172040 | tf_op jit(solution)/shard_map/ppermute | solution.py:170
  7.8 0.7 broadcast_select_fusion.14
  8.5 0.1 pad_add_fusion
  8.6 0.1 copy.32
  8.6 0.1 eq.53
  8.7 0.3 fusion.11
  9.0 0.1 convert_element_type.77
  9.1 0.7 broadcast_select_fusion.12
  9.8 0.1 pad_maximum_fusion.2
  9.9 0.1 copy.36
  10.0 0.4 select_reduce_fusion
  10.4 0.8 broadcast_select_fusion.10
  11.3 1.9 %convolution_convert_fusion = bf16[512,1792]{1,0:T(8,128)(2,1)} fusion(bf16[16,1792]{1,0:T(8,128)(2,1)S(1)} %get-tuple-element.28, bf16[16,1792]{1,0:T(8,128)(2,1)S(1)} %get-tuple-element.27, bf16[32,512]{1,0:T(8,128)(2,1)S(1)} %get-tuple-element.20), kind=kOutput, calls=%fused_computation.1 | convolution fusion | flops 59867136 | bytes 1982464 | tf_op jit(solution)/shard_map/dot_general | solution.py:206
  13.1 13.3 %all-to-all-start = ((bf16[64,8,1792]{2,1,0:T(8,128)(2,1)}), bf16[64,8,1792]{2,1,0:T(8,128)(2,1)}, u32[]{:S(2)}, u32[]{:S(2)}) async-start(bf16[64,8,1792]{2,1,0:T(8,128)(2,1)} %bitcast.10), calls=%async_computation | async-start | bytes 3670016 | tf_op jit(solution)/shard_map/all_to_all | solution.py:209
  26.5 1.4 dynamic-slice_bitcast_fusion
  27.8 2.5 %collective-permute-start.10 = (bf16[1792,256]{1,0:T(8,128)(2,1)}, bf16[1792,256]{1,0:T(8,128)(2,1)S(1)}, u32[]{:S(2)}, u32[]{:S(2)}) collective-permute-start(bf16[1792,256]{1,0:T(8,128)(2,1)} %get-tuple-element.23), channel_id=1, source_target_pairs={{0,3},{1,0},{2,1},{3,2},{4,7},{5,4},{6,5},{7,6},{8,11},{9,8},{10,9... | collective-permute-start | bytes 2752520 | tf_op jit(solution)/shard_map/ppermute | solution.py:18
  30.3 19.5 %collective-permute-done.10 = bf16[1792,256]{1,0:T(8,128)(2,1)S(1)} collective-permute-done((bf16[1792,256]{1,0:T(8,128)(2,1)}, bf16[1792,256]{1,0:T(8,128)(2,1)S(1)}, u32[]{:S(2)}, u32[]{:S(2)}) %collective-permute-start.10) | collective-permute-done | bytes 917536 | tf_op jit(solution)/shard_map/ppermute | solution.py:18
  49.8 3.1 %collective-permute-done.9 = bf16[1792,256]{1,0:T(8,128)(2,1)} collective-permute-done((bf16[1792,256]{1,0:T(8,128)(2,1)}, bf16[1792,256]{1,0:T(8,128)(2,1)}, u32[]{:S(2)}, u32[]{:S(2)}) %collective-permute-start.9) | collective-permute-done | bytes 917536 | tf_op jit(solution)/shard_map/ppermute | solution.py:18
  52.9 1.3 broadcast_select_fusion.1
  54.2 0.1 collective-permute-start.11
  54.3 1.4 constant_dynamic-slice_fusion.1
  55.7 1.5 collective-permute-start.14
  57.2 17.4 %collective-permute-done.11 = bf16[1792,256]{1,0:T(8,128)(2,1)} collective-permute-done((bf16[1792,256]{1,0:T(8,128)(2,1)S(1)}, bf16[1792,256]{1,0:T(8,128)(2,1)}, u32[]{:S(2)}, u32[]{:S(2)}) %collective-permute-start.11) | collective-permute-done | bytes 917536 | tf_op jit(solution)/shard_map/ppermute | solution.py:181
  74.5 2.4 %fusion.5 = f32[512,256]{1,0:T(8,128)S(1)} fusion(bf16[1792,256]{1,0:T(8,128)(2,1)} %collective-permute-done.11, bf16[64,8,1792]{2,1,0:T(8,128)(2,1)} %all-to-all-done), kind=kOutput, calls=%fused_computation.7 | convolution fusion | flops 469762048 | bytes 3276800 | tf_op jit(solution)/shard_map/dot_general | solution.py:249
  76.9 0.8 copy-done.9
  77.7 2.5 %fusion.3 = f32[512,256]{1,0:T(8,128)S(1)} fusion(bf16[1792,256]{1,0:T(8,128)(2,1)} %collective-permute-done.9, bf16[64,8,1792]{2,1,0:T(8,128)(2,1)} %all-to-all-done), kind=kOutput, calls=%fused_computation.5 | convolution fusion | flops 469762048 | bytes 3276800 | tf_op jit(solution)/shard_map/dot_general | solution.py:249
  80.2 2.4 %fusion.7 = f32[512,256]{1,0:T(8,128)S(1)} fusion(bf16[1792,256]{1,0:T(8,128)(2,1)S(1)} %copy-done.14, bf16[64,8,1792]{2,1,0:T(8,128)(2,1)} %all-to-all-done), kind=kOutput, calls=%fused_computation.9 | convolution fusion | flops 469762048 | bytes 3276800 | tf_op jit(solution)/shard_map/dot_general | solution.py:249
  82.6 2.3 %fusion.9 = f32[512,256]{1,0:T(8,128)S(1)} fusion(bf16[64,8,1792]{2,1,0:T(8,128)(2,1)} %all-to-all-done, bf16[1,3584,256]{2,1,0:T(8,128)(2,1)S(1)} %copy-done.12, s32[]{:T(128)S(6)} %select_n.240), kind=kOutput, calls=%fused_computation.11 | convolution fusion | flops 469762048 | bytes 3276804 | tf_op jit(solution)/shard_map/dot_general | solution.py:249
  85.1 1.1 pad_maximum_fusion
  86.2 8.0 %collective-permute-done.13 = bf16[1792,256]{1,0:T(8,128)(2,1)} collective-permute-done((bf16[1792,256]{1,0:T(8,128)(2,1)}, bf16[1792,256]{1,0:T(8,128)(2,1)}, u32[]{:S(2)}, u32[]{:S(2)}) %collective-permute-start.13) | collective-permute-done | bytes 917536 | tf_op jit(solution)/shard_map/ppermute | solution.py:18
  94.2 1.0 broadcast_select_fusion
  95.2 1.5 collective-permute-start.15
  96.7 10.9 %collective-permute-done.12 = bf16[4,512,256]{2,1,0:T(8,128)(2,1)} collective-permute-done((bf16[4,512,256]{2,1,0:T(8,128)(2,1)}, bf16[4,512,256]{2,1,0:T(8,128)(2,1)}, u32[]{:S(2)}, u32[]{:S(2)}) %collective-permute-start.12) | collective-permute-done | bytes 1048608 | tf_op jit(solution)/shard_map/ppermute | solution.py:250
  107.6 1.8 fusion.13
  109.3 2.1 %fusion.16 = f32[512,1792]{1,0:T(8,128)S(1)} fusion(bf16[1792,256]{1,0:T(8,128)(2,1)} %collective-permute-done.13, f32[512,256]{1,0:T(8,128)S(1)} %copy-done.8, pred[]{:T(512)S(6)} %eq.119, bf16[4,512,256]{2,1,0:T(8,128)(2,1)} %collective-permute-done.12), kind=kOutput, calls=%fused_computation.35 | convolution fusion | flops 470810624 | bytes 5636097 | tf_op jit(solution)/shard_map/dot_general | solution.py:258
  111.5 3.3 %collective-permute-done.15 = bf16[1792,256]{1,0:T(8,128)(2,1)} collective-permute-done((bf16[1792,256]{1,0:T(8,128)(2,1)}, bf16[1792,256]{1,0:T(8,128)(2,1)}, u32[]{:S(2)}, u32[]{:S(2)}) %collective-permute-start.15) | collective-permute-done | bytes 917536 | tf_op jit(solution)/shard_map/ppermute | solution.py:181
  114.8 2.1 %fusion.17 = f32[512,1792]{1,0:T(8,128)S(1)} fusion(bf16[1792,256]{1,0:T(8,128)(2,1)} %collective-permute-done.15, f32[512,256]{1,0:T(8,128)S(1)} %copy-done.10, pred[]{:T(512)S(6)} %eq.119, bf16[4,512,256]{2,1,0:T(8,128)(2,1)} %collective-permute-done.12), kind=kOutput, calls=%fused_computation.36 | convolution fusion | flops 470810624 | bytes 5636097 | tf_op jit(solution)/shard_map/dot_general | solution.py:258
  116.9 3.1 %fusion = bf16[64,8,1792]{2,1,0:T(8,128)(2,1)} fusion(f32[512,1792]{1,0:T(8,128)S(1)} %fusion.17, f32[512,1792]{1,0:T(8,128)S(1)} %fusion.13, f32[512,1792]{1,0:T(8,128)S(1)} %fusion.16, bf16[1792,256]{1,0:T(8,128)(2,1)S(1)} %collective-permute-done.14, f32[512,256]{1,0:T(8,128)S(1)} %copy-done.6, pred[]{:T(512)S(6)} %eq.119, ...), kind=kOutput, calls=%fused_computation.2 | convolution fusion | flops 474480640 | bytes 14811137 | tf_op jit(solution)/shard_map/dot_general | solution.py:258
  120.0 14.3 %all-to-all-start.1 = ((bf16[64,8,1792]{2,1,0:T(8,128)(2,1)}), bf16[64,8,1792]{2,1,0:T(8,128)(2,1)}, u32[]{:S(2)}, u32[]{:S(2)}) async-start(bf16[64,8,1792]{2,1,0:T(8,128)(2,1)} %fusion), calls=%async_computation.1 | async-start | bytes 3670016 | tf_op jit(solution)/shard_map/all_to_all | solution.py:261
  135.7 0.1 select_reduce_fusion.2
  135.9 0.1 min.15
  136.1 0.1 select_reduce_fusion.1.pages
  136.2 0.1 maximum_maximum_fusion
  136.3 1.5 collective-permute-start.2
  137.9 0.4 collective-permute-start.3
  138.2 2.1 %collective-permute-start.4 = (bf16[80,576]{1,0:T(8,128)(2,1)S(1)}, bf16[80,576]{1,0:T(8,128)(2,1)S(1)}, u32[]{:S(2)}, u32[]{:S(2)}) collective-permute-start(bf16[80,576]{1,0:T(8,128)(2,1)S(1)} %maximum_maximum_fusion), channel_id=1, source_target_pairs={{0,3},{1,0},{2,1},{3,2},{4,7},{5,4},{6,5},{7,6},{8,11},{9,8},{10,9... | collective-permute-start | bytes 276488 | tf_op jit(solution)/shard_map/ppermute | solution.py:18
  140.4 1.1 collective-permute-done.2
  141.5 1.8 collective-permute-done.3
  143.3 0.8 collective-permute-done.4
  144.1 0.1 select_select_fusion
  144.3 1.7 copy-done.1
  146.0 18.9 %attention.1 = (bf16[16,64,512]{2,1,0:T(8,128)(2,1)}, bf16[16,64,512]{2,1,0:T(8,128)(2,1)}, bf16[64,512]{1,0:T(8,128)(2,1)S(1)}) custom-call(s32[16]{0:T(128)S(1)} %bitcast.80, s32[128]{0:T(128)S(1)} %select_reduce_fusion.1.pages, s32[1]{0:T(128)} %bitcast.75.moved, bf16[16,64,576]{2,1,0:T(8,128)(2,1)S(1)} %copy-done.2, bf16[16,64,576]{2,1,0:T(8,128)(2,1)S(1)} %copy-done, ...), custom_call_target="tpu_custom_call" | custom-call | flops 12000000000 | bytes 8000000 | tf_op jit(solution)/shard_map/attention/pallas_call | solution.py:89
  165.0 1.9 %collective-permute-start.5 = (bf16[64,512]{1,0:T(8,128)(2,1)S(1)}, bf16[64,512]{1,0:T(8,128)(2,1)S(1)}, u32[]{:S(2)}, u32[]{:S(2)}) collective-permute-start(bf16[64,512]{1,0:T(8,128)(2,1)S(1)} %get-tuple-element.31), channel_id=1, source_target_pairs={{0,1},{1,2},{2,3},{3,0},{4,5},{5,6},{6,7},{7,4},{8,9},{9,10},{10,1... | collective-permute-start | bytes 196616 | tf_op jit(solution)/shard_map/ppermute | solution.py:18
  166.9 2.3 %collective-permute-start.6 = (bf16[64,512]{1,0:T(8,128)(2,1)S(1)}, bf16[64,512]{1,0:T(8,128)(2,1)S(1)}, u32[]{:S(2)}, u32[]{:S(2)}) collective-permute-start(bf16[64,512]{1,0:T(8,128)(2,1)S(1)} %get-tuple-element.33), channel_id=1, source_target_pairs={{0,2},{1,3},{2,0},{3,1},{4,6},{5,7},{6,4},{7,5},{8,10},{9,11},{10,... | collective-permute-start | bytes 196616 | tf_op jit(solution)/shard_map/ppermute | solution.py:18
  169.2 0.2 collective-permute-start.7
  169.4 9.1 %all-to-all-done.1 = bf16[64,8,1792]{2,1,0:T(8,128)(2,1)} async-done(((bf16[64,8,1792]{2,1,0:T(8,128)(2,1)}), bf16[64,8,1792]{2,1,0:T(8,128)(2,1)}, u32[]{:S(2)}, u32[]{:S(2)}) %all-to-all-start.1) | async-done | bytes 1835040 | tf_op jit(solution)/shard_map/all_to_all | solution.py:261
  178.5 1.9 %fusion.1 = f32[64,1792]{1,0:T(8,128)S(1)} fusion(bf16[64,8,1792]{2,1,0:T(8,128)(2,1)} %all-to-all-done.1, bf16[32,512]{1,0:T(8,128)(2,1)S(1)} %get-tuple-element.30, bf16[32,512]{1,0:T(8,128)(2,1)S(1)} %get-tuple-element.29), kind=kOutput, calls=%fused_computation.3 | convolution fusion | flops 117571584 | bytes 2359296 | tf_op jit(solution)/shard_map/dot_general | solution.py:272
  180.5 0.7 collective-permute-start.16
  181.3 0.7 bitcast_dynamic-update-slice_fusion
  181.9 2.9 %collective-permute-done.16 = bf16[16,1792]{1,0:T(8,128)(2,1)S(1)} collective-permute-done((bf16[16,1792]{1,0:T(8,128)(2,1)S(1)}, bf16[16,1792]{1,0:T(8,128)(2,1)S(1)}, u32[]{:S(2)}, u32[]{:S(2)}) %collective-permute-start.16) | collective-permute-done | bytes 57376 | tf_op jit(solution)/shard_map/ppermute | solution.py:276
  184.9 0.7 pad_maximum_fusion.1
  (66 shorter events, 0.6 us)
Async XLA Ops:
  0.6 7.2 %collective-permute-start = (s32[16,8]{0,1:T(8,128)}, s32[16,8]{0,1:T(8,128)S(1)}, u32[]{:S(2)}, u32[]{:S(2)}) collective-permute-start(s32[16,8]{0,1:T(8,128)} %param.15), channel_id=1, source_target_pairs={{1,2},{2,1},{3,0},{0,3},{5,6},{6,5},{7,4},{4,7},{9,10},{10,9},{11,... | collective-permute-start | bytes 1544 | tf_op jit(solution)/shard_map/ppermute | solution.py:168
  4.3 4.9 %collective-permute-start.8 = (f32[16,8]{0,1:T(8,128)}, f32[16,8]{0,1:T(8,128)S(1)}, u32[]{:S(2)}, u32[]{:S(2)}) collective-permute-start(f32[16,8]{0,1:T(8,128)} %param.16), channel_id=1, source_target_pairs={{1,2},{2,1},{3,0},{0,3},{5,6},{6,5},{7,4},{4,7},{9,10},{10,9},{11,... | collective-permute-start | bytes 1544 | tf_op jit(solution)/shard_map/ppermute | solution.py:172
  5.2 5.2 %collective-permute-start.1 = (bf16[16,1792]{1,0:T(8,128)(2,1)S(1)}, bf16[16,1792]{1,0:T(8,128)(2,1)S(1)}, u32[]{:S(2)}, u32[]{:S(2)}) collective-permute-start(bf16[16,1792]{1,0:T(8,128)(2,1)S(1)} %constant_dynamic-slice_fusion.3), channel_id=1, source_target_pairs={{1,2},{2,1},{3,0},{0,3},{5,6},{6,5},{7,4},{4,7},{9,10},{10,9},{11,... | collective-permute-start | bytes 172040 | tf_op jit(solution)/shard_map/ppermute | solution.py:170
  13.1 13.3 %copy-start.11 = (bf16[1,3584,256]{2,1,0:T(8,128)(2,1)S(1)}, bf16[1,3584,256]{2,1,0:T(8,128)(2,1)}, u32[]{:S(2)}) copy-start(bf16[1,3584,256]{2,1,0:T(8,128)(2,1)} %param.17) | copy-start | bytes 5505028
  13.1 61.4 %all-to-all-start = ((bf16[64,8,1792]{2,1,0:T(8,128)(2,1)}), bf16[64,8,1792]{2,1,0:T(8,128)(2,1)}, u32[]{:S(2)}, u32[]{:S(2)}) async-start(bf16[64,8,1792]{2,1,0:T(8,128)(2,1)} %bitcast.10), calls=%async_computation | async-start | bytes 3670016 | tf_op jit(solution)/shard_map/all_to_all | solution.py:209
  27.8 26.5 %copy-start.4 = (bf16[1,3584,256]{2,1,0:T(8,128)(2,1)S(1)}, bf16[1,3584,256]{2,1,0:T(8,128)(2,1)}, u32[]{:S(2)}) copy-start(bf16[1,3584,256]{2,1,0:T(8,128)(2,1)} %param.18) | copy-start | bytes 5505028
  27.8 22.0 %collective-permute-start.10 = (bf16[1792,256]{1,0:T(8,128)(2,1)}, bf16[1792,256]{1,0:T(8,128)(2,1)S(1)}, u32[]{:S(2)}, u32[]{:S(2)}) collective-permute-start(bf16[1792,256]{1,0:T(8,128)(2,1)} %get-tuple-element.23), channel_id=1, source_target_pairs={{0,3},{1,0},{2,1},{3,2},{4,7},{5,4},{6,5},{7,6},{8,11},{9,8},{10,9... | collective-permute-start | bytes 2752520 | tf_op jit(solution)/shard_map/ppermute | solution.py:18
  30.3 22.6 %collective-permute-start.9 = (bf16[1792,256]{1,0:T(8,128)(2,1)}, bf16[1792,256]{1,0:T(8,128)(2,1)}, u32[]{:S(2)}, u32[]{:S(2)}) collective-permute-start(bf16[1792,256]{1,0:T(8,128)(2,1)} %get-tuple-element.24), channel_id=1, source_target_pairs={{0,1},{1,2},{2,3},{3,0},{4,5},{5,6},{6,7},{7,4},{8,9},{9,10},{10,1... | collective-permute-start | bytes 2752520 | tf_op jit(solution)/shard_map/ppermute | solution.py:18
  49.8 5.9 %copy-start.13 = (bf16[1792,256]{1,0:T(8,128)(2,1)}, bf16[1792,256]{1,0:T(8,128)(2,1)S(1)}, u32[]{:S(2)}) copy-start(bf16[1792,256]{1,0:T(8,128)(2,1)S(1)} %collective-permute-done.10) | copy-start | bytes 2752516
  54.2 20.3 %collective-permute-start.11 = (bf16[1792,256]{1,0:T(8,128)(2,1)S(1)}, bf16[1792,256]{1,0:T(8,128)(2,1)}, u32[]{:S(2)}, u32[]{:S(2)}) collective-permute-start(bf16[1792,256]{1,0:T(8,128)(2,1)S(1)} %broadcast_select_fusion.1), channel_id=1, source_target_pairs={{0,1},{1,0},{2,3},{3,2},{4,5},{5,4},{6,7},{7,6},{8,9},{9,8},{10,11... | collective-permute-start | bytes 2752520 | tf_op jit(solution)/shard_map/ppermute | solution.py:181
  55.7 38.5 %collective-permute-start.13 = (bf16[1792,256]{1,0:T(8,128)(2,1)}, bf16[1792,256]{1,0:T(8,128)(2,1)}, u32[]{:S(2)}, u32[]{:S(2)}) collective-permute-start(bf16[1792,256]{1,0:T(8,128)(2,1)} %get-tuple-element.21), channel_id=1, source_target_pairs={{0,3},{1,0},{2,1},{3,2},{4,7},{5,4},{6,5},{7,6},{8,11},{9,8},{10,9... | collective-permute-start | bytes 2752520 | tf_op jit(solution)/shard_map/ppermute | solution.py:18
  55.7 38.5 %collective-permute-start.14 = (bf16[1792,256]{1,0:T(8,128)(2,1)}, bf16[1792,256]{1,0:T(8,128)(2,1)S(1)}, u32[]{:S(2)}, u32[]{:S(2)}) collective-permute-start(bf16[1792,256]{1,0:T(8,128)(2,1)} %get-tuple-element.22), channel_id=1, source_target_pairs={{0,1},{1,2},{2,3},{3,0},{4,5},{5,6},{6,7},{7,4},{8,9},{9,10},{10,1... | collective-permute-start | bytes 2752520 | tf_op jit(solution)/shard_map/ppermute | solution.py:18
  76.9 0.8 copy-start.9
  77.7 2.5 %copy-start.14 = (bf16[1792,256]{1,0:T(8,128)(2,1)S(1)}, bf16[1792,256]{1,0:T(8,128)(2,1)}, u32[]{:S(2)}) copy-start(bf16[1792,256]{1,0:T(8,128)(2,1)} %copy-done.13) | copy-start | bytes 2752516
  80.2 4.8 %copy-start.5 = (f32[512,256]{1,0:T(8,128)}, f32[512,256]{1,0:T(8,128)S(1)}, u32[]{:S(2)}) copy-start(f32[512,256]{1,0:T(8,128)S(1)} %fusion.3) | copy-start | bytes 1572868
  80.2 2.4 %copy-start.12 = (bf16[1,3584,256]{2,1,0:T(8,128)(2,1)S(1)}, bf16[1,3584,256]{2,1,0:T(8,128)(2,1)}, u32[]{:S(2)}) copy-start(bf16[1,3584,256]{2,1,0:T(8,128)(2,1)} %param.17) | copy-start | bytes 5505028
  82.6 2.4 %copy-start.7 = (f32[512,256]{1,0:T(8,128)}, f32[512,256]{1,0:T(8,128)S(1)}, u32[]{:S(2)}) copy-start(f32[512,256]{1,0:T(8,128)S(1)} %fusion.7) | copy-start | bytes 1572868
  86.2 21.4 %collective-permute-start.12 = (bf16[4,512,256]{2,1,0:T(8,128)(2,1)}, bf16[4,512,256]{2,1,0:T(8,128)(2,1)}, u32[]{:S(2)}, u32[]{:S(2)}) collective-permute-start(bf16[4,512,256]{2,1,0:T(8,128)(2,1)} %pad_maximum_fusion), channel_id=1, source_target_pairs={{1,2},{2,1},{3,0},{0,3},{5,6},{6,5},{7,4},{4,7},{9,10},{10,9},{11,... | collective-permute-start | bytes 3145736 | tf_op jit(solution)/shard_map/ppermute | solution.py:250
  95.2 19.5 %collective-permute-start.15 = (bf16[1792,256]{1,0:T(8,128)(2,1)}, bf16[1792,256]{1,0:T(8,128)(2,1)}, u32[]{:S(2)}, u32[]{:S(2)}) collective-permute-start(bf16[1792,256]{1,0:T(8,128)(2,1)} %broadcast_select_fusion), channel_id=1, source_target_pairs={{0,1},{1,0},{2,3},{3,2},{4,5},{5,4},{6,7},{7,6},{8,9},{9,8},{10,11... | collective-permute-start | bytes 2752520 | tf_op jit(solution)/shard_map/ppermute | solution.py:181
  96.7 12.7 %copy-start.8 = (f32[512,256]{1,0:T(8,128)S(1)}, f32[512,256]{1,0:T(8,128)}, u32[]{:S(2)}) copy-start(f32[512,256]{1,0:T(8,128)} %copy-done.7) | copy-start | bytes 1572868
  109.3 5.4 %copy-start.10 = (f32[512,256]{1,0:T(8,128)S(1)}, f32[512,256]{1,0:T(8,128)}, u32[]{:S(2)}) copy-start(f32[512,256]{1,0:T(8,128)} %copy-done.9) | copy-start | bytes 1572868
  111.5 5.4 %copy-start.6 = (f32[512,256]{1,0:T(8,128)S(1)}, f32[512,256]{1,0:T(8,128)}, u32[]{:S(2)}) copy-start(f32[512,256]{1,0:T(8,128)} %copy-done.5) | copy-start | bytes 1572868
  120.0 15.6 %copy-start.16 = (bf16[16,576]{1,0:T(8,128)(2,1)S(1)}, bf16[16,576]{1,0:T(8,128)(2,1)}, u32[]{:S(2)}) copy-start(bf16[16,576]{1,0:T(8,128)(2,1)} %param.20) | copy-start | bytes 55300
  120.0 15.7 %copy-start.3 = (s32[1,16]{1,0:T(1,128)S(1)}, s32[1,16]{1,0:T(1,128)}, u32[]{:S(2)}) copy-start(s32[1,16]{1,0:T(1,128)} %param.24) | copy-start | bytes 196
  120.0 16.1 %copy-start.17 = (s32[1,32]{1,0:T(1,128)S(1)}, s32[1,32]{1,0:T(1,128)}, u32[]{:S(2)}) copy-start(s32[1,32]{1,0:T(1,128)} %param.25) | copy-start | bytes 388
  120.0 16.2 %copy-start.15 = (bf16[16,576]{1,0:T(8,128)(2,1)S(1)}, bf16[16,576]{1,0:T(8,128)(2,1)}, u32[]{:S(2)}) copy-start(bf16[16,576]{1,0:T(8,128)(2,1)} %param.22) | copy-start | bytes 55300
  120.0 16.2 %copy-start = (bf16[16,64,576]{2,1,0:T(8,128)(2,1)S(1)}, bf16[16,64,576]{2,1,0:T(8,128)(2,1)}, u32[]{:S(2)}) copy-start(bf16[16,64,576]{2,1,0:T(8,128)(2,1)} %q_two) | copy-start | bytes 3538948
  120.0 24.2 %copy-start.2 = (bf16[16,64,576]{2,1,0:T(8,128)(2,1)S(1)}, bf16[16,64,576]{2,1,0:T(8,128)(2,1)}, u32[]{:S(2)}) copy-start(bf16[16,64,576]{2,1,0:T(8,128)(2,1)} %q_one.1) | copy-start | bytes 3538948
  120.0 58.5 %all-to-all-start.1 = ((bf16[64,8,1792]{2,1,0:T(8,128)(2,1)}), bf16[64,8,1792]{2,1,0:T(8,128)(2,1)}, u32[]{:S(2)}, u32[]{:S(2)}) async-start(bf16[64,8,1792]{2,1,0:T(8,128)(2,1)} %fusion), calls=%async_computation.1 | async-start | bytes 3670016 | tf_op jit(solution)/shard_map/all_to_all | solution.py:261
  136.3 5.2 %collective-permute-start.2 = (bf16[80,576]{1,0:T(8,128)(2,1)S(1)}, bf16[80,576]{1,0:T(8,128)(2,1)S(1)}, u32[]{:S(2)}, u32[]{:S(2)}) collective-permute-start(bf16[80,576]{1,0:T(8,128)(2,1)S(1)} %maximum_maximum_fusion), channel_id=1, source_target_pairs={{0,1},{1,2},{2,3},{3,0},{4,5},{5,6},{6,7},{7,4},{8,9},{9,10},{10,1... | collective-permute-start | bytes 276488 | tf_op jit(solution)/shard_map/ppermute | solution.py:18
  137.9 5.5 %collective-permute-start.3 = (bf16[80,576]{1,0:T(8,128)(2,1)S(1)}, bf16[80,576]{1,0:T(8,128)(2,1)S(1)}, u32[]{:S(2)}, u32[]{:S(2)}) collective-permute-start(bf16[80,576]{1,0:T(8,128)(2,1)S(1)} %maximum_maximum_fusion), channel_id=1, source_target_pairs={{0,2},{1,3},{2,0},{3,1},{4,6},{5,7},{6,4},{7,5},{8,10},{9,11},{10,... | collective-permute-start | bytes 276488 | tf_op jit(solution)/shard_map/ppermute | solution.py:18
  138.2 5.9 %collective-permute-start.4 = (bf16[80,576]{1,0:T(8,128)(2,1)S(1)}, bf16[80,576]{1,0:T(8,128)(2,1)S(1)}, u32[]{:S(2)}, u32[]{:S(2)}) collective-permute-start(bf16[80,576]{1,0:T(8,128)(2,1)S(1)} %maximum_maximum_fusion), channel_id=1, source_target_pairs={{0,3},{1,0},{2,1},{3,2},{4,7},{5,4},{6,5},{7,6},{8,11},{9,8},{10,9... | collective-permute-start | bytes 276488 | tf_op jit(solution)/shard_map/ppermute | solution.py:18
  144.3 1.7 copy-start.1
  165.0 16.3 %collective-permute-start.5 = (bf16[64,512]{1,0:T(8,128)(2,1)S(1)}, bf16[64,512]{1,0:T(8,128)(2,1)S(1)}, u32[]{:S(2)}, u32[]{:S(2)}) collective-permute-start(bf16[64,512]{1,0:T(8,128)(2,1)S(1)} %get-tuple-element.31), channel_id=1, source_target_pairs={{0,1},{1,2},{2,3},{3,0},{4,5},{5,6},{6,7},{7,4},{8,9},{9,10},{10,1... | collective-permute-start | bytes 196616 | tf_op jit(solution)/shard_map/ppermute | solution.py:18
  166.9 14.4 %collective-permute-start.6 = (bf16[64,512]{1,0:T(8,128)(2,1)S(1)}, bf16[64,512]{1,0:T(8,128)(2,1)S(1)}, u32[]{:S(2)}, u32[]{:S(2)}) collective-permute-start(bf16[64,512]{1,0:T(8,128)(2,1)S(1)} %get-tuple-element.33), channel_id=1, source_target_pairs={{0,2},{1,3},{2,0},{3,1},{4,6},{5,7},{6,4},{7,5},{8,10},{9,11},{10,... | collective-permute-start | bytes 196616 | tf_op jit(solution)/shard_map/ppermute | solution.py:18
  169.2 12.0 %collective-permute-start.7 = (bf16[64,512]{1,0:T(8,128)(2,1)S(1)}, bf16[64,512]{1,0:T(8,128)(2,1)S(1)}, u32[]{:S(2)}, u32[]{:S(2)}) collective-permute-start(bf16[64,512]{1,0:T(8,128)(2,1)S(1)} %get-tuple-element.32), channel_id=1, source_target_pairs={{0,3},{1,0},{2,1},{3,2},{4,7},{5,4},{6,5},{7,6},{8,11},{9,8},{10,9... | collective-permute-start | bytes 196616 | tf_op jit(solution)/shard_map/ppermute | solution.py:18
  180.5 4.3 %collective-permute-start.16 = (bf16[16,1792]{1,0:T(8,128)(2,1)S(1)}, bf16[16,1792]{1,0:T(8,128)(2,1)S(1)}, u32[]{:S(2)}, u32[]{:S(2)}) collective-permute-start(bf16[16,1792]{1,0:T(8,128)(2,1)S(1)} %broadcast_select_fusion.7), channel_id=1, source_target_pairs={{1,2},{2,1},{3,0},{0,3},{5,6},{6,5},{7,4},{4,7},{9,10},{10,9},{11,... | collective-permute-start | bytes 172040 | tf_op jit(solution)/shard_map/ppermute | solution.py:276

commit v5 on v4

--- a/solution.py
+++ b/solution.py
@@ -1,4 +1,3 @@
-import functools
 import math
 
 import jax
@@ -114,6 +113,94 @@
         ),
         name="attention",
     )(lens, pages, moved, q_one, q_two, q_in, kv_one, kv_two, kv_in, pool)
+
+
+def up_kernel(rows, *refs):
+    weights, (whole, sent) = refs[:4], refs[4:]
+    step = pl.program_id(0)
+    for i, weight in enumerate(weights):
+        part = jnp.dot(rows[...], weight[...], preferred_element_type=jnp.float32)
+
+        @pl.when(step == 0)
+        def _():
+            whole[i] = part
+
+        @pl.when(step > 0)
+        def _():
+            whole[i] += part
+
+    @pl.when(step == pl.num_programs(0) - 1)
+    def _():
+        sent[...] = whole[...].astype(jnp.bfloat16)
+
+
+def up_project(rows, weights, steps):
+    count, depth = rows.shape
+    units = weights[0].shape[1]
+    shape = (len(weights), count, units)
+    out = pl.BlockSpec(shape, lambda k: (0, 0, 0))
+    return pl.pallas_call(
+        up_kernel,
+        grid=(steps,),
+        in_specs=[pl.BlockSpec((count, depth // steps), lambda k: (0, k))]
+        + [pl.BlockSpec((depth // steps, units), lambda k: (k, 0))] * len(weights),
+        out_specs=[out, out],
+        out_shape=[
+            jax.ShapeDtypeStruct(shape, jnp.float32),
+            jax.ShapeDtypeStruct(shape, jnp.bfloat16),
+        ],
+        compiler_params=pltpu.CompilerParams(vmem_limit_bytes=32 * 1024 * 1024),
+        cost_estimate=pl.CostEstimate(
+            flops=2 * len(weights) * count * depth * units,
+            bytes_accessed=9_000_000,
+            transcendentals=0,
+        ),
+        name="up_project",
+    )(rows, *weights)
+
+
+def down_kernel(shift, mine, theirs, *refs):
+    weights, out, held = refs[:4], refs[4], refs[5]
+
+    @pl.when(pl.program_id(0) == 0)
+    def _():
+        for i in range(len(weights)):
+            other = theirs[lax.rem(i + shift[0], len(weights))].astype(jnp.float32)
+            value = mine[i] + other
+            held[i] = (value / (1.0 + jnp.exp(-value))).astype(jnp.bfloat16)
+
+    total = None
+    for i, weight in enumerate(weights):
+        part = lax.dot_general(
+            held[i], weight[...], (((1,), (1,)), ((), ())), preferred_element_type=jnp.float32
+        )
+        total = part if total is None else total + part
+    out[...] = total.astype(jnp.bfloat16)
+
+
+def down_project(shift, mine, theirs, weights, steps):
+    count, units = mine.shape[1:]
+    depth = weights[0].shape[0]
+    whole = pl.BlockSpec(mine.shape, lambda k, *_: (0, 0, 0))
+    return pl.pallas_call(
+        down_kernel,
+        grid_spec=pltpu.PrefetchScalarGridSpec(
+            num_scalar_prefetch=1,
+            grid=(steps,),
+            in_specs=[whole, whole]
+            + [pl.BlockSpec((depth // steps, units), lambda k, *_: (k, 0))] * len(weights),
+            out_specs=pl.BlockSpec((count, depth // steps), lambda k, *_: (0, k)),
+            scratch_shapes=[pltpu.VMEM(mine.shape, jnp.bfloat16)],
+        ),
+        out_shape=jax.ShapeDtypeStruct((count, depth), jnp.bfloat16),
+        compiler_params=pltpu.CompilerParams(vmem_limit_bytes=32 * 1024 * 1024),
+        cost_estimate=pl.CostEstimate(
+            flops=2 * len(weights) * count * depth * units,
+            bytes_accessed=9_000_000,
+            transcendentals=mine.size,
+        ),
+        name="down_project",
+    )(shift, mine, theirs, *weights)
 
 
 def page_table(cache_len, page_perm, page_rows, pool_pages):
@@ -165,11 +252,10 @@
     def part(value, which, axis):
         return lax.dynamic_slice_in_dim(value, which * half, half, axis)
 
-    ids = in_order(expert_ids, lax.ppermute(expert_ids, "grp", partner), 0)
     rows = in_order(
         part(hidden, side, 1), lax.ppermute(part(hidden, 1 - side, 1), "grp", partner), 0
     )
-    pair_gates = lax.ppermute(gate_weights, "grp", partner)
+    ids = in_order(expert_ids, lax.ppermute(expert_ids, "grp", partner), 0)
 
     def spread(weight):
         ahead = jnp.where((me == 0) | (me == 3), 0, 1)
@@ -245,31 +331,23 @@
         arrived_out = arrived_out + hop(jnp.where(offset == r, out_moved, zero), "grp", r)
     attn_second = lax.dynamic_update_index_in_dim(attn_second, arrived_out, moved_slot, 0)
 
-    f32dot = functools.partial(jnp.dot, preferred_element_type=jnp.float32)
-    mine = [f32dot(arrived, weight) for weight in up_all]
-    theirs = lax.ppermute(jnp.stack([m.astype(jnp.bfloat16) for m in mine]), "grp", partner)
-    odd = me % 2 == 1
-    held = []
-    for i in range(grp_size):
-        other = jnp.where(odd, theirs[(i - 1) % grp_size], theirs[(i + 1) % grp_size])
-        held.append(jax.nn.silu(mine[i] + other.astype(jnp.float32)).astype(jnp.bfloat16))
-    produced = 0.0
-    for h, weight in zip(held, down_all):
-        produced = produced + lax.dot_general(
-            h, weight, (((1,), (1,)), ((), ())), preferred_element_type=jnp.float32
-        )
+    mine, rounded = up_project(arrived, up_all, 2)
+    theirs = lax.ppermute(rounded, "grp", partner)
+    shift = jnp.where(me % 2 == 1, grp_size - 1, 1).astype(jnp.int32)
+    produced = down_project(shift[None], mine, theirs, down_all, 7)
     returned = lax.all_to_all(
-        produced.astype(jnp.bfloat16).reshape(ep_size, rank, half),
+        produced.reshape(ep_size, rank, half),
         "ep",
         split_axis=0,
         concat_axis=0,
         tiled=True,
     ).reshape(lanes_all, half)
-    gates = in_order(gate_weights, pair_gates, 0)
+    (late_gates,) = after(outgoing, gate_weights)
+    gates = in_order(gate_weights, lax.ppermute(late_gates, "grp", partner), 0)
     mixing = jnp.sum(jnp.where(match, gates[:, :, None], 0.0), axis=1)
     high = lax.reduce_precision(mixing, 8, 7)
     mixing = jnp.concatenate([high, mixing - high], axis=0).astype(jnp.bfloat16)
-    mixed = f32dot(mixing, returned)
+    mixed = jnp.dot(mixing, returned, preferred_element_type=jnp.float32)
     summed = (mixed[: 2 * samples] + mixed[2 * samples :]).astype(jnp.bfloat16)
     first, second = summed[:samples], summed[samples:]
     own = jnp.where(side == 0, first, second)

time: 188 us -> 188 us (level)
  matrix products: 22.7 us -> 4.11 us
  Pallas kernels: 18.9 us -> 34.6 us
  local copies, waits for them, and re-layouts: 6.77 us -> 14.7 us
  other arithmetic: 8.24 us -> 5.2 us
  starting transfers between devices: 48.6 us -> 45.6 us
    dot_general x9 -> x1, matrix products: 20.6 us -> 1.94 us  [shards(): mixed = jnp.dot(mixing, returned, preferred_element_type=jnp.float32)]
    pallas_call x0 -> x2, Pallas kernels: none -> 15.6 us  [the longest x1 8.06 us: up_project(): pl.pallas_call(up_kernel, grid=(steps,), in_specs=[pl.BlockSpec((count, d...]
    ppermute x2, waiting for transfers between devices: 20.6 us -> 35.6 us  [pass_on(): return lax.ppermute(jnp.where(me % 2 == 0, prev, nxt), 'grp', relay)]
    ppermute x2, waiting for transfers between devices: 10.9 us -> 0.46 us  [the longest x1 0.46 us: shards(): gates = in_order(gate_weights, lax.ppermute(late_gates, 'grp', partner), 0)]
    unnamed x36 -> x38, local copies, waits for them, and re-layouts: 2.59 us -> 10.4 us
    ppermute x10, waiting for transfers between devices: 34.3 us -> 30.4 us  [hop(): lax.ppermute(value, axis, [(i, (i + step) % size) for i in range(size)])]
    ppermute x10, starting transfers between devices: 12.4 us -> 8.75 us  [hop(): lax.ppermute(value, axis, [(i, (i + step) % size) for i in range(size)])]
    ppermute x2, starting transfers between devices: 0.1 us -> 3.12 us  [the longest x1 1.65 us: shards(): gates = in_order(gate_weights, lax.ppermute(late_gates, 'grp', partner), 0)]
  transfers between devices with their start and end apart: 19 -> 19, of which waited for: 11 -> 14; matrix products, arithmetic and copies ran while one was open for 14% -> 6% of each run, Pallas kernels for 10% -> 15%
where the time goes in v5:
time: 188 us; the launch traced here: 185 us
  waiting for transfers between devices  78.9 us (42%)
  starting transfers between devices  45.6 us (24%)
  Pallas kernels  34.6 us (18%)
  local copies, waits for them, and re-layouts  14.7 us (8%)
  other arithmetic  5.2 us (3%)
  matrix products  4.11 us (2%)
  between operations  2.25 us (1%)
    ppermute x2, waiting for transfers between devices, pass_on(): return lax.ppermute(jnp.where(me % 2 == 0, prev, nxt), 'grp', relay)  35.6 us
    ppermute x10, waiting for transfers between devices, hop(): lax.ppermute(value, axis, [(i, (i + step) % size) for i in range(size)])  30.4 us
    pallas_call x1, Pallas kernels, attention(): pl.pallas_call(attention_kernel, grid_spec=pltpu.PrefetchScalarGridSpec(n...  19 us
    all_to_all x1, starting transfers between devices, shards(): lax.all_to_all(produced.reshape(ep_size, rank, half), 'ep', split_axis=0,...  14.2 us
    all_to_all x1, starting transfers between devices, shards(): lax.all_to_all(outgoing.reshape(ep_size, rank, half), 'ep', split_axis=0,...  13.9 us
    unnamed x38, local copies, waits for them, and re-layouts  10.4 us
    ppermute x10, starting transfers between devices, hop(): lax.ppermute(value, axis, [(i, (i + step) % size) for i in range(size)])  8.75 us
    pallas_call x1, Pallas kernels, up_project(): pl.pallas_call(up_kernel, grid=(steps,), in_specs=[pl.BlockSpec((count, d...  8.06 us
  transfers between devices with their start and end apart: 19, of which 14 were waited for; matrix products, arithmetic and copies ran while one was open for 6% of the time, Pallas kernels for 15%

profile of v5, /device:TPU:1, one launch (start us, length us, event | category | flops | bytes accessed | tf_op | source)
XLA Modules:
  0.0 185.3 jit_solution(8382780501497933735)
XLA Ops:
  0.6 3.7 %collective-permute-start = (s32[16,8]{0,1:T(8,128)}, s32[16,8]{0,1:T(8,128)S(1)}, u32[]{:S(2)}, u32[]{:S(2)}) collective-permute-start(s32[16,8]{0,1:T(8,128)} %param.15), channel_id=1, source_target_pairs={{1,2},{2,1},{3,0},{0,3},{5,6},{6,5},{7,4},{4,7},{9,10},{10,9},{11,... | collective-permute-start | bytes 1544 | tf_op jit(solution)/shard_map/ppermute | solution.py:258
  4.3 0.8 constant_dynamic-slice_fusion.4
  5.2 0.3 collective-permute-done
  5.5 0.7 broadcast_select_fusion.14
  6.3 0.1 eq.53
  6.4 0.3 fusion.2
  6.7 0.1 convert_element_type.26
  6.8 0.2 convert_reduce_fusion
  7.1 2.3 %collective-permute-done.1 = bf16[16,1792]{1,0:T(8,128)(2,1)S(1)} collective-permute-done((bf16[16,1792]{1,0:T(8,128)(2,1)S(1)}, bf16[16,1792]{1,0:T(8,128)(2,1)S(1)}, u32[]{:S(2)}, u32[]{:S(2)}) %collective-permute-start.1) | collective-permute-done | bytes 57376 | tf_op jit(solution)/shard_map/ppermute | solution.py:256
  9.3 0.8 broadcast_select_fusion.10
  10.2 1.9 %convolution_convert_fusion = bf16[512,1792]{1,0:T(8,128)(2,1)} fusion(bf16[16,1792]{1,0:T(8,128)(2,1)S(1)} %get-tuple-element.34, bf16[16,1792]{1,0:T(8,128)(2,1)S(1)} %get-tuple-element.33, bf16[32,512]{1,0:T(8,128)(2,1)S(1)} %convert_reduce_fusion), kind=kOutput, calls=%fused_computation | convolution fusion | flops 59867136 | bytes 1982464 | tf_op jit(solution)/shard_map/dot_general | solution.py:292
  12.1 13.9 %all-to-all-start = ((bf16[64,8,1792]{2,1,0:T(8,128)(2,1)}), bf16[64,8,1792]{2,1,0:T(8,128)(2,1)}, u32[]{:S(2)}, u32[]{:S(2)}) async-start(bf16[64,8,1792]{2,1,0:T(8,128)(2,1)} %bitcast.11), calls=%async_computation | async-start | bytes 3670016 | tf_op jit(solution)/shard_map/all_to_all | solution.py:295
  26.0 1.4 dynamic-slice_bitcast_fusion
  27.4 0.1 collective-permute-start.10
  27.5 1.3 collective-permute-start.9
  28.9 20.2 %collective-permute-done.10.refs_1_ = bf16[1792,256]{1,0:T(8,128)(2,1)S(1)} collective-permute-done((bf16[1792,256]{1,0:T(8,128)(2,1)}, bf16[1792,256]{1,0:T(8,128)(2,1)S(1)}, u32[]{:S(2)}, u32[]{:S(2)}) %collective-permute-start.10) | collective-permute-done | bytes 917536 | tf_op jit(solution)/shard_map/ppermute | solution.py:17
  49.1 0.8 collective-permute-done.9.refs_3_
  49.9 0.1 broadcast_select_fusion.1
  50.0 0.2 collective-permute-start.11
  50.3 1.5 constant_dynamic-slice_fusion
  51.7 1.3 collective-permute-start.14
  53.1 1.3 collective-permute-start.13
  54.4 16.1 %collective-permute-done.11.refs_2_ = bf16[1792,256]{1,0:T(8,128)(2,1)S(1)} collective-permute-done((bf16[1792,256]{1,0:T(8,128)(2,1)S(1)}, bf16[1792,256]{1,0:T(8,128)(2,1)S(1)}, u32[]{:S(2)}, u32[]{:S(2)}) %collective-permute-start.11) | collective-permute-done | bytes 917536 | tf_op jit(solution)/shard_map/ppermute | solution.py:267
  70.5 0.9 copy-done.10
  71.4 1.2 copy-done.2
  72.6 1.2 copy-done.4
  73.8 1.2 copy-done.6
  75.0 1.2 copy-done.11
  76.1 8.1 %up_project.1 = (f32[4,512,256]{2,1,0:T(8,128)S(1)}, bf16[4,512,256]{2,1,0:T(8,128)(2,1)}) custom-call(bf16[512,1792]{1,0:T(8,128)(2,1)} %bitcast.12.rows, bf16[1792,256]{1,0:T(8,128)(2,1)S(1)} %copy-done.2, bf16[1792,256]{1,0:T(8,128)(2,1)S(1)} %copy-done.4, bf16[1792,256]{1,0:T(8,128)(2,1)S(1)} %copy-done.11, bf16[1792,256]{1,0:T(8,128)(2,1)S(1)} %copy-done.6), custom_call_target="tpu_custom_call" | custom-call | flops 1879048192 | bytes 9000000 | tf_op jit(solution)/shard_map/up_project/pallas_call | solution.py:142
  84.2 1.3 copy-done
  85.5 1.5 collective-permute-start.12
  87.0 1.1 collective-permute-done.14.refs_3_
  88.1 2.0 %collective-permute-done.13.refs_1_ = bf16[1792,256]{1,0:T(8,128)(2,1)S(1)} collective-permute-done((bf16[1792,256]{1,0:T(8,128)(2,1)}, bf16[1792,256]{1,0:T(8,128)(2,1)S(1)}, u32[]{:S(2)}, u32[]{:S(2)}) %collective-permute-start.13) | collective-permute-done | bytes 917536 | tf_op jit(solution)/shard_map/ppermute | solution.py:17
  90.1 1.0 broadcast_select_fusion
  91.1 0.1 collective-permute-start.15
  91.2 19.5 %collective-permute-done.15.refs_2_ = bf16[1792,256]{1,0:T(8,128)(2,1)} collective-permute-done((bf16[1792,256]{1,0:T(8,128)(2,1)}, bf16[1792,256]{1,0:T(8,128)(2,1)}, u32[]{:S(2)}, u32[]{:S(2)}) %collective-permute-start.15) | collective-permute-done | bytes 917536 | tf_op jit(solution)/shard_map/ppermute | solution.py:267
  110.7 1.6 copy-done.1
  112.3 7.6 %down_project.1 = bf16[512,1792]{1,0:T(8,128)(2,1)} custom-call(s32[1]{0:T(128)} %bitcast.10.shift, f32[4,512,256]{2,1,0:T(8,128)S(1)} %copy-done.1, bf16[4,512,256]{2,1,0:T(8,128)(2,1)} %collective-permute-done.12.theirs, bf16[1792,256]{1,0:T(8,128)(2,1)S(1)} %get-tuple-element.27.refs_0_, bf16[1792,256]{1,0:T(8,128)(2,1)S(1)} %collective-permute-done.13.refs_1_, ...), custom_call_target="tpu_custom_call" | custom-call | flops 1879048192 | bytes 9000000 | tf_op jit(solution)/shard_map/down_project/pallas_call | solution.py:185
  120.0 14.2 %all-to-all-start.1 = ((bf16[64,8,1792]{2,1,0:T(8,128)(2,1)}), bf16[64,8,1792]{2,1,0:T(8,128)(2,1)}, u32[]{:S(2)}, u32[]{:S(2)}) async-start(bf16[64,8,1792]{2,1,0:T(8,128)(2,1)} %bitcast.17), calls=%async_computation.1 | async-start | bytes 3670016 | tf_op jit(solution)/shard_map/all_to_all | solution.py:338
  135.5 0.1 select_reduce_fusion.2
  135.7 0.1 min.15
  135.9 0.1 select_reduce_fusion.1.pages
  136.0 1.7 collective-permute-start.8
  137.7 0.1 maximum_maximum_fusion
  137.8 1.2 collective-permute-start.4
  139.0 0.3 collective-permute-start.3
  139.3 0.4 collective-permute-start.2
  139.7 0.5 collective-permute-done.8
  140.2 0.1 copy.36
  140.3 0.2 select_reduce_fusion
  140.5 1.2 collective-permute-done.4
  141.8 2.6 %collective-permute-done.3 = bf16[80,576]{1,0:T(8,128)(2,1)S(1)} collective-permute-done((bf16[80,576]{1,0:T(8,128)(2,1)S(1)}, bf16[80,576]{1,0:T(8,128)(2,1)S(1)}, u32[]{:S(2)}, u32[]{:S(2)}) %collective-permute-start.3) | collective-permute-done | bytes 92192 | tf_op jit(solution)/shard_map/ppermute | solution.py:17
  144.4 2.5 %collective-permute-done.2 = bf16[80,576]{1,0:T(8,128)(2,1)S(1)} collective-permute-done((bf16[80,576]{1,0:T(8,128)(2,1)S(1)}, bf16[80,576]{1,0:T(8,128)(2,1)S(1)}, u32[]{:S(2)}, u32[]{:S(2)}) %collective-permute-start.2) | collective-permute-done | bytes 92192 | tf_op jit(solution)/shard_map/ppermute | solution.py:17
  146.9 0.1 select_select_fusion
  147.1 1.7 copy-done.8
  148.8 19.0 %attention.1 = (bf16[16,64,512]{2,1,0:T(8,128)(2,1)}, bf16[16,64,512]{2,1,0:T(8,128)(2,1)}, bf16[64,512]{1,0:T(8,128)(2,1)S(1)}) custom-call(s32[16]{0:T(128)S(1)} %bitcast.33, s32[128]{0:T(128)S(1)} %select_reduce_fusion.1.pages, s32[1]{0:T(128)} %bitcast.28.moved, bf16[16,64,576]{2,1,0:T(8,128)(2,1)S(1)} %copy-done.9, bf16[16,64,576]{2,1,0:T(8,128)(2,1)S(1)} %copy-done.7, ...), custom_call_target="tpu_custom_call" | custom-call | flops 12000000000 | bytes 8000000 | tf_op jit(solution)/shard_map/attention/pallas_call | solution.py:88
  167.8 0.1 collective-permute-start.5
  167.9 2.7 %collective-permute-start.7 = (bf16[64,512]{1,0:T(8,128)(2,1)S(1)}, bf16[64,512]{1,0:T(8,128)(2,1)S(1)}, u32[]{:S(2)}, u32[]{:S(2)}) collective-permute-start(bf16[64,512]{1,0:T(8,128)(2,1)S(1)} %get-tuple-element.38), channel_id=1, source_target_pairs={{0,3},{1,0},{2,1},{3,2},{4,7},{5,4},{6,5},{7,6},{8,11},{9,8},{10,9... | collective-permute-start | bytes 196616 | tf_op jit(solution)/shard_map/ppermute | solution.py:17
  170.5 7.8 %all-to-all-done.1 = bf16[64,8,1792]{2,1,0:T(8,128)(2,1)} async-done(((bf16[64,8,1792]{2,1,0:T(8,128)(2,1)}), bf16[64,8,1792]{2,1,0:T(8,128)(2,1)}, u32[]{:S(2)}, u32[]{:S(2)}) %all-to-all-start.1) | async-done | bytes 1835040 | tf_op jit(solution)/shard_map/all_to_all | solution.py:338
  178.3 1.9 %fusion = f32[64,1792]{1,0:T(8,128)S(1)} fusion(bf16[64,8,1792]{2,1,0:T(8,128)(2,1)} %all-to-all-done.1, bf16[32,512]{1,0:T(8,128)(2,1)S(1)} %get-tuple-element.36, bf16[32,512]{1,0:T(8,128)(2,1)S(1)} %get-tuple-element.35), kind=kOutput, calls=%fused_computation.1 | convolution fusion | flops 117571584 | bytes 2359296 | tf_op jit(solution)/shard_map/dot_general | solution.py:350
  180.3 1.7 collective-permute-start.16
  182.0 0.7 bitcast_dynamic-update-slice_fusion
  182.7 2.0 %collective-permute-done.16 = bf16[16,1792]{1,0:T(8,128)(2,1)S(1)} collective-permute-done((bf16[16,1792]{1,0:T(8,128)(2,1)S(1)}, bf16[16,1792]{1,0:T(8,128)(2,1)S(1)}, u32[]{:S(2)}, u32[]{:S(2)}) %collective-permute-start.16) | collective-permute-done | bytes 57376 | tf_op jit(solution)/shard_map/ppermute | solution.py:354
  184.7 0.7 pad_maximum_fusion
  (59 shorter events, 0.7 us)
Async XLA Ops:
  0.6 4.9 %collective-permute-start = (s32[16,8]{0,1:T(8,128)}, s32[16,8]{0,1:T(8,128)S(1)}, u32[]{:S(2)}, u32[]{:S(2)}) collective-permute-start(s32[16,8]{0,1:T(8,128)} %param.15), channel_id=1, source_target_pairs={{1,2},{2,1},{3,0},{0,3},{5,6},{6,5},{7,4},{4,7},{9,10},{10,9},{11,... | collective-permute-start | bytes 1544 | tf_op jit(solution)/shard_map/ppermute | solution.py:258
  5.1 4.2 %collective-permute-start.1 = (bf16[16,1792]{1,0:T(8,128)(2,1)S(1)}, bf16[16,1792]{1,0:T(8,128)(2,1)S(1)}, u32[]{:S(2)}, u32[]{:S(2)}) collective-permute-start(bf16[16,1792]{1,0:T(8,128)(2,1)S(1)} %constant_dynamic-slice_fusion.4), channel_id=1, source_target_pairs={{1,2},{2,1},{3,0},{0,3},{5,6},{6,5},{7,4},{4,7},{9,10},{10,9},{11,... | collective-permute-start | bytes 172040 | tf_op jit(solution)/shard_map/ppermute | solution.py:256
  12.1 13.9 %copy-start.13 = (bf16[1,3584,256]{2,1,0:T(8,128)(2,1)S(1)}, bf16[1,3584,256]{2,1,0:T(8,128)(2,1)}, u32[]{:S(2)}) copy-start(bf16[1,3584,256]{2,1,0:T(8,128)(2,1)} %param.17) | copy-start | bytes 5505028
  12.1 59.3 %all-to-all-start = ((bf16[64,8,1792]{2,1,0:T(8,128)(2,1)}), bf16[64,8,1792]{2,1,0:T(8,128)(2,1)}, u32[]{:S(2)}, u32[]{:S(2)}) async-start(bf16[64,8,1792]{2,1,0:T(8,128)(2,1)} %bitcast.11), calls=%async_computation | async-start | bytes 3670016 | tf_op jit(solution)/shard_map/all_to_all | solution.py:295
  27.4 21.7 %collective-permute-start.10 = (bf16[1792,256]{1,0:T(8,128)(2,1)}, bf16[1792,256]{1,0:T(8,128)(2,1)S(1)}, u32[]{:S(2)}, u32[]{:S(2)}) collective-permute-start(bf16[1792,256]{1,0:T(8,128)(2,1)} %get-tuple-element.28), channel_id=1, source_target_pairs={{0,3},{1,0},{2,1},{3,2},{4,7},{5,4},{6,5},{7,6},{8,11},{9,8},{10,9... | collective-permute-start | bytes 2752520 | tf_op jit(solution)/shard_map/ppermute | solution.py:17
  27.5 22.4 %collective-permute-start.9 = (bf16[1792,256]{1,0:T(8,128)(2,1)S(1)}, bf16[1792,256]{1,0:T(8,128)(2,1)S(1)}, u32[]{:S(2)}, u32[]{:S(2)}) collective-permute-start(bf16[1792,256]{1,0:T(8,128)(2,1)S(1)} %get-tuple-element.30), channel_id=1, source_target_pairs={{0,1},{1,2},{2,3},{3,0},{4,5},{5,6},{6,7},{7,4},{8,9},{9,10},{10,1... | collective-permute-start | bytes 2752520 | tf_op jit(solution)/shard_map/ppermute | solution.py:17
  28.9 21.4 %copy-start.14 = (bf16[1,3584,256]{2,1,0:T(8,128)(2,1)S(1)}, bf16[1,3584,256]{2,1,0:T(8,128)(2,1)}, u32[]{:S(2)}) copy-start(bf16[1,3584,256]{2,1,0:T(8,128)(2,1)} %param.18) | copy-start | bytes 5505028
  49.1 0.9 copy-start.3
  49.9 1.8 copy-start.5
  50.0 20.5 %collective-permute-start.11 = (bf16[1792,256]{1,0:T(8,128)(2,1)S(1)}, bf16[1792,256]{1,0:T(8,128)(2,1)S(1)}, u32[]{:S(2)}, u32[]{:S(2)}) collective-permute-start(bf16[1792,256]{1,0:T(8,128)(2,1)S(1)} %broadcast_select_fusion.1), channel_id=1, source_target_pairs={{0,1},{1,0},{2,3},{3,2},{4,5},{5,4},{6,7},{7,6},{8,9},{9,8},{10,11... | collective-permute-start | bytes 2752520 | tf_op jit(solution)/shard_map/ppermute | solution.py:267
  51.7 36.4 %collective-permute-start.14 = (bf16[1792,256]{1,0:T(8,128)(2,1)}, bf16[1792,256]{1,0:T(8,128)(2,1)S(1)}, u32[]{:S(2)}, u32[]{:S(2)}) collective-permute-start(bf16[1792,256]{1,0:T(8,128)(2,1)} %get-tuple-element.25), channel_id=1, source_target_pairs={{0,1},{1,2},{2,3},{3,0},{4,5},{5,6},{6,7},{7,4},{8,9},{9,10},{10,1... | collective-permute-start | bytes 2752520 | tf_op jit(solution)/shard_map/ppermute | solution.py:17
  53.1 37.0 %collective-permute-start.13 = (bf16[1792,256]{1,0:T(8,128)(2,1)}, bf16[1792,256]{1,0:T(8,128)(2,1)S(1)}, u32[]{:S(2)}, u32[]{:S(2)}) collective-permute-start(bf16[1792,256]{1,0:T(8,128)(2,1)} %get-tuple-element.26), channel_id=1, source_target_pairs={{0,3},{1,0},{2,1},{3,2},{4,7},{5,4},{6,5},{7,6},{8,11},{9,8},{10,9... | collective-permute-start | bytes 2752520 | tf_op jit(solution)/shard_map/ppermute | solution.py:17
  70.5 0.9 copy-start.10
  71.4 1.2 copy-start.2
  72.6 1.2 copy-start.4
  73.8 1.2 copy-start.6
  75.0 1.2 copy-start.11
  84.2 1.3 copy-start
  85.5 25.2 %collective-permute-start.12 = (bf16[4,512,256]{2,1,0:T(8,128)(2,1)}, bf16[4,512,256]{2,1,0:T(8,128)(2,1)}, u32[]{:S(2)}, u32[]{:S(2)}) collective-permute-start(bf16[4,512,256]{2,1,0:T(8,128)(2,1)} %get-tuple-element.23), channel_id=1, source_target_pairs={{1,2},{2,1},{3,0},{0,3},{5,6},{6,5},{7,4},{4,7},{9,10},{10,9},{11,... | collective-permute-start | bytes 3145736 | tf_op jit(solution)/shard_map/ppermute | solution.py:335
  91.1 19.7 %collective-permute-start.15 = (bf16[1792,256]{1,0:T(8,128)(2,1)}, bf16[1792,256]{1,0:T(8,128)(2,1)}, u32[]{:S(2)}, u32[]{:S(2)}) collective-permute-start(bf16[1792,256]{1,0:T(8,128)(2,1)} %broadcast_select_fusion), channel_id=1, source_target_pairs={{0,1},{1,0},{2,3},{3,2},{4,5},{5,4},{6,7},{7,6},{8,9},{9,8},{10,11... | collective-permute-start | bytes 2752520 | tf_op jit(solution)/shard_map/ppermute | solution.py:267
  110.7 1.6 copy-start.1
  119.9 15.6 %copy-start.12 = (s32[1,16]{1,0:T(1,128)S(1)}, s32[1,16]{1,0:T(1,128)}, u32[]{:S(2)}) copy-start(s32[1,16]{1,0:T(1,128)} %param.24) | copy-start | bytes 196
  119.9 15.9 %copy-start.16 = (bf16[16,576]{1,0:T(8,128)(2,1)S(1)}, bf16[16,576]{1,0:T(8,128)(2,1)}, u32[]{:S(2)}) copy-start(bf16[16,576]{1,0:T(8,128)(2,1)} %param.20) | copy-start | bytes 55300
  119.9 16.0 %copy-start.18 = (s32[1,32]{1,0:T(1,128)S(1)}, s32[1,32]{1,0:T(1,128)}, u32[]{:S(2)}) copy-start(s32[1,32]{1,0:T(1,128)} %param.25) | copy-start | bytes 388
  119.9 16.1 %copy-start.17 = (f32[16,8]{0,1:T(8,128)S(1)}, f32[16,8]{0,1:T(8,128)}, u32[]{:S(2)}) copy-start(f32[16,8]{0,1:T(8,128)} %param.16) | copy-start | bytes 1540
  119.9 17.7 %copy-start.15 = (bf16[16,576]{1,0:T(8,128)(2,1)S(1)}, bf16[16,576]{1,0:T(8,128)(2,1)}, u32[]{:S(2)}) copy-start(bf16[16,576]{1,0:T(8,128)(2,1)} %param.22) | copy-start | bytes 55300
  119.9 17.7 %copy-start.7 = (bf16[16,64,576]{2,1,0:T(8,128)(2,1)S(1)}, bf16[16,64,576]{2,1,0:T(8,128)(2,1)}, u32[]{:S(2)}) copy-start(bf16[16,64,576]{2,1,0:T(8,128)(2,1)} %q_two) | copy-start | bytes 3538948
  119.9 27.1 %copy-start.9 = (bf16[16,64,576]{2,1,0:T(8,128)(2,1)S(1)}, bf16[16,64,576]{2,1,0:T(8,128)(2,1)}, u32[]{:S(2)}) copy-start(bf16[16,64,576]{2,1,0:T(8,128)(2,1)} %q_one.1) | copy-start | bytes 3538948
  120.0 58.4 %all-to-all-start.1 = ((bf16[64,8,1792]{2,1,0:T(8,128)(2,1)}), bf16[64,8,1792]{2,1,0:T(8,128)(2,1)}, u32[]{:S(2)}, u32[]{:S(2)}) async-start(bf16[64,8,1792]{2,1,0:T(8,128)(2,1)} %bitcast.17), calls=%async_computation.1 | async-start | bytes 3670016 | tf_op jit(solution)/shard_map/all_to_all | solution.py:338
  136.0 4.1 %collective-permute-start.8 = (f32[16,8]{0,1:T(8,128)S(1)}, f32[16,8]{0,1:T(8,128)S(1)}, u32[]{:S(2)}, u32[]{:S(2)}) collective-permute-start(f32[16,8]{0,1:T(8,128)S(1)} %copy-done.17), channel_id=1, source_target_pairs={{1,2},{2,1},{3,0},{0,3},{5,6},{6,5},{7,4},{4,7},{9,10},{10,9},{11,... | collective-permute-start | bytes 1544 | tf_op jit(solution)/shard_map/ppermute | solution.py:346
  137.8 4.0 %collective-permute-start.4 = (bf16[80,576]{1,0:T(8,128)(2,1)S(1)}, bf16[80,576]{1,0:T(8,128)(2,1)S(1)}, u32[]{:S(2)}, u32[]{:S(2)}) collective-permute-start(bf16[80,576]{1,0:T(8,128)(2,1)S(1)} %maximum_maximum_fusion), channel_id=1, source_target_pairs={{0,3},{1,0},{2,1},{3,2},{4,7},{5,4},{6,5},{7,6},{8,11},{9,8},{10,9... | collective-permute-start | bytes 276488 | tf_op jit(solution)/shard_map/ppermute | solution.py:17
  139.0 5.4 %collective-permute-start.3 = (bf16[80,576]{1,0:T(8,128)(2,1)S(1)}, bf16[80,576]{1,0:T(8,128)(2,1)S(1)}, u32[]{:S(2)}, u32[]{:S(2)}) collective-permute-start(bf16[80,576]{1,0:T(8,128)(2,1)S(1)} %maximum_maximum_fusion), channel_id=1, source_target_pairs={{0,2},{1,3},{2,0},{3,1},{4,6},{5,7},{6,4},{7,5},{8,10},{9,11},{10,... | collective-permute-start | bytes 276488 | tf_op jit(solution)/shard_map/ppermute | solution.py:17
  139.3 7.6 %collective-permute-start.2 = (bf16[80,576]{1,0:T(8,128)(2,1)S(1)}, bf16[80,576]{1,0:T(8,128)(2,1)S(1)}, u32[]{:S(2)}, u32[]{:S(2)}) collective-permute-start(bf16[80,576]{1,0:T(8,128)(2,1)S(1)} %maximum_maximum_fusion), channel_id=1, source_target_pairs={{0,1},{1,2},{2,3},{3,0},{4,5},{5,6},{6,7},{7,4},{8,9},{9,10},{10,1... | collective-permute-start | bytes 276488 | tf_op jit(solution)/shard_map/ppermute | solution.py:17
  147.0 1.7 copy-start.8
  167.8 14.2 %collective-permute-start.5 = (bf16[64,512]{1,0:T(8,128)(2,1)S(1)}, bf16[64,512]{1,0:T(8,128)(2,1)S(1)}, u32[]{:S(2)}, u32[]{:S(2)}) collective-permute-start(bf16[64,512]{1,0:T(8,128)(2,1)S(1)} %get-tuple-element.37), channel_id=1, source_target_pairs={{0,1},{1,2},{2,3},{3,0},{4,5},{5,6},{6,7},{7,4},{8,9},{9,10},{10,1... | collective-permute-start | bytes 196616 | tf_op jit(solution)/shard_map/ppermute | solution.py:17
  167.9 14.1 %collective-permute-start.7 = (bf16[64,512]{1,0:T(8,128)(2,1)S(1)}, bf16[64,512]{1,0:T(8,128)(2,1)S(1)}, u32[]{:S(2)}, u32[]{:S(2)}) collective-permute-start(bf16[64,512]{1,0:T(8,128)(2,1)S(1)} %get-tuple-element.38), channel_id=1, source_target_pairs={{0,3},{1,0},{2,1},{3,2},{4,7},{5,4},{6,5},{7,6},{8,11},{9,8},{10,9... | collective-permute-start | bytes 196616 | tf_op jit(solution)/shard_map/ppermute | solution.py:17
  170.5 11.5 %collective-permute-start.6 = (bf16[64,512]{1,0:T(8,128)(2,1)S(1)}, bf16[64,512]{1,0:T(8,128)(2,1)S(1)}, u32[]{:S(2)}, u32[]{:S(2)}) collective-permute-start(bf16[64,512]{1,0:T(8,128)(2,1)S(1)} %get-tuple-element.39), channel_id=1, source_target_pairs={{0,2},{1,3},{2,0},{3,1},{4,6},{5,7},{6,4},{7,5},{8,10},{9,11},{10,... | collective-permute-start | bytes 196616 | tf_op jit(solution)/shard_map/ppermute | solution.py:17
  180.3 4.3 %collective-permute-start.16 = (bf16[16,1792]{1,0:T(8,128)(2,1)S(1)}, bf16[16,1792]{1,0:T(8,128)(2,1)S(1)}, u32[]{:S(2)}, u32[]{:S(2)}) collective-permute-start(bf16[16,1792]{1,0:T(8,128)(2,1)S(1)} %broadcast_select_fusion.7), channel_id=1, source_target_pairs={{1,2},{2,1},{3,0},{0,3},{5,6},{6,5},{7,4},{4,7},{9,10},{10,9},{11,... | collective-permute-start | bytes 172040 | tf_op jit(solution)/shard_map/ppermute | solution.py:354

commit v6 on v5

--- a/solution.py
+++ b/solution.py
@@ -10,6 +10,7 @@
 LAT = 512
 MAXP = 8
 NEG = -1e30
+PAIRS = ((1, 2), (2, 1), (3, 0), (0, 3))
 
 
 def hop(value, axis, step):
@@ -117,39 +118,28 @@
 
 def up_kernel(rows, *refs):
     weights, (whole, sent) = refs[:4], refs[4:]
-    step = pl.program_id(0)
     for i, weight in enumerate(weights):
         part = jnp.dot(rows[...], weight[...], preferred_element_type=jnp.float32)
-
-        @pl.when(step == 0)
-        def _():
-            whole[i] = part
-
-        @pl.when(step > 0)
-        def _():
-            whole[i] += part
-
-    @pl.when(step == pl.num_programs(0) - 1)
-    def _():
-        sent[...] = whole[...].astype(jnp.bfloat16)
+        whole[i] = part
+        sent[i] = part.astype(jnp.bfloat16)
 
 
 def up_project(rows, weights, steps):
     count, depth = rows.shape
     units = weights[0].shape[1]
     shape = (len(weights), count, units)
-    out = pl.BlockSpec(shape, lambda k: (0, 0, 0))
+    out = pl.BlockSpec((len(weights), count // steps, units), lambda k: (0, k, 0))
     return pl.pallas_call(
         up_kernel,
         grid=(steps,),
-        in_specs=[pl.BlockSpec((count, depth // steps), lambda k: (0, k))]
-        + [pl.BlockSpec((depth // steps, units), lambda k: (k, 0))] * len(weights),
+        in_specs=[pl.BlockSpec((count // steps, depth), lambda k: (k, 0))]
+        + [pl.BlockSpec((depth, units), lambda k: (0, 0))] * len(weights),
         out_specs=[out, out],
         out_shape=[
             jax.ShapeDtypeStruct(shape, jnp.float32),
             jax.ShapeDtypeStruct(shape, jnp.bfloat16),
         ],
-        compiler_params=pltpu.CompilerParams(vmem_limit_bytes=32 * 1024 * 1024),
+        compiler_params=pltpu.CompilerParams(vmem_limit_bytes=58 * 1024 * 1024),
         cost_estimate=pl.CostEstimate(
             flops=2 * len(weights) * count * depth * units,
             bytes_accessed=9_000_000,
@@ -193,7 +183,7 @@
             scratch_shapes=[pltpu.VMEM(mine.shape, jnp.bfloat16)],
         ),
         out_shape=jax.ShapeDtypeStruct((count, depth), jnp.bfloat16),
-        compiler_params=pltpu.CompilerParams(vmem_limit_bytes=32 * 1024 * 1024),
+        compiler_params=pltpu.CompilerParams(vmem_limit_bytes=24 * 1024 * 1024),
         cost_estimate=pl.CostEstimate(
             flops=2 * len(weights) * count * depth * units,
             bytes_accessed=9_000_000,
@@ -240,31 +230,39 @@
     steps = range(grp_size)
 
     half = width // 2
-    side = me // 2
-    partner = [(1, 2), (2, 1), (3, 0), (0, 3)]
-    relay = [(0, 1), (1, 0), (2, 3), (3, 2)]
-
-    def in_order(own, other, axis):
-        first = jnp.where(side == 0, own, other)
-        second = jnp.where(side == 0, other, own)
-        return jnp.concatenate([first, second], axis=axis)
+    core = lax.axis_index("ep") % 2
+    turned = [(me - c) % grp_size for c in range(2)]
+    side = [turned[c] // 2 for c in range(2)]
+    here = jnp.where(core == 0, turned[0], turned[1])
+    partner = [[((a + c) % grp_size, (b + c) % grp_size) for a, b in PAIRS] for c in range(2)]
+
+    def by_core(pairs):
+        return [
+            (e * grp_size + (a + e % 2) % grp_size, e * grp_size + (b + e % 2) % grp_size)
+            for e in range(ep_size)
+            for a, b in pairs
+        ]
 
     def part(value, which, axis):
         return lax.dynamic_slice_in_dim(value, which * half, half, axis)
 
-    rows = in_order(
-        part(hidden, side, 1), lax.ppermute(part(hidden, 1 - side, 1), "grp", partner), 0
-    )
-    ids = in_order(expert_ids, lax.ppermute(expert_ids, "grp", partner), 0)
+    rows, id_list = [], [expert_ids]
+    for c in range(2):
+        id_list.append(lax.ppermute(expert_ids, "grp", partner[c]))
+        rows.append(part(hidden, side[c], 1))
+        rows.append(lax.ppermute(part(hidden, 1 - side[c], 1), "grp", partner[c]))
+    rows = jnp.concatenate(rows, axis=0)
 
     def spread(weight):
-        ahead = jnp.where((me == 0) | (me == 3), 0, 1)
+        ahead = jnp.where((here == 0) | (here == 3), 0, 1)
         prev = hop(part(weight, ahead, 0), "grp", 1)
         nxt = hop(part(weight, 1 - ahead, 0), "grp", -1)
-        return part(weight, side, 0), prev, nxt
+        return part(weight, here // 2, 0), prev, nxt
 
     def pass_on(prev, nxt):
-        return lax.ppermute(jnp.where(me % 2 == 0, prev, nxt), "grp", relay)
+        return lax.ppermute(
+            jnp.where(here % 2 == 0, prev, nxt), ("ep", "grp"), by_core([(0, 1), (1, 0), (2, 3), (3, 2)])
+        )
 
     up_own, up_prev, up_next = spread(w_up[0])
     up_prev, up_next, down = lax.optimization_barrier((up_prev, up_next, w_down[0]))
@@ -276,7 +274,7 @@
 
     rank = 2 * capacity
     lanes_all = ep_size * rank
-    flat_ids = ids.reshape(-1)
+    flat_ids = jnp.concatenate(id_list, axis=0).reshape(-1)
     entries = flat_ids.shape[0]
     hits = flat_ids[:, None] == jnp.arange(ep_size, dtype=jnp.int32)[None, :]
     order = jnp.arange(entries, dtype=jnp.int32)
@@ -286,7 +284,18 @@
         lower.astype(jnp.bfloat16), hits.astype(jnp.bfloat16), preferred_element_type=jnp.float32
     )
     earlier = jnp.sum(jnp.where(hits, ahead, 0.0), axis=1).astype(jnp.int32)
-    place = (flat_ids * rank + (order // per) * capacity + earlier).reshape(2 * samples, picks)
+    place = (flat_ids * rank + earlier).reshape(3, samples, picks)
+    own_at, first_at, second_at = place[0], place[1], place[2]
+    even = (expert_ids % 2) == 0
+    place = jnp.concatenate(
+        [
+            jnp.where(even, own_at + side[0] * capacity, -1),
+            jnp.where((id_list[1] % 2) == 0, first_at + (1 - side[0]) * capacity, -1),
+            jnp.where(even, -1, own_at + side[1] * capacity),
+            jnp.where((id_list[2] % 2) == 0, -1, second_at + (1 - side[1]) * capacity),
+        ],
+        axis=0,
+    )
     match = place[:, :, None] == jnp.arange(lanes_all, dtype=jnp.int32)[None, None, :]
     placing = jnp.sum(match.astype(jnp.float32), axis=1).astype(jnp.bfloat16)
     outgoing = lax.dot_general(
@@ -332,9 +341,9 @@
     attn_second = lax.dynamic_update_index_in_dim(attn_second, arrived_out, moved_slot, 0)
 
     mine, rounded = up_project(arrived, up_all, 2)
-    theirs = lax.ppermute(rounded, "grp", partner)
-    shift = jnp.where(me % 2 == 1, grp_size - 1, 1).astype(jnp.int32)
-    produced = down_project(shift[None], mine, theirs, down_all, 7)
+    theirs = lax.ppermute(rounded, ("ep", "grp"), by_core(PAIRS))
+    shift = jnp.where(here % 2 == 1, grp_size - 1, 1).astype(jnp.int32)
+    produced = down_project(shift[None], mine, theirs, down_all, 2)
     returned = lax.all_to_all(
         produced.reshape(ep_size, rank, half),
         "ep",
@@ -343,16 +352,27 @@
         tiled=True,
     ).reshape(lanes_all, half)
     (late_gates,) = after(outgoing, gate_weights)
-    gates = in_order(gate_weights, lax.ppermute(late_gates, "grp", partner), 0)
+    gates = jnp.concatenate(
+        [
+            gate_weights,
+            lax.ppermute(late_gates, "grp", partner[0]),
+            gate_weights,
+            lax.ppermute(late_gates, "grp", partner[1]),
+        ],
+        axis=0,
+    )
     mixing = jnp.sum(jnp.where(match, gates[:, :, None], 0.0), axis=1)
     high = lax.reduce_precision(mixing, 8, 7)
     mixing = jnp.concatenate([high, mixing - high], axis=0).astype(jnp.bfloat16)
     mixed = jnp.dot(mixing, returned, preferred_element_type=jnp.float32)
-    summed = (mixed[: 2 * samples] + mixed[2 * samples :]).astype(jnp.bfloat16)
-    first, second = summed[:samples], summed[samples:]
-    own = jnp.where(side == 0, first, second)
-    other = lax.ppermute(jnp.where(side == 0, second, first), "grp", partner)
-    moe_out = in_order(own, other, 1)
+    summed = (mixed[: 4 * samples] + mixed[4 * samples :]).reshape(4, samples, half)
+    first, second = 0.0, 0.0
+    for c in range(2):
+        own = summed[2 * c]
+        other = lax.ppermute(summed[2 * c + 1], "grp", partner[c])
+        first = first + jnp.where(side[c] == 0, own, other)
+        second = second + jnp.where(side[c] == 0, other, own)
+    moe_out = jnp.concatenate([first, second], axis=1).astype(jnp.bfloat16)
     return (attn_first, attn_second, moe_out)
 
 

time: 188 us -> 183 us (0.973)
  local copies, waits for them, and re-layouts: 14.7 us -> 8.65 us
  waiting for transfers between devices: 78.9 us -> 84.7 us
  Pallas kernels: 34.6 us -> 30.2 us
    ppermute x10, waiting for transfers between devices: 30.4 us -> 37.2 us  [hop(): lax.ppermute(value, axis, [(i, (i + step) % size) for i in range(size)])]
    unnamed x38 -> x25, local copies, waits for them, and re-layouts: 10.4 us -> 4.13 us
    ppermute x10, starting transfers between devices: 8.75 us -> 11.2 us  [hop(): lax.ppermute(value, axis, [(i, (i + step) % size) for i in range(size)])]
    all_to_all x1, starting transfers between devices: 14.2 us -> 11.7 us  [shards(): lax.all_to_all(produced.reshape(ep_size, rank, half), 'ep', split_axis=0,...]
    pallas_call x1, Pallas kernels: 8.06 us -> 5.71 us  [up_project(): pl.pallas_call(up_kernel, grid=(steps,), in_specs=[pl.BlockSpec((count //...]
    pallas_call x1, Pallas kernels: 7.57 us -> 5.54 us  [down_project(): pl.pallas_call(down_kernel, grid_spec=pltpu.PrefetchScalarGridSpec(num_sc...]
    ppermute x7 -> x11, waiting for transfers between devices: 40.7 us -> 39.7 us  [the longest x2 34 us: pass_on(): lax.ppermute(jnp.where(here % 2 == 0, prev, nxt), ('ep', 'grp'), by_core(...]
    ppermute x7 -> x11, starting transfers between devices: 8.8 us -> 9.33 us  [the longest x2 3.75 us: pass_on(): lax.ppermute(jnp.where(here % 2 == 0, prev, nxt), ('ep', 'grp'), by_core(...]
  transfers between devices with their start and end apart: 19 -> 23, of which waited for: 14 -> 10; matrix products, arithmetic and copies ran while one was open for 6% -> 6% of each run, Pallas kernels for 15% -> 14%
where the time goes in v6:
time: 183 us; the launch traced here: 180 us
  waiting for transfers between devices  84.7 us (46%)
  starting transfers between devices  46.3 us (25%)
  Pallas kernels  30.2 us (17%)
  local copies, waits for them, and re-layouts  8.65 us (5%)
  matrix products  4.15 us (2%)
  other arithmetic  3.97 us (2%)
  between operations  2.43 us (1%)
    ppermute x10, waiting for transfers between devices, hop(): lax.ppermute(value, axis, [(i, (i + step) % size) for i in range(size)])  37.2 us
    ppermute x2, waiting for transfers between devices, pass_on(): lax.ppermute(jnp.where(here % 2 == 0, prev, nxt), ('ep', 'grp'), by_core(...  34 us
    pallas_call x1, Pallas kernels, attention(): pl.pallas_call(attention_kernel, grid_spec=pltpu.PrefetchScalarGridSpec(n...  19 us
    all_to_all x1, starting transfers between devices, shards(): lax.all_to_all(outgoing.reshape(ep_size, rank, half), 'ep', split_axis=0,...  14 us
    all_to_all x1, starting transfers between devices, shards(): lax.all_to_all(produced.reshape(ep_size, rank, half), 'ep', split_axis=0,...  11.7 us
    ppermute x10, starting transfers between devices, hop(): lax.ppermute(value, axis, [(i, (i + step) % size) for i in range(size)])  11.2 us
    all_to_all x1, waiting for transfers between devices, shards(): lax.all_to_all(produced.reshape(ep_size, rank, half), 'ep', split_axis=0,...  7.81 us
    pallas_call x1, Pallas kernels, up_project(): pl.pallas_call(up_kernel, grid=(steps,), in_specs=[pl.BlockSpec((count //...  5.71 us
  transfers between devices with their start and end apart: 23, of which 10 were waited for; matrix products, arithmetic and copies ran while one was open for 6% of the time, Pallas kernels for 14%

profile of v6, /device:TPU:1, one launch (start us, length us, event | category | flops | bytes accessed | tf_op | source)
XLA Modules:
  0.0 180.4 jit_solution(12642087219007566608)
XLA Ops:
  0.6 0.8 copy.46
  1.4 3.6 %collective-permute-start = (s32[16,8]{1,0:T(8,128)S(1)}, s32[16,8]{1,0:T(8,128)S(1)}, u32[]{:S(2)}, u32[]{:S(2)}) collective-permute-start(s32[16,8]{1,0:T(8,128)S(1)} %copy.46), channel_id=1, source_target_pairs={{1,2},{2,1},{3,0},{0,3},{5,6},{6,5},{7,4},{4,7},{9,10},{10,9},{11,... | collective-permute-start | bytes 1544 | tf_op jit(solution)/shard_map/ppermute | solution.py:251
  5.0 0.0 collective-permute-start.1
  5.0 0.9 constant_dynamic-slice_fusion.7
  5.9 0.7 collective-permute-start.2
  6.6 0.9 collective-permute-start.3
  7.5 0.0 collective-permute-done
  7.6 0.1 eq.120
  7.7 0.3 fusion.2
  8.0 0.1 convert_element_type.23
  8.1 0.4 convert_reduce_fusion
  8.5 1.7 collective-permute-done.2
  10.2 1.9 %convolution_convert_fusion = bf16[512,1792]{1,0:T(8,128)(2,1)} fusion(bf16[16,1792]{1,0:T(8,128)(2,1)S(1)} %collective-permute-done.3, bf16[16,1792]{1,0:T(8,128)(2,1)S(1)} %get-tuple-element.40, bf16[16,1792]{1,0:T(8,128)(2,1)S(1)} %collective-permute-done.2, bf16[16,1792]{1,0:T(8,128)(2,1)S(1)} %get-tuple-element.37, bf16[64,512]{1,0:T(8,128)(2,1)S(1)} %convert_reduce_fusion), kind=kOutput, calls=%fused_computation | convolution fusion | flops 119275520 | bytes 2129920 | tf_op jit(solution)/shard_map/dot_general | solution.py:301
  12.1 14.0 %all-to-all-start = ((bf16[64,8,1792]{2,1,0:T(8,128)(2,1)}), bf16[64,8,1792]{2,1,0:T(8,128)(2,1)}, u32[]{:S(2)}, u32[]{:S(2)}) async-start(bf16[64,8,1792]{2,1,0:T(8,128)(2,1)} %bitcast.11), calls=%async_computation | async-start | bytes 3670016 | tf_op jit(solution)/shard_map/all_to_all | solution.py:304
  26.2 1.6 dynamic-slice_bitcast_fusion
  27.8 1.7 collective-permute-start.13
  29.6 20.0 %collective-permute-done.13.refs_1_ = bf16[1792,256]{1,0:T(8,128)(2,1)S(1)} collective-permute-done((bf16[1792,256]{1,0:T(8,128)(2,1)}, bf16[1792,256]{1,0:T(8,128)(2,1)S(1)}, u32[]{:S(2)}, u32[]{:S(2)}) %collective-permute-start.13) | collective-permute-done | bytes 917536 | tf_op jit(solution)/shard_map/ppermute | solution.py:18
  49.6 2.6 %collective-permute-done.12.refs_3_ = bf16[1792,256]{1,0:T(8,128)(2,1)} collective-permute-done((bf16[1792,256]{1,0:T(8,128)(2,1)}, bf16[1792,256]{1,0:T(8,128)(2,1)}, u32[]{:S(2)}, u32[]{:S(2)}) %collective-permute-start.12) | collective-permute-done | bytes 917536 | tf_op jit(solution)/shard_map/ppermute | solution.py:18
  52.2 0.1 broadcast_select_fusion.1
  52.3 1.9 %collective-permute-start.14 = (bf16[1792,256]{1,0:T(8,128)(2,1)S(1)}, bf16[1792,256]{1,0:T(8,128)(2,1)}, u32[]{:S(2)}, u32[]{:S(2)}) collective-permute-start(bf16[1792,256]{1,0:T(8,128)(2,1)S(1)} %broadcast_select_fusion.1), channel_id=1, source_target_pairs={{0,1},{1,0},{2,3},{3,2},{5,6},{6,5},{7,4},{4,7},{8,9},{9,8},{10,11... | collective-permute-start | bytes 2752520 | tf_op jit(solution)/shard_map/ppermute | solution.py:263
  54.2 1.4 constant_dynamic-slice_fusion
  55.6 2.7 %collective-permute-start.16 = (bf16[1792,256]{1,0:T(8,128)(2,1)}, bf16[1792,256]{1,0:T(8,128)(2,1)S(1)}, u32[]{:S(2)}, u32[]{:S(2)}) collective-permute-start(bf16[1792,256]{1,0:T(8,128)(2,1)} %get-tuple-element.26), channel_id=1, source_target_pairs={{0,3},{1,0},{2,1},{3,2},{4,7},{5,4},{6,5},{7,6},{8,11},{9,8},{10,9... | collective-permute-start | bytes 2752520 | tf_op jit(solution)/shard_map/ppermute | solution.py:18
  58.3 12.7 %collective-permute-done.14.refs_2_ = bf16[1792,256]{1,0:T(8,128)(2,1)} collective-permute-done((bf16[1792,256]{1,0:T(8,128)(2,1)S(1)}, bf16[1792,256]{1,0:T(8,128)(2,1)}, u32[]{:S(2)}, u32[]{:S(2)}) %collective-permute-start.14) | collective-permute-done | bytes 917536 | tf_op jit(solution)/shard_map/ppermute | solution.py:263
  71.0 5.7 %up_project.1 = (f32[4,512,256]{2,1,0:T(8,128)}, bf16[4,512,256]{2,1,0:T(8,128)(2,1)}) custom-call(bf16[512,1792]{1,0:T(8,128)(2,1)} %bitcast.12.rows, bf16[1792,256]{1,0:T(8,128)(2,1)} %get-tuple-element.29.refs_0_, bf16[1792,256]{1,0:T(8,128)(2,1)} %copy-done.7, bf16[1792,256]{1,0:T(8,128)(2,1)} %collective-permute-done.14.refs_2_, ...), custom_call_target="tpu_custom_call" | custom-call | flops 1879048192 | bytes 9000000 | tf_op jit(solution)/shard_map/up_project/pallas_call | solution.py:132
  76.7 8.8 %collective-permute-done.17.refs_3_ = bf16[1792,256]{1,0:T(8,128)(2,1)S(1)} collective-permute-done((bf16[1792,256]{1,0:T(8,128)(2,1)}, bf16[1792,256]{1,0:T(8,128)(2,1)S(1)}, u32[]{:S(2)}, u32[]{:S(2)}) %collective-permute-start.17) | collective-permute-done | bytes 917536 | tf_op jit(solution)/shard_map/ppermute | solution.py:18
  85.5 1.0 broadcast_select_fusion
  86.5 1.8 %collective-permute-start.18 = (bf16[1792,256]{1,0:T(8,128)(2,1)}, bf16[1792,256]{1,0:T(8,128)(2,1)}, u32[]{:S(2)}, u32[]{:S(2)}) collective-permute-start(bf16[1792,256]{1,0:T(8,128)(2,1)} %broadcast_select_fusion), channel_id=1, source_target_pairs={{0,1},{1,0},{2,3},{3,2},{5,6},{6,5},{7,4},{4,7},{8,9},{9,8},{10,11... | collective-permute-start | bytes 2752520 | tf_op jit(solution)/shard_map/ppermute | solution.py:263
  88.4 21.3 %collective-permute-done.18.refs_2_ = bf16[1792,256]{1,0:T(8,128)(2,1)} collective-permute-done((bf16[1792,256]{1,0:T(8,128)(2,1)}, bf16[1792,256]{1,0:T(8,128)(2,1)}, u32[]{:S(2)}, u32[]{:S(2)}) %collective-permute-start.18) | collective-permute-done | bytes 917536 | tf_op jit(solution)/shard_map/ppermute | solution.py:263
  109.6 1.6 copy-done
  111.2 5.5 %down_project.1 = bf16[512,1792]{1,0:T(8,128)(2,1)} custom-call(s32[1]{0:T(128)} %bitcast.10.shift, f32[4,512,256]{2,1,0:T(8,128)S(1)} %copy-done, bf16[4,512,256]{2,1,0:T(8,128)(2,1)} %collective-permute-done.15.theirs, bf16[1792,256]{1,0:T(8,128)(2,1)S(1)} %get-tuple-element.27.refs_0_, bf16[1792,256]{1,0:T(8,128)(2,1)S(1)} %collective-permute-done.16.refs_1_, ...), custom_call_target="tpu_custom_call" | custom-call | flops 1879048192 | bytes 9000000 | tf_op jit(solution)/shard_map/down_project/pallas_call | solution.py:175
  116.8 0.0 copy-start.10
  116.8 0.0 copy-start.8
  116.8 0.0 copy-start.1
  116.8 0.0 copy-start.3
  116.8 11.7 %all-to-all-start.1 = ((bf16[64,8,1792]{2,1,0:T(8,128)(2,1)}), bf16[64,8,1792]{2,1,0:T(8,128)(2,1)}, u32[]{:S(2)}, u32[]{:S(2)}) async-start(bf16[64,8,1792]{2,1,0:T(8,128)(2,1)} %bitcast.17), calls=%async_computation.1 | async-start | bytes 3670016 | tf_op jit(solution)/shard_map/all_to_all | solution.py:347
  129.9 0.1 select_reduce_fusion.2
  130.0 0.1 add_minimum_fusion
  130.1 0.1 min.15
  130.3 0.1 pad.10.clone
  130.3 0.1 select_reduce_fusion.1.pages
  130.4 0.1 collective-permute-start.11
  130.5 0.1 collective-permute-start.10
  130.7 0.1 maximum_maximum_fusion
  130.8 2.7 %collective-permute-start.6 = (bf16[80,576]{1,0:T(8,128)(2,1)S(1)}, bf16[80,576]{1,0:T(8,128)(2,1)S(1)}, u32[]{:S(2)}, u32[]{:S(2)}) collective-permute-start(bf16[80,576]{1,0:T(8,128)(2,1)S(1)} %maximum_maximum_fusion), channel_id=1, source_target_pairs={{0,3},{1,0},{2,1},{3,2},{4,7},{5,4},{6,5},{7,6},{8,11},{9,8},{10,9... | collective-permute-start | bytes 276488 | tf_op jit(solution)/shard_map/ppermute | solution.py:18
  133.5 0.6 collective-permute-start.5
  134.1 0.8 collective-permute-start.4
  134.9 0.1 pad_maximum_fusion.1
  135.0 0.1 copy.54
  135.1 0.4 select_reduce_fusion
  135.5 3.4 %collective-permute-done.5 = bf16[80,576]{1,0:T(8,128)(2,1)S(1)} collective-permute-done((bf16[80,576]{1,0:T(8,128)(2,1)S(1)}, bf16[80,576]{1,0:T(8,128)(2,1)S(1)}, u32[]{:S(2)}, u32[]{:S(2)}) %collective-permute-start.5) | collective-permute-done | bytes 92192 | tf_op jit(solution)/shard_map/ppermute | solution.py:18
  138.9 2.4 %collective-permute-done.4 = bf16[80,576]{1,0:T(8,128)(2,1)S(1)} collective-permute-done((bf16[80,576]{1,0:T(8,128)(2,1)S(1)}, bf16[80,576]{1,0:T(8,128)(2,1)S(1)}, u32[]{:S(2)}, u32[]{:S(2)}) %collective-permute-start.4) | collective-permute-done | bytes 92192 | tf_op jit(solution)/shard_map/ppermute | solution.py:18
  141.3 0.1 select_select_fusion
  141.5 0.0 copy-start.2
  141.5 1.7 copy-done.2
  143.2 19.0 %attention.1 = (bf16[16,64,512]{2,1,0:T(8,128)(2,1)}, bf16[16,64,512]{2,1,0:T(8,128)(2,1)}, bf16[64,512]{1,0:T(8,128)(2,1)S(1)}) custom-call(s32[16]{0:T(128)S(1)} %bitcast.33, s32[128]{0:T(128)S(1)} %select_reduce_fusion.1.pages, s32[1]{0:T(128)} %bitcast.28.moved, bf16[16,64,576]{2,1,0:T(8,128)(2,1)S(1)} %copy-done.3, bf16[16,64,576]{2,1,0:T(8,128)(2,1)S(1)} %copy-done.1, ...), custom_call_target="tpu_custom_call" | custom-call | flops 12000000000 | bytes 8000000 | tf_op jit(solution)/shard_map/attention/pallas_call | solution.py:89
  162.2 0.1 collective-permute-start.7
  162.3 2.7 %collective-permute-start.9 = (bf16[64,512]{1,0:T(8,128)(2,1)S(1)}, bf16[64,512]{1,0:T(8,128)(2,1)S(1)}, u32[]{:S(2)}, u32[]{:S(2)}) collective-permute-start(bf16[64,512]{1,0:T(8,128)(2,1)S(1)} %get-tuple-element.42), channel_id=1, source_target_pairs={{0,3},{1,0},{2,1},{3,2},{4,7},{5,4},{6,5},{7,6},{8,11},{9,8},{10,9... | collective-permute-start | bytes 196616 | tf_op jit(solution)/shard_map/ppermute | solution.py:18
  165.0 7.8 %all-to-all-done.1 = bf16[64,8,1792]{2,1,0:T(8,128)(2,1)} async-done(((bf16[64,8,1792]{2,1,0:T(8,128)(2,1)}), bf16[64,8,1792]{2,1,0:T(8,128)(2,1)}, u32[]{:S(2)}, u32[]{:S(2)}) %all-to-all-start.1) | async-done | bytes 1835040 | tf_op jit(solution)/shard_map/all_to_all | solution.py:347
  172.8 1.9 %fusion = f32[128,1792]{1,0:T(8,128)S(1)} fusion(bf16[64,8,1792]{2,1,0:T(8,128)(2,1)} %all-to-all-done.1, bf16[64,512]{1,0:T(8,128)(2,1)S(1)} %get-tuple-element.36, bf16[64,512]{1,0:T(8,128)(2,1)S(1)} %get-tuple-element.35), kind=kOutput, calls=%fused_computation.1 | convolution fusion | flops 235143168 | bytes 2883584 | tf_op jit(solution)/shard_map/dot_general | solution.py:367
  174.8 0.1 collective-permute-start.19
  174.9 0.1 collective-permute-start.20
  175.0 0.7 bitcast_dynamic-update-slice_fusion
  175.7 4.0 %collective-permute-done.19 = f32[16,1792]{1,0:T(8,128)S(1)} collective-permute-done((f32[16,1792]{1,0:T(8,128)S(1)}, f32[16,1792]{1,0:T(8,128)S(1)}, u32[]{:S(2)}, u32[]{:S(2)}) %collective-permute-start.19) | collective-permute-done | bytes 114720 | tf_op jit(solution)/shard_map/ppermute | solution.py:372
  179.7 0.7 pad_maximum_fusion
  (52 shorter events, 0.4 us)
Async XLA Ops:
  1.4 6.2 %collective-permute-start = (s32[16,8]{1,0:T(8,128)S(1)}, s32[16,8]{1,0:T(8,128)S(1)}, u32[]{:S(2)}, u32[]{:S(2)}) collective-permute-start(s32[16,8]{1,0:T(8,128)S(1)} %copy.46), channel_id=1, source_target_pairs={{1,2},{2,1},{3,0},{0,3},{5,6},{6,5},{7,4},{4,7},{9,10},{10,9},{11,... | collective-permute-start | bytes 1544 | tf_op jit(solution)/shard_map/ppermute | solution.py:251
  5.0 2.6 %collective-permute-start.1 = (s32[16,8]{1,0:T(8,128)S(1)}, s32[16,8]{1,0:T(8,128)S(1)}, u32[]{:S(2)}, u32[]{:S(2)}) collective-permute-start(s32[16,8]{1,0:T(8,128)S(1)} %copy.46), channel_id=1, source_target_pairs={{2,3},{3,2},{0,1},{1,0},{6,7},{7,6},{4,5},{5,4},{10,11},{11,10},{8... | collective-permute-start | bytes 1544 | tf_op jit(solution)/shard_map/ppermute | solution.py:251
  5.9 4.3 %collective-permute-start.2 = (bf16[16,1792]{1,0:T(8,128)(2,1)S(1)}, bf16[16,1792]{1,0:T(8,128)(2,1)S(1)}, u32[]{:S(2)}, u32[]{:S(2)}) collective-permute-start(bf16[16,1792]{1,0:T(8,128)(2,1)S(1)} %get-tuple-element.38), channel_id=1, source_target_pairs={{1,2},{2,1},{3,0},{0,3},{5,6},{6,5},{7,4},{4,7},{9,10},{10,9},{11,... | collective-permute-start | bytes 172040 | tf_op jit(solution)/shard_map/ppermute | solution.py:253
  6.6 3.6 %collective-permute-start.3 = (bf16[16,1792]{1,0:T(8,128)(2,1)S(1)}, bf16[16,1792]{1,0:T(8,128)(2,1)S(1)}, u32[]{:S(2)}, u32[]{:S(2)}) collective-permute-start(bf16[16,1792]{1,0:T(8,128)(2,1)S(1)} %get-tuple-element.39), channel_id=1, source_target_pairs={{2,3},{3,2},{0,1},{1,0},{6,7},{7,6},{4,5},{5,4},{10,11},{11,10},{8... | collective-permute-start | bytes 172040 | tf_op jit(solution)/shard_map/ppermute | solution.py:253
  12.1 14.1 %copy-start.5 = (bf16[1,3584,256]{2,1,0:T(8,128)(2,1)S(1)}, bf16[1,3584,256]{2,1,0:T(8,128)(2,1)}, u32[]{:S(2)}) copy-start(bf16[1,3584,256]{2,1,0:T(8,128)(2,1)} %param.17) | copy-start | bytes 5505028
  12.1 58.9 %all-to-all-start = ((bf16[64,8,1792]{2,1,0:T(8,128)(2,1)}), bf16[64,8,1792]{2,1,0:T(8,128)(2,1)}, u32[]{:S(2)}, u32[]{:S(2)}) async-start(bf16[64,8,1792]{2,1,0:T(8,128)(2,1)} %bitcast.11), calls=%async_computation | async-start | bytes 3670016 | tf_op jit(solution)/shard_map/all_to_all | solution.py:304
  27.8 26.4 %copy-start.6 = (bf16[1,3584,256]{2,1,0:T(8,128)(2,1)S(1)}, bf16[1,3584,256]{2,1,0:T(8,128)(2,1)}, u32[]{:S(2)}) copy-start(bf16[1,3584,256]{2,1,0:T(8,128)(2,1)} %param.18) | copy-start | bytes 5505028
  27.8 21.7 %collective-permute-start.13 = (bf16[1792,256]{1,0:T(8,128)(2,1)}, bf16[1792,256]{1,0:T(8,128)(2,1)S(1)}, u32[]{:S(2)}, u32[]{:S(2)}) collective-permute-start(bf16[1792,256]{1,0:T(8,128)(2,1)} %get-tuple-element.28), channel_id=1, source_target_pairs={{0,3},{1,0},{2,1},{3,2},{4,7},{5,4},{6,5},{7,6},{8,11},{9,8},{10,9... | collective-permute-start | bytes 2752520 | tf_op jit(solution)/shard_map/ppermute | solution.py:18
  29.6 22.6 %collective-permute-start.12 = (bf16[1792,256]{1,0:T(8,128)(2,1)}, bf16[1792,256]{1,0:T(8,128)(2,1)}, u32[]{:S(2)}, u32[]{:S(2)}) collective-permute-start(bf16[1792,256]{1,0:T(8,128)(2,1)} %get-tuple-element.30), channel_id=1, source_target_pairs={{0,1},{1,2},{2,3},{3,0},{4,5},{5,6},{6,7},{7,4},{8,9},{9,10},{10,1... | collective-permute-start | bytes 2752520 | tf_op jit(solution)/shard_map/ppermute | solution.py:18
  49.6 2.7 %copy-start.7 = (bf16[1792,256]{1,0:T(8,128)(2,1)}, bf16[1792,256]{1,0:T(8,128)(2,1)S(1)}, u32[]{:S(2)}) copy-start(bf16[1792,256]{1,0:T(8,128)(2,1)S(1)} %collective-permute-done.13.refs_1_) | copy-start | bytes 2752516
  52.3 18.7 %collective-permute-start.14 = (bf16[1792,256]{1,0:T(8,128)(2,1)S(1)}, bf16[1792,256]{1,0:T(8,128)(2,1)}, u32[]{:S(2)}, u32[]{:S(2)}) collective-permute-start(bf16[1792,256]{1,0:T(8,128)(2,1)S(1)} %broadcast_select_fusion.1), channel_id=1, source_target_pairs={{0,1},{1,0},{2,3},{3,2},{5,6},{6,5},{7,4},{4,7},{8,9},{9,8},{10,11... | collective-permute-start | bytes 2752520 | tf_op jit(solution)/shard_map/ppermute | solution.py:263
  55.6 29.9 %collective-permute-start.17 = (bf16[1792,256]{1,0:T(8,128)(2,1)}, bf16[1792,256]{1,0:T(8,128)(2,1)S(1)}, u32[]{:S(2)}, u32[]{:S(2)}) collective-permute-start(bf16[1792,256]{1,0:T(8,128)(2,1)} %get-tuple-element.25), channel_id=1, source_target_pairs={{0,1},{1,2},{2,3},{3,0},{4,5},{5,6},{6,7},{7,4},{8,9},{9,10},{10,1... | collective-permute-start | bytes 2752520 | tf_op jit(solution)/shard_map/ppermute | solution.py:18
  55.6 29.9 %collective-permute-start.16 = (bf16[1792,256]{1,0:T(8,128)(2,1)}, bf16[1792,256]{1,0:T(8,128)(2,1)S(1)}, u32[]{:S(2)}, u32[]{:S(2)}) collective-permute-start(bf16[1792,256]{1,0:T(8,128)(2,1)} %get-tuple-element.26), channel_id=1, source_target_pairs={{0,3},{1,0},{2,1},{3,2},{4,7},{5,4},{6,5},{7,6},{8,11},{9,8},{10,9... | collective-permute-start | bytes 2752520 | tf_op jit(solution)/shard_map/ppermute | solution.py:18
  76.7 32.9 %collective-permute-start.15 = (bf16[4,512,256]{2,1,0:T(8,128)(2,1)}, bf16[4,512,256]{2,1,0:T(8,128)(2,1)}, u32[]{:S(2)}, u32[]{:S(2)}) collective-permute-start(bf16[4,512,256]{2,1,0:T(8,128)(2,1)} %get-tuple-element.23), channel_id=1, source_target_pairs={{1,2},{2,1},{3,0},{0,3},{6,7},{7,6},{4,5},{5,4},{9,10},{10,9},{11,... | collective-permute-start | bytes 3145736 | tf_op jit(solution)/shard_map/ppermute | solution.py:344
  86.5 23.1 %collective-permute-start.18 = (bf16[1792,256]{1,0:T(8,128)(2,1)}, bf16[1792,256]{1,0:T(8,128)(2,1)}, u32[]{:S(2)}, u32[]{:S(2)}) collective-permute-start(bf16[1792,256]{1,0:T(8,128)(2,1)} %broadcast_select_fusion), channel_id=1, source_target_pairs={{0,1},{1,0},{2,3},{3,2},{5,6},{6,5},{7,4},{4,7},{8,9},{9,8},{10,11... | collective-permute-start | bytes 2752520 | tf_op jit(solution)/shard_map/ppermute | solution.py:263
  109.6 1.6 copy-start
  116.8 13.1 %copy-start.4 = (s32[1,16]{1,0:T(1,128)S(1)}, s32[1,16]{1,0:T(1,128)}, u32[]{:S(2)}) copy-start(s32[1,16]{1,0:T(1,128)} %param.24) | copy-start | bytes 196
  116.8 13.4 %copy-start.9 = (bf16[16,576]{1,0:T(8,128)(2,1)S(1)}, bf16[16,576]{1,0:T(8,128)(2,1)}, u32[]{:S(2)}) copy-start(bf16[16,576]{1,0:T(8,128)(2,1)} %param.20) | copy-start | bytes 55300
  116.8 13.6 %copy-start.11 = (s32[1,32]{1,0:T(1,128)S(1)}, s32[1,32]{1,0:T(1,128)}, u32[]{:S(2)}) copy-start(s32[1,32]{1,0:T(1,128)} %param.25) | copy-start | bytes 388
  116.8 13.7 %copy-start.10 = (f32[16,8]{0,1:T(8,128)S(1)}, f32[16,8]{0,1:T(8,128)}, u32[]{:S(2)}) copy-start(f32[16,8]{0,1:T(8,128)} %param.16) | copy-start | bytes 1540
  116.8 13.8 %copy-start.8 = (bf16[16,576]{1,0:T(8,128)(2,1)S(1)}, bf16[16,576]{1,0:T(8,128)(2,1)}, u32[]{:S(2)}) copy-start(bf16[16,576]{1,0:T(8,128)(2,1)} %param.22) | copy-start | bytes 55300
  116.8 13.9 %copy-start.1 = (bf16[16,64,576]{2,1,0:T(8,128)(2,1)S(1)}, bf16[16,64,576]{2,1,0:T(8,128)(2,1)}, u32[]{:S(2)}) copy-start(bf16[16,64,576]{2,1,0:T(8,128)(2,1)} %q_two) | copy-start | bytes 3538948
  116.8 24.6 %copy-start.3 = (bf16[16,64,576]{2,1,0:T(8,128)(2,1)S(1)}, bf16[16,64,576]{2,1,0:T(8,128)(2,1)}, u32[]{:S(2)}) copy-start(bf16[16,64,576]{2,1,0:T(8,128)(2,1)} %q_one.1) | copy-start | bytes 3538948
  116.8 55.9 %all-to-all-start.1 = ((bf16[64,8,1792]{2,1,0:T(8,128)(2,1)}), bf16[64,8,1792]{2,1,0:T(8,128)(2,1)}, u32[]{:S(2)}, u32[]{:S(2)}) async-start(bf16[64,8,1792]{2,1,0:T(8,128)(2,1)} %bitcast.17), calls=%async_computation.1 | async-start | bytes 3670016 | tf_op jit(solution)/shard_map/all_to_all | solution.py:347
  130.4 4.5 %collective-permute-start.11 = (f32[16,8]{0,1:T(8,128)S(1)}, f32[16,8]{0,1:T(8,128)S(1)}, u32[]{:S(2)}, u32[]{:S(2)}) collective-permute-start(f32[16,8]{0,1:T(8,128)S(1)} %copy-done.10), channel_id=1, source_target_pairs={{2,3},{3,2},{0,1},{1,0},{6,7},{7,6},{4,5},{5,4},{10,11},{11,10},{8... | collective-permute-start | bytes 1544 | tf_op jit(solution)/shard_map/ppermute | solution.py:360
  130.5 4.4 %collective-permute-start.10 = (f32[16,8]{0,1:T(8,128)S(1)}, f32[16,8]{0,1:T(8,128)S(1)}, u32[]{:S(2)}, u32[]{:S(2)}) collective-permute-start(f32[16,8]{0,1:T(8,128)S(1)} %copy-done.10), channel_id=1, source_target_pairs={{1,2},{2,1},{3,0},{0,3},{5,6},{6,5},{7,4},{4,7},{9,10},{10,9},{11,... | collective-permute-start | bytes 1544 | tf_op jit(solution)/shard_map/ppermute | solution.py:358
  130.8 4.7 %collective-permute-start.6 = (bf16[80,576]{1,0:T(8,128)(2,1)S(1)}, bf16[80,576]{1,0:T(8,128)(2,1)S(1)}, u32[]{:S(2)}, u32[]{:S(2)}) collective-permute-start(bf16[80,576]{1,0:T(8,128)(2,1)S(1)} %maximum_maximum_fusion), channel_id=1, source_target_pairs={{0,3},{1,0},{2,1},{3,2},{4,7},{5,4},{6,5},{7,6},{8,11},{9,8},{10,9... | collective-permute-start | bytes 276488 | tf_op jit(solution)/shard_map/ppermute | solution.py:18
  133.5 5.4 %collective-permute-start.5 = (bf16[80,576]{1,0:T(8,128)(2,1)S(1)}, bf16[80,576]{1,0:T(8,128)(2,1)S(1)}, u32[]{:S(2)}, u32[]{:S(2)}) collective-permute-start(bf16[80,576]{1,0:T(8,128)(2,1)S(1)} %maximum_maximum_fusion), channel_id=1, source_target_pairs={{0,2},{1,3},{2,0},{3,1},{4,6},{5,7},{6,4},{7,5},{8,10},{9,11},{10,... | collective-permute-start | bytes 276488 | tf_op jit(solution)/shard_map/ppermute | solution.py:18
  134.1 7.2 %collective-permute-start.4 = (bf16[80,576]{1,0:T(8,128)(2,1)S(1)}, bf16[80,576]{1,0:T(8,128)(2,1)S(1)}, u32[]{:S(2)}, u32[]{:S(2)}) collective-permute-start(bf16[80,576]{1,0:T(8,128)(2,1)S(1)} %maximum_maximum_fusion), channel_id=1, source_target_pairs={{0,1},{1,2},{2,3},{3,0},{4,5},{5,6},{6,7},{7,4},{8,9},{9,10},{10,1... | collective-permute-start | bytes 276488 | tf_op jit(solution)/shard_map/ppermute | solution.py:18
  141.5 1.7 copy-start.2
  162.2 12.8 %collective-permute-start.7 = (bf16[64,512]{1,0:T(8,128)(2,1)S(1)}, bf16[64,512]{1,0:T(8,128)(2,1)S(1)}, u32[]{:S(2)}, u32[]{:S(2)}) collective-permute-start(bf16[64,512]{1,0:T(8,128)(2,1)S(1)} %get-tuple-element.41), channel_id=1, source_target_pairs={{0,1},{1,2},{2,3},{3,0},{4,5},{5,6},{6,7},{7,4},{8,9},{9,10},{10,1... | collective-permute-start | bytes 196616 | tf_op jit(solution)/shard_map/ppermute | solution.py:18
  162.3 12.7 %collective-permute-start.9 = (bf16[64,512]{1,0:T(8,128)(2,1)S(1)}, bf16[64,512]{1,0:T(8,128)(2,1)S(1)}, u32[]{:S(2)}, u32[]{:S(2)}) collective-permute-start(bf16[64,512]{1,0:T(8,128)(2,1)S(1)} %get-tuple-element.42), channel_id=1, source_target_pairs={{0,3},{1,0},{2,1},{3,2},{4,7},{5,4},{6,5},{7,6},{8,11},{9,8},{10,9... | collective-permute-start | bytes 196616 | tf_op jit(solution)/shard_map/ppermute | solution.py:18
  165.0 10.0 %collective-permute-start.8 = (bf16[64,512]{1,0:T(8,128)(2,1)S(1)}, bf16[64,512]{1,0:T(8,128)(2,1)S(1)}, u32[]{:S(2)}, u32[]{:S(2)}) collective-permute-start(bf16[64,512]{1,0:T(8,128)(2,1)S(1)} %get-tuple-element.43), channel_id=1, source_target_pairs={{0,2},{1,3},{2,0},{3,1},{4,6},{5,7},{6,4},{7,5},{8,10},{9,11},{10,... | collective-permute-start | bytes 196616 | tf_op jit(solution)/shard_map/ppermute | solution.py:18
  174.8 4.9 %collective-permute-start.19 = (f32[16,1792]{1,0:T(8,128)S(1)}, f32[16,1792]{1,0:T(8,128)S(1)}, u32[]{:S(2)}, u32[]{:S(2)}) collective-permute-start(f32[16,1792]{1,0:T(8,128)S(1)} %get-tuple-element.33), channel_id=1, source_target_pairs={{1,2},{2,1},{3,0},{0,3},{5,6},{6,5},{7,4},{4,7},{9,10},{10,9},{11,... | collective-permute-start | bytes 344072 | tf_op jit(solution)/shard_map/ppermute | solution.py:372
  174.9 4.8 %collective-permute-start.20 = (f32[16,1792]{1,0:T(8,128)S(1)}, f32[16,1792]{1,0:T(8,128)S(1)}, u32[]{:S(2)}, u32[]{:S(2)}) collective-permute-start(f32[16,1792]{1,0:T(8,128)S(1)} %get-tuple-element.34), channel_id=1, source_target_pairs={{2,3},{3,2},{0,1},{1,0},{6,7},{7,6},{4,5},{5,4},{10,11},{11,10},{8... | collective-permute-start | bytes 344072 | tf_op jit(solution)/shard_map/ppermute | solution.py:372

commit v7 on v6

--- a/solution.py
+++ b/solution.py
@@ -114,6 +114,38 @@
         ),
         name="attention",
     )(lens, pages, moved, q_one, q_two, q_in, kv_one, kv_two, kv_in, pool)
+
+
+def choose_kernel(which, first, second, out, sem):
+    @pl.when(which[0] == 0)
+    def _():
+        copy = pltpu.make_async_copy(first, out, sem)
+        copy.start()
+        copy.wait()
+
+    @pl.when(which[0] != 0)
+    def _():
+        copy = pltpu.make_async_copy(second, out, sem)
+        copy.start()
+        copy.wait()
+
+
+def choose(which, first, second, flops):
+    return pl.pallas_call(
+        choose_kernel,
+        grid_spec=pltpu.PrefetchScalarGridSpec(
+            num_scalar_prefetch=1,
+            grid=(1,),
+            in_specs=[pl.BlockSpec(memory_space=pl.ANY)] * 2,
+            out_specs=pl.BlockSpec(memory_space=pl.ANY),
+            scratch_shapes=[pltpu.SemaphoreType.DMA],
+        ),
+        out_shape=jax.ShapeDtypeStruct(first.shape, first.dtype),
+        cost_estimate=pl.CostEstimate(
+            flops=flops, bytes_accessed=2 * first.size * 2, transcendentals=0
+        ),
+        name="choose",
+    )(which, first, second)
 
 
 def up_kernel(rows, *refs):
@@ -259,16 +291,16 @@
         nxt = hop(part(weight, 1 - ahead, 0), "grp", -1)
         return part(weight, here // 2, 0), prev, nxt
 
-    def pass_on(prev, nxt):
-        return lax.ppermute(
-            jnp.where(here % 2 == 0, prev, nxt), ("ep", "grp"), by_core([(0, 1), (1, 0), (2, 3), (3, 2)])
-        )
+    def pass_on(prev, nxt, flops):
+        picked = choose((here % 2)[None], prev, nxt, flops)
+        far = lax.ppermute(picked, ("ep", "grp"), by_core([(0, 1), (1, 0), (2, 3), (3, 2)]))
+        return far
 
     up_own, up_prev, up_next = spread(w_up[0])
     up_prev, up_next, down = lax.optimization_barrier((up_prev, up_next, w_down[0]))
-    up_far = pass_on(up_prev, up_next)
+    up_far = pass_on(up_prev, up_next, 10_000_000_000)
     down_own, down_prev, down_next = spread(down)
-    down_far = pass_on(down_prev, down_next)
+    down_far = pass_on(down_prev, down_next, 0)
     up_all = [up_own, up_next, up_far, up_prev]
     down_all = [down_own, down_next, down_far, down_prev]
 
@@ -340,6 +372,7 @@
         arrived_out = arrived_out + hop(jnp.where(offset == r, out_moved, zero), "grp", r)
     attn_second = lax.dynamic_update_index_in_dim(attn_second, arrived_out, moved_slot, 0)
 
+    (arrived,) = after(down_far, arrived)
     mine, rounded = up_project(arrived, up_all, 2)
     theirs = lax.ppermute(rounded, ("ep", "grp"), by_core(PAIRS))
     shift = jnp.where(here % 2 == 1, grp_size - 1, 1).astype(jnp.int32)

time: 183 us -> 243 us (1.33)
  Pallas kernels: 30.2 us -> 87.5 us
  waiting for transfers between devices: 84.7 us -> 78.7 us
  starting transfers between devices: 46.3 us -> 51.6 us
  local copies, waits for them, and re-layouts: 8.65 us -> 13.7 us
    pallas_call x0 -> x2, Pallas kernels: none -> 57.8 us  [choose(): pl.pallas_call(choose_kernel, grid_spec=pltpu.PrefetchScalarGridSpec(num_...]
    ppermute x2, waiting for transfers between devices: 34 us -> 12.1 us  [pass_on(): lax.ppermute(picked, ('ep', 'grp'), by_core([(0, 1), (1, 0), (2, 3), (3,...]
    ppermute x2, waiting for transfers between devices: 1.69 us -> 19.3 us  [shards(): rows.append(lax.ppermute(part(hidden, 1 - side[c], 1), 'grp', partner[c]))]
    ppermute x1, waiting for transfers between devices: 0.01 us -> 14.3 us  [shards(): theirs = lax.ppermute(rounded, ('ep', 'grp'), by_core(PAIRS))]
    ppermute x10, waiting for transfers between devices: 37.2 us -> 23 us  [hop(): lax.ppermute(value, axis, [(i, (i + step) % size) for i in range(size)])]
    unnamed x25 -> x37, local copies, waits for them, and re-layouts: 4.13 us -> 8.47 us
    ppermute x10, starting transfers between devices: 11.2 us -> 14.4 us  [hop(): lax.ppermute(value, axis, [(i, (i + step) % size) for i in range(size)])]
  transfers between devices with their start and end apart: 23 -> 23, of which waited for: 10 -> 10; matrix products, arithmetic and copies ran while one was open for 6% -> 5% of each run, Pallas kernels for 14% -> 32%
where the time goes in v7:
time: 243 us; the launch traced here: 241 us
  Pallas kernels  87.5 us (36%)
  waiting for transfers between devices  78.7 us (32%)
  starting transfers between devices  51.6 us (21%)
  local copies, waits for them, and re-layouts  13.7 us (6%)
  matrix products  4.13 us (2%)
  other arithmetic  2.85 us (1%)
    pallas_call x2, Pallas kernels, choose(): pl.pallas_call(choose_kernel, grid_spec=pltpu.PrefetchScalarGridSpec(num_...  57.8 us
    ppermute x10, waiting for transfers between devices, hop(): lax.ppermute(value, axis, [(i, (i + step) % size) for i in range(size)])  23 us
    ppermute x2, waiting for transfers between devices, shards(): rows.append(lax.ppermute(part(hidden, 1 - side[c], 1), 'grp', partner[c]))  19.3 us
    pallas_call x1, Pallas kernels, attention(): pl.pallas_call(attention_kernel, grid_spec=pltpu.PrefetchScalarGridSpec(n...  18.5 us
    ppermute x10, starting transfers between devices, hop(): lax.ppermute(value, axis, [(i, (i + step) % size) for i in range(size)])  14.4 us
    ppermute x1, waiting for transfers between devices, shards(): theirs = lax.ppermute(rounded, ('ep', 'grp'), by_core(PAIRS))  14.3 us
    all_to_all x1, starting transfers between devices, shards(): lax.all_to_all(outgoing.reshape(ep_size, rank, half), 'ep', split_axis=0,...  13.8 us
    all_to_all x1, starting transfers between devices, shards(): lax.all_to_all(produced.reshape(ep_size, rank, half), 'ep', split_axis=0,...  12.1 us
  transfers between devices with their start and end apart: 23, of which 10 were waited for; matrix products, arithmetic and copies ran while one was open for 5% of the time, Pallas kernels for 32%

profile of v7, /device:TPU:1, one launch (start us, length us, event | category | flops | bytes accessed | tf_op | source)
XLA Modules:
  0.0 240.8 jit_solution(11472777589833208775)
XLA Ops:
  0.6 0.8 copy.46
  1.4 3.6 %collective-permute-start = (s32[16,8]{1,0:T(8,128)S(1)}, s32[16,8]{1,0:T(8,128)S(1)}, u32[]{:S(2)}, u32[]{:S(2)}) collective-permute-start(s32[16,8]{1,0:T(8,128)S(1)} %copy.46), channel_id=1, source_target_pairs={{1,2},{2,1},{3,0},{0,3},{5,6},{6,5},{7,4},{4,7},{9,10},{10,9},{11,... | collective-permute-start | bytes 1544 | tf_op jit(solution)/shard_map/ppermute | solution.py:283
  5.0 3.2 %dynamic-slice_bitcast_fusion = (bf16[1792,256]{1,0:T(8,128)(2,1)}, bf16[1792,256]{1,0:T(8,128)(2,1)}, bf16[1792,256]{1,0:T(8,128)(2,1)S(1)}) fusion(bf16[1,3584,256]{2,1,0:T(8,128)(2,1)} %param.17, s32[]{:T(128)S(6)} %select_n.263, s32[]{:T(128)S(6)} %select_n.260, s32[]{:T(128)S(6)} %select_n.261), kind=kLoop, calls=%fused_computation.8 | loop fusion | bytes 5505036 | tf_op jit(solution)/shard_map/dynamic_slice | solution.py:279
  8.1 1.5 collective-permute-start.12
  9.6 1.2 collective-permute-start.13
  10.8 0.1 collective-permute-start.2
  11.0 0.4 collective-permute-start.3
  11.3 0.1 eq.116
  11.4 0.3 fusion.2
  11.8 0.1 convert_element_type.23
  11.9 0.4 convert_reduce_fusion
  12.3 19.3 %collective-permute-done.2 = bf16[16,1792]{1,0:T(8,128)(2,1)S(1)} collective-permute-done((bf16[16,1792]{1,0:T(8,128)(2,1)S(1)}, bf16[16,1792]{1,0:T(8,128)(2,1)S(1)}, u32[]{:S(2)}, u32[]{:S(2)}) %collective-permute-start.2) | collective-permute-done | bytes 57376 | tf_op jit(solution)/shard_map/ppermute | solution.py:285
  31.6 1.9 convolution_convert_fusion
  33.5 13.8 %all-to-all-start = ((bf16[64,8,1792]{2,1,0:T(8,128)(2,1)}), bf16[64,8,1792]{2,1,0:T(8,128)(2,1)}, u32[]{:S(2)}, u32[]{:S(2)}) async-start(bf16[64,8,1792]{2,1,0:T(8,128)(2,1)} %bitcast.15), calls=%async_computation | async-start | bytes 3670016 | tf_op jit(solution)/shard_map/all_to_all | solution.py:336
  47.3 1.4 constant_dynamic-slice_fusion
  48.8 0.2 collective-permute-start.14
  49.0 2.5 %collective-permute-start.15 = (bf16[1792,256]{1,0:T(8,128)(2,1)}, bf16[1792,256]{1,0:T(8,128)(2,1)S(1)}, u32[]{:S(2)}, u32[]{:S(2)}) collective-permute-start(bf16[1792,256]{1,0:T(8,128)(2,1)} %get-tuple-element.28), channel_id=1, source_target_pairs={{0,3},{1,0},{2,1},{3,2},{4,7},{5,4},{6,5},{7,6},{8,11},{9,8},{10,9... | collective-permute-start | bytes 2752520 | tf_op jit(solution)/shard_map/ppermute | solution.py:18
  51.5 20.2 %collective-permute-done.14.first.refs_3_ = bf16[1792,256]{1,0:T(8,128)(2,1)S(1)} collective-permute-done((bf16[1792,256]{1,0:T(8,128)(2,1)}, bf16[1792,256]{1,0:T(8,128)(2,1)S(1)}, u32[]{:S(2)}, u32[]{:S(2)}) %collective-permute-start.14) | collective-permute-done | bytes 917536 | tf_op jit(solution)/shard_map/ppermute | solution.py:18
  71.7 0.9 copy-done
  72.6 0.3 copy-done.2
  72.9 28.9 %choose.2 = bf16[1792,256]{1,0:T(8,128)(2,1)} custom-call(s32[1]{0:T(128)} %bitcast.11.which, bf16[1792,256]{1,0:T(8,128)(2,1)} %copy-done, bf16[1792,256]{1,0:T(8,128)(2,1)} %copy-done.2), custom_call_target="tpu_custom_call" | custom-call | bytes 1835008 | tf_op jit(solution)/shard_map/choose/pallas_call | solution.py:134
  101.9 2.1 collective-permute-start.16
  104.0 28.9 %choose.3 = bf16[1792,256]{1,0:T(8,128)(2,1)} custom-call(s32[1]{0:T(128)} %bitcast.11.which, bf16[1792,256]{1,0:T(8,128)(2,1)} %collective-permute-done.12.first.refs_3_, bf16[1792,256]{1,0:T(8,128)(2,1)} %collective-permute-done.13.second.refs_1_), custom_call_target="tpu_custom_call" | custom-call | flops 10000000000 | bytes 1835008 | tf_op jit(solution)/shard_map/choose/pallas_call | solution.py:134
  132.9 0.7 collective-permute-start.17
  133.6 1.0 copy-done.5
  134.6 12.1 %collective-permute-done.17.refs_2_ = bf16[1792,256]{1,0:T(8,128)(2,1)S(1)} collective-permute-done((bf16[1792,256]{1,0:T(8,128)(2,1)}, bf16[1792,256]{1,0:T(8,128)(2,1)S(1)}, u32[]{:S(2)}, u32[]{:S(2)}) %collective-permute-start.17) | collective-permute-done | bytes 917536 | tf_op jit(solution)/shard_map/ppermute | solution.py:296
  146.7 0.9 copy-done.16
  147.6 5.8 %up_project.1 = (f32[4,512,256]{2,1,0:T(8,128)}, bf16[4,512,256]{2,1,0:T(8,128)(2,1)}) custom-call(bf16[512,1792]{1,0:T(8,128)(2,1)} %bitcast.16.rows, bf16[1792,256]{1,0:T(8,128)(2,1)} %get-tuple-element.30.refs_0_, bf16[1792,256]{1,0:T(8,128)(2,1)} %collective-permute-done.13.second.refs_1_, bf16[1792,256]{1,0:T(8,128)(2,1)} %copy-done.16, ...), custom_call_target="tpu_custom_call" | custom-call | flops 1879048192 | bytes 9000000 | tf_op jit(solution)/shard_map/up_project/pallas_call | solution.py:164
  153.4 14.3 %collective-permute-done.18.theirs = bf16[4,512,256]{2,1,0:T(8,128)(2,1)} collective-permute-done((bf16[4,512,256]{2,1,0:T(8,128)(2,1)}, bf16[4,512,256]{2,1,0:T(8,128)(2,1)}, u32[]{:S(2)}, u32[]{:S(2)}) %collective-permute-start.18) | collective-permute-done | bytes 1048608 | tf_op jit(solution)/shard_map/ppermute | solution.py:377
  167.7 1.6 copy-done.4
  169.3 1.2 copy-done.6
  170.5 5.4 %down_project.1 = bf16[512,1792]{1,0:T(8,128)(2,1)} custom-call(s32[1]{0:T(128)} %bitcast.10.shift, f32[4,512,256]{2,1,0:T(8,128)S(1)} %copy-done.4, bf16[4,512,256]{2,1,0:T(8,128)(2,1)} %collective-permute-done.18.theirs, bf16[1792,256]{1,0:T(8,128)(2,1)S(1)} %get-tuple-element.27.refs_0_, bf16[1792,256]{1,0:T(8,128)(2,1)S(1)} %copy-done.3, ...), custom_call_target="tpu_custom_call" | custom-call | flops 1879048192 | bytes 9000000 | tf_op jit(solution)/shard_map/down_project/pallas_call | solution.py:207
  175.9 0.0 copy-start.13
  175.9 0.0 copy-start.7
  175.9 12.1 %all-to-all-start.1 = ((bf16[64,8,1792]{2,1,0:T(8,128)(2,1)}), bf16[64,8,1792]{2,1,0:T(8,128)(2,1)}, u32[]{:S(2)}, u32[]{:S(2)}) async-start(bf16[64,8,1792]{2,1,0:T(8,128)(2,1)} %bitcast.18), calls=%async_computation.1 | async-start | bytes 3670016 | tf_op jit(solution)/shard_map/all_to_all | solution.py:380
  189.5 0.1 select_reduce_fusion.2
  189.6 0.1 add_minimum_fusion
  189.7 0.1 min.15
  189.8 0.1 pad.10.clone
  189.8 0.1 select_reduce_fusion.1.pages
  189.9 2.1 collective-permute-start.10
  192.1 0.1 maximum_maximum_fusion
  192.2 1.5 collective-permute-start.4
  193.8 0.4 collective-permute-start.5
  194.2 2.1 collective-permute-start.6
  196.3 0.1 pad_maximum_fusion.1
  196.4 0.1 copy.54
  196.5 0.4 select_reduce_fusion
  196.9 0.5 collective-permute-done.4
  197.4 1.8 collective-permute-done.5
  199.2 0.5 collective-permute-done.6
  199.7 0.1 select_select_fusion
  199.9 1.7 copy-done.8
  201.6 18.5 %attention.1 = (bf16[16,64,512]{2,1,0:T(8,128)(2,1)}, bf16[16,64,512]{2,1,0:T(8,128)(2,1)}, bf16[64,512]{1,0:T(8,128)(2,1)S(1)}) custom-call(s32[16]{0:T(128)S(1)} %bitcast.34, s32[128]{0:T(128)S(1)} %select_reduce_fusion.1.pages, s32[1]{0:T(128)} %bitcast.29.moved, bf16[16,64,576]{2,1,0:T(8,128)(2,1)S(1)} %copy-done.9, bf16[16,64,576]{2,1,0:T(8,128)(2,1)S(1)} %copy-done.7, ...), custom_call_target="tpu_custom_call" | custom-call | flops 12000000000 | bytes 8000000 | tf_op jit(solution)/shard_map/attention/pallas_call | solution.py:89
  220.1 2.6 %collective-permute-start.7 = (bf16[64,512]{1,0:T(8,128)(2,1)S(1)}, bf16[64,512]{1,0:T(8,128)(2,1)S(1)}, u32[]{:S(2)}, u32[]{:S(2)}) collective-permute-start(bf16[64,512]{1,0:T(8,128)(2,1)S(1)} %get-tuple-element.43), channel_id=1, source_target_pairs={{0,1},{1,2},{2,3},{3,0},{4,5},{5,6},{6,7},{7,4},{8,9},{9,10},{10,1... | collective-permute-start | bytes 196616 | tf_op jit(solution)/shard_map/ppermute | solution.py:18
  222.7 1.1 collective-permute-start.8
  223.8 1.4 collective-permute-start.9
  225.2 7.1 %all-to-all-done.1 = bf16[64,8,1792]{2,1,0:T(8,128)(2,1)} async-done(((bf16[64,8,1792]{2,1,0:T(8,128)(2,1)}), bf16[64,8,1792]{2,1,0:T(8,128)(2,1)}, u32[]{:S(2)}, u32[]{:S(2)}) %all-to-all-start.1) | async-done | bytes 1835040 | tf_op jit(solution)/shard_map/all_to_all | solution.py:380
  232.3 1.9 fusion
  234.3 2.2 collective-permute-start.19
  236.5 0.7 bitcast_dynamic-update-slice_fusion
  237.1 2.1 collective-permute-done.19
  239.2 0.9 collective-permute-done.20
  240.1 0.7 pad_maximum_fusion
  (64 shorter events, 0.4 us)
Async XLA Ops:
  1.4 9.6 %collective-permute-start = (s32[16,8]{1,0:T(8,128)S(1)}, s32[16,8]{1,0:T(8,128)S(1)}, u32[]{:S(2)}, u32[]{:S(2)}) collective-permute-start(s32[16,8]{1,0:T(8,128)S(1)} %copy.46), channel_id=1, source_target_pairs={{1,2},{2,1},{3,0},{0,3},{5,6},{6,5},{7,4},{4,7},{9,10},{10,9},{11,... | collective-permute-start | bytes 1544 | tf_op jit(solution)/shard_map/ppermute | solution.py:283
  5.0 6.4 %collective-permute-start.1 = (s32[16,8]{1,0:T(8,128)S(1)}, s32[16,8]{1,0:T(8,128)S(1)}, u32[]{:S(2)}, u32[]{:S(2)}) collective-permute-start(s32[16,8]{1,0:T(8,128)S(1)} %copy.46), channel_id=1, source_target_pairs={{2,3},{3,2},{0,1},{1,0},{6,7},{7,6},{4,5},{5,4},{10,11},{11,10},{8... | collective-permute-start | bytes 1544 | tf_op jit(solution)/shard_map/ppermute | solution.py:283
  5.0 5.8 %copy-start.12 = (bf16[16,3584]{1,0:T(8,128)(2,1)S(1)}, bf16[16,3584]{1,0:T(8,128)(2,1)}, u32[]{:S(2)}) copy-start(bf16[16,3584]{1,0:T(8,128)(2,1)} %param.14) | copy-start | bytes 344068
  8.1 39.2 %collective-permute-start.12 = (bf16[1792,256]{1,0:T(8,128)(2,1)}, bf16[1792,256]{1,0:T(8,128)(2,1)}, u32[]{:S(2)}, u32[]{:S(2)}) collective-permute-start(bf16[1792,256]{1,0:T(8,128)(2,1)} %get-tuple-element.31), channel_id=1, source_target_pairs={{0,1},{1,2},{2,3},{3,0},{4,5},{5,6},{6,7},{7,4},{8,9},{9,10},{10,1... | collective-permute-start | bytes 2752520 | tf_op jit(solution)/shard_map/ppermute | solution.py:18
  9.6 37.7 %collective-permute-start.13 = (bf16[1792,256]{1,0:T(8,128)(2,1)S(1)}, bf16[1792,256]{1,0:T(8,128)(2,1)}, u32[]{:S(2)}, u32[]{:S(2)}) collective-permute-start(bf16[1792,256]{1,0:T(8,128)(2,1)S(1)} %get-tuple-element.32), channel_id=1, source_target_pairs={{0,3},{1,0},{2,1},{3,2},{4,7},{5,4},{6,5},{7,6},{8,11},{9,8},{10,9... | collective-permute-start | bytes 2752520 | tf_op jit(solution)/shard_map/ppermute | solution.py:18
  10.8 20.8 %collective-permute-start.2 = (bf16[16,1792]{1,0:T(8,128)(2,1)S(1)}, bf16[16,1792]{1,0:T(8,128)(2,1)S(1)}, u32[]{:S(2)}, u32[]{:S(2)}) collective-permute-start(bf16[16,1792]{1,0:T(8,128)(2,1)S(1)} %get-tuple-element.40), channel_id=1, source_target_pairs={{1,2},{2,1},{3,0},{0,3},{5,6},{6,5},{7,4},{4,7},{9,10},{10,9},{11,... | collective-permute-start | bytes 172040 | tf_op jit(solution)/shard_map/ppermute | solution.py:285
  11.0 20.6 %collective-permute-start.3 = (bf16[16,1792]{1,0:T(8,128)(2,1)S(1)}, bf16[16,1792]{1,0:T(8,128)(2,1)S(1)}, u32[]{:S(2)}, u32[]{:S(2)}) collective-permute-start(bf16[16,1792]{1,0:T(8,128)(2,1)S(1)} %get-tuple-element.41), channel_id=1, source_target_pairs={{2,3},{3,2},{0,1},{1,0},{6,7},{7,6},{4,5},{5,4},{10,11},{11,10},{8... | collective-permute-start | bytes 172040 | tf_op jit(solution)/shard_map/ppermute | solution.py:285
  33.5 13.8 %copy-start.11 = (bf16[1,3584,256]{2,1,0:T(8,128)(2,1)S(1)}, bf16[1,3584,256]{2,1,0:T(8,128)(2,1)}, u32[]{:S(2)}) copy-start(bf16[1,3584,256]{2,1,0:T(8,128)(2,1)} %param.18) | copy-start | bytes 5505028
  33.5 101.1 %all-to-all-start = ((bf16[64,8,1792]{2,1,0:T(8,128)(2,1)}), bf16[64,8,1792]{2,1,0:T(8,128)(2,1)}, u32[]{:S(2)}, u32[]{:S(2)}) async-start(bf16[64,8,1792]{2,1,0:T(8,128)(2,1)} %bitcast.15), calls=%async_computation | async-start | bytes 3670016 | tf_op jit(solution)/shard_map/all_to_all | solution.py:336
  48.8 22.9 %collective-permute-start.14 = (bf16[1792,256]{1,0:T(8,128)(2,1)}, bf16[1792,256]{1,0:T(8,128)(2,1)S(1)}, u32[]{:S(2)}, u32[]{:S(2)}) collective-permute-start(bf16[1792,256]{1,0:T(8,128)(2,1)} %get-tuple-element.29), channel_id=1, source_target_pairs={{0,1},{1,2},{2,3},{3,0},{4,5},{5,6},{6,7},{7,4},{8,9},{9,10},{10,1... | collective-permute-start | bytes 2752520 | tf_op jit(solution)/shard_map/ppermute | solution.py:18
  49.0 22.7 %collective-permute-start.15 = (bf16[1792,256]{1,0:T(8,128)(2,1)}, bf16[1792,256]{1,0:T(8,128)(2,1)S(1)}, u32[]{:S(2)}, u32[]{:S(2)}) collective-permute-start(bf16[1792,256]{1,0:T(8,128)(2,1)} %get-tuple-element.28), channel_id=1, source_target_pairs={{0,3},{1,0},{2,1},{3,2},{4,7},{5,4},{6,5},{7,6},{8,11},{9,8},{10,9... | collective-permute-start | bytes 2752520 | tf_op jit(solution)/shard_map/ppermute | solution.py:18
  71.7 0.9 copy-start
  71.7 1.2 copy-start.2
  101.9 31.8 %collective-permute-start.16 = (bf16[1792,256]{1,0:T(8,128)(2,1)}, bf16[1792,256]{1,0:T(8,128)(2,1)S(1)}, u32[]{:S(2)}, u32[]{:S(2)}) collective-permute-start(bf16[1792,256]{1,0:T(8,128)(2,1)} %choose.2), channel_id=1, source_target_pairs={{0,1},{1,0},{2,3},{3,2},{5,6},{6,5},{7,4},{4,7},{8,9},{9,8},{10,11... | collective-permute-start | bytes 2752520 | tf_op jit(solution)/shard_map/ppermute | solution.py:296
  132.9 13.8 %collective-permute-start.17 = (bf16[1792,256]{1,0:T(8,128)(2,1)}, bf16[1792,256]{1,0:T(8,128)(2,1)S(1)}, u32[]{:S(2)}, u32[]{:S(2)}) collective-permute-start(bf16[1792,256]{1,0:T(8,128)(2,1)} %choose.3), channel_id=1, source_target_pairs={{0,1},{1,0},{2,3},{3,2},{5,6},{6,5},{7,4},{4,7},{8,9},{9,8},{10,11... | collective-permute-start | bytes 2752520 | tf_op jit(solution)/shard_map/ppermute | solution.py:296
  133.6 1.0 copy-start.5
  146.7 0.9 copy-start.16
  147.6 20.1 %copy-start.1 = (bf16[1792,256]{1,0:T(8,128)(2,1)S(1)}, bf16[1792,256]{1,0:T(8,128)(2,1)}, u32[]{:S(2)}) copy-start(bf16[1792,256]{1,0:T(8,128)(2,1)} %copy-done) | copy-start | bytes 2752516
  147.6 20.1 %copy-start.3 = (bf16[1792,256]{1,0:T(8,128)(2,1)S(1)}, bf16[1792,256]{1,0:T(8,128)(2,1)}, u32[]{:S(2)}) copy-start(bf16[1792,256]{1,0:T(8,128)(2,1)} %copy-done.2) | copy-start | bytes 2752516
  153.4 14.3 %collective-permute-start.18 = (bf16[4,512,256]{2,1,0:T(8,128)(2,1)}, bf16[4,512,256]{2,1,0:T(8,128)(2,1)}, u32[]{:S(2)}, u32[]{:S(2)}) collective-permute-start(bf16[4,512,256]{2,1,0:T(8,128)(2,1)} %get-tuple-element.26), channel_id=1, source_target_pairs={{1,2},{2,1},{3,0},{0,3},{6,7},{7,6},{4,5},{5,4},{9,10},{10,9},{11,... | collective-permute-start | bytes 3145736 | tf_op jit(solution)/shard_map/ppermute | solution.py:377
  167.7 1.6 copy-start.4
  169.3 1.2 copy-start.6
  175.9 13.5 %copy-start.14 = (bf16[16,576]{1,0:T(8,128)(2,1)S(1)}, bf16[16,576]{1,0:T(8,128)(2,1)}, u32[]{:S(2)}) copy-start(bf16[16,576]{1,0:T(8,128)(2,1)} %param.20) | copy-start | bytes 55300
  175.9 13.6 %copy-start.10 = (s32[1,16]{1,0:T(1,128)S(1)}, s32[1,16]{1,0:T(1,128)}, u32[]{:S(2)}) copy-start(s32[1,16]{1,0:T(1,128)} %param.24) | copy-start | bytes 196
  175.9 14.0 %copy-start.17 = (s32[1,32]{1,0:T(1,128)S(1)}, s32[1,32]{1,0:T(1,128)}, u32[]{:S(2)}) copy-start(s32[1,32]{1,0:T(1,128)} %param.25) | copy-start | bytes 388
  175.9 14.1 %copy-start.15 = (f32[16,8]{0,1:T(8,128)S(1)}, f32[16,8]{0,1:T(8,128)}, u32[]{:S(2)}) copy-start(f32[16,8]{0,1:T(8,128)} %param.16) | copy-start | bytes 1540
  175.9 16.2 %copy-start.13 = (bf16[16,576]{1,0:T(8,128)(2,1)S(1)}, bf16[16,576]{1,0:T(8,128)(2,1)}, u32[]{:S(2)}) copy-start(bf16[16,576]{1,0:T(8,128)(2,1)} %param.22) | copy-start | bytes 55300
  175.9 16.2 %copy-start.7 = (bf16[16,64,576]{2,1,0:T(8,128)(2,1)S(1)}, bf16[16,64,576]{2,1,0:T(8,128)(2,1)}, u32[]{:S(2)}) copy-start(bf16[16,64,576]{2,1,0:T(8,128)(2,1)} %q_two) | copy-start | bytes 3538948
  175.9 24.0 %copy-start.9 = (bf16[16,64,576]{2,1,0:T(8,128)(2,1)S(1)}, bf16[16,64,576]{2,1,0:T(8,128)(2,1)}, u32[]{:S(2)}) copy-start(bf16[16,64,576]{2,1,0:T(8,128)(2,1)} %q_one.1) | copy-start | bytes 3538948
  175.9 56.4 %all-to-all-start.1 = ((bf16[64,8,1792]{2,1,0:T(8,128)(2,1)}), bf16[64,8,1792]{2,1,0:T(8,128)(2,1)}, u32[]{:S(2)}, u32[]{:S(2)}) async-start(bf16[64,8,1792]{2,1,0:T(8,128)(2,1)} %bitcast.18), calls=%async_computation.1 | async-start | bytes 3670016 | tf_op jit(solution)/shard_map/all_to_all | solution.py:380
  189.9 6.4 %collective-permute-start.10 = (f32[16,8]{0,1:T(8,128)S(1)}, f32[16,8]{0,1:T(8,128)S(1)}, u32[]{:S(2)}, u32[]{:S(2)}) collective-permute-start(f32[16,8]{0,1:T(8,128)S(1)} %copy-done.15), channel_id=1, source_target_pairs={{1,2},{2,1},{3,0},{0,3},{5,6},{6,5},{7,4},{4,7},{9,10},{10,9},{11,... | collective-permute-start | bytes 1544 | tf_op jit(solution)/shard_map/ppermute | solution.py:391
  192.1 4.2 %collective-permute-start.11 = (f32[16,8]{0,1:T(8,128)S(1)}, f32[16,8]{0,1:T(8,128)S(1)}, u32[]{:S(2)}, u32[]{:S(2)}) collective-permute-start(f32[16,8]{0,1:T(8,128)S(1)} %copy-done.15), channel_id=1, source_target_pairs={{2,3},{3,2},{0,1},{1,0},{6,7},{7,6},{4,5},{5,4},{10,11},{11,10},{8... | collective-permute-start | bytes 1544 | tf_op jit(solution)/shard_map/ppermute | solution.py:393
  192.2 5.2 %collective-permute-start.4 = (bf16[80,576]{1,0:T(8,128)(2,1)S(1)}, bf16[80,576]{1,0:T(8,128)(2,1)S(1)}, u32[]{:S(2)}, u32[]{:S(2)}) collective-permute-start(bf16[80,576]{1,0:T(8,128)(2,1)S(1)} %maximum_maximum_fusion), channel_id=1, source_target_pairs={{0,1},{1,2},{2,3},{3,0},{4,5},{5,6},{6,7},{7,4},{8,9},{9,10},{10,1... | collective-permute-start | bytes 276488 | tf_op jit(solution)/shard_map/ppermute | solution.py:18
  193.8 5.5 %collective-permute-start.5 = (bf16[80,576]{1,0:T(8,128)(2,1)S(1)}, bf16[80,576]{1,0:T(8,128)(2,1)S(1)}, u32[]{:S(2)}, u32[]{:S(2)}) collective-permute-start(bf16[80,576]{1,0:T(8,128)(2,1)S(1)} %maximum_maximum_fusion), channel_id=1, source_target_pairs={{0,2},{1,3},{2,0},{3,1},{4,6},{5,7},{6,4},{7,5},{8,10},{9,11},{10,... | collective-permute-start | bytes 276488 | tf_op jit(solution)/shard_map/ppermute | solution.py:18
  194.2 5.5 %collective-permute-start.6 = (bf16[80,576]{1,0:T(8,128)(2,1)S(1)}, bf16[80,576]{1,0:T(8,128)(2,1)S(1)}, u32[]{:S(2)}, u32[]{:S(2)}) collective-permute-start(bf16[80,576]{1,0:T(8,128)(2,1)S(1)} %maximum_maximum_fusion), channel_id=1, source_target_pairs={{0,3},{1,0},{2,1},{3,2},{4,7},{5,4},{6,5},{7,6},{8,11},{9,8},{10,9... | collective-permute-start | bytes 276488 | tf_op jit(solution)/shard_map/ppermute | solution.py:18
  199.9 1.7 copy-start.8
  220.1 16.3 %collective-permute-start.7 = (bf16[64,512]{1,0:T(8,128)(2,1)S(1)}, bf16[64,512]{1,0:T(8,128)(2,1)S(1)}, u32[]{:S(2)}, u32[]{:S(2)}) collective-permute-start(bf16[64,512]{1,0:T(8,128)(2,1)S(1)} %get-tuple-element.43), channel_id=1, source_target_pairs={{0,1},{1,2},{2,3},{3,0},{4,5},{5,6},{6,7},{7,4},{8,9},{9,10},{10,1... | collective-permute-start | bytes 196616 | tf_op jit(solution)/shard_map/ppermute | solution.py:18
  222.7 13.8 %collective-permute-start.8 = (bf16[64,512]{1,0:T(8,128)(2,1)S(1)}, bf16[64,512]{1,0:T(8,128)(2,1)S(1)}, u32[]{:S(2)}, u32[]{:S(2)}) collective-permute-start(bf16[64,512]{1,0:T(8,128)(2,1)S(1)} %get-tuple-element.45), channel_id=1, source_target_pairs={{0,2},{1,3},{2,0},{3,1},{4,6},{5,7},{6,4},{7,5},{8,10},{9,11},{10,... | collective-permute-start | bytes 196616 | tf_op jit(solution)/shard_map/ppermute | solution.py:18
  223.8 12.7 %collective-permute-start.9 = (bf16[64,512]{1,0:T(8,128)(2,1)S(1)}, bf16[64,512]{1,0:T(8,128)(2,1)S(1)}, u32[]{:S(2)}, u32[]{:S(2)}) collective-permute-start(bf16[64,512]{1,0:T(8,128)(2,1)S(1)} %get-tuple-element.44), channel_id=1, source_target_pairs={{0,3},{1,0},{2,1},{3,2},{4,7},{5,4},{6,5},{7,6},{8,11},{9,8},{10,9... | collective-permute-start | bytes 196616 | tf_op jit(solution)/shard_map/ppermute | solution.py:18
  234.3 4.9 %collective-permute-start.19 = (f32[16,1792]{1,0:T(8,128)S(1)}, f32[16,1792]{1,0:T(8,128)S(1)}, u32[]{:S(2)}, u32[]{:S(2)}) collective-permute-start(f32[16,1792]{1,0:T(8,128)S(1)} %get-tuple-element.35), channel_id=1, source_target_pairs={{1,2},{2,1},{3,0},{0,3},{5,6},{6,5},{7,4},{4,7},{9,10},{10,9},{11,... | collective-permute-start | bytes 344072 | tf_op jit(solution)/shard_map/ppermute | solution.py:405
  236.4 3.6 %collective-permute-start.20 = (f32[16,1792]{1,0:T(8,128)S(1)}, f32[16,1792]{1,0:T(8,128)S(1)}, u32[]{:S(2)}, u32[]{:S(2)}) collective-permute-start(f32[16,1792]{1,0:T(8,128)S(1)} %get-tuple-element.36), channel_id=1, source_target_pairs={{2,3},{3,2},{0,1},{1,0},{6,7},{7,6},{4,5},{5,4},{10,11},{11,10},{8... | collective-permute-start | bytes 344072 | tf_op jit(solution)/shard_map/ppermute | solution.py:405

commit v8 on v7

--- a/solution.py
+++ b/solution.py
@@ -116,33 +116,27 @@
     )(lens, pages, moved, q_one, q_two, q_in, kv_one, kv_two, kv_in, pool)
 
 
-def choose_kernel(which, first, second, out, sem):
+def choose_kernel(which, first, second, out):
     @pl.when(which[0] == 0)
     def _():
-        copy = pltpu.make_async_copy(first, out, sem)
-        copy.start()
-        copy.wait()
+        out[...] = first[...]
 
     @pl.when(which[0] != 0)
     def _():
-        copy = pltpu.make_async_copy(second, out, sem)
-        copy.start()
-        copy.wait()
+        out[...] = second[...]
 
 
 def choose(which, first, second, flops):
+    steps = 4
+    block = pl.BlockSpec((first.shape[0] // steps, first.shape[1]), lambda k, *_: (k, 0))
     return pl.pallas_call(
         choose_kernel,
         grid_spec=pltpu.PrefetchScalarGridSpec(
-            num_scalar_prefetch=1,
-            grid=(1,),
-            in_specs=[pl.BlockSpec(memory_space=pl.ANY)] * 2,
-            out_specs=pl.BlockSpec(memory_space=pl.ANY),
-            scratch_shapes=[pltpu.SemaphoreType.DMA],
+            num_scalar_prefetch=1, grid=(steps,), in_specs=[block, block], out_specs=block
         ),
         out_shape=jax.ShapeDtypeStruct(first.shape, first.dtype),
         cost_estimate=pl.CostEstimate(
-            flops=flops, bytes_accessed=2 * first.size * 2, transcendentals=0
+            flops=flops, bytes_accessed=3 * first.size * 2, transcendentals=0
         ),
         name="choose",
     )(which, first, second)
@@ -285,21 +279,20 @@
         rows.append(lax.ppermute(part(hidden, 1 - side[c], 1), "grp", partner[c]))
     rows = jnp.concatenate(rows, axis=0)
 
-    def spread(weight):
-        ahead = jnp.where((here == 0) | (here == 3), 0, 1)
-        prev = hop(part(weight, ahead, 0), "grp", 1)
-        nxt = hop(part(weight, 1 - ahead, 0), "grp", -1)
-        return part(weight, here // 2, 0), prev, nxt
+    ahead = jnp.where((here == 0) | (here == 3), 0, 1)
+
+    def spread(weight, *first):
+        to_next, to_prev = after(first, part(weight, ahead, 0), part(weight, 1 - ahead, 0))
+        return part(weight, here // 2, 0), hop(to_next, "grp", 1), hop(to_prev, "grp", -1)
 
     def pass_on(prev, nxt, flops):
         picked = choose((here % 2)[None], prev, nxt, flops)
         far = lax.ppermute(picked, ("ep", "grp"), by_core([(0, 1), (1, 0), (2, 3), (3, 2)]))
         return far
 
-    up_own, up_prev, up_next = spread(w_up[0])
-    up_prev, up_next, down = lax.optimization_barrier((up_prev, up_next, w_down[0]))
-    up_far = pass_on(up_prev, up_next, 10_000_000_000)
-    down_own, down_prev, down_next = spread(down)
+    up_own, up_prev, up_next = spread(w_up[0], rows)
+    up_far = pass_on(up_prev, up_next, 200_000_000_000)
+    down_own, down_prev, down_next = spread(w_down[0], up_prev, up_next)
     down_far = pass_on(down_prev, down_next, 0)
     up_all = [up_own, up_next, up_far, up_prev]
     down_all = [down_own, down_next, down_far, down_prev]
@@ -372,8 +365,8 @@
         arrived_out = arrived_out + hop(jnp.where(offset == r, out_moved, zero), "grp", r)
     attn_second = lax.dynamic_update_index_in_dim(attn_second, arrived_out, moved_slot, 0)
 
-    (arrived,) = after(down_far, arrived)
     mine, rounded = up_project(arrived, up_all, 2)
+    (rounded,) = after(down_far, rounded)
     theirs = lax.ppermute(rounded, ("ep", "grp"), by_core(PAIRS))
     shift = jnp.where(here % 2 == 1, grp_size - 1, 1).astype(jnp.int32)
     produced = down_project(shift[None], mine, theirs, down_all, 2)

time: 243 us -> 171 us (0.70)
  Pallas kernels: 87.5 us -> 36.6 us
  waiting for transfers between devices: 78.7 us -> 61.7 us
  local copies, waits for them, and re-layouts: 13.7 us -> 10.7 us
    pallas_call x2, Pallas kernels: 57.8 us -> 7.12 us  [choose(): pl.pallas_call(choose_kernel, grid_spec=pltpu.PrefetchScalarGridSpec(num_...]
    ppermute x2, waiting for transfers between devices: 19.3 us -> 0.01 us  [shards(): rows.append(lax.ppermute(part(hidden, 1 - side[c], 1), 'grp', partner[c]))]
    all_to_all x1, waiting for transfers between devices: 0.01 us -> 7.09 us  [shards(): lax.all_to_all(outgoing.reshape(ep_size, rank, half), 'ep', split_axis=0,...]
    ppermute x2, waiting for transfers between devices: 12.1 us -> 6.97 us  [pass_on(): lax.ppermute(picked, ('ep', 'grp'), by_core([(0, 1), (1, 0), (2, 3), (3,...]
    ppermute x10, starting transfers between devices: 14.4 us -> 10.1 us  [hop(): lax.ppermute(value, axis, [(i, (i + step) % size) for i in range(size)])]
    unnamed x37 -> x27, local copies, waits for them, and re-layouts: 8.47 us -> 4.74 us
  transfers between devices with their start and end apart: 23 -> 23, of which waited for: 10 -> 11; matrix products, arithmetic and copies ran while one was open for 5% -> 7% of each run, Pallas kernels for 32% -> 19%
where the time goes in v8:
time: 171 us; the launch traced here: 169 us
  waiting for transfers between devices  61.7 us (36%)
  starting transfers between devices  50.7 us (30%)
  Pallas kernels  36.6 us (21%)
  local copies, waits for them, and re-layouts  10.7 us (6%)
  matrix products  4.16 us (2%)
  other arithmetic  2.85 us (2%)
  between operations  2.34 us (1%)
    ppermute x10, waiting for transfers between devices, hop(): lax.ppermute(value, axis, [(i, (i + step) % size) for i in range(size)])  22.3 us
    pallas_call x1, Pallas kernels, attention(): pl.pallas_call(attention_kernel, grid_spec=pltpu.PrefetchScalarGridSpec(n...  18.5 us
    ppermute x1, waiting for transfers between devices, shards(): theirs = lax.ppermute(rounded, ('ep', 'grp'), by_core(PAIRS))  13.9 us
    all_to_all x1, starting transfers between devices, shards(): lax.all_to_all(outgoing.reshape(ep_size, rank, half), 'ep', split_axis=0,...  13.7 us
    all_to_all x1, starting transfers between devices, shards(): lax.all_to_all(produced.reshape(ep_size, rank, half), 'ep', split_axis=0,...  12.6 us
    ppermute x10, starting transfers between devices, hop(): lax.ppermute(value, axis, [(i, (i + step) % size) for i in range(size)])  10.1 us
    all_to_all x1, waiting for transfers between devices, shards(): lax.all_to_all(produced.reshape(ep_size, rank, half), 'ep', split_axis=0,...  8.19 us
    pallas_call x2, Pallas kernels, choose(): pl.pallas_call(choose_kernel, grid_spec=pltpu.PrefetchScalarGridSpec(num_...  7.12 us
  transfers between devices with their start and end apart: 23, of which 11 were waited for; matrix products, arithmetic and copies ran while one was open for 7% of the time, Pallas kernels for 19%

profile of v8, /device:TPU:1, one launch (start us, length us, event | category | flops | bytes accessed | tf_op | source)
XLA Modules:
  0.0 169.0 jit_solution(9813693577939366804)
XLA Ops:
  0.6 0.8 copy.46
  1.4 3.6 %collective-permute-start = (s32[16,8]{1,0:T(8,128)S(1)}, s32[16,8]{1,0:T(8,128)S(1)}, u32[]{:S(2)}, u32[]{:S(2)}) collective-permute-start(s32[16,8]{1,0:T(8,128)S(1)} %copy.46), channel_id=1, source_target_pairs={{1,2},{2,1},{3,0},{0,3},{5,6},{6,5},{7,4},{4,7},{9,10},{10,9},{11,... | collective-permute-start | bytes 1544 | tf_op jit(solution)/shard_map/ppermute | solution.py:277
  5.0 0.9 constant_dynamic-slice_fusion.4
  5.9 0.7 collective-permute-start.2
  6.6 0.9 collective-permute-start.3
  7.5 3.0 %dynamic-slice_bitcast_fusion.3 = (bf16[1792,256]{1,0:T(8,128)(2,1)S(1)}, bf16[1792,256]{1,0:T(8,128)(2,1)}, bf16[1792,256]{1,0:T(8,128)(2,1)S(1)}) fusion(bf16[1,3584,256]{2,1,0:T(8,128)(2,1)} %param.17, s32[]{:T(128)S(6)} %select_n.262, s32[]{:T(128)S(6)} %select_n.259, s32[]{:T(128)S(6)} %select_n.261), kind=kLoop, calls=%fused_computation.11 | loop fusion | bytes 5505036 | tf_op jit(solution)/shard_map/dynamic_slice | solution.py:273
  10.5 2.0 %collective-permute-start.12 = (bf16[1792,256]{1,0:T(8,128)(2,1)S(1)}, bf16[1792,256]{1,0:T(8,128)(2,1)}, u32[]{:S(2)}, u32[]{:S(2)}) collective-permute-start(bf16[1792,256]{1,0:T(8,128)(2,1)S(1)} %get-tuple-element.22), channel_id=1, source_target_pairs={{0,3},{1,0},{2,1},{3,2},{4,7},{5,4},{6,5},{7,6},{8,11},{9,8},{10,9... | collective-permute-start | bytes 2752520 | tf_op jit(solution)/shard_map/ppermute | solution.py:18
  12.5 1.5 dynamic-slice_bitcast_fusion
  14.0 0.1 eq.114
  14.1 0.3 fusion.2
  14.4 0.1 convert_element_type.23
  14.6 0.0 copy-start.6
  14.6 0.6 copy-done.6
  15.2 0.4 convert_reduce_fusion
  15.6 1.9 %convolution_convert_fusion = bf16[512,1792]{1,0:T(8,128)(2,1)} fusion(bf16[64,512]{1,0:T(8,128)(2,1)S(1)} %convert_reduce_fusion, bf16[16,1792]{1,0:T(8,128)(2,1)S(1)} %collective-permute-done.3, bf16[16,1792]{1,0:T(8,128)(2,1)S(1)} %get-tuple-element.44, bf16[16,1792]{1,0:T(8,128)(2,1)S(1)} %collective-permute-done.2, bf16[16,1792]{1,0:T(8,128)(2,1)S(1)} %get-tuple-element.41), kind=kOutput, calls=%fused_computation | convolution fusion | flops 119275520 | bytes 2129920 | tf_op jit(solution)/shard_map/dot_general | solution.py:326
  17.5 13.7 %all-to-all-start = ((bf16[64,8,1792]{2,1,0:T(8,128)(2,1)}), bf16[64,8,1792]{2,1,0:T(8,128)(2,1)}, u32[]{:S(2)}, u32[]{:S(2)}) async-start(bf16[64,8,1792]{2,1,0:T(8,128)(2,1)} %bitcast.11), calls=%async_computation | async-start | bytes 3670016 | tf_op jit(solution)/shard_map/all_to_all | solution.py:329
  31.3 3.8 %collective-permute-done.13.first.refs_3_ = bf16[1792,256]{1,0:T(8,128)(2,1)} collective-permute-done((bf16[1792,256]{1,0:T(8,128)(2,1)S(1)}, bf16[1792,256]{1,0:T(8,128)(2,1)}, u32[]{:S(2)}, u32[]{:S(2)}) %collective-permute-start.13) | collective-permute-done | bytes 917536 | tf_op jit(solution)/shard_map/ppermute | solution.py:18
  35.1 2.7 %collective-permute-start.16 = (bf16[1792,256]{1,0:T(8,128)(2,1)}, bf16[1792,256]{1,0:T(8,128)(2,1)}, u32[]{:S(2)}, u32[]{:S(2)}) collective-permute-start(bf16[1792,256]{1,0:T(8,128)(2,1)} %get-tuple-element.26), channel_id=1, source_target_pairs={{0,3},{1,0},{2,1},{3,2},{4,7},{5,4},{6,5},{7,6},{8,11},{9,8},{10,9... | collective-permute-start | bytes 2752520 | tf_op jit(solution)/shard_map/ppermute | solution.py:18
  37.7 3.5 %choose.2 = bf16[1792,256]{1,0:T(8,128)(2,1)} custom-call(s32[1]{0:T(128)} %bitcast.16.which, bf16[1792,256]{1,0:T(8,128)(2,1)} %collective-permute-done.13.first.refs_3_, bf16[1792,256]{1,0:T(8,128)(2,1)} %collective-permute-done.12.second.refs_1_), custom_call_target="tpu_custom_call" | custom-call | flops 199999995904 | bytes 2752512 | tf_op jit(solution)/shard_map/choose/pallas_call | solution.py:132
  41.3 0.0 collective-permute-start.14
  41.3 14.1 %collective-permute-done.15.first.refs_3_ = bf16[1792,256]{1,0:T(8,128)(2,1)} collective-permute-done((bf16[1792,256]{1,0:T(8,128)(2,1)}, bf16[1792,256]{1,0:T(8,128)(2,1)}, u32[]{:S(2)}, u32[]{:S(2)}) %collective-permute-start.15) | collective-permute-done | bytes 917536 | tf_op jit(solution)/shard_map/ppermute | solution.py:18
  55.4 3.6 %choose.3 = bf16[1792,256]{1,0:T(8,128)(2,1)} custom-call(s32[1]{0:T(128)} %bitcast.16.which, bf16[1792,256]{1,0:T(8,128)(2,1)} %collective-permute-done.15.first.refs_3_, bf16[1792,256]{1,0:T(8,128)(2,1)} %collective-permute-done.16.second.refs_1_), custom_call_target="tpu_custom_call" | custom-call | bytes 2752512 | tf_op jit(solution)/shard_map/choose/pallas_call | solution.py:132
  59.0 2.4 %collective-permute-start.17 = (bf16[1792,256]{1,0:T(8,128)(2,1)}, bf16[1792,256]{1,0:T(8,128)(2,1)S(1)}, u32[]{:S(2)}, u32[]{:S(2)}) collective-permute-start(bf16[1792,256]{1,0:T(8,128)(2,1)} %choose.3), channel_id=1, source_target_pairs={{0,1},{1,0},{2,3},{3,2},{5,6},{6,5},{7,4},{4,7},{8,9},{9,8},{10,11... | collective-permute-start | bytes 2752520 | tf_op jit(solution)/shard_map/ppermute | solution.py:290
  61.4 7.0 %collective-permute-done.14.refs_2_ = bf16[1792,256]{1,0:T(8,128)(2,1)S(1)} collective-permute-done((bf16[1792,256]{1,0:T(8,128)(2,1)}, bf16[1792,256]{1,0:T(8,128)(2,1)S(1)}, u32[]{:S(2)}, u32[]{:S(2)}) %collective-permute-start.14) | collective-permute-done | bytes 917536 | tf_op jit(solution)/shard_map/ppermute | solution.py:290
  68.4 7.1 %all-to-all-done = bf16[64,8,1792]{2,1,0:T(8,128)(2,1)} async-done(((bf16[64,8,1792]{2,1,0:T(8,128)(2,1)}), bf16[64,8,1792]{2,1,0:T(8,128)(2,1)}, u32[]{:S(2)}, u32[]{:S(2)}) %all-to-all-start) | async-done | bytes 1835040 | tf_op jit(solution)/shard_map/all_to_all | solution.py:329
  75.5 5.7 %up_project.1 = (f32[4,512,256]{2,1,0:T(8,128)}, bf16[4,512,256]{2,1,0:T(8,128)(2,1)}) custom-call(bf16[512,1792]{1,0:T(8,128)(2,1)} %bitcast.12.rows, bf16[1792,256]{1,0:T(8,128)(2,1)} %get-tuple-element.33.refs_0_, bf16[1792,256]{1,0:T(8,128)(2,1)} %collective-permute-done.12.second.refs_1_, bf16[1792,256]{1,0:T(8,128)(2,1)} %copy-done.11, ...), custom_call_target="tpu_custom_call" | custom-call | flops 1879048192 | bytes 9000000 | tf_op jit(solution)/shard_map/up_project/pallas_call | solution.py:158
  81.2 0.5 collective-permute-start.18
  81.7 13.9 %collective-permute-done.18.theirs = bf16[4,512,256]{2,1,0:T(8,128)(2,1)S(1)} collective-permute-done((bf16[4,512,256]{2,1,0:T(8,128)(2,1)}, bf16[4,512,256]{2,1,0:T(8,128)(2,1)S(1)}, u32[]{:S(2)}, u32[]{:S(2)}) %collective-permute-start.18) | collective-permute-done | bytes 1048608 | tf_op jit(solution)/shard_map/ppermute | solution.py:370
  95.6 1.6 copy-done
  97.2 5.3 %down_project.1 = bf16[512,1792]{1,0:T(8,128)(2,1)} custom-call(s32[1]{0:T(128)} %bitcast.10.shift, f32[4,512,256]{2,1,0:T(8,128)S(1)} %copy-done, bf16[4,512,256]{2,1,0:T(8,128)(2,1)S(1)} %collective-permute-done.18.theirs, bf16[1792,256]{1,0:T(8,128)(2,1)S(1)} %get-tuple-element.29.refs_0_, bf16[1792,256]{1,0:T(8,128)(2,1)} %collective-permute-done.16.second.refs_1_, ...), custom_call_target="tpu_custom_call" | custom-call | flops 1879048192 | bytes 9000000 | tf_op jit(solution)/shard_map/down_project/pallas_call | solution.py:201
  102.5 0.0 copy-start.10
  102.5 0.0 copy-start.8
  102.5 0.0 copy-start.1
  102.5 0.0 copy-start.7
  102.5 12.6 %all-to-all-start.1 = ((bf16[64,8,1792]{2,1,0:T(8,128)(2,1)}), bf16[64,8,1792]{2,1,0:T(8,128)(2,1)}, u32[]{:S(2)}, u32[]{:S(2)}) async-start(bf16[64,8,1792]{2,1,0:T(8,128)(2,1)} %bitcast.20), calls=%async_computation.1 | async-start | bytes 3670016 | tf_op jit(solution)/shard_map/all_to_all | solution.py:373
  116.5 0.1 select_reduce_fusion.2
  116.6 0.1 add_minimum_fusion
  116.7 0.1 min.15
  116.9 0.1 pad.10.clone
  117.0 0.1 select_reduce_fusion.1.pages
  117.0 0.1 collective-permute-start.11
  117.1 3.0 %collective-permute-start.10 = (f32[16,8]{0,1:T(8,128)S(1)}, f32[16,8]{0,1:T(8,128)S(1)}, u32[]{:S(2)}, u32[]{:S(2)}) collective-permute-start(f32[16,8]{0,1:T(8,128)S(1)} %copy-done.10), channel_id=1, source_target_pairs={{1,2},{2,1},{3,0},{0,3},{5,6},{6,5},{7,4},{4,7},{9,10},{10,9},{11,... | collective-permute-start | bytes 1544 | tf_op jit(solution)/shard_map/ppermute | solution.py:384
  120.2 0.1 maximum_maximum_fusion
  120.3 0.1 collective-permute-start.6
  120.4 2.5 %collective-permute-start.5 = (bf16[80,576]{1,0:T(8,128)(2,1)S(1)}, bf16[80,576]{1,0:T(8,128)(2,1)S(1)}, u32[]{:S(2)}, u32[]{:S(2)}) collective-permute-start(bf16[80,576]{1,0:T(8,128)(2,1)S(1)} %maximum_maximum_fusion), channel_id=1, source_target_pairs={{0,2},{1,3},{2,0},{3,1},{4,6},{5,7},{6,4},{7,5},{8,10},{9,11},{10,... | collective-permute-start | bytes 276488 | tf_op jit(solution)/shard_map/ppermute | solution.py:18
  123.0 0.1 pad_maximum_fusion.2
  123.1 0.1 copy.54
  123.2 0.4 select_reduce_fusion
  123.6 0.7 collective-permute-done.6
  124.3 1.6 collective-permute-done.5
  125.9 2.1 %collective-permute-done.4 = bf16[80,576]{1,0:T(8,128)(2,1)S(1)} collective-permute-done((bf16[80,576]{1,0:T(8,128)(2,1)S(1)}, bf16[80,576]{1,0:T(8,128)(2,1)S(1)}, u32[]{:S(2)}, u32[]{:S(2)}) %collective-permute-start.4) | collective-permute-done | bytes 92192 | tf_op jit(solution)/shard_map/ppermute | solution.py:18
  128.0 0.1 select_select_fusion
  128.2 1.7 %copy-done.2 = bf16[32,64,576]{2,1,0:T(8,128)(2,1)S(1)} copy-done((bf16[32,64,576]{2,1,0:T(8,128)(2,1)S(1)}, bf16[32,64,576]{2,1,0:T(8,128)(2,1)}, u32[]{:S(2)}) %copy-start.2) | copy-done | bytes 2359320
  129.9 18.5 %attention.1 = (bf16[16,64,512]{2,1,0:T(8,128)(2,1)}, bf16[16,64,512]{2,1,0:T(8,128)(2,1)}, bf16[64,512]{1,0:T(8,128)(2,1)S(1)}) custom-call(s32[16]{0:T(128)S(1)} %bitcast.39, s32[128]{0:T(128)S(1)} %select_reduce_fusion.1.pages, s32[1]{0:T(128)} %bitcast.34.moved, bf16[16,64,576]{2,1,0:T(8,128)(2,1)S(1)} %copy-done.3, bf16[16,64,576]{2,1,0:T(8,128)(2,1)S(1)} %copy-done.1, ...), custom_call_target="tpu_custom_call" | custom-call | flops 12000000000 | bytes 8000000 | tf_op jit(solution)/shard_map/attention/pallas_call | solution.py:89
  148.4 0.9 collective-permute-start.7
  149.3 1.8 %collective-permute-start.9 = (bf16[64,512]{1,0:T(8,128)(2,1)S(1)}, bf16[64,512]{1,0:T(8,128)(2,1)S(1)}, u32[]{:S(2)}, u32[]{:S(2)}) collective-permute-start(bf16[64,512]{1,0:T(8,128)(2,1)S(1)} %get-tuple-element.46), channel_id=1, source_target_pairs={{0,3},{1,0},{2,1},{3,2},{4,7},{5,4},{6,5},{7,6},{8,11},{9,8},{10,9... | collective-permute-start | bytes 196616 | tf_op jit(solution)/shard_map/ppermute | solution.py:18
  151.2 0.0 collective-permute-start.8
  151.2 8.2 %all-to-all-done.1 = bf16[64,8,1792]{2,1,0:T(8,128)(2,1)} async-done(((bf16[64,8,1792]{2,1,0:T(8,128)(2,1)}), bf16[64,8,1792]{2,1,0:T(8,128)(2,1)}, u32[]{:S(2)}, u32[]{:S(2)}) %all-to-all-start.1) | async-done | bytes 1835040 | tf_op jit(solution)/shard_map/all_to_all | solution.py:373
  159.4 1.9 %fusion = f32[128,1792]{1,0:T(8,128)S(1)} fusion(bf16[64,8,1792]{2,1,0:T(8,128)(2,1)} %all-to-all-done.1, bf16[64,512]{1,0:T(8,128)(2,1)S(1)} %get-tuple-element.40, bf16[64,512]{1,0:T(8,128)(2,1)S(1)} %get-tuple-element.39), kind=kOutput, calls=%fused_computation.1 | convolution fusion | flops 235143168 | bytes 2883584 | tf_op jit(solution)/shard_map/dot_general | solution.py:393
  161.4 3.0 %collective-permute-start.19 = (f32[16,1792]{1,0:T(8,128)S(1)}, f32[16,1792]{1,0:T(8,128)S(1)}, u32[]{:S(2)}, u32[]{:S(2)}) collective-permute-start(f32[16,1792]{1,0:T(8,128)S(1)} %get-tuple-element.37), channel_id=1, source_target_pairs={{1,2},{2,1},{3,0},{0,3},{5,6},{6,5},{7,4},{4,7},{9,10},{10,9},{11,... | collective-permute-start | bytes 344072 | tf_op jit(solution)/shard_map/ppermute | solution.py:398
  164.4 0.7 bitcast_dynamic-update-slice_fusion
  165.1 1.5 collective-permute-done.19
  166.6 1.8 %collective-permute-done.20 = f32[16,1792]{1,0:T(8,128)S(1)} collective-permute-done((f32[16,1792]{1,0:T(8,128)S(1)}, f32[16,1792]{1,0:T(8,128)S(1)}, u32[]{:S(2)}, u32[]{:S(2)}) %collective-permute-start.20) | collective-permute-done | bytes 114720 | tf_op jit(solution)/shard_map/ppermute | solution.py:398
  168.4 0.7 pad_maximum_fusion.1
  (54 shorter events, 0.4 us)
Async XLA Ops:
  1.4 12.6 %collective-permute-start = (s32[16,8]{1,0:T(8,128)S(1)}, s32[16,8]{1,0:T(8,128)S(1)}, u32[]{:S(2)}, u32[]{:S(2)}) collective-permute-start(s32[16,8]{1,0:T(8,128)S(1)} %copy.46), channel_id=1, source_target_pairs={{1,2},{2,1},{3,0},{0,3},{5,6},{6,5},{7,4},{4,7},{9,10},{10,9},{11,... | collective-permute-start | bytes 1544 | tf_op jit(solution)/shard_map/ppermute | solution.py:277
  5.0 9.0 %collective-permute-start.1 = (s32[16,8]{1,0:T(8,128)S(1)}, s32[16,8]{1,0:T(8,128)S(1)}, u32[]{:S(2)}, u32[]{:S(2)}) collective-permute-start(s32[16,8]{1,0:T(8,128)S(1)} %copy.46), channel_id=1, source_target_pairs={{2,3},{3,2},{0,1},{1,0},{6,7},{7,6},{4,5},{5,4},{10,11},{11,10},{8... | collective-permute-start | bytes 1544 | tf_op jit(solution)/shard_map/ppermute | solution.py:277
  5.9 9.7 %collective-permute-start.2 = (bf16[16,1792]{1,0:T(8,128)(2,1)S(1)}, bf16[16,1792]{1,0:T(8,128)(2,1)S(1)}, u32[]{:S(2)}, u32[]{:S(2)}) collective-permute-start(bf16[16,1792]{1,0:T(8,128)(2,1)S(1)} %get-tuple-element.42), channel_id=1, source_target_pairs={{1,2},{2,1},{3,0},{0,3},{5,6},{6,5},{7,4},{4,7},{9,10},{10,9},{11,... | collective-permute-start | bytes 172040 | tf_op jit(solution)/shard_map/ppermute | solution.py:279
  6.6 9.0 %collective-permute-start.3 = (bf16[16,1792]{1,0:T(8,128)(2,1)S(1)}, bf16[16,1792]{1,0:T(8,128)(2,1)S(1)}, u32[]{:S(2)}, u32[]{:S(2)}) collective-permute-start(bf16[16,1792]{1,0:T(8,128)(2,1)S(1)} %get-tuple-element.43), channel_id=1, source_target_pairs={{2,3},{3,2},{0,1},{1,0},{6,7},{7,6},{4,5},{5,4},{10,11},{11,10},{8... | collective-permute-start | bytes 172040 | tf_op jit(solution)/shard_map/ppermute | solution.py:279
  7.5 4.9 %copy-start.5 = (bf16[1,3584,256]{2,1,0:T(8,128)(2,1)S(1)}, bf16[1,3584,256]{2,1,0:T(8,128)(2,1)}, u32[]{:S(2)}) copy-start(bf16[1,3584,256]{2,1,0:T(8,128)(2,1)} %param.18) | copy-start | bytes 5505028
  10.5 20.8 %collective-permute-start.12 = (bf16[1792,256]{1,0:T(8,128)(2,1)S(1)}, bf16[1792,256]{1,0:T(8,128)(2,1)}, u32[]{:S(2)}, u32[]{:S(2)}) collective-permute-start(bf16[1792,256]{1,0:T(8,128)(2,1)S(1)} %get-tuple-element.22), channel_id=1, source_target_pairs={{0,3},{1,0},{2,1},{3,2},{4,7},{5,4},{6,5},{7,6},{8,11},{9,8},{10,9... | collective-permute-start | bytes 2752520 | tf_op jit(solution)/shard_map/ppermute | solution.py:18
  14.0 21.1 %collective-permute-start.13 = (bf16[1792,256]{1,0:T(8,128)(2,1)S(1)}, bf16[1792,256]{1,0:T(8,128)(2,1)}, u32[]{:S(2)}, u32[]{:S(2)}) collective-permute-start(bf16[1792,256]{1,0:T(8,128)(2,1)S(1)} %get-tuple-element.23), channel_id=1, source_target_pairs={{0,1},{1,2},{2,3},{3,0},{4,5},{5,6},{6,7},{7,4},{8,9},{9,10},{10,1... | collective-permute-start | bytes 2752520 | tf_op jit(solution)/shard_map/ppermute | solution.py:18
  14.6 0.6 copy-start.6
  17.5 57.9 %all-to-all-start = ((bf16[64,8,1792]{2,1,0:T(8,128)(2,1)}), bf16[64,8,1792]{2,1,0:T(8,128)(2,1)}, u32[]{:S(2)}, u32[]{:S(2)}) async-start(bf16[64,8,1792]{2,1,0:T(8,128)(2,1)} %bitcast.11), calls=%async_computation | async-start | bytes 3670016 | tf_op jit(solution)/shard_map/all_to_all | solution.py:329
  35.1 20.4 %collective-permute-start.15 = (bf16[1792,256]{1,0:T(8,128)(2,1)}, bf16[1792,256]{1,0:T(8,128)(2,1)}, u32[]{:S(2)}, u32[]{:S(2)}) collective-permute-start(bf16[1792,256]{1,0:T(8,128)(2,1)} %get-tuple-element.25), channel_id=1, source_target_pairs={{0,1},{1,2},{2,3},{3,0},{4,5},{5,6},{6,7},{7,4},{8,9},{9,10},{10,1... | collective-permute-start | bytes 2752520 | tf_op jit(solution)/shard_map/ppermute | solution.py:18
  35.1 20.4 %collective-permute-start.16 = (bf16[1792,256]{1,0:T(8,128)(2,1)}, bf16[1792,256]{1,0:T(8,128)(2,1)}, u32[]{:S(2)}, u32[]{:S(2)}) collective-permute-start(bf16[1792,256]{1,0:T(8,128)(2,1)} %get-tuple-element.26), channel_id=1, source_target_pairs={{0,3},{1,0},{2,1},{3,2},{4,7},{5,4},{6,5},{7,6},{8,11},{9,8},{10,9... | collective-permute-start | bytes 2752520 | tf_op jit(solution)/shard_map/ppermute | solution.py:18
  41.3 27.1 %collective-permute-start.14 = (bf16[1792,256]{1,0:T(8,128)(2,1)}, bf16[1792,256]{1,0:T(8,128)(2,1)S(1)}, u32[]{:S(2)}, u32[]{:S(2)}) collective-permute-start(bf16[1792,256]{1,0:T(8,128)(2,1)} %choose.2), channel_id=1, source_target_pairs={{0,1},{1,0},{2,3},{3,2},{5,6},{6,5},{7,4},{4,7},{8,9},{9,8},{10,11... | collective-permute-start | bytes 2752520 | tf_op jit(solution)/shard_map/ppermute | solution.py:290
  59.0 22.2 %collective-permute-start.17 = (bf16[1792,256]{1,0:T(8,128)(2,1)}, bf16[1792,256]{1,0:T(8,128)(2,1)S(1)}, u32[]{:S(2)}, u32[]{:S(2)}) collective-permute-start(bf16[1792,256]{1,0:T(8,128)(2,1)} %choose.3), channel_id=1, source_target_pairs={{0,1},{1,0},{2,3},{3,2},{5,6},{6,5},{7,4},{4,7},{8,9},{9,8},{10,11... | collective-permute-start | bytes 2752520 | tf_op jit(solution)/shard_map/ppermute | solution.py:290
  68.4 7.1 %copy-start.11 = (bf16[1792,256]{1,0:T(8,128)(2,1)}, bf16[1792,256]{1,0:T(8,128)(2,1)S(1)}, u32[]{:S(2)}) copy-start(bf16[1792,256]{1,0:T(8,128)(2,1)S(1)} %collective-permute-done.14.refs_2_) | copy-start | bytes 2752516
  81.2 14.4 %collective-permute-start.18 = (bf16[4,512,256]{2,1,0:T(8,128)(2,1)}, bf16[4,512,256]{2,1,0:T(8,128)(2,1)S(1)}, u32[]{:S(2)}, u32[]{:S(2)}) collective-permute-start(bf16[4,512,256]{2,1,0:T(8,128)(2,1)} %get-tuple-element.28), channel_id=1, source_target_pairs={{1,2},{2,1},{3,0},{0,3},{6,7},{7,6},{4,5},{5,4},{9,10},{10,9},{11,... | collective-permute-start | bytes 3145736 | tf_op jit(solution)/shard_map/ppermute | solution.py:370
  95.6 1.6 copy-start
  102.5 14.0 %copy-start.4 = (s32[1,16]{1,0:T(1,128)S(1)}, s32[1,16]{1,0:T(1,128)}, u32[]{:S(2)}) copy-start(s32[1,16]{1,0:T(1,128)} %param.24) | copy-start | bytes 196
  102.5 14.4 %copy-start.9 = (bf16[16,576]{1,0:T(8,128)(2,1)S(1)}, bf16[16,576]{1,0:T(8,128)(2,1)}, u32[]{:S(2)}) copy-start(bf16[16,576]{1,0:T(8,128)(2,1)} %param.20) | copy-start | bytes 55300
  102.5 14.5 %copy-start.12 = (s32[1,32]{1,0:T(1,128)S(1)}, s32[1,32]{1,0:T(1,128)}, u32[]{:S(2)}) copy-start(s32[1,32]{1,0:T(1,128)} %param.25) | copy-start | bytes 388
  102.5 14.6 %copy-start.10 = (f32[16,8]{0,1:T(8,128)S(1)}, f32[16,8]{0,1:T(8,128)}, u32[]{:S(2)}) copy-start(f32[16,8]{0,1:T(8,128)} %param.16) | copy-start | bytes 1540
  102.5 17.7 %copy-start.8 = (bf16[16,576]{1,0:T(8,128)(2,1)S(1)}, bf16[16,576]{1,0:T(8,128)(2,1)}, u32[]{:S(2)}) copy-start(bf16[16,576]{1,0:T(8,128)(2,1)} %param.22) | copy-start | bytes 55300
  102.5 17.7 %copy-start.1 = (bf16[16,64,576]{2,1,0:T(8,128)(2,1)S(1)}, bf16[16,64,576]{2,1,0:T(8,128)(2,1)}, u32[]{:S(2)}) copy-start(bf16[16,64,576]{2,1,0:T(8,128)(2,1)} %q_two) | copy-start | bytes 3538948
  102.5 20.7 %copy-start.7 = (s32[64,8]{1,0:T(8,128)S(1)}, s32[64,8]{1,0:T(8,128)}, u32[]{:S(2)}) copy-start(s32[64,8]{1,0:T(8,128)} %copy-done.6) | copy-start | bytes 6148
  102.5 25.6 %copy-start.3 = (bf16[16,64,576]{2,1,0:T(8,128)(2,1)S(1)}, bf16[16,64,576]{2,1,0:T(8,128)(2,1)}, u32[]{:S(2)}) copy-start(bf16[16,64,576]{2,1,0:T(8,128)(2,1)} %q_one.1) | copy-start | bytes 3538948
  102.5 56.9 %all-to-all-start.1 = ((bf16[64,8,1792]{2,1,0:T(8,128)(2,1)}), bf16[64,8,1792]{2,1,0:T(8,128)(2,1)}, u32[]{:S(2)}, u32[]{:S(2)}) async-start(bf16[64,8,1792]{2,1,0:T(8,128)(2,1)} %bitcast.20), calls=%async_computation.1 | async-start | bytes 3670016 | tf_op jit(solution)/shard_map/all_to_all | solution.py:373
  117.0 5.9 %collective-permute-start.11 = (f32[16,8]{0,1:T(8,128)S(1)}, f32[16,8]{0,1:T(8,128)S(1)}, u32[]{:S(2)}, u32[]{:S(2)}) collective-permute-start(f32[16,8]{0,1:T(8,128)S(1)} %copy-done.10), channel_id=1, source_target_pairs={{2,3},{3,2},{0,1},{1,0},{6,7},{7,6},{4,5},{5,4},{10,11},{11,10},{8... | collective-permute-start | bytes 1544 | tf_op jit(solution)/shard_map/ppermute | solution.py:386
  117.1 5.8 %collective-permute-start.10 = (f32[16,8]{0,1:T(8,128)S(1)}, f32[16,8]{0,1:T(8,128)S(1)}, u32[]{:S(2)}, u32[]{:S(2)}) collective-permute-start(f32[16,8]{0,1:T(8,128)S(1)} %copy-done.10), channel_id=1, source_target_pairs={{1,2},{2,1},{3,0},{0,3},{5,6},{6,5},{7,4},{4,7},{9,10},{10,9},{11,... | collective-permute-start | bytes 1544 | tf_op jit(solution)/shard_map/ppermute | solution.py:384
  120.3 4.0 %collective-permute-start.6 = (bf16[80,576]{1,0:T(8,128)(2,1)S(1)}, bf16[80,576]{1,0:T(8,128)(2,1)S(1)}, u32[]{:S(2)}, u32[]{:S(2)}) collective-permute-start(bf16[80,576]{1,0:T(8,128)(2,1)S(1)} %maximum_maximum_fusion), channel_id=1, source_target_pairs={{0,3},{1,0},{2,1},{3,2},{4,7},{5,4},{6,5},{7,6},{8,11},{9,8},{10,9... | collective-permute-start | bytes 276488 | tf_op jit(solution)/shard_map/ppermute | solution.py:18
  120.4 5.5 %collective-permute-start.5 = (bf16[80,576]{1,0:T(8,128)(2,1)S(1)}, bf16[80,576]{1,0:T(8,128)(2,1)S(1)}, u32[]{:S(2)}, u32[]{:S(2)}) collective-permute-start(bf16[80,576]{1,0:T(8,128)(2,1)S(1)} %maximum_maximum_fusion), channel_id=1, source_target_pairs={{0,2},{1,3},{2,0},{3,1},{4,6},{5,7},{6,4},{7,5},{8,10},{9,11},{10,... | collective-permute-start | bytes 276488 | tf_op jit(solution)/shard_map/ppermute | solution.py:18
  122.9 5.0 %collective-permute-start.4 = (bf16[80,576]{1,0:T(8,128)(2,1)S(1)}, bf16[80,576]{1,0:T(8,128)(2,1)S(1)}, u32[]{:S(2)}, u32[]{:S(2)}) collective-permute-start(bf16[80,576]{1,0:T(8,128)(2,1)S(1)} %maximum_maximum_fusion), channel_id=1, source_target_pairs={{0,1},{1,2},{2,3},{3,0},{4,5},{5,6},{6,7},{7,4},{8,9},{9,10},{10,1... | collective-permute-start | bytes 276488 | tf_op jit(solution)/shard_map/ppermute | solution.py:18
  128.1 1.7 %copy-start.2 = (bf16[32,64,576]{2,1,0:T(8,128)(2,1)S(1)}, bf16[32,64,576]{2,1,0:T(8,128)(2,1)}, u32[]{:S(2)}) copy-start(bf16[32,64,576]{2,1,0:T(8,128)(2,1)} %pool.1) | copy-start | bytes 7077892
  148.4 16.0 %collective-permute-start.7 = (bf16[64,512]{1,0:T(8,128)(2,1)S(1)}, bf16[64,512]{1,0:T(8,128)(2,1)S(1)}, u32[]{:S(2)}, u32[]{:S(2)}) collective-permute-start(bf16[64,512]{1,0:T(8,128)(2,1)S(1)} %get-tuple-element.45), channel_id=1, source_target_pairs={{0,1},{1,2},{2,3},{3,0},{4,5},{5,6},{6,7},{7,4},{8,9},{9,10},{10,1... | collective-permute-start | bytes 196616 | tf_op jit(solution)/shard_map/ppermute | solution.py:18
  149.3 15.1 %collective-permute-start.9 = (bf16[64,512]{1,0:T(8,128)(2,1)S(1)}, bf16[64,512]{1,0:T(8,128)(2,1)S(1)}, u32[]{:S(2)}, u32[]{:S(2)}) collective-permute-start(bf16[64,512]{1,0:T(8,128)(2,1)S(1)} %get-tuple-element.46), channel_id=1, source_target_pairs={{0,3},{1,0},{2,1},{3,2},{4,7},{5,4},{6,5},{7,6},{8,11},{9,8},{10,9... | collective-permute-start | bytes 196616 | tf_op jit(solution)/shard_map/ppermute | solution.py:18
  151.2 13.3 %collective-permute-start.8 = (bf16[64,512]{1,0:T(8,128)(2,1)S(1)}, bf16[64,512]{1,0:T(8,128)(2,1)S(1)}, u32[]{:S(2)}, u32[]{:S(2)}) collective-permute-start(bf16[64,512]{1,0:T(8,128)(2,1)S(1)} %get-tuple-element.47), channel_id=1, source_target_pairs={{0,2},{1,3},{2,0},{3,1},{4,6},{5,7},{6,4},{7,5},{8,10},{9,11},{10,... | collective-permute-start | bytes 196616 | tf_op jit(solution)/shard_map/ppermute | solution.py:18
  161.4 5.2 %collective-permute-start.19 = (f32[16,1792]{1,0:T(8,128)S(1)}, f32[16,1792]{1,0:T(8,128)S(1)}, u32[]{:S(2)}, u32[]{:S(2)}) collective-permute-start(f32[16,1792]{1,0:T(8,128)S(1)} %get-tuple-element.37), channel_id=1, source_target_pairs={{1,2},{2,1},{3,0},{0,3},{5,6},{6,5},{7,4},{4,7},{9,10},{10,9},{11,... | collective-permute-start | bytes 344072 | tf_op jit(solution)/shard_map/ppermute | solution.py:398
  164.4 3.9 %collective-permute-start.20 = (f32[16,1792]{1,0:T(8,128)S(1)}, f32[16,1792]{1,0:T(8,128)S(1)}, u32[]{:S(2)}, u32[]{:S(2)}) collective-permute-start(f32[16,1792]{1,0:T(8,128)S(1)} %get-tuple-element.38), channel_id=1, source_target_pairs={{2,3},{3,2},{0,1},{1,0},{6,7},{7,6},{4,5},{5,4},{10,11},{11,10},{8... | collective-permute-start | bytes 344072 | tf_op jit(solution)/shard_map/ppermute | solution.py:398

commit v9 on v8

--- a/solution.py
+++ b/solution.py
@@ -257,27 +257,32 @@
 
     half = width // 2
     core = lax.axis_index("ep") % 2
-    turned = [(me - c) % grp_size for c in range(2)]
-    side = [turned[c] // 2 for c in range(2)]
-    here = jnp.where(core == 0, turned[0], turned[1])
-    partner = [[((a + c) % grp_size, (b + c) % grp_size) for a, b in PAIRS] for c in range(2)]
-
-    def by_core(pairs):
+    cores = (core, 1 - core)
+    turned = [(me - c) % grp_size for c in cores]
+    side = [t // 2 for t in turned]
+    here = turned[0]
+
+    def by_core(pairs, flip=0):
         return [
-            (e * grp_size + (a + e % 2) % grp_size, e * grp_size + (b + e % 2) % grp_size)
+            (e * grp_size + (a + (e + flip) % 2) % grp_size, e * grp_size + (b + (e + flip) % 2) % grp_size)
             for e in range(ep_size)
             for a, b in pairs
         ]
 
+    def swap_planes(value, k):
+        return lax.ppermute(value, ("ep", "grp"), by_core(PAIRS, k))
+
+    def swap_cores(value):
+        return lax.ppermute(value, "ep", [(e, e + 1 - 2 * (e % 2)) for e in range(ep_size)])
+
     def part(value, which, axis):
         return lax.dynamic_slice_in_dim(value, which * half, half, axis)
 
     rows, id_list = [], [expert_ids]
-    for c in range(2):
-        id_list.append(lax.ppermute(expert_ids, "grp", partner[c]))
-        rows.append(part(hidden, side[c], 1))
-        rows.append(lax.ppermute(part(hidden, 1 - side[c], 1), "grp", partner[c]))
-    rows = jnp.concatenate(rows, axis=0)
+    for k in range(2):
+        id_list.append(swap_planes(expert_ids, k))
+        theirs = swap_planes(part(hidden, 1 - side[k], 1), k)
+        rows.append(jnp.concatenate([part(hidden, side[k], 1), theirs], axis=0))
 
     ahead = jnp.where((here == 0) | (here == 3), 0, 1)
 
@@ -287,18 +292,18 @@
 
     def pass_on(prev, nxt, flops):
         picked = choose((here % 2)[None], prev, nxt, flops)
-        far = lax.ppermute(picked, ("ep", "grp"), by_core([(0, 1), (1, 0), (2, 3), (3, 2)]))
-        return far
-
-    up_own, up_prev, up_next = spread(w_up[0], rows)
+        return lax.ppermute(picked, ("ep", "grp"), by_core([(0, 1), (1, 0), (2, 3), (3, 2)]))
+
+    up_own, up_prev, up_next = spread(w_up[0], *rows)
     up_far = pass_on(up_prev, up_next, 200_000_000_000)
     down_own, down_prev, down_next = spread(w_down[0], up_prev, up_next)
-    down_far = pass_on(down_prev, down_next, 0)
+    down_far = pass_on(down_prev, down_next, 200_000_000_000)
     up_all = [up_own, up_next, up_far, up_prev]
     down_all = [down_own, down_next, down_far, down_prev]
 
     rank = 2 * capacity
-    lanes_all = ep_size * rank
+    peers = ep_size // 2
+    lanes = peers * rank
     flat_ids = jnp.concatenate(id_list, axis=0).reshape(-1)
     entries = flat_ids.shape[0]
     hits = flat_ids[:, None] == jnp.arange(ep_size, dtype=jnp.int32)[None, :]
@@ -309,26 +314,36 @@
         lower.astype(jnp.bfloat16), hits.astype(jnp.bfloat16), preferred_element_type=jnp.float32
     )
     earlier = jnp.sum(jnp.where(hits, ahead, 0.0), axis=1).astype(jnp.int32)
-    place = (flat_ids * rank + earlier).reshape(3, samples, picks)
-    own_at, first_at, second_at = place[0], place[1], place[2]
-    even = (expert_ids % 2) == 0
-    place = jnp.concatenate(
-        [
-            jnp.where(even, own_at + side[0] * capacity, -1),
-            jnp.where((id_list[1] % 2) == 0, first_at + (1 - side[0]) * capacity, -1),
-            jnp.where(even, -1, own_at + side[1] * capacity),
-            jnp.where((id_list[2] % 2) == 0, -1, second_at + (1 - side[1]) * capacity),
-        ],
-        axis=0,
-    )
-    match = place[:, :, None] == jnp.arange(lanes_all, dtype=jnp.int32)[None, None, :]
-    placing = jnp.sum(match.astype(jnp.float32), axis=1).astype(jnp.bfloat16)
-    outgoing = lax.dot_general(
-        placing, rows, (((0,), (0,)), ((), ())), preferred_element_type=jnp.float32
-    ).astype(jnp.bfloat16)
-    arrived = lax.all_to_all(
-        outgoing.reshape(ep_size, rank, half), "ep", split_axis=0, concat_axis=0, tiled=True
-    ).reshape(lanes_all, half)
+    place = ((flat_ids // 2) * rank + earlier).reshape(3, samples, picks)
+    groups = [[2 * j + c for j in range(peers)] for c in range(2)]
+
+    def exchange(value):
+        return lax.all_to_all(
+            value.reshape(peers, rank, half),
+            "ep",
+            split_axis=0,
+            concat_axis=0,
+            axis_index_groups=groups,
+            tiled=True,
+        ).reshape(lanes, half)
+
+    match, arrived = [], []
+    for k in range(2):
+        at = jnp.concatenate(
+            [
+                jnp.where(expert_ids % 2 == cores[k], place[0] + side[k] * capacity, -1),
+                jnp.where(
+                    id_list[k + 1] % 2 == cores[k], place[k + 1] + (1 - side[k]) * capacity, -1
+                ),
+            ],
+            axis=0,
+        )
+        match.append(at[:, :, None] == jnp.arange(lanes, dtype=jnp.int32)[None, None, :])
+        placing = jnp.sum(match[k].astype(jnp.float32), axis=1).astype(jnp.bfloat16)
+        outgoing = lax.dot_general(
+            placing, rows[k], (((0,), (0,)), ((), ())), preferred_element_type=jnp.float32
+        ).astype(jnp.bfloat16)
+        arrived.append(exchange(outgoing if k == 0 else swap_cores(outgoing)))
 
     moved_slot = mig_slot[0, 0]
     moved_target = mig_dest[0, 0]
@@ -365,39 +380,22 @@
         arrived_out = arrived_out + hop(jnp.where(offset == r, out_moved, zero), "grp", r)
     attn_second = lax.dynamic_update_index_in_dim(attn_second, arrived_out, moved_slot, 0)
 
-    mine, rounded = up_project(arrived, up_all, 2)
-    (rounded,) = after(down_far, rounded)
-    theirs = lax.ppermute(rounded, ("ep", "grp"), by_core(PAIRS))
     shift = jnp.where(here % 2 == 1, grp_size - 1, 1).astype(jnp.int32)
-    produced = down_project(shift[None], mine, theirs, down_all, 2)
-    returned = lax.all_to_all(
-        produced.reshape(ep_size, rank, half),
-        "ep",
-        split_axis=0,
-        concat_axis=0,
-        tiled=True,
-    ).reshape(lanes_all, half)
     (late_gates,) = after(outgoing, gate_weights)
-    gates = jnp.concatenate(
-        [
-            gate_weights,
-            lax.ppermute(late_gates, "grp", partner[0]),
-            gate_weights,
-            lax.ppermute(late_gates, "grp", partner[1]),
-        ],
-        axis=0,
-    )
-    mixing = jnp.sum(jnp.where(match, gates[:, :, None], 0.0), axis=1)
-    high = lax.reduce_precision(mixing, 8, 7)
-    mixing = jnp.concatenate([high, mixing - high], axis=0).astype(jnp.bfloat16)
-    mixed = jnp.dot(mixing, returned, preferred_element_type=jnp.float32)
-    summed = (mixed[: 4 * samples] + mixed[4 * samples :]).reshape(4, samples, half)
     first, second = 0.0, 0.0
-    for c in range(2):
-        own = summed[2 * c]
-        other = lax.ppermute(summed[2 * c + 1], "grp", partner[c])
-        first = first + jnp.where(side[c] == 0, own, other)
-        second = second + jnp.where(side[c] == 0, other, own)
+    for k in range(2):
+        mine, rounded = up_project(arrived[k], up_all, 1)
+        produced = down_project(shift[None], mine, swap_planes(rounded, 0), down_all, 2)
+        returned = exchange(produced if k == 0 else swap_cores(produced))
+        gates = jnp.concatenate([gate_weights, swap_planes(late_gates, k)], axis=0)
+        mixing = jnp.sum(jnp.where(match[k], gates[:, :, None], 0.0), axis=1)
+        high = lax.reduce_precision(mixing, 8, 7)
+        mixing = jnp.concatenate([high, mixing - high], axis=0).astype(jnp.bfloat16)
+        mixed = jnp.dot(mixing, returned, preferred_element_type=jnp.float32)
+        summed = (mixed[: 2 * samples] + mixed[2 * samples :]).reshape(2, samples, half)
+        own, other = summed[0], swap_planes(summed[1], k)
+        first = first + jnp.where(side[k] == 0, own, other)
+        second = second + jnp.where(side[k] == 0, other, own)
     moe_out = jnp.concatenate([first, second], axis=1).astype(jnp.bfloat16)
     return (attn_first, attn_second, moe_out)
 

time: 171 us -> 195 us (1.14)
  starting transfers between devices: 50.7 us -> 73.7 us
  waiting for transfers between devices: 61.7 us -> 53.1 us
  Pallas kernels: 36.6 us -> 42.1 us
  local copies, waits for them, and re-layouts: 10.7 us -> 14.3 us
    ppermute x9 -> x12, waiting for transfers between devices: 17.1 us -> 34.7 us  [the longest x10 34.7 us: swap_planes(): return lax.ppermute(value, ('ep', 'grp'), by_core(PAIRS, k))]
    ppermute x10, waiting for transfers between devices: 22.3 us -> 6.96 us  [hop(): lax.ppermute(value, axis, [(i, (i + step) % size) for i in range(size)])]
    all_to_all x2 -> x4, starting transfers between devices: 26.4 us -> 36.7 us  [exchange(): lax.all_to_all(value.reshape(peers, rank, half), 'ep', split_axis=0, conc...]
    ppermute x2, waiting for transfers between devices: 6.97 us -> 0.23 us  [pass_on(): lax.ppermute(picked, ('ep', 'grp'), by_core([(0, 1), (1, 0), (2, 3), (3,...]
    ppermute x2, starting transfers between devices: 2.42 us -> 8.51 us  [pass_on(): lax.ppermute(picked, ('ep', 'grp'), by_core([(0, 1), (1, 0), (2, 3), (3,...]
    ppermute x9 -> x12, starting transfers between devices: 11.9 us -> 16.4 us  [the longest x10 12.5 us: swap_planes(): return lax.ppermute(value, ('ep', 'grp'), by_core(PAIRS, k))]
    all_to_all x2 -> x4, waiting for transfers between devices: 15.3 us -> 11.2 us  [exchange(): lax.all_to_all(value.reshape(peers, rank, half), 'ep', split_axis=0, conc...]
    pallas_call x1 -> x2, Pallas kernels: 5.71 us -> 9.19 us  [up_project(): pl.pallas_call(up_kernel, grid=(steps,), in_specs=[pl.BlockSpec((count //...]
  transfers between devices with their start and end apart: 23 -> 28, of which waited for: 11 -> 9; matrix products, arithmetic and copies ran while one was open for 7% -> 8% of each run, Pallas kernels for 19% -> 22%
where the time goes in v9:
time: 195 us; the launch traced here: 194 us
  starting transfers between devices  73.7 us (38%)
  waiting for transfers between devices  53.1 us (27%)
  Pallas kernels  42.1 us (22%)
  local copies, waits for them, and re-layouts  14.3 us (7%)
  matrix products  4.76 us (2%)
  other arithmetic  3.86 us (2%)
  between operations  2.41 us (1%)
    all_to_all x4, starting transfers between devices, exchange(): lax.all_to_all(value.reshape(peers, rank, half), 'ep', split_axis=0, conc...  36.7 us
    ppermute x10, waiting for transfers between devices, swap_planes(): return lax.ppermute(value, ('ep', 'grp'), by_core(PAIRS, k))  34.7 us
    pallas_call x1, Pallas kernels, attention(): pl.pallas_call(attention_kernel, grid_spec=pltpu.PrefetchScalarGridSpec(n...  19 us
    ppermute x10, starting transfers between devices, swap_planes(): return lax.ppermute(value, ('ep', 'grp'), by_core(PAIRS, k))  12.5 us
    ppermute x10, starting transfers between devices, hop(): lax.ppermute(value, axis, [(i, (i + step) % size) for i in range(size)])  12.1 us
    all_to_all x4, waiting for transfers between devices, exchange(): lax.all_to_all(value.reshape(peers, rank, half), 'ep', split_axis=0, conc...  11.2 us
    pallas_call x2, Pallas kernels, up_project(): pl.pallas_call(up_kernel, grid=(steps,), in_specs=[pl.BlockSpec((count //...  9.19 us
    ppermute x2, starting transfers between devices, pass_on(): lax.ppermute(picked, ('ep', 'grp'), by_core([(0, 1), (1, 0), (2, 3), (3,...  8.51 us
  transfers between devices with their start and end apart: 28, of which 9 were waited for; matrix products, arithmetic and copies ran while one was open for 8% of the time, Pallas kernels for 22%

profile of v9, /device:TPU:1, one launch (start us, length us, event | category | flops | bytes accessed | tf_op | source)
XLA Modules:
  0.0 194.2 jit_solution(13789447509031044420)
XLA Ops:
  0.6 0.8 copy.53
  1.4 2.1 %collective-permute-start = (s32[16,8]{1,0:T(8,128)S(1)}, s32[16,8]{1,0:T(8,128)S(1)}, u32[]{:S(2)}, u32[]{:S(2)}) collective-permute-start(s32[16,8]{1,0:T(8,128)S(1)} %copy.53), channel_id=1, source_target_pairs={{1,2},{2,1},{3,0},{0,3},{6,7},{7,6},{4,5},{5,4},{9,10},{10,9},{11,... | collective-permute-start | bytes 1544 | tf_op jit(solution)/shard_map/ppermute | solution.py:273
  3.5 1.9 collective-permute-start.1
  5.4 0.9 constant_dynamic-slice_fusion.1
  6.3 0.9 collective-permute-start.2
  7.2 3.4 %dynamic-slice_bitcast_fusion.3 = (bf16[1792,256]{1,0:T(8,128)(2,1)}, bf16[1792,256]{1,0:T(8,128)(2,1)}, bf16[1792,256]{1,0:T(8,128)(2,1)}) fusion(bf16[1,3584,256]{2,1,0:T(8,128)(2,1)} %param.17, s32[]{:T(128)S(6)} %select_n.265, s32[]{:T(128)S(6)} %select_n.261, s32[]{:T(128)S(6)} %select_n.264), kind=kLoop, calls=%fused_computation.12 | loop fusion | bytes 5505036 | tf_op jit(solution)/shard_map/dynamic_slice | solution.py:279
  10.7 1.9 collective-permute-start.11
  12.6 1.5 dynamic-slice_bitcast_fusion
  14.2 0.1 eq.137
  14.3 0.3 fusion.1
  14.6 0.1 convert_element_type.33
  14.8 0.6 copy-done.9
  15.4 0.2 convert_reduce_fusion.1
  15.5 1.4 convolution_convert_fusion.1
  16.9 2.7 %collective-permute-start.19 = (f32[16,8]{0,1:T(8,128)S(1)}, f32[16,8]{0,1:T(8,128)S(1)}, u32[]{:S(2)}, u32[]{:S(2)}) collective-permute-start(f32[16,8]{0,1:T(8,128)S(1)} %copy-done.15), channel_id=1, source_target_pairs={{2,3},{3,2},{0,1},{1,0},{5,6},{6,5},{7,4},{4,7},{10,11},{11,10},{8... | collective-permute-start | bytes 1544 | tf_op jit(solution)/shard_map/ppermute | solution.py:273
  19.6 14.9 %collective-permute-done.19 = f32[16,8]{0,1:T(8,128)S(1)} collective-permute-done((f32[16,8]{0,1:T(8,128)S(1)}, f32[16,8]{0,1:T(8,128)S(1)}, u32[]{:S(2)}, u32[]{:S(2)}) %collective-permute-start.19) | collective-permute-done | bytes 544 | tf_op jit(solution)/shard_map/ppermute | solution.py:273
  34.4 0.7 collective-permute-start.20
  35.1 0.7 pad_maximum_fusion.3
  35.8 0.8 select_reduce_fusion.1
  36.7 1.3 fusion
  38.0 11.1 %all-to-all-start = ((bf16[32,8,1792]{2,1,0:T(8,128)(2,1)}), bf16[32,8,1792]{2,1,0:T(8,128)(2,1)}, u32[]{:S(2)}, u32[]{:S(2)}) async-start(bf16[32,8,1792]{2,1,0:T(8,128)(2,1)} %fusion), calls=%async_computation | async-start | bytes 1835008 | tf_op jit(solution)/shard_map/all_to_all | solution.py:321
  49.2 3.7 %collective-permute-start.15 = (bf16[1792,256]{1,0:T(8,128)(2,1)}, bf16[1792,256]{1,0:T(8,128)(2,1)}, u32[]{:S(2)}, u32[]{:S(2)}) collective-permute-start(bf16[1792,256]{1,0:T(8,128)(2,1)} %get-tuple-element.27), channel_id=1, source_target_pairs={{0,3},{1,0},{2,1},{3,2},{4,7},{5,4},{6,5},{7,6},{8,11},{9,8},{10,9... | collective-permute-start | bytes 2752520 | tf_op jit(solution)/shard_map/ppermute | solution.py:18
  52.9 3.6 %choose.2 = bf16[1792,256]{1,0:T(8,128)(2,1)} custom-call(s32[1]{0:T(128)} %bitcast.16.which, bf16[1792,256]{1,0:T(8,128)(2,1)} %copy-done.8, bf16[1792,256]{1,0:T(8,128)(2,1)} %copy-done.7), custom_call_target="tpu_custom_call" | custom-call | flops 199999995904 | bytes 2752512 | tf_op jit(solution)/shard_map/choose/pallas_call | solution.py:132
  56.5 2.7 %collective-permute-start.13 = (bf16[1792,256]{1,0:T(8,128)(2,1)}, bf16[1792,256]{1,0:T(8,128)(2,1)}, u32[]{:S(2)}, u32[]{:S(2)}) collective-permute-start(bf16[1792,256]{1,0:T(8,128)(2,1)} %choose.2), channel_id=1, source_target_pairs={{0,1},{1,0},{2,3},{3,2},{5,6},{6,5},{7,4},{4,7},{8,9},{9,8},{10,11... | collective-permute-start | bytes 2752520 | tf_op jit(solution)/shard_map/ppermute | solution.py:295
  59.1 11.2 %all-to-all-done = bf16[32,8,1792]{2,1,0:T(8,128)(2,1)} async-done(((bf16[32,8,1792]{2,1,0:T(8,128)(2,1)}), bf16[32,8,1792]{2,1,0:T(8,128)(2,1)}, u32[]{:S(2)}, u32[]{:S(2)}) %all-to-all-start) | async-done | bytes 917536 | tf_op jit(solution)/shard_map/all_to_all | solution.py:321
  70.4 6.6 %all-to-all-start.2 = ((bf16[32,8,1792]{2,1,0:T(8,128)(2,1)}), bf16[32,8,1792]{2,1,0:T(8,128)(2,1)}, u32[]{:S(2)}, u32[]{:S(2)}) async-start(bf16[32,8,1792]{2,1,0:T(8,128)(2,1)} %bitcast.22), calls=%async_computation.2 | async-start | bytes 1835008 | tf_op jit(solution)/shard_map/all_to_all | solution.py:321
  77.0 3.6 %choose.3 = bf16[1792,256]{1,0:T(8,128)(2,1)} custom-call(s32[1]{0:T(128)} %bitcast.16.which, bf16[1792,256]{1,0:T(8,128)(2,1)} %collective-permute-done.16.first.refs_3_, bf16[1792,256]{1,0:T(8,128)(2,1)} %collective-permute-done.15.second.refs_1_), custom_call_target="tpu_custom_call" | custom-call | flops 199999995904 | bytes 2752512 | tf_op jit(solution)/shard_map/choose/pallas_call | solution.py:132
  80.6 5.8 %collective-permute-start.17 = (bf16[1792,256]{1,0:T(8,128)(2,1)}, bf16[1792,256]{1,0:T(8,128)(2,1)S(1)}, u32[]{:S(2)}, u32[]{:S(2)}) collective-permute-start(bf16[1792,256]{1,0:T(8,128)(2,1)} %choose.3), channel_id=1, source_target_pairs={{0,1},{1,0},{2,3},{3,2},{5,6},{6,5},{7,4},{4,7},{8,9},{9,8},{10,11... | collective-permute-start | bytes 2752520 | tf_op jit(solution)/shard_map/ppermute | solution.py:295
  86.4 0.2 collective-permute-done.13.refs_2_
  86.6 4.6 %up_project.2 = (f32[4,256,256]{2,1,0:T(8,128)}, bf16[4,256,256]{2,1,0:T(8,128)(2,1)}) custom-call(bf16[256,1792]{1,0:T(8,128)(2,1)} %bitcast.12.rows, bf16[1792,256]{1,0:T(8,128)(2,1)} %get-tuple-element.37.refs_0_, bf16[1792,256]{1,0:T(8,128)(2,1)} %copy-done.7, bf16[1792,256]{1,0:T(8,128)(2,1)} %collective-permute-done.13.refs_2_, bf16[1792,256]{1,0:T(8,128)(2,1)} %copy-done.8), custom_call_target="tpu_custom_call" | custom-call | flops 939524096 | bytes 9000000 | tf_op jit(solution)/shard_map/up_project/pallas_call | solution.py:158
  92.6 0.1 select_reduce_fusion.3
  92.7 10.9 %collective-permute-done.14.theirs = bf16[4,256,256]{2,1,0:T(8,128)(2,1)S(1)} collective-permute-done((bf16[4,256,256]{2,1,0:T(8,128)(2,1)}, bf16[4,256,256]{2,1,0:T(8,128)(2,1)S(1)}, u32[]{:S(2)}, u32[]{:S(2)}) %collective-permute-start.14) | collective-permute-done | bytes 524320 | tf_op jit(solution)/shard_map/ppermute | solution.py:273
  103.6 1.2 copy-done
  104.8 3.8 %down_project.2 = bf16[256,1792]{1,0:T(8,128)(2,1)} custom-call(s32[1]{0:T(128)} %bitcast.10.shift, f32[4,256,256]{2,1,0:T(8,128)S(1)} %copy-done, bf16[4,256,256]{2,1,0:T(8,128)(2,1)S(1)} %collective-permute-done.14.theirs, bf16[1792,256]{1,0:T(8,128)(2,1)S(1)} %get-tuple-element.34.refs_0_, bf16[1792,256]{1,0:T(8,128)(2,1)} %collective-permute-done.15.second.refs_1_, ...), custom_call_target="tpu_custom_call" | custom-call | flops 939524096 | bytes 9000000 | tf_op jit(solution)/shard_map/down_project/pallas_call | solution.py:201
  108.6 9.5 %all-to-all-start.1 = ((bf16[32,8,1792]{2,1,0:T(8,128)(2,1)}), bf16[32,8,1792]{2,1,0:T(8,128)(2,1)}, u32[]{:S(2)}, u32[]{:S(2)}) async-start(bf16[32,8,1792]{2,1,0:T(8,128)(2,1)} %bitcast.20), calls=%async_computation.1 | async-start | bytes 1835008 | tf_op jit(solution)/shard_map/all_to_all | solution.py:321
  118.2 4.6 %up_project.3 = (f32[4,256,256]{2,1,0:T(8,128)}, bf16[4,256,256]{2,1,0:T(8,128)(2,1)}) custom-call(bf16[256,1792]{1,0:T(8,128)(2,1)} %bitcast.23.rows, bf16[1792,256]{1,0:T(8,128)(2,1)} %get-tuple-element.37.refs_0_, bf16[1792,256]{1,0:T(8,128)(2,1)} %copy-done.7, bf16[1792,256]{1,0:T(8,128)(2,1)} %collective-permute-done.13.refs_2_, bf16[1792,256]{1,0:T(8,128)(2,1)} %copy-done.8), custom_call_target="tpu_custom_call" | custom-call | flops 939524096 | bytes 9000000 | tf_op jit(solution)/shard_map/up_project/pallas_call | solution.py:158
  122.7 1.6 collective-permute-start.21
  124.4 0.1 min.15
  124.6 0.1 select_reduce_fusion.2.pages
  124.7 0.9 dynamic-slice_bitcast_fusion.6
  125.6 5.9 %collective-permute-done.21.theirs = bf16[4,256,256]{2,1,0:T(8,128)(2,1)S(1)} collective-permute-done((bf16[4,256,256]{2,1,0:T(8,128)(2,1)}, bf16[4,256,256]{2,1,0:T(8,128)(2,1)S(1)}, u32[]{:S(2)}, u32[]{:S(2)}) %collective-permute-start.21) | collective-permute-done | bytes 524320 | tf_op jit(solution)/shard_map/ppermute | solution.py:273
  131.5 1.2 copy-done.1
  132.7 3.0 %down_project.3 = bf16[256,1792]{1,0:T(8,128)(2,1)S(1)} custom-call(s32[1]{0:T(128)} %bitcast.10.shift, f32[4,256,256]{2,1,0:T(8,128)S(1)} %copy-done.1, bf16[4,256,256]{2,1,0:T(8,128)(2,1)S(1)} %collective-permute-done.21.theirs, bf16[1792,256]{1,0:T(8,128)(2,1)S(1)} %get-tuple-element.34.refs_0_, bf16[1792,256]{1,0:T(8,128)(2,1)} %collective-permute-done.15.second.refs_1_, ...), custom_call_target="tpu_custom_call" | custom-call | flops 939524096 | bytes 9000000 | tf_op jit(solution)/shard_map/down_project/pallas_call | solution.py:201
  135.8 3.2 %collective-permute-start.22 = (bf16[256,1792]{1,0:T(8,128)(2,1)S(1)}, bf16[256,1792]{1,0:T(8,128)(2,1)}, u32[]{:S(2)}, u32[]{:S(2)}) collective-permute-start(bf16[256,1792]{1,0:T(8,128)(2,1)S(1)} %down_project.3), channel_id=1, source_target_pairs={{0,4},{4,0},{8,12},{12,8},{16,20},{20,16},{24,28},{28,24},{32,36},... | collective-permute-start | bytes 2752520 | tf_op jit(solution)/shard_map/ppermute | solution.py:276
  139.0 0.1 maximum_maximum_fusion
  139.0 3.0 %collective-permute-start.5 = (bf16[80,576]{1,0:T(8,128)(2,1)S(1)}, bf16[80,576]{1,0:T(8,128)(2,1)S(1)}, u32[]{:S(2)}, u32[]{:S(2)}) collective-permute-start(bf16[80,576]{1,0:T(8,128)(2,1)S(1)} %maximum_maximum_fusion), channel_id=1, source_target_pairs={{0,3},{1,0},{2,1},{3,2},{4,7},{5,4},{6,5},{7,6},{8,11},{9,8},{10,9... | collective-permute-start | bytes 276488 | tf_op jit(solution)/shard_map/ppermute | solution.py:18
  142.1 0.7 collective-permute-start.3
  142.9 0.2 select_reduce_fusion
  143.1 3.4 %collective-permute-done.5 = bf16[80,576]{1,0:T(8,128)(2,1)S(1)} collective-permute-done((bf16[80,576]{1,0:T(8,128)(2,1)S(1)}, bf16[80,576]{1,0:T(8,128)(2,1)S(1)}, u32[]{:S(2)}, u32[]{:S(2)}) %collective-permute-start.5) | collective-permute-done | bytes 92192 | tf_op jit(solution)/shard_map/ppermute | solution.py:18
  146.4 1.4 collective-permute-done.4
  147.8 2.2 %collective-permute-done.3 = bf16[80,576]{1,0:T(8,128)(2,1)S(1)} collective-permute-done((bf16[80,576]{1,0:T(8,128)(2,1)S(1)}, bf16[80,576]{1,0:T(8,128)(2,1)S(1)}, u32[]{:S(2)}, u32[]{:S(2)}) %collective-permute-start.3) | collective-permute-done | bytes 92192 | tf_op jit(solution)/shard_map/ppermute | solution.py:18
  150.0 0.1 select_select_fusion
  150.2 9.5 %all-to-all-start.3 = ((bf16[32,8,1792]{2,1,0:T(8,128)(2,1)}), bf16[32,8,1792]{2,1,0:T(8,128)(2,1)S(1)}, u32[]{:S(2)}, u32[]{:S(2)}) async-start(bf16[32,8,1792]{2,1,0:T(8,128)(2,1)} %bitcast.24), calls=%async_computation.3 | async-start | bytes 1835008 | tf_op jit(solution)/shard_map/all_to_all | solution.py:321
  159.7 1.3 copy-done.2
  161.0 1.7 copy-done.3
  162.7 19.0 %attention.1 = (bf16[16,64,512]{2,1,0:T(8,128)(2,1)}, bf16[16,64,512]{2,1,0:T(8,128)(2,1)}, bf16[64,512]{1,0:T(8,128)(2,1)S(1)}) custom-call(s32[16]{0:T(128)S(1)} %bitcast.47, s32[128]{0:T(128)S(1)} %select_reduce_fusion.2.pages, s32[1]{0:T(128)} %bitcast.42.moved, bf16[16,64,576]{2,1,0:T(8,128)(2,1)S(1)} %copy-done.4, bf16[16,64,576]{2,1,0:T(8,128)(2,1)S(1)} %copy-done.2, ...), custom_call_target="tpu_custom_call" | custom-call | flops 12000000000 | bytes 8000000 | tf_op jit(solution)/shard_map/attention/pallas_call | solution.py:89
  181.8 2.7 %collective-permute-start.8 = (bf16[64,512]{1,0:T(8,128)(2,1)S(1)}, bf16[64,512]{1,0:T(8,128)(2,1)S(1)}, u32[]{:S(2)}, u32[]{:S(2)}) collective-permute-start(bf16[64,512]{1,0:T(8,128)(2,1)S(1)} %get-tuple-element.46), channel_id=1, source_target_pairs={{0,3},{1,0},{2,1},{3,2},{4,7},{5,4},{6,5},{7,6},{8,11},{9,8},{10,9... | collective-permute-start | bytes 196616 | tf_op jit(solution)/shard_map/ppermute | solution.py:18
  184.5 1.5 fusion.4
  186.0 0.7 collective-permute-start.18
  186.7 0.3 fusion.2
  187.0 2.8 %collective-permute-start.23 = (f32[16,1792]{1,0:T(8,128)S(1)}, f32[16,1792]{1,0:T(8,128)S(1)}, u32[]{:S(2)}, u32[]{:S(2)}) collective-permute-start(f32[16,1792]{1,0:T(8,128)S(1)} %slice.75), channel_id=1, source_target_pairs={{2,3},{3,2},{0,1},{1,0},{5,6},{6,5},{7,4},{4,7},{10,11},{11,10},{8... | collective-permute-start | bytes 344072 | tf_op jit(solution)/shard_map/ppermute | solution.py:273
  189.8 0.7 bitcast_dynamic-update-slice_fusion
  190.5 3.1 %collective-permute-done.23 = f32[16,1792]{1,0:T(8,128)S(1)} collective-permute-done((f32[16,1792]{1,0:T(8,128)S(1)}, f32[16,1792]{1,0:T(8,128)S(1)}, u32[]{:S(2)}, u32[]{:S(2)}) %collective-permute-start.23) | collective-permute-done | bytes 114720 | tf_op jit(solution)/shard_map/ppermute | solution.py:273
  193.6 0.7 pad_maximum_fusion.2
  (82 shorter events, 0.9 us)
Async XLA Ops:
  1.4 12.7 %collective-permute-start = (s32[16,8]{1,0:T(8,128)S(1)}, s32[16,8]{1,0:T(8,128)S(1)}, u32[]{:S(2)}, u32[]{:S(2)}) collective-permute-start(s32[16,8]{1,0:T(8,128)S(1)} %copy.53), channel_id=1, source_target_pairs={{1,2},{2,1},{3,0},{0,3},{6,7},{7,6},{4,5},{5,4},{9,10},{10,9},{11,... | collective-permute-start | bytes 1544 | tf_op jit(solution)/shard_map/ppermute | solution.py:273
  3.5 10.6 %collective-permute-start.1 = (s32[16,8]{1,0:T(8,128)S(1)}, s32[16,8]{1,0:T(8,128)S(1)}, u32[]{:S(2)}, u32[]{:S(2)}) collective-permute-start(s32[16,8]{1,0:T(8,128)S(1)} %copy.53), channel_id=1, source_target_pairs={{2,3},{3,2},{0,1},{1,0},{5,6},{6,5},{7,4},{4,7},{10,11},{11,10},{8... | collective-permute-start | bytes 1544 | tf_op jit(solution)/shard_map/ppermute | solution.py:273
  6.3 9.2 %collective-permute-start.2 = (bf16[16,1792]{1,0:T(8,128)(2,1)S(1)}, bf16[16,1792]{1,0:T(8,128)(2,1)S(1)}, u32[]{:S(2)}, u32[]{:S(2)}) collective-permute-start(bf16[16,1792]{1,0:T(8,128)(2,1)S(1)} %get-tuple-element.42), channel_id=1, source_target_pairs={{2,3},{3,2},{0,1},{1,0},{5,6},{6,5},{7,4},{4,7},{10,11},{11,10},{8... | collective-permute-start | bytes 172040 | tf_op jit(solution)/shard_map/ppermute | solution.py:273
  7.2 29.5 %collective-permute-start.10 = (bf16[16,1792]{1,0:T(8,128)(2,1)S(1)}, bf16[16,1792]{1,0:T(8,128)(2,1)S(1)}, u32[]{:S(2)}, u32[]{:S(2)}) collective-permute-start(bf16[16,1792]{1,0:T(8,128)(2,1)S(1)} %get-tuple-element.44), channel_id=1, source_target_pairs={{1,2},{2,1},{3,0},{0,3},{6,7},{7,6},{4,5},{5,4},{9,10},{10,9},{11,... | collective-permute-start | bytes 172040 | tf_op jit(solution)/shard_map/ppermute | solution.py:273
  7.2 5.4 %copy-start.6 = (bf16[1,3584,256]{2,1,0:T(8,128)(2,1)S(1)}, bf16[1,3584,256]{2,1,0:T(8,128)(2,1)}, u32[]{:S(2)}) copy-start(bf16[1,3584,256]{2,1,0:T(8,128)(2,1)} %param.18) | copy-start | bytes 5505028
  10.7 38.5 %collective-permute-start.11 = (bf16[1792,256]{1,0:T(8,128)(2,1)}, bf16[1792,256]{1,0:T(8,128)(2,1)S(1)}, u32[]{:S(2)}, u32[]{:S(2)}) collective-permute-start(bf16[1792,256]{1,0:T(8,128)(2,1)} %get-tuple-element.23), channel_id=1, source_target_pairs={{0,3},{1,0},{2,1},{3,2},{4,7},{5,4},{6,5},{7,6},{8,11},{9,8},{10,9... | collective-permute-start | bytes 2752520 | tf_op jit(solution)/shard_map/ppermute | solution.py:18
  14.1 2.8 %copy-start.15 = (f32[16,8]{0,1:T(8,128)S(1)}, f32[16,8]{0,1:T(8,128)}, u32[]{:S(2)}) copy-start(f32[16,8]{0,1:T(8,128)} %param.16) | copy-start | bytes 1540
  14.1 35.1 %collective-permute-start.12 = (bf16[1792,256]{1,0:T(8,128)(2,1)}, bf16[1792,256]{1,0:T(8,128)(2,1)S(1)}, u32[]{:S(2)}, u32[]{:S(2)}) collective-permute-start(bf16[1792,256]{1,0:T(8,128)(2,1)} %get-tuple-element.24), channel_id=1, source_target_pairs={{0,1},{1,2},{2,3},{3,0},{4,5},{5,6},{6,7},{7,4},{8,9},{9,10},{10,1... | collective-permute-start | bytes 2752520 | tf_op jit(solution)/shard_map/ppermute | solution.py:18
  14.8 0.6 copy-start.9
  16.9 17.5 %collective-permute-start.19 = (f32[16,8]{0,1:T(8,128)S(1)}, f32[16,8]{0,1:T(8,128)S(1)}, u32[]{:S(2)}, u32[]{:S(2)}) collective-permute-start(f32[16,8]{0,1:T(8,128)S(1)} %copy-done.15), channel_id=1, source_target_pairs={{2,3},{3,2},{0,1},{1,0},{5,6},{6,5},{7,4},{4,7},{10,11},{11,10},{8... | collective-permute-start | bytes 1544 | tf_op jit(solution)/shard_map/ppermute | solution.py:273
  19.6 15.5 %collective-permute-start.9 = (f32[16,8]{0,1:T(8,128)S(1)}, f32[16,8]{0,1:T(8,128)S(1)}, u32[]{:S(2)}, u32[]{:S(2)}) collective-permute-start(f32[16,8]{0,1:T(8,128)S(1)} %copy-done.15), channel_id=1, source_target_pairs={{1,2},{2,1},{3,0},{0,3},{6,7},{7,6},{4,5},{5,4},{9,10},{10,9},{11,... | collective-permute-start | bytes 1544 | tf_op jit(solution)/shard_map/ppermute | solution.py:273
  34.4 24.7 %collective-permute-start.20 = (bf16[256,1792]{1,0:T(8,128)(2,1)}, bf16[256,1792]{1,0:T(8,128)(2,1)}, u32[]{:S(2)}, u32[]{:S(2)}) collective-permute-start(bf16[256,1792]{1,0:T(8,128)(2,1)} %convolution_convert_fusion.1), channel_id=1, source_target_pairs={{0,4},{4,0},{8,12},{12,8},{16,20},{20,16},{24,28},{28,24},{32,36},... | collective-permute-start | bytes 2752520 | tf_op jit(solution)/shard_map/ppermute | solution.py:276
  38.0 32.4 %all-to-all-start = ((bf16[32,8,1792]{2,1,0:T(8,128)(2,1)}), bf16[32,8,1792]{2,1,0:T(8,128)(2,1)}, u32[]{:S(2)}, u32[]{:S(2)}) async-start(bf16[32,8,1792]{2,1,0:T(8,128)(2,1)} %fusion), calls=%async_computation | async-start | bytes 1835008 | tf_op jit(solution)/shard_map/all_to_all | solution.py:321
  49.2 3.7 %copy-start.7 = (bf16[1792,256]{1,0:T(8,128)(2,1)}, bf16[1792,256]{1,0:T(8,128)(2,1)S(1)}, u32[]{:S(2)}) copy-start(bf16[1792,256]{1,0:T(8,128)(2,1)S(1)} %collective-permute-done.11.second.refs_1_) | copy-start | bytes 2752516
  49.2 3.7 %copy-start.8 = (bf16[1792,256]{1,0:T(8,128)(2,1)}, bf16[1792,256]{1,0:T(8,128)(2,1)S(1)}, u32[]{:S(2)}) copy-start(bf16[1792,256]{1,0:T(8,128)(2,1)S(1)} %collective-permute-done.12.first.refs_3_) | copy-start | bytes 2752516
  49.2 27.8 %collective-permute-start.15 = (bf16[1792,256]{1,0:T(8,128)(2,1)}, bf16[1792,256]{1,0:T(8,128)(2,1)}, u32[]{:S(2)}, u32[]{:S(2)}) collective-permute-start(bf16[1792,256]{1,0:T(8,128)(2,1)} %get-tuple-element.27), channel_id=1, source_target_pairs={{0,3},{1,0},{2,1},{3,2},{4,7},{5,4},{6,5},{7,6},{8,11},{9,8},{10,9... | collective-permute-start | bytes 2752520 | tf_op jit(solution)/shard_map/ppermute | solution.py:18
  52.9 24.1 %collective-permute-start.16 = (bf16[1792,256]{1,0:T(8,128)(2,1)}, bf16[1792,256]{1,0:T(8,128)(2,1)}, u32[]{:S(2)}, u32[]{:S(2)}) collective-permute-start(bf16[1792,256]{1,0:T(8,128)(2,1)} %get-tuple-element.28), channel_id=1, source_target_pairs={{0,1},{1,2},{2,3},{3,0},{4,5},{5,6},{6,7},{7,4},{8,9},{9,10},{10,1... | collective-permute-start | bytes 2752520 | tf_op jit(solution)/shard_map/ppermute | solution.py:18
  56.5 30.1 %collective-permute-start.13 = (bf16[1792,256]{1,0:T(8,128)(2,1)}, bf16[1792,256]{1,0:T(8,128)(2,1)}, u32[]{:S(2)}, u32[]{:S(2)}) collective-permute-start(bf16[1792,256]{1,0:T(8,128)(2,1)} %choose.2), channel_id=1, source_target_pairs={{0,1},{1,0},{2,3},{3,2},{5,6},{6,5},{7,4},{4,7},{8,9},{9,8},{10,11... | collective-permute-start | bytes 2752520 | tf_op jit(solution)/shard_map/ppermute | solution.py:295
  70.4 38.2 %all-to-all-start.2 = ((bf16[32,8,1792]{2,1,0:T(8,128)(2,1)}), bf16[32,8,1792]{2,1,0:T(8,128)(2,1)}, u32[]{:S(2)}, u32[]{:S(2)}) async-start(bf16[32,8,1792]{2,1,0:T(8,128)(2,1)} %bitcast.22), calls=%async_computation.2 | async-start | bytes 1835008 | tf_op jit(solution)/shard_map/all_to_all | solution.py:321
  80.6 23.0 %collective-permute-start.17 = (bf16[1792,256]{1,0:T(8,128)(2,1)}, bf16[1792,256]{1,0:T(8,128)(2,1)S(1)}, u32[]{:S(2)}, u32[]{:S(2)}) collective-permute-start(bf16[1792,256]{1,0:T(8,128)(2,1)} %choose.3), channel_id=1, source_target_pairs={{0,1},{1,0},{2,3},{3,2},{5,6},{6,5},{7,4},{4,7},{8,9},{9,8},{10,11... | collective-permute-start | bytes 2752520 | tf_op jit(solution)/shard_map/ppermute | solution.py:295
  86.6 5.9 %copy-start.5 = (s32[1,16]{1,0:T(1,128)S(1)}, s32[1,16]{1,0:T(1,128)}, u32[]{:S(2)}) copy-start(s32[1,16]{1,0:T(1,128)} %param.24) | copy-start | bytes 196
  91.2 12.4 %collective-permute-start.14 = (bf16[4,256,256]{2,1,0:T(8,128)(2,1)}, bf16[4,256,256]{2,1,0:T(8,128)(2,1)S(1)}, u32[]{:S(2)}, u32[]{:S(2)}) collective-permute-start(bf16[4,256,256]{2,1,0:T(8,128)(2,1)} %get-tuple-element.26), channel_id=1, source_target_pairs={{1,2},{2,1},{3,0},{0,3},{6,7},{7,6},{4,5},{5,4},{9,10},{10,9},{11,... | collective-permute-start | bytes 1572872 | tf_op jit(solution)/shard_map/ppermute | solution.py:273
  103.6 1.2 copy-start
  108.6 41.6 %all-to-all-start.1 = ((bf16[32,8,1792]{2,1,0:T(8,128)(2,1)}), bf16[32,8,1792]{2,1,0:T(8,128)(2,1)}, u32[]{:S(2)}, u32[]{:S(2)}) async-start(bf16[32,8,1792]{2,1,0:T(8,128)(2,1)} %bitcast.20), calls=%async_computation.1 | async-start | bytes 1835008 | tf_op jit(solution)/shard_map/all_to_all | solution.py:321
  118.1 6.4 %copy-start.13 = (bf16[16,576]{1,0:T(8,128)(2,1)S(1)}, bf16[16,576]{1,0:T(8,128)(2,1)}, u32[]{:S(2)}) copy-start(bf16[16,576]{1,0:T(8,128)(2,1)} %param.20) | copy-start | bytes 55300
  118.1 6.5 %copy-start.16 = (s32[1,32]{1,0:T(1,128)S(1)}, s32[1,32]{1,0:T(1,128)}, u32[]{:S(2)}) copy-start(s32[1,32]{1,0:T(1,128)} %param.25) | copy-start | bytes 388
  118.1 6.6 %copy-start.12 = (bf16[16,576]{1,0:T(8,128)(2,1)S(1)}, bf16[16,576]{1,0:T(8,128)(2,1)}, u32[]{:S(2)}) copy-start(bf16[16,576]{1,0:T(8,128)(2,1)} %param.22) | copy-start | bytes 55300
  122.7 8.7 %collective-permute-start.21 = (bf16[4,256,256]{2,1,0:T(8,128)(2,1)}, bf16[4,256,256]{2,1,0:T(8,128)(2,1)S(1)}, u32[]{:S(2)}, u32[]{:S(2)}) collective-permute-start(bf16[4,256,256]{2,1,0:T(8,128)(2,1)} %get-tuple-element.30), channel_id=1, source_target_pairs={{1,2},{2,1},{3,0},{0,3},{6,7},{7,6},{4,5},{5,4},{9,10},{10,9},{11,... | collective-permute-start | bytes 1572872 | tf_op jit(solution)/shard_map/ppermute | solution.py:273
  131.5 1.2 copy-start.1
  132.7 10.1 %copy-start.14 = (f32[32,8]{0,1:T(8,128)S(1)}, f32[32,8]{0,1:T(8,128)}, u32[]{:S(2)}) copy-start(f32[32,8]{0,1:T(8,128)} %get-tuple-element.57) | copy-start | bytes 3076
  132.7 10.1 %copy-start.10 = (s32[32,8]{1,0:T(8,128)S(1)}, s32[32,8]{1,0:T(8,128)}, u32[]{:S(2)}) copy-start(s32[32,8]{1,0:T(8,128)} %copy-done.9) | copy-start | bytes 3076
  132.7 10.3 %copy-start.11 = (f32[32,256]{1,0:T(8,128)S(1)}, f32[32,256]{1,0:T(8,128)}, u32[]{:S(2)}) copy-start(f32[32,256]{1,0:T(8,128)} %get-tuple-element.31) | copy-start | bytes 98308
  135.8 23.9 %copy-start.4 = (bf16[16,64,576]{2,1,0:T(8,128)(2,1)S(1)}, bf16[16,64,576]{2,1,0:T(8,128)(2,1)}, u32[]{:S(2)}) copy-start(bf16[16,64,576]{2,1,0:T(8,128)(2,1)} %q_one.1) | copy-start | bytes 3538948
  135.8 14.4 %collective-permute-start.22 = (bf16[256,1792]{1,0:T(8,128)(2,1)S(1)}, bf16[256,1792]{1,0:T(8,128)(2,1)}, u32[]{:S(2)}, u32[]{:S(2)}) collective-permute-start(bf16[256,1792]{1,0:T(8,128)(2,1)S(1)} %down_project.3), channel_id=1, source_target_pairs={{0,4},{4,0},{8,12},{12,8},{16,20},{20,16},{24,28},{28,24},{32,36},... | collective-permute-start | bytes 2752520 | tf_op jit(solution)/shard_map/ppermute | solution.py:276
  139.0 7.4 %collective-permute-start.5 = (bf16[80,576]{1,0:T(8,128)(2,1)S(1)}, bf16[80,576]{1,0:T(8,128)(2,1)S(1)}, u32[]{:S(2)}, u32[]{:S(2)}) collective-permute-start(bf16[80,576]{1,0:T(8,128)(2,1)S(1)} %maximum_maximum_fusion), channel_id=1, source_target_pairs={{0,3},{1,0},{2,1},{3,2},{4,7},{5,4},{6,5},{7,6},{8,11},{9,8},{10,9... | collective-permute-start | bytes 276488 | tf_op jit(solution)/shard_map/ppermute | solution.py:18
  142.1 5.7 %collective-permute-start.4 = (bf16[80,576]{1,0:T(8,128)(2,1)S(1)}, bf16[80,576]{1,0:T(8,128)(2,1)S(1)}, u32[]{:S(2)}, u32[]{:S(2)}) collective-permute-start(bf16[80,576]{1,0:T(8,128)(2,1)S(1)} %maximum_maximum_fusion), channel_id=1, source_target_pairs={{0,2},{1,3},{2,0},{3,1},{4,6},{5,7},{6,4},{7,5},{8,10},{9,11},{10,... | collective-permute-start | bytes 276488 | tf_op jit(solution)/shard_map/ppermute | solution.py:18
  142.1 8.0 %collective-permute-start.3 = (bf16[80,576]{1,0:T(8,128)(2,1)S(1)}, bf16[80,576]{1,0:T(8,128)(2,1)S(1)}, u32[]{:S(2)}, u32[]{:S(2)}) collective-permute-start(bf16[80,576]{1,0:T(8,128)(2,1)S(1)} %maximum_maximum_fusion), channel_id=1, source_target_pairs={{0,1},{1,2},{2,3},{3,0},{4,5},{5,6},{6,7},{7,4},{8,9},{9,10},{10,1... | collective-permute-start | bytes 276488 | tf_op jit(solution)/shard_map/ppermute | solution.py:18
  150.2 36.5 %all-to-all-start.3 = ((bf16[32,8,1792]{2,1,0:T(8,128)(2,1)}), bf16[32,8,1792]{2,1,0:T(8,128)(2,1)S(1)}, u32[]{:S(2)}, u32[]{:S(2)}) async-start(bf16[32,8,1792]{2,1,0:T(8,128)(2,1)} %bitcast.24), calls=%async_computation.3 | async-start | bytes 1835008 | tf_op jit(solution)/shard_map/all_to_all | solution.py:321
  159.7 1.3 copy-start.2
  161.0 1.7 copy-start.3
  181.7 8.0 %collective-permute-start.6 = (bf16[64,512]{1,0:T(8,128)(2,1)S(1)}, bf16[64,512]{1,0:T(8,128)(2,1)S(1)}, u32[]{:S(2)}, u32[]{:S(2)}) collective-permute-start(bf16[64,512]{1,0:T(8,128)(2,1)S(1)} %get-tuple-element.45), channel_id=1, source_target_pairs={{0,1},{1,2},{2,3},{3,0},{4,5},{5,6},{6,7},{7,4},{8,9},{9,10},{10,1... | collective-permute-start | bytes 196616 | tf_op jit(solution)/shard_map/ppermute | solution.py:18
  181.8 8.0 %collective-permute-start.8 = (bf16[64,512]{1,0:T(8,128)(2,1)S(1)}, bf16[64,512]{1,0:T(8,128)(2,1)S(1)}, u32[]{:S(2)}, u32[]{:S(2)}) collective-permute-start(bf16[64,512]{1,0:T(8,128)(2,1)S(1)} %get-tuple-element.46), channel_id=1, source_target_pairs={{0,3},{1,0},{2,1},{3,2},{4,7},{5,4},{6,5},{7,6},{8,11},{9,8},{10,9... | collective-permute-start | bytes 196616 | tf_op jit(solution)/shard_map/ppermute | solution.py:18
  184.5 5.3 %collective-permute-start.7 = (bf16[64,512]{1,0:T(8,128)(2,1)S(1)}, bf16[64,512]{1,0:T(8,128)(2,1)S(1)}, u32[]{:S(2)}, u32[]{:S(2)}) collective-permute-start(bf16[64,512]{1,0:T(8,128)(2,1)S(1)} %get-tuple-element.47), channel_id=1, source_target_pairs={{0,2},{1,3},{2,0},{3,1},{4,6},{5,7},{6,4},{7,5},{8,10},{9,11},{10,... | collective-permute-start | bytes 196616 | tf_op jit(solution)/shard_map/ppermute | solution.py:18
  186.0 4.5 %collective-permute-start.18 = (f32[16,1792]{1,0:T(8,128)S(1)}, f32[16,1792]{1,0:T(8,128)S(1)}, u32[]{:S(2)}, u32[]{:S(2)}) collective-permute-start(f32[16,1792]{1,0:T(8,128)S(1)} %slice.71), channel_id=1, source_target_pairs={{1,2},{2,1},{3,0},{0,3},{6,7},{7,6},{4,5},{5,4},{9,10},{10,9},{11,... | collective-permute-start | bytes 344072 | tf_op jit(solution)/shard_map/ppermute | solution.py:273
  187.0 6.5 %collective-permute-start.23 = (f32[16,1792]{1,0:T(8,128)S(1)}, f32[16,1792]{1,0:T(8,128)S(1)}, u32[]{:S(2)}, u32[]{:S(2)}) collective-permute-start(f32[16,1792]{1,0:T(8,128)S(1)} %slice.75), channel_id=1, source_target_pairs={{2,3},{3,2},{0,1},{1,0},{5,6},{6,5},{7,4},{4,7},{10,11},{11,10},{8... | collective-permute-start | bytes 344072 | tf_op jit(solution)/shard_map/ppermute | solution.py:273

commit v10 on v9

--- a/solution.py
+++ b/solution.py
@@ -278,11 +278,21 @@
     def part(value, which, axis):
         return lax.dynamic_slice_in_dim(value, which * half, half, axis)
 
-    rows, id_list = [], [expert_ids]
+    rows, id_list, gate_list = [], [expert_ids], [gate_weights]
+    term = lax.reduce_precision(gate_weights, 8, 7)
+    rest = gate_weights - term
+    next_term = lax.reduce_precision(rest, 8, 7)
+    small = jnp.concatenate(
+        [expert_ids.astype(jnp.float32), term, next_term, rest - next_term], axis=1
+    ).astype(jnp.bfloat16)
+    small = jnp.pad(small, ((0, 0), (0, 128 - 4 * picks)))
     for k in range(2):
-        id_list.append(swap_planes(expert_ids, k))
-        theirs = swap_planes(part(hidden, 1 - side[k], 1), k)
-        rows.append(jnp.concatenate([part(hidden, side[k], 1), theirs], axis=0))
+        sent = jnp.concatenate([part(hidden, 1 - side[k], 1), small], axis=1)
+        theirs = swap_planes(sent, k)
+        extra = theirs[:, half : half + 4 * picks].astype(jnp.float32).reshape(samples, 4, picks)
+        id_list.append(extra[:, 0].astype(jnp.int32))
+        gate_list.append((extra[:, 1] + extra[:, 2]) + extra[:, 3])
+        rows.append(jnp.concatenate([part(hidden, side[k], 1), theirs[:, :half]], axis=0))
 
     ahead = jnp.where((here == 0) | (here == 3), 0, 1)
 
@@ -345,20 +355,40 @@
         ).astype(jnp.bfloat16)
         arrived.append(exchange(outgoing if k == 0 else swap_cores(outgoing)))
 
-    moved_slot = mig_slot[0, 0]
-    moved_target = mig_dest[0, 0]
-    query_second, kv_second = after(outgoing, query_second, kv_second)
-    q_here = lax.dynamic_index_in_dim(query_second, moved_slot, 0, keepdims=False)
-    kv_here = lax.dynamic_index_in_dim(kv_second, moved_slot, 0, keepdims=True)
-    packet = jnp.concatenate(
-        [q_here, kv_here, jnp.zeros((15, q_here.shape[1]), jnp.bfloat16)], axis=0
-    )
-    offset = (moved_target - me) % grp_size
-    got = packet
-    for r in steps[1:]:
-        got = jnp.where(offset == r, hop(packet, "grp", -r), got)
-    heads = q_here.shape[0]
-    q_in, kv_in = got[:heads], got[heads : heads + 1]
+    shift = jnp.where(here % 2 == 1, grp_size - 1, 1).astype(jnp.int32)
+    first, second = 0.0, 0.0
+    for k in range(2):
+        mine, rounded = up_project(arrived[k], up_all, 1)
+        theirs = swap_planes(rounded, 0)
+        if k == 1:
+            (theirs,) = after((q_in, kv_in), theirs)
+        produced = down_project(shift[None], mine, theirs, down_all, 2)
+        if k == 0:
+            moved_slot = mig_slot[0, 0]
+            moved_target = mig_dest[0, 0]
+            late_query, late_kv = after(produced, query_second, kv_second)
+            q_here = lax.dynamic_index_in_dim(late_query, moved_slot, 0, keepdims=False)
+            kv_here = lax.dynamic_index_in_dim(late_kv, moved_slot, 0, keepdims=True)
+            packet = jnp.concatenate(
+                [q_here, kv_here, jnp.zeros((15, q_here.shape[1]), jnp.bfloat16)], axis=0
+            )
+            offset = (moved_target - me) % grp_size
+            got = packet
+            for r in steps[1:]:
+                got = jnp.where(offset == r, hop(packet, "grp", -r), got)
+            heads = q_here.shape[0]
+            q_in, kv_in = got[:heads], got[heads : heads + 1]
+        returned = exchange(produced if k == 0 else swap_cores(produced))
+        gates = jnp.concatenate([gate_weights, gate_list[k + 1]], axis=0)
+        mixing = jnp.sum(jnp.where(match[k], gates[:, :, None], 0.0), axis=1)
+        high = lax.reduce_precision(mixing, 8, 7)
+        mixing = jnp.concatenate([high, mixing - high], axis=0).astype(jnp.bfloat16)
+        mixed = jnp.dot(mixing, returned, preferred_element_type=jnp.float32)
+        summed = (mixed[: 2 * samples] + mixed[2 * samples :]).reshape(2, samples, half)
+        own, other = summed[0], swap_planes(summed[1], k)
+        first = first + jnp.where(side[k] == 0, own, other)
+        second = second + jnp.where(side[k] == 0, other, own)
+    moe_out = jnp.concatenate([first, second], axis=1).astype(jnp.bfloat16)
 
     lens = cache_len[0]
     pages = page_table(lens, page_perm[0], cache_pool.shape[1], cache_pool.shape[0])
@@ -380,23 +410,6 @@
         arrived_out = arrived_out + hop(jnp.where(offset == r, out_moved, zero), "grp", r)
     attn_second = lax.dynamic_update_index_in_dim(attn_second, arrived_out, moved_slot, 0)
 
-    shift = jnp.where(here % 2 == 1, grp_size - 1, 1).astype(jnp.int32)
-    (late_gates,) = after(outgoing, gate_weights)
-    first, second = 0.0, 0.0
-    for k in range(2):
-        mine, rounded = up_project(arrived[k], up_all, 1)
-        produced = down_project(shift[None], mine, swap_planes(rounded, 0), down_all, 2)
-        returned = exchange(produced if k == 0 else swap_cores(produced))
-        gates = jnp.concatenate([gate_weights, swap_planes(late_gates, k)], axis=0)
-        mixing = jnp.sum(jnp.where(match[k], gates[:, :, None], 0.0), axis=1)
-        high = lax.reduce_precision(mixing, 8, 7)
-        mixing = jnp.concatenate([high, mixing - high], axis=0).astype(jnp.bfloat16)
-        mixed = jnp.dot(mixing, returned, preferred_element_type=jnp.float32)
-        summed = (mixed[: 2 * samples] + mixed[2 * samples :]).reshape(2, samples, half)
-        own, other = summed[0], swap_planes(summed[1], k)
-        first = first + jnp.where(side[k] == 0, own, other)
-        second = second + jnp.where(side[k] == 0, other, own)
-    moe_out = jnp.concatenate([first, second], axis=1).astype(jnp.bfloat16)
     return (attn_first, attn_second, moe_out)
 
 

time: 195 us -> 172 us (0.88)
  waiting for transfers between devices: 53.1 us -> 37.3 us
  starting transfers between devices: 73.7 us -> 65.4 us
    ppermute x10 -> x6, waiting for transfers between devices: 34.7 us -> 11.8 us  [swap_planes(): return lax.ppermute(value, ('ep', 'grp'), by_core(PAIRS, k))]
    ppermute x2, waiting for transfers between devices: 0.23 us -> 6.21 us  [pass_on(): lax.ppermute(picked, ('ep', 'grp'), by_core([(0, 1), (1, 0), (2, 3), (3,...]
    ppermute x10 -> x6, starting transfers between devices: 12.5 us -> 7.08 us  [swap_planes(): return lax.ppermute(value, ('ep', 'grp'), by_core(PAIRS, k))]
    ppermute x2, starting transfers between devices: 8.51 us -> 3.95 us  [pass_on(): lax.ppermute(picked, ('ep', 'grp'), by_core([(0, 1), (1, 0), (2, 3), (3,...]
    ppermute x2, starting transfers between devices: 3.82 us -> 6.43 us  [swap_cores(): lax.ppermute(value, 'ep', [(e, e + 1 - 2 * (e % 2)) for e in range(ep_siz...]
    ppermute x10, starting transfers between devices: 12.1 us -> 9.54 us  [hop(): lax.ppermute(value, axis, [(i, (i + step) % size) for i in range(size)])]
    all_to_all x4, waiting for transfers between devices: 11.2 us -> 9.18 us  [exchange(): lax.all_to_all(value.reshape(peers, rank, half), 'ep', split_axis=0, conc...]
    unnamed x35 -> x29, local copies, waits for them, and re-layouts: 6.91 us -> 5.62 us
  transfers between devices with their start and end apart: 28 -> 24, of which waited for: 9 -> 7; matrix products, arithmetic and copies ran while one was open for 8% -> 9% of each run, Pallas kernels for 22% -> 25%
where the time goes in v10:
time: 172 us; the launch traced here: 171 us
  starting transfers between devices  65.4 us (38%)
  Pallas kernels  42 us (24%)
  waiting for transfers between devices  37.3 us (22%)
  local copies, waits for them, and re-layouts  13.5 us (8%)
  other arithmetic  5.53 us (3%)
  matrix products  4.76 us (3%)
  between operations  2.42 us (1%)
    all_to_all x4, starting transfers between devices, exchange(): lax.all_to_all(value.reshape(peers, rank, half), 'ep', split_axis=0, conc...  38.4 us
    pallas_call x1, Pallas kernels, attention(): pl.pallas_call(attention_kernel, grid_spec=pltpu.PrefetchScalarGridSpec(n...  19 us
    ppermute x6, waiting for transfers between devices, swap_planes(): return lax.ppermute(value, ('ep', 'grp'), by_core(PAIRS, k))  11.8 us
    ppermute x10, starting transfers between devices, hop(): lax.ppermute(value, axis, [(i, (i + step) % size) for i in range(size)])  9.54 us
    all_to_all x4, waiting for transfers between devices, exchange(): lax.all_to_all(value.reshape(peers, rank, half), 'ep', split_axis=0, conc...  9.18 us
    pallas_call x2, Pallas kernels, up_project(): pl.pallas_call(up_kernel, grid=(steps,), in_specs=[pl.BlockSpec((count //...  9.14 us
    ppermute x10, waiting for transfers between devices, hop(): lax.ppermute(value, axis, [(i, (i + step) % size) for i in range(size)])  8.41 us
    pallas_call x2, Pallas kernels, choose(): pl.pallas_call(choose_kernel, grid_spec=pltpu.PrefetchScalarGridSpec(num_...  7.1 us
  transfers between devices with their start and end apart: 24, of which 7 were waited for; matrix products, arithmetic and copies ran while one was open for 9% of the time, Pallas kernels for 25%

profile of v10, /device:TPU:1, one launch (start us, length us, event | category | flops | bytes accessed | tf_op | source)
XLA Modules:
  0.0 170.9 jit_solution(15576910492849205056)
XLA Ops:
  0.7 0.7 convert_convert_fusion
  1.4 0.7 reduce-precision_convert_fusion.3
  2.1 0.1 copy.49
  2.2 0.9 constant_dynamic-slice_fusion.1
  3.2 3.7 %collective-permute-start.1 = (bf16[16,1920]{1,0:T(8,128)(2,1)S(1)}, bf16[16,1920]{1,0:T(8,128)(2,1)S(1)}, u32[]{:S(2)}, u32[]{:S(2)}) collective-permute-start(bf16[16,1920]{1,0:T(8,128)(2,1)S(1)} %get-tuple-element.64), channel_id=1, source_target_pairs={{2,3},{3,2},{0,1},{1,0},{5,6},{6,5},{7,4},{4,7},{10,11},{11,10},{8... | collective-permute-start | bytes 184328 | tf_op jit(solution)/shard_map/ppermute | solution.py:273
  6.8 3.5 %dynamic-slice_bitcast_fusion.3 = (bf16[1792,256]{1,0:T(8,128)(2,1)}, bf16[1792,256]{1,0:T(8,128)(2,1)}, bf16[1792,256]{1,0:T(8,128)(2,1)}) fusion(bf16[1,3584,256]{2,1,0:T(8,128)(2,1)} %param.17, s32[]{:T(128)S(6)} %select_n.246, s32[]{:T(128)S(6)} %select_n.242, s32[]{:T(128)S(6)} %select_n.245), kind=kLoop, calls=%fused_computation.12 | loop fusion | bytes 5505036 | tf_op jit(solution)/shard_map/dynamic_slice | solution.py:279
  10.3 0.6 collective-permute-start.2
  10.9 0.8 collective-permute-start.3
  11.8 1.5 dynamic-slice_bitcast_fusion
  13.6 0.1 copy.41
  13.6 0.1 eq.139
  13.7 0.3 fusion.1
  14.1 0.1 convert_element_type.58
  14.2 0.1 fusion.29
  14.3 0.1 add_select_fusion.5
  14.7 0.1 copy.43
  14.9 0.1 copy.47
  14.9 0.8 select_reduce_fusion.1
  15.8 1.3 fusion
  17.1 11.2 %all-to-all-start = ((bf16[32,8,1792]{2,1,0:T(8,128)(2,1)}), bf16[32,8,1792]{2,1,0:T(8,128)(2,1)}, u32[]{:S(2)}, u32[]{:S(2)}) async-start(bf16[32,8,1792]{2,1,0:T(8,128)(2,1)} %fusion), calls=%async_computation | async-start | bytes 1835008 | tf_op jit(solution)/shard_map/all_to_all | solution.py:331
  28.3 0.8 select_reduce_fusion
  29.1 1.3 convolution_convert_fusion
  30.5 2.5 %collective-permute-start.16 = (bf16[256,1792]{1,0:T(8,128)(2,1)}, bf16[256,1792]{1,0:T(8,128)(2,1)}, u32[]{:S(2)}, u32[]{:S(2)}) collective-permute-start(bf16[256,1792]{1,0:T(8,128)(2,1)} %convolution_convert_fusion), channel_id=1, source_target_pairs={{0,4},{4,0},{8,12},{12,8},{16,20},{20,16},{24,28},{28,24},{32,36},... | collective-permute-start | bytes 2752520 | tf_op jit(solution)/shard_map/ppermute | solution.py:276
  33.0 2.0 %collective-permute-start.6 = (bf16[1792,256]{1,0:T(8,128)(2,1)}, bf16[1792,256]{1,0:T(8,128)(2,1)}, u32[]{:S(2)}, u32[]{:S(2)}) collective-permute-start(bf16[1792,256]{1,0:T(8,128)(2,1)} %get-tuple-element.21), channel_id=1, source_target_pairs={{0,3},{1,0},{2,1},{3,2},{4,7},{5,4},{6,5},{7,6},{8,11},{9,8},{10,9... | collective-permute-start | bytes 2752520 | tf_op jit(solution)/shard_map/ppermute | solution.py:18
  35.0 3.5 %choose.2 = bf16[1792,256]{1,0:T(8,128)(2,1)} custom-call(s32[1]{0:T(128)} %bitcast.15.which, bf16[1792,256]{1,0:T(8,128)(2,1)} %collective-permute-done.3.first.refs_3_, bf16[1792,256]{1,0:T(8,128)(2,1)} %collective-permute-done.2.second.refs_1_), custom_call_target="tpu_custom_call" | custom-call | flops 199999995904 | bytes 2752512 | tf_op jit(solution)/shard_map/choose/pallas_call | solution.py:132
  38.6 2.7 %collective-permute-start.4 = (bf16[1792,256]{1,0:T(8,128)(2,1)}, bf16[1792,256]{1,0:T(8,128)(2,1)}, u32[]{:S(2)}, u32[]{:S(2)}) collective-permute-start(bf16[1792,256]{1,0:T(8,128)(2,1)} %choose.2), channel_id=1, source_target_pairs={{0,1},{1,0},{2,3},{3,2},{5,6},{6,5},{7,4},{4,7},{8,9},{9,8},{10,11... | collective-permute-start | bytes 2752520 | tf_op jit(solution)/shard_map/ppermute | solution.py:305
  41.3 9.2 %all-to-all-done = bf16[32,8,1792]{2,1,0:T(8,128)(2,1)} async-done(((bf16[32,8,1792]{2,1,0:T(8,128)(2,1)}), bf16[32,8,1792]{2,1,0:T(8,128)(2,1)}, u32[]{:S(2)}, u32[]{:S(2)}) %all-to-all-start) | async-done | bytes 917536 | tf_op jit(solution)/shard_map/all_to_all | solution.py:331
  50.4 6.7 %all-to-all-start.2 = ((bf16[32,8,1792]{2,1,0:T(8,128)(2,1)}), bf16[32,8,1792]{2,1,0:T(8,128)(2,1)}, u32[]{:S(2)}, u32[]{:S(2)}) async-start(bf16[32,8,1792]{2,1,0:T(8,128)(2,1)} %bitcast.28), calls=%async_computation.2 | async-start | bytes 1835008 | tf_op jit(solution)/shard_map/all_to_all | solution.py:331
  57.2 0.6 collective-permute-done.7.first.refs_3_
  57.7 3.6 %choose.3 = bf16[1792,256]{1,0:T(8,128)(2,1)} custom-call(s32[1]{0:T(128)} %bitcast.15.which, bf16[1792,256]{1,0:T(8,128)(2,1)} %collective-permute-done.7.first.refs_3_, bf16[1792,256]{1,0:T(8,128)(2,1)} %collective-permute-done.6.second.refs_1_), custom_call_target="tpu_custom_call" | custom-call | flops 199999995904 | bytes 2752512 | tf_op jit(solution)/shard_map/choose/pallas_call | solution.py:132
  61.3 1.3 collective-permute-start.8
  62.5 6.2 %collective-permute-done.4.refs_2_ = bf16[1792,256]{1,0:T(8,128)(2,1)} collective-permute-done((bf16[1792,256]{1,0:T(8,128)(2,1)}, bf16[1792,256]{1,0:T(8,128)(2,1)}, u32[]{:S(2)}, u32[]{:S(2)}) %collective-permute-start.4) | collective-permute-done | bytes 917536 | tf_op jit(solution)/shard_map/ppermute | solution.py:305
  68.7 4.5 %up_project.2 = (f32[4,256,256]{2,1,0:T(8,128)}, bf16[4,256,256]{2,1,0:T(8,128)(2,1)}) custom-call(bf16[256,1792]{1,0:T(8,128)(2,1)} %bitcast.11.rows, bf16[1792,256]{1,0:T(8,128)(2,1)} %get-tuple-element.39.refs_0_, bf16[1792,256]{1,0:T(8,128)(2,1)} %collective-permute-done.2.second.refs_1_, bf16[1792,256]{1,0:T(8,128)(2,1)} %collective-permute-done.4.refs_2_, ...), custom_call_target="tpu_custom_call" | custom-call | flops 939524096 | bytes 9000000 | tf_op jit(solution)/shard_map/up_project/pallas_call | solution.py:158
  74.0 9.0 %collective-permute-done.5.theirs = bf16[4,256,256]{2,1,0:T(8,128)(2,1)S(1)} collective-permute-done((bf16[4,256,256]{2,1,0:T(8,128)(2,1)}, bf16[4,256,256]{2,1,0:T(8,128)(2,1)S(1)}, u32[]{:S(2)}, u32[]{:S(2)}) %collective-permute-start.5) | collective-permute-done | bytes 524320 | tf_op jit(solution)/shard_map/ppermute | solution.py:273
  83.0 1.2 copy-done.1
  84.2 3.7 %down_project.2 = bf16[256,1792]{1,0:T(8,128)(2,1)} custom-call(s32[1]{0:T(128)} %bitcast.5.shift, f32[4,256,256]{2,1,0:T(8,128)S(1)} %copy-done.1, bf16[4,256,256]{2,1,0:T(8,128)(2,1)S(1)} %collective-permute-done.5.theirs, bf16[1792,256]{1,0:T(8,128)(2,1)S(1)} %get-tuple-element.36.refs_0_, bf16[1792,256]{1,0:T(8,128)(2,1)} %collective-permute-done.6.second.refs_1_, ...), custom_call_target="tpu_custom_call" | custom-call | flops 939524096 | bytes 9000000 | tf_op jit(solution)/shard_map/down_project/pallas_call | solution.py:201
  88.0 0.9 dynamic-slice_bitcast_fusion.6
  88.9 11.3 %all-to-all-start.1 = ((bf16[32,8,1792]{2,1,0:T(8,128)(2,1)}), bf16[32,8,1792]{2,1,0:T(8,128)(2,1)}, u32[]{:S(2)}, u32[]{:S(2)}) async-start(bf16[32,8,1792]{2,1,0:T(8,128)(2,1)} %bitcast.25), calls=%async_computation.1 | async-start | bytes 1835008 | tf_op jit(solution)/shard_map/all_to_all | solution.py:331
  100.2 4.6 %up_project.3 = (f32[4,256,256]{2,1,0:T(8,128)}, bf16[4,256,256]{2,1,0:T(8,128)(2,1)}) custom-call(bf16[256,1792]{1,0:T(8,128)(2,1)} %bitcast.29.rows, bf16[1792,256]{1,0:T(8,128)(2,1)} %get-tuple-element.39.refs_0_, bf16[1792,256]{1,0:T(8,128)(2,1)} %collective-permute-done.2.second.refs_1_, bf16[1792,256]{1,0:T(8,128)(2,1)} %collective-permute-done.4.refs_2_, ...), custom_call_target="tpu_custom_call" | custom-call | flops 939524096 | bytes 9000000 | tf_op jit(solution)/shard_map/up_project/pallas_call | solution.py:158
  104.8 0.1 maximum_maximum_fusion
  104.9 0.4 collective-permute-start.11
  105.3 2.9 %collective-permute-start.10 = (bf16[80,576]{1,0:T(8,128)(2,1)S(1)}, bf16[80,576]{1,0:T(8,128)(2,1)S(1)}, u32[]{:S(2)}, u32[]{:S(2)}) collective-permute-start(bf16[80,576]{1,0:T(8,128)(2,1)S(1)} %maximum_maximum_fusion), channel_id=1, source_target_pairs={{0,2},{1,3},{2,0},{3,1},{4,6},{5,7},{6,4},{7,5},{8,10},{9,11},{10,... | collective-permute-start | bytes 276488 | tf_op jit(solution)/shard_map/ppermute | solution.py:18
  108.9 7.8 %collective-permute-done.11 = bf16[80,576]{1,0:T(8,128)(2,1)S(1)} collective-permute-done((bf16[80,576]{1,0:T(8,128)(2,1)S(1)}, bf16[80,576]{1,0:T(8,128)(2,1)S(1)}, u32[]{:S(2)}, u32[]{:S(2)}) %collective-permute-start.11) | collective-permute-done | bytes 92192 | tf_op jit(solution)/shard_map/ppermute | solution.py:18
  116.7 0.1 select_select_fusion
  116.9 1.2 copy-done
  118.2 3.1 %down_project.3 = bf16[256,1792]{1,0:T(8,128)(2,1)S(1)} custom-call(s32[1]{0:T(128)} %bitcast.5.shift, f32[4,256,256]{2,1,0:T(8,128)S(1)} %copy-done, bf16[4,256,256]{2,1,0:T(8,128)(2,1)S(1)} %collective-permute-done.17.theirs, bf16[1792,256]{1,0:T(8,128)(2,1)S(1)} %get-tuple-element.36.refs_0_, bf16[1792,256]{1,0:T(8,128)(2,1)} %collective-permute-done.6.second.refs_1_, ...), custom_call_target="tpu_custom_call" | custom-call | flops 939524096 | bytes 9000000 | tf_op jit(solution)/shard_map/down_project/pallas_call | solution.py:201
  121.2 3.9 %collective-permute-start.18 = (bf16[256,1792]{1,0:T(8,128)(2,1)S(1)}, bf16[256,1792]{1,0:T(8,128)(2,1)}, u32[]{:S(2)}, u32[]{:S(2)}) collective-permute-start(bf16[256,1792]{1,0:T(8,128)(2,1)S(1)} %down_project.3), channel_id=1, source_target_pairs={{0,4},{4,0},{8,12},{12,8},{16,20},{20,16},{24,28},{28,24},{32,36},... | collective-permute-start | bytes 2752520 | tf_op jit(solution)/shard_map/ppermute | solution.py:276
  125.2 0.1 select_reduce_fusion.3
  125.4 0.1 min.15
  125.6 0.1 select_reduce_fusion.2.pages
  125.7 1.7 collective-permute-done.18
  127.4 9.3 %all-to-all-start.3 = ((bf16[32,8,1792]{2,1,0:T(8,128)(2,1)}), bf16[32,8,1792]{2,1,0:T(8,128)(2,1)S(1)}, u32[]{:S(2)}, u32[]{:S(2)}) async-start(bf16[32,8,1792]{2,1,0:T(8,128)(2,1)} %bitcast.30), calls=%async_computation.3 | async-start | bytes 1835008 | tf_op jit(solution)/shard_map/all_to_all | solution.py:331
  136.7 1.7 %copy-done.3 = bf16[32,64,576]{2,1,0:T(8,128)(2,1)S(1)} copy-done((bf16[32,64,576]{2,1,0:T(8,128)(2,1)S(1)}, bf16[32,64,576]{2,1,0:T(8,128)(2,1)}, u32[]{:S(2)}) %copy-start.3) | copy-done | bytes 2359320
  138.4 1.3 copy-done.4
  139.7 19.0 %attention.1 = (bf16[16,64,512]{2,1,0:T(8,128)(2,1)}, bf16[16,64,512]{2,1,0:T(8,128)(2,1)}, bf16[64,512]{1,0:T(8,128)(2,1)S(1)}) custom-call(s32[16]{0:T(128)S(1)} %bitcast.61, s32[128]{0:T(128)S(1)} %select_reduce_fusion.2.pages, s32[1]{0:T(128)} %bitcast.56.moved, bf16[16,64,576]{2,1,0:T(8,128)(2,1)S(1)} %copy-done.4, bf16[16,64,576]{2,1,0:T(8,128)(2,1)S(1)} %copy-done.2, ...), custom_call_target="tpu_custom_call" | custom-call | flops 12000000000 | bytes 8000000 | tf_op jit(solution)/shard_map/attention/pallas_call | solution.py:89
  158.7 0.1 collective-permute-start.12
  158.8 2.7 %collective-permute-start.14 = (bf16[64,512]{1,0:T(8,128)(2,1)S(1)}, bf16[64,512]{1,0:T(8,128)(2,1)S(1)}, u32[]{:S(2)}, u32[]{:S(2)}) collective-permute-start(bf16[64,512]{1,0:T(8,128)(2,1)S(1)} %get-tuple-element.48), channel_id=1, source_target_pairs={{0,3},{1,0},{2,1},{3,2},{4,7},{5,4},{6,5},{7,6},{8,11},{9,8},{10,9... | collective-permute-start | bytes 196616 | tf_op jit(solution)/shard_map/ppermute | solution.py:18
  161.5 1.5 fusion.4
  163.0 0.7 collective-permute-start.15
  163.6 0.3 fusion.2
  164.0 2.8 %collective-permute-start.19 = (f32[16,1792]{1,0:T(8,128)S(1)}, f32[16,1792]{1,0:T(8,128)S(1)}, u32[]{:S(2)}, u32[]{:S(2)}) collective-permute-start(f32[16,1792]{1,0:T(8,128)S(1)} %slice.132), channel_id=1, source_target_pairs={{2,3},{3,2},{0,1},{1,0},{5,6},{6,5},{7,4},{4,7},{10,11},{11,10},{8... | collective-permute-start | bytes 344072 | tf_op jit(solution)/shard_map/ppermute | solution.py:273
  166.7 0.7 bitcast_dynamic-update-slice_fusion
  167.4 2.8 %collective-permute-done.19 = f32[16,1792]{1,0:T(8,128)S(1)} collective-permute-done((f32[16,1792]{1,0:T(8,128)S(1)}, f32[16,1792]{1,0:T(8,128)S(1)}, u32[]{:S(2)}, u32[]{:S(2)}) %collective-permute-start.19) | collective-permute-done | bytes 114720 | tf_op jit(solution)/shard_map/ppermute | solution.py:273
  170.3 0.7 pad_maximum_fusion.2
  (82 shorter events, 1.2 us)
Async XLA Ops:
  3.2 10.1 %collective-permute-start.1 = (bf16[16,1920]{1,0:T(8,128)(2,1)S(1)}, bf16[16,1920]{1,0:T(8,128)(2,1)S(1)}, u32[]{:S(2)}, u32[]{:S(2)}) collective-permute-start(bf16[16,1920]{1,0:T(8,128)(2,1)S(1)} %get-tuple-element.64), channel_id=1, source_target_pairs={{2,3},{3,2},{0,1},{1,0},{5,6},{6,5},{7,4},{4,7},{10,11},{11,10},{8... | collective-permute-start | bytes 184328 | tf_op jit(solution)/shard_map/ppermute | solution.py:273
  6.8 6.6 %collective-permute-start = (bf16[16,1920]{1,0:T(8,128)(2,1)S(1)}, bf16[16,1920]{1,0:T(8,128)(2,1)S(1)}, u32[]{:S(2)}, u32[]{:S(2)}) collective-permute-start(bf16[16,1920]{1,0:T(8,128)(2,1)S(1)} %get-tuple-element.65), channel_id=1, source_target_pairs={{1,2},{2,1},{3,0},{0,3},{6,7},{7,6},{4,5},{5,4},{9,10},{10,9},{11,... | collective-permute-start | bytes 184328 | tf_op jit(solution)/shard_map/ppermute | solution.py:273
  6.8 5.0 %copy-start.6 = (bf16[1,3584,256]{2,1,0:T(8,128)(2,1)S(1)}, bf16[1,3584,256]{2,1,0:T(8,128)(2,1)}, u32[]{:S(2)}) copy-start(bf16[1,3584,256]{2,1,0:T(8,128)(2,1)} %param.18) | copy-start | bytes 5505028
  10.3 22.7 %collective-permute-start.2 = (bf16[1792,256]{1,0:T(8,128)(2,1)}, bf16[1792,256]{1,0:T(8,128)(2,1)}, u32[]{:S(2)}, u32[]{:S(2)}) collective-permute-start(bf16[1792,256]{1,0:T(8,128)(2,1)} %get-tuple-element.17), channel_id=1, source_target_pairs={{0,3},{1,0},{2,1},{3,2},{4,7},{5,4},{6,5},{7,6},{8,11},{9,8},{10,9... | collective-permute-start | bytes 2752520 | tf_op jit(solution)/shard_map/ppermute | solution.py:18
  10.9 22.1 %collective-permute-start.3 = (bf16[1792,256]{1,0:T(8,128)(2,1)}, bf16[1792,256]{1,0:T(8,128)(2,1)}, u32[]{:S(2)}, u32[]{:S(2)}) collective-permute-start(bf16[1792,256]{1,0:T(8,128)(2,1)} %get-tuple-element.18), channel_id=1, source_target_pairs={{0,1},{1,2},{2,3},{3,0},{4,5},{5,6},{6,7},{7,4},{8,9},{9,10},{10,1... | collective-permute-start | bytes 2752520 | tf_op jit(solution)/shard_map/ppermute | solution.py:18
  11.8 1.7 %copy-start.9 = (s32[16,8]{0,1:T(8,128)S(1)}, s32[16,8]{0,1:T(8,128)}, u32[]{:S(2)}) copy-start(s32[16,8]{0,1:T(8,128)} %param.15) | copy-start | bytes 1540
  11.8 2.6 %copy-start.12 = (f32[16,8]{0,1:T(8,128)S(1)}, f32[16,8]{0,1:T(8,128)}, u32[]{:S(2)}) copy-start(f32[16,8]{0,1:T(8,128)} %param.16) | copy-start | bytes 1540
  17.1 33.3 %all-to-all-start = ((bf16[32,8,1792]{2,1,0:T(8,128)(2,1)}), bf16[32,8,1792]{2,1,0:T(8,128)(2,1)}, u32[]{:S(2)}, u32[]{:S(2)}) async-start(bf16[32,8,1792]{2,1,0:T(8,128)(2,1)} %fusion), calls=%async_computation | async-start | bytes 1835008 | tf_op jit(solution)/shard_map/all_to_all | solution.py:331
  30.5 10.8 %collective-permute-start.16 = (bf16[256,1792]{1,0:T(8,128)(2,1)}, bf16[256,1792]{1,0:T(8,128)(2,1)}, u32[]{:S(2)}, u32[]{:S(2)}) collective-permute-start(bf16[256,1792]{1,0:T(8,128)(2,1)} %convolution_convert_fusion), channel_id=1, source_target_pairs={{0,4},{4,0},{8,12},{12,8},{16,20},{20,16},{24,28},{28,24},{32,36},... | collective-permute-start | bytes 2752520 | tf_op jit(solution)/shard_map/ppermute | solution.py:276
  33.0 24.1 %collective-permute-start.6 = (bf16[1792,256]{1,0:T(8,128)(2,1)}, bf16[1792,256]{1,0:T(8,128)(2,1)}, u32[]{:S(2)}, u32[]{:S(2)}) collective-permute-start(bf16[1792,256]{1,0:T(8,128)(2,1)} %get-tuple-element.21), channel_id=1, source_target_pairs={{0,3},{1,0},{2,1},{3,2},{4,7},{5,4},{6,5},{7,6},{8,11},{9,8},{10,9... | collective-permute-start | bytes 2752520 | tf_op jit(solution)/shard_map/ppermute | solution.py:18
  35.0 22.7 %collective-permute-start.7 = (bf16[1792,256]{1,0:T(8,128)(2,1)}, bf16[1792,256]{1,0:T(8,128)(2,1)}, u32[]{:S(2)}, u32[]{:S(2)}) collective-permute-start(bf16[1792,256]{1,0:T(8,128)(2,1)} %get-tuple-element.22), channel_id=1, source_target_pairs={{0,1},{1,2},{2,3},{3,0},{4,5},{5,6},{6,7},{7,4},{8,9},{9,10},{10,1... | collective-permute-start | bytes 2752520 | tf_op jit(solution)/shard_map/ppermute | solution.py:18
  38.6 30.2 %collective-permute-start.4 = (bf16[1792,256]{1,0:T(8,128)(2,1)}, bf16[1792,256]{1,0:T(8,128)(2,1)}, u32[]{:S(2)}, u32[]{:S(2)}) collective-permute-start(bf16[1792,256]{1,0:T(8,128)(2,1)} %choose.2), channel_id=1, source_target_pairs={{0,1},{1,0},{2,3},{3,2},{5,6},{6,5},{7,4},{4,7},{8,9},{9,8},{10,11... | collective-permute-start | bytes 2752520 | tf_op jit(solution)/shard_map/ppermute | solution.py:305
  50.4 38.5 %all-to-all-start.2 = ((bf16[32,8,1792]{2,1,0:T(8,128)(2,1)}), bf16[32,8,1792]{2,1,0:T(8,128)(2,1)}, u32[]{:S(2)}, u32[]{:S(2)}) async-start(bf16[32,8,1792]{2,1,0:T(8,128)(2,1)} %bitcast.28), calls=%async_computation.2 | async-start | bytes 1835008 | tf_op jit(solution)/shard_map/all_to_all | solution.py:331
  61.3 21.7 %collective-permute-start.8 = (bf16[1792,256]{1,0:T(8,128)(2,1)}, bf16[1792,256]{1,0:T(8,128)(2,1)S(1)}, u32[]{:S(2)}, u32[]{:S(2)}) collective-permute-start(bf16[1792,256]{1,0:T(8,128)(2,1)} %choose.3), channel_id=1, source_target_pairs={{0,1},{1,0},{2,3},{3,2},{5,6},{6,5},{7,4},{4,7},{8,9},{9,8},{10,11... | collective-permute-start | bytes 2752520 | tf_op jit(solution)/shard_map/ppermute | solution.py:305
  73.3 9.7 %collective-permute-start.5 = (bf16[4,256,256]{2,1,0:T(8,128)(2,1)}, bf16[4,256,256]{2,1,0:T(8,128)(2,1)S(1)}, u32[]{:S(2)}, u32[]{:S(2)}) collective-permute-start(bf16[4,256,256]{2,1,0:T(8,128)(2,1)} %get-tuple-element.20), channel_id=1, source_target_pairs={{1,2},{2,1},{3,0},{0,3},{6,7},{7,6},{4,5},{5,4},{9,10},{10,9},{11,... | collective-permute-start | bytes 1572872 | tf_op jit(solution)/shard_map/ppermute | solution.py:273
  83.0 1.2 copy-start.1
  84.2 3.7 %copy-start.10 = (bf16[16,576]{1,0:T(8,128)(2,1)S(1)}, bf16[16,576]{1,0:T(8,128)(2,1)}, u32[]{:S(2)}) copy-start(bf16[16,576]{1,0:T(8,128)(2,1)} %param.22) | copy-start | bytes 55300
  88.9 38.5 %all-to-all-start.1 = ((bf16[32,8,1792]{2,1,0:T(8,128)(2,1)}), bf16[32,8,1792]{2,1,0:T(8,128)(2,1)}, u32[]{:S(2)}, u32[]{:S(2)}) async-start(bf16[32,8,1792]{2,1,0:T(8,128)(2,1)} %bitcast.25), calls=%async_computation.1 | async-start | bytes 1835008 | tf_op jit(solution)/shard_map/all_to_all | solution.py:331
  104.8 12.1 %collective-permute-start.17 = (bf16[4,256,256]{2,1,0:T(8,128)(2,1)}, bf16[4,256,256]{2,1,0:T(8,128)(2,1)S(1)}, u32[]{:S(2)}, u32[]{:S(2)}) collective-permute-start(bf16[4,256,256]{2,1,0:T(8,128)(2,1)} %get-tuple-element.29), channel_id=1, source_target_pairs={{1,2},{2,1},{3,0},{0,3},{6,7},{7,6},{4,5},{5,4},{9,10},{10,9},{11,... | collective-permute-start | bytes 1572872 | tf_op jit(solution)/shard_map/ppermute | solution.py:273
  104.9 11.8 %collective-permute-start.11 = (bf16[80,576]{1,0:T(8,128)(2,1)S(1)}, bf16[80,576]{1,0:T(8,128)(2,1)S(1)}, u32[]{:S(2)}, u32[]{:S(2)}) collective-permute-start(bf16[80,576]{1,0:T(8,128)(2,1)S(1)} %maximum_maximum_fusion), channel_id=1, source_target_pairs={{0,3},{1,0},{2,1},{3,2},{4,7},{5,4},{6,5},{7,6},{8,11},{9,8},{10,9... | collective-permute-start | bytes 276488 | tf_op jit(solution)/shard_map/ppermute | solution.py:18
  105.3 11.4 %collective-permute-start.10 = (bf16[80,576]{1,0:T(8,128)(2,1)S(1)}, bf16[80,576]{1,0:T(8,128)(2,1)S(1)}, u32[]{:S(2)}, u32[]{:S(2)}) collective-permute-start(bf16[80,576]{1,0:T(8,128)(2,1)S(1)} %maximum_maximum_fusion), channel_id=1, source_target_pairs={{0,2},{1,3},{2,0},{3,1},{4,6},{5,7},{6,4},{7,5},{8,10},{9,11},{10,... | collective-permute-start | bytes 276488 | tf_op jit(solution)/shard_map/ppermute | solution.py:18
  108.2 8.5 %collective-permute-start.9 = (bf16[80,576]{1,0:T(8,128)(2,1)S(1)}, bf16[80,576]{1,0:T(8,128)(2,1)S(1)}, u32[]{:S(2)}, u32[]{:S(2)}) collective-permute-start(bf16[80,576]{1,0:T(8,128)(2,1)S(1)} %maximum_maximum_fusion), channel_id=1, source_target_pairs={{0,1},{1,2},{2,3},{3,0},{4,5},{5,6},{6,7},{7,4},{8,9},{9,10},{10,1... | collective-permute-start | bytes 276488 | tf_op jit(solution)/shard_map/ppermute | solution.py:18
  116.9 1.2 copy-start
  118.1 7.0 %copy-start.5 = (s32[1,16]{1,0:T(1,128)S(1)}, s32[1,16]{1,0:T(1,128)}, u32[]{:S(2)}) copy-start(s32[1,16]{1,0:T(1,128)} %param.24) | copy-start | bytes 196
  118.1 7.3 %copy-start.11 = (bf16[16,576]{1,0:T(8,128)(2,1)S(1)}, bf16[16,576]{1,0:T(8,128)(2,1)}, u32[]{:S(2)}) copy-start(bf16[16,576]{1,0:T(8,128)(2,1)} %param.20) | copy-start | bytes 55300
  118.1 7.4 %copy-start.13 = (s32[1,32]{1,0:T(1,128)S(1)}, s32[1,32]{1,0:T(1,128)}, u32[]{:S(2)}) copy-start(s32[1,32]{1,0:T(1,128)} %param.25) | copy-start | bytes 388
  118.1 7.5 %copy-start.8 = (f32[32,256]{1,0:T(8,128)S(1)}, f32[32,256]{1,0:T(8,128)}, u32[]{:S(2)}) copy-start(f32[32,256]{1,0:T(8,128)} %get-tuple-element.33) | copy-start | bytes 98308
  118.1 7.5 %copy-start.7 = (f32[32,256]{1,0:T(8,128)S(1)}, f32[32,256]{1,0:T(8,128)}, u32[]{:S(2)}) copy-start(f32[32,256]{1,0:T(8,128)} %get-tuple-element.31) | copy-start | bytes 98308
  121.2 15.4 %copy-start.2 = (bf16[16,64,576]{2,1,0:T(8,128)(2,1)S(1)}, bf16[16,64,576]{2,1,0:T(8,128)(2,1)}, u32[]{:S(2)}) copy-start(bf16[16,64,576]{2,1,0:T(8,128)(2,1)} %q_two.1) | copy-start | bytes 3538948
  121.2 6.1 %collective-permute-start.18 = (bf16[256,1792]{1,0:T(8,128)(2,1)S(1)}, bf16[256,1792]{1,0:T(8,128)(2,1)}, u32[]{:S(2)}, u32[]{:S(2)}) collective-permute-start(bf16[256,1792]{1,0:T(8,128)(2,1)S(1)} %down_project.3), channel_id=1, source_target_pairs={{0,4},{4,0},{8,12},{12,8},{16,20},{20,16},{24,28},{28,24},{32,36},... | collective-permute-start | bytes 2752520 | tf_op jit(solution)/shard_map/ppermute | solution.py:276
  127.4 36.3 %all-to-all-start.3 = ((bf16[32,8,1792]{2,1,0:T(8,128)(2,1)}), bf16[32,8,1792]{2,1,0:T(8,128)(2,1)S(1)}, u32[]{:S(2)}, u32[]{:S(2)}) async-start(bf16[32,8,1792]{2,1,0:T(8,128)(2,1)} %bitcast.30), calls=%async_computation.3 | async-start | bytes 1835008 | tf_op jit(solution)/shard_map/all_to_all | solution.py:331
  136.7 1.7 %copy-start.3 = (bf16[32,64,576]{2,1,0:T(8,128)(2,1)S(1)}, bf16[32,64,576]{2,1,0:T(8,128)(2,1)}, u32[]{:S(2)}) copy-start(bf16[32,64,576]{2,1,0:T(8,128)(2,1)} %pool.1) | copy-start | bytes 7077892
  138.4 1.3 copy-start.4
  158.7 8.0 %collective-permute-start.12 = (bf16[64,512]{1,0:T(8,128)(2,1)S(1)}, bf16[64,512]{1,0:T(8,128)(2,1)S(1)}, u32[]{:S(2)}, u32[]{:S(2)}) collective-permute-start(bf16[64,512]{1,0:T(8,128)(2,1)S(1)} %get-tuple-element.47), channel_id=1, source_target_pairs={{0,1},{1,2},{2,3},{3,0},{4,5},{5,6},{6,7},{7,4},{8,9},{9,10},{10,1... | collective-permute-start | bytes 196616 | tf_op jit(solution)/shard_map/ppermute | solution.py:18
  158.8 8.0 %collective-permute-start.14 = (bf16[64,512]{1,0:T(8,128)(2,1)S(1)}, bf16[64,512]{1,0:T(8,128)(2,1)S(1)}, u32[]{:S(2)}, u32[]{:S(2)}) collective-permute-start(bf16[64,512]{1,0:T(8,128)(2,1)S(1)} %get-tuple-element.48), channel_id=1, source_target_pairs={{0,3},{1,0},{2,1},{3,2},{4,7},{5,4},{6,5},{7,6},{8,11},{9,8},{10,9... | collective-permute-start | bytes 196616 | tf_op jit(solution)/shard_map/ppermute | solution.py:18
  161.5 5.3 %collective-permute-start.13 = (bf16[64,512]{1,0:T(8,128)(2,1)S(1)}, bf16[64,512]{1,0:T(8,128)(2,1)S(1)}, u32[]{:S(2)}, u32[]{:S(2)}) collective-permute-start(bf16[64,512]{1,0:T(8,128)(2,1)S(1)} %get-tuple-element.49), channel_id=1, source_target_pairs={{0,2},{1,3},{2,0},{3,1},{4,6},{5,7},{6,4},{7,5},{8,10},{9,11},{10,... | collective-permute-start | bytes 196616 | tf_op jit(solution)/shard_map/ppermute | solution.py:18
  163.0 4.5 %collective-permute-start.15 = (f32[16,1792]{1,0:T(8,128)S(1)}, f32[16,1792]{1,0:T(8,128)S(1)}, u32[]{:S(2)}, u32[]{:S(2)}) collective-permute-start(f32[16,1792]{1,0:T(8,128)S(1)} %slice.125), channel_id=1, source_target_pairs={{1,2},{2,1},{3,0},{0,3},{6,7},{7,6},{4,5},{5,4},{9,10},{10,9},{11,... | collective-permute-start | bytes 344072 | tf_op jit(solution)/shard_map/ppermute | solution.py:273
  164.0 6.3 %collective-permute-start.19 = (f32[16,1792]{1,0:T(8,128)S(1)}, f32[16,1792]{1,0:T(8,128)S(1)}, u32[]{:S(2)}, u32[]{:S(2)}) collective-permute-start(f32[16,1792]{1,0:T(8,128)S(1)} %slice.132), channel_id=1, source_target_pairs={{2,3},{3,2},{0,1},{1,0},{5,6},{6,5},{7,4},{4,7},{10,11},{11,10},{8... | collective-permute-start | bytes 344072 | tf_op jit(solution)/shard_map/ppermute | solution.py:273

commit v11 on v8

--- a/solution.py
+++ b/solution.py
@@ -142,25 +142,30 @@
     )(which, first, second)
 
 
-def up_kernel(rows, *refs):
-    weights, (whole, sent) = refs[:4], refs[4:]
+def up_kernel(_, rows, *refs):
+    weights, (whole, sent) = refs[:-2], refs[-2:]
     for i, weight in enumerate(weights):
         part = jnp.dot(rows[...], weight[...], preferred_element_type=jnp.float32)
         whole[i] = part
         sent[i] = part.astype(jnp.bfloat16)
 
 
-def up_project(rows, weights, steps):
+def up_project(which, rows, weights, steps):
     count, depth = rows.shape
     units = weights[0].shape[1]
     shape = (len(weights), count, units)
-    out = pl.BlockSpec((len(weights), count // steps, units), lambda k: (0, k, 0))
+    out = pl.BlockSpec((len(weights), count // steps, units), lambda k, *_: (0, k, 0))
+    halves = pl.BlockSpec((depth, units), lambda k, half: (half[0], 0))
+    whole = pl.BlockSpec((depth, units), lambda k, *_: (0, 0))
     return pl.pallas_call(
         up_kernel,
-        grid=(steps,),
-        in_specs=[pl.BlockSpec((count // steps, depth), lambda k: (k, 0))]
-        + [pl.BlockSpec((depth, units), lambda k: (0, 0))] * len(weights),
-        out_specs=[out, out],
+        grid_spec=pltpu.PrefetchScalarGridSpec(
+            num_scalar_prefetch=1,
+            grid=(steps,),
+            in_specs=[pl.BlockSpec((count // steps, depth), lambda k, *_: (k, 0))]
+            + [whole if w.shape[0] == depth else halves for w in weights],
+            out_specs=[out, out],
+        ),
         out_shape=[
             jax.ShapeDtypeStruct(shape, jnp.float32),
             jax.ShapeDtypeStruct(shape, jnp.bfloat16),
@@ -168,20 +173,23 @@
         compiler_params=pltpu.CompilerParams(vmem_limit_bytes=58 * 1024 * 1024),
         cost_estimate=pl.CostEstimate(
             flops=2 * len(weights) * count * depth * units,
-            bytes_accessed=9_000_000,
+            bytes_accessed=5_000_000,
             transcendentals=0,
         ),
         name="up_project",
-    )(rows, *weights)
-
-
-def down_kernel(shift, mine, theirs, *refs):
+    )(which, rows, *weights)
+
+
+def down_kernel(scalars, mine_a, mine_b, theirs_a, theirs_b, *refs):
     weights, out, held = refs[:4], refs[4], refs[5]
 
     @pl.when(pl.program_id(0) == 0)
     def _():
-        for i in range(len(weights)):
-            other = theirs[lax.rem(i + shift[0], len(weights))].astype(jnp.float32)
+        mine = [mine_a[0], mine_a[1], mine_b[0], mine_b[1]]
+        theirs = [theirs_a.at[0], theirs_a.at[1], theirs_b.at[0], theirs_b.at[1]]
+        for i in range(4):
+            up, down = theirs[(i + 1) % 4][...], theirs[(i - 1) % 4][...]
+            other = jnp.where(scalars[1] == 1, up.astype(jnp.float32), down.astype(jnp.float32))
             value = mine[i] + other
             held[i] = (value / (1.0 + jnp.exp(-value))).astype(jnp.bfloat16)
 
@@ -194,29 +202,31 @@
     out[...] = total.astype(jnp.bfloat16)
 
 
-def down_project(shift, mine, theirs, weights, steps):
-    count, units = mine.shape[1:]
-    depth = weights[0].shape[0]
-    whole = pl.BlockSpec(mine.shape, lambda k, *_: (0, 0, 0))
+def down_project(scalars, mine, theirs, weights, steps):
+    count, units = mine[0].shape[1:]
+    depth = weights[1].shape[0]
+    whole = pl.BlockSpec(mine[0].shape, lambda k, *_: (0, 0, 0))
+    tile = (depth // steps, units)
     return pl.pallas_call(
         down_kernel,
         grid_spec=pltpu.PrefetchScalarGridSpec(
             num_scalar_prefetch=1,
             grid=(steps,),
-            in_specs=[whole, whole]
-            + [pl.BlockSpec((depth // steps, units), lambda k, *_: (k, 0))] * len(weights),
+            in_specs=[whole] * 4
+            + [pl.BlockSpec(tile, lambda k, at: (at[0] * steps + k, 0))]
+            + [pl.BlockSpec(tile, lambda k, *_: (k, 0))] * 3,
             out_specs=pl.BlockSpec((count, depth // steps), lambda k, *_: (0, k)),
-            scratch_shapes=[pltpu.VMEM(mine.shape, jnp.bfloat16)],
+            scratch_shapes=[pltpu.VMEM((4, count, units), jnp.bfloat16)],
         ),
         out_shape=jax.ShapeDtypeStruct((count, depth), jnp.bfloat16),
         compiler_params=pltpu.CompilerParams(vmem_limit_bytes=24 * 1024 * 1024),
         cost_estimate=pl.CostEstimate(
-            flops=2 * len(weights) * count * depth * units,
+            flops=8 * count * depth * units,
             bytes_accessed=9_000_000,
-            transcendentals=mine.size,
+            transcendentals=4 * count * units,
         ),
         name="down_project",
-    )(shift, mine, theirs, *weights)
+    )(scalars, *mine, *theirs, *weights)
 
 
 def page_table(cache_len, page_perm, page_rows, pool_pages):
@@ -272,30 +282,38 @@
     def part(value, which, axis):
         return lax.dynamic_slice_in_dim(value, which * half, half, axis)
 
-    rows, id_list = [], [expert_ids]
+    rows, id_list, gate_list = [], [expert_ids], []
+    term = lax.reduce_precision(gate_weights, 8, 7)
+    rest = gate_weights - term
+    next_term = lax.reduce_precision(rest, 8, 7)
+    small = jnp.concatenate(
+        [expert_ids.astype(jnp.float32), term, next_term, rest - next_term], axis=1
+    ).astype(jnp.bfloat16)
+    small = jnp.pad(small, ((0, 0), (0, 128 - 4 * picks)))
     for c in range(2):
-        id_list.append(lax.ppermute(expert_ids, "grp", partner[c]))
-        rows.append(part(hidden, side[c], 1))
-        rows.append(lax.ppermute(part(hidden, 1 - side[c], 1), "grp", partner[c]))
+        sent = jnp.concatenate([part(hidden, 1 - side[c], 1), small], axis=1)
+        theirs = lax.ppermute(sent, "grp", partner[c])
+        extra = theirs[:, half : half + 4 * picks].astype(jnp.float32).reshape(samples, 4, picks)
+        id_list.append(extra[:, 0].astype(jnp.int32))
+        gate_list += [gate_weights, (extra[:, 1] + extra[:, 2]) + extra[:, 3]]
+        rows += [part(hidden, side[c], 1), theirs[:, :half]]
     rows = jnp.concatenate(rows, axis=0)
 
     ahead = jnp.where((here == 0) | (here == 3), 0, 1)
 
     def spread(weight, *first):
         to_next, to_prev = after(first, part(weight, ahead, 0), part(weight, 1 - ahead, 0))
-        return part(weight, here // 2, 0), hop(to_next, "grp", 1), hop(to_prev, "grp", -1)
+        return hop(to_next, "grp", 1), hop(to_prev, "grp", -1)
 
     def pass_on(prev, nxt, flops):
         picked = choose((here % 2)[None], prev, nxt, flops)
         far = lax.ppermute(picked, ("ep", "grp"), by_core([(0, 1), (1, 0), (2, 3), (3, 2)]))
         return far
 
-    up_own, up_prev, up_next = spread(w_up[0], rows)
+    up_prev, up_next = spread(w_up[0], rows)
     up_far = pass_on(up_prev, up_next, 200_000_000_000)
-    down_own, down_prev, down_next = spread(w_down[0], up_prev, up_next)
+    down_prev, down_next = spread(w_down[0], up_prev, up_next)
     down_far = pass_on(down_prev, down_next, 0)
-    up_all = [up_own, up_next, up_far, up_prev]
-    down_all = [down_own, down_next, down_far, down_prev]
 
     rank = 2 * capacity
     lanes_all = ep_size * rank
@@ -365,11 +383,19 @@
         arrived_out = arrived_out + hop(jnp.where(offset == r, out_moved, zero), "grp", r)
     attn_second = lax.dynamic_update_index_in_dim(attn_second, arrived_out, moved_slot, 0)
 
-    mine, rounded = up_project(arrived, up_all, 2)
-    (rounded,) = after(down_far, rounded)
-    theirs = lax.ppermute(rounded, ("ep", "grp"), by_core(PAIRS))
-    shift = jnp.where(here % 2 == 1, grp_size - 1, 1).astype(jnp.int32)
-    produced = down_project(shift[None], mine, theirs, down_all, 2)
+    scalars = jnp.stack([here // 2, 1 - here % 2]).astype(jnp.int32)
+    mine_a, sent_a = up_project(scalars, arrived, [w_up[0], up_next], 2)
+    theirs_a = lax.ppermute(sent_a, ("ep", "grp"), by_core(PAIRS))
+    mine_b, sent_b = up_project(scalars, arrived, [up_far, up_prev], 2)
+    (sent_b,) = after(down_far, sent_b)
+    theirs_b = lax.ppermute(sent_b, ("ep", "grp"), by_core(PAIRS))
+    produced = down_project(
+        scalars,
+        [mine_a, mine_b],
+        [theirs_a, theirs_b],
+        [w_down[0], down_next, down_far, down_prev],
+        2,
+    )
     returned = lax.all_to_all(
         produced.reshape(ep_size, rank, half),
         "ep",
@@ -377,16 +403,7 @@
         concat_axis=0,
         tiled=True,
     ).reshape(lanes_all, half)
-    (late_gates,) = after(outgoing, gate_weights)
-    gates = jnp.concatenate(
-        [
-            gate_weights,
-            lax.ppermute(late_gates, "grp", partner[0]),
-            gate_weights,
-            lax.ppermute(late_gates, "grp", partner[1]),
-        ],
-        axis=0,
-    )
+    gates = jnp.concatenate(gate_list, axis=0)
     mixing = jnp.sum(jnp.where(match, gates[:, :, None], 0.0), axis=1)
     high = lax.reduce_precision(mixing, 8, 7)
     mixing = jnp.concatenate([high, mixing - high], axis=0).astype(jnp.bfloat16)

time: 171 us -> 166 us (0.971)
  starting transfers between devices: 50.7 us -> 40.2 us
  Pallas kernels: 36.6 us -> 41.3 us
  other arithmetic: 2.85 us -> 5.71 us
    all_to_all x1, waiting for transfers between devices: 7.09 us -> 16.6 us  [shards(): lax.all_to_all(outgoing.reshape(ep_size, rank, half), 'ep', split_axis=0,...]
    ppermute x2, waiting for transfers between devices: 6.97 us -> 0.01 us  [pass_on(): lax.ppermute(picked, ('ep', 'grp'), by_core([(0, 1), (1, 0), (2, 3), (3,...]
    ppermute x7 -> x4, waiting for transfers between devices: 13.9 us -> 8.39 us  [the longest x1 6.31 us: shards(): theirs_b = lax.ppermute(sent_b, ('ep', 'grp'), by_core(PAIRS))]
    pallas_call x1 -> x2, Pallas kernels: 5.71 us -> 9.22 us  [up_project(): pl.pallas_call(up_kernel, grid_spec=pltpu.PrefetchScalarGridSpec(num_scal...]
    ppermute x7 -> x4, starting transfers between devices: 8.85 us -> 5.71 us  [the longest x2 3.65 us: shards(): theirs = lax.ppermute(sent, 'grp', partner[c])]
    all_to_all x1, starting transfers between devices: 12.6 us -> 9.96 us  [shards(): lax.all_to_all(produced.reshape(ep_size, rank, half), 'ep', split_axis=0,...]
    ppermute x2, starting transfers between devices: 3.03 us -> 0.77 us  [shards(): other = lax.ppermute(summed[2 * c + 1], 'grp', partner[c])]
    another operation x2 -> x5, other arithmetic: 0.05 us -> 2.05 us
  transfers between devices with their start and end apart: 23 -> 20, of which waited for: 11 -> 12; matrix products, arithmetic and copies ran while one was open for 7% -> 8% of each run, Pallas kernels for 19% -> 22%
where the time goes in v11:
time: 166 us; the launch traced here: 164 us
  waiting for transfers between devices  60.7 us (37%)
  Pallas kernels  41.3 us (25%)
  starting transfers between devices  40.2 us (24%)
  local copies, waits for them, and re-layouts  9.3 us (6%)
  other arithmetic  5.71 us (3%)
  matrix products  4.1 us (2%)
  between operations  2.37 us (1%)
    ppermute x10, waiting for transfers between devices, hop(): lax.ppermute(value, axis, [(i, (i + step) % size) for i in range(size)])  22.9 us
    pallas_call x1, Pallas kernels, attention(): pl.pallas_call(attention_kernel, grid_spec=pltpu.PrefetchScalarGridSpec(n...  18.9 us
    all_to_all x1, waiting for transfers between devices, shards(): lax.all_to_all(outgoing.reshape(ep_size, rank, half), 'ep', split_axis=0,...  16.6 us
    all_to_all x1, starting transfers between devices, shards(): lax.all_to_all(outgoing.reshape(ep_size, rank, half), 'ep', split_axis=0,...  13.3 us
    all_to_all x1, starting transfers between devices, shards(): lax.all_to_all(produced.reshape(ep_size, rank, half), 'ep', split_axis=0,...  9.96 us
    all_to_all x1, waiting for transfers between devices, shards(): lax.all_to_all(produced.reshape(ep_size, rank, half), 'ep', split_axis=0,...  9.35 us
    pallas_call x2, Pallas kernels, up_project(): pl.pallas_call(up_kernel, grid_spec=pltpu.PrefetchScalarGridSpec(num_scal...  9.22 us
    ppermute x10, starting transfers between devices, hop(): lax.ppermute(value, axis, [(i, (i + step) % size) for i in range(size)])  8.44 us
  transfers between devices with their start and end apart: 20, of which 12 were waited for; matrix products, arithmetic and copies ran while one was open for 8% of the time, Pallas kernels for 22%

profile of v11, /device:TPU:1, one launch (start us, length us, event | category | flops | bytes accessed | tf_op | source)
XLA Modules:
  0.0 163.6 jit_solution(4263951498903522711)
XLA Ops:
  0.7 0.7 convert_convert_fusion
  1.4 0.7 reduce-precision_convert_fusion.2
  2.1 0.1 copy.43
  2.2 0.9 constant_dynamic-slice_fusion.2
  3.1 3.7 %collective-permute-start = (bf16[16,1920]{1,0:T(8,128)(2,1)S(1)}, bf16[16,1920]{1,0:T(8,128)(2,1)S(1)}, u32[]{:S(2)}, u32[]{:S(2)}) collective-permute-start(bf16[16,1920]{1,0:T(8,128)(2,1)S(1)} %get-tuple-element.58), channel_id=1, source_target_pairs={{1,2},{2,1},{3,0},{0,3},{5,6},{6,5},{7,4},{4,7},{9,10},{10,9},{11,... | collective-permute-start | bytes 184328 | tf_op jit(solution)/shard_map/ppermute | solution.py:295
  6.8 2.9 %dynamic-slice_bitcast_fusion.2 = (bf16[1792,256]{1,0:T(8,128)(2,1)}, bf16[1792,256]{1,0:T(8,128)(2,1)}) fusion(bf16[1,3584,256]{2,1,0:T(8,128)(2,1)} %param.17, s32[]{:T(128)S(6)} %select_n.252, s32[]{:T(128)S(6)} %select_n.251), kind=kLoop, calls=%fused_computation.10 | loop fusion | bytes 3670024 | tf_op jit(solution)/shard_map/dynamic_slice | solution.py:283
  9.7 0.6 collective-permute-start.8
  10.4 0.8 collective-permute-start.9
  11.2 1.4 dynamic-slice_bitcast_fusion
  12.6 0.1 copy.34
  12.7 0.1 copy.36
  12.9 0.1 copy.37
  12.9 0.1 eq.111
  13.0 0.3 fusion.2
  13.4 0.1 convert_element_type.48
  13.5 0.1 multiply_add_fusion
  13.6 0.1 add_select_fusion.6
  13.7 0.1 pad_add_fusion.1
  13.8 0.1 copy.39
  13.9 0.1 pad_maximum_fusion.3
  13.9 0.1 copy.42
  14.0 1.3 select_reduce_fusion
  15.4 1.9 %convolution_convert_fusion = bf16[512,1792]{1,0:T(8,128)(2,1)} fusion(bf16[64,512]{1,0:T(8,128)(2,1)S(1)} %get-tuple-element.32, bf16[16,1792]{1,0:T(8,128)(2,1)S(1)} %slice.107, bf16[16,1792]{1,0:T(8,128)(2,1)S(1)} %get-tuple-element.46, bf16[16,1792]{1,0:T(8,128)(2,1)S(1)} %slice.106, bf16[16,1792]{1,0:T(8,128)(2,1)S(1)} %get-tuple-element.43), kind=kOutput, calls=%fused_computation | convolution fusion | flops 119275520 | bytes 2129920 | tf_op jit(solution)/shard_map/dot_general | solution.py:344
  17.2 13.3 %all-to-all-start = ((bf16[64,8,1792]{2,1,0:T(8,128)(2,1)}), bf16[64,8,1792]{2,1,0:T(8,128)(2,1)}, u32[]{:S(2)}, u32[]{:S(2)}) async-start(bf16[64,8,1792]{2,1,0:T(8,128)(2,1)} %bitcast.55), calls=%async_computation | async-start | bytes 3670016 | tf_op jit(solution)/shard_map/all_to_all | solution.py:347
  30.5 0.3 collective-permute-done.8.refs_1_.second
  30.8 0.6 collective-permute-done.9.first.refs_1_
  31.4 0.8 collective-permute-start.12
  32.3 1.9 %collective-permute-start.13 = (bf16[1792,256]{1,0:T(8,128)(2,1)}, bf16[1792,256]{1,0:T(8,128)(2,1)}, u32[]{:S(2)}, u32[]{:S(2)}) collective-permute-start(bf16[1792,256]{1,0:T(8,128)(2,1)} %get-tuple-element.28), channel_id=1, source_target_pairs={{0,3},{1,0},{2,1},{3,2},{4,7},{5,4},{6,5},{7,6},{8,11},{9,8},{10,9... | collective-permute-start | bytes 2752520 | tf_op jit(solution)/shard_map/ppermute | solution.py:18
  34.1 3.5 %choose.2 = bf16[1792,256]{1,0:T(8,128)(2,1)} custom-call(s32[1]{0:T(128)} %bitcast.23.which, bf16[1792,256]{1,0:T(8,128)(2,1)} %collective-permute-done.9.first.refs_1_, bf16[1792,256]{1,0:T(8,128)(2,1)} %copy-done.8), custom_call_target="tpu_custom_call" | custom-call | flops 199999995904 | bytes 2752512 | tf_op jit(solution)/shard_map/choose/pallas_call | solution.py:132
  37.7 13.9 %collective-permute-done.12.first.refs_3_ = bf16[1792,256]{1,0:T(8,128)(2,1)} collective-permute-done((bf16[1792,256]{1,0:T(8,128)(2,1)}, bf16[1792,256]{1,0:T(8,128)(2,1)}, u32[]{:S(2)}, u32[]{:S(2)}) %collective-permute-start.12) | collective-permute-done | bytes 917536 | tf_op jit(solution)/shard_map/ppermute | solution.py:18
  51.6 0.4 collective-permute-done.13.second.refs_1_
  52.0 3.6 %choose.3 = bf16[1792,256]{1,0:T(8,128)(2,1)} custom-call(s32[1]{0:T(128)} %bitcast.23.which, bf16[1792,256]{1,0:T(8,128)(2,1)} %collective-permute-done.12.first.refs_3_, bf16[1792,256]{1,0:T(8,128)(2,1)} %collective-permute-done.13.second.refs_1_), custom_call_target="tpu_custom_call" | custom-call | bytes 2752512 | tf_op jit(solution)/shard_map/choose/pallas_call | solution.py:132
  55.6 2.0 %collective-permute-start.14 = (bf16[1792,256]{1,0:T(8,128)(2,1)}, bf16[1792,256]{1,0:T(8,128)(2,1)S(1)}, u32[]{:S(2)}, u32[]{:S(2)}) collective-permute-start(bf16[1792,256]{1,0:T(8,128)(2,1)} %choose.3), channel_id=1, source_target_pairs={{0,1},{1,0},{2,3},{3,2},{5,6},{6,5},{7,4},{4,7},{8,9},{9,8},{10,11... | collective-permute-start | bytes 2752520 | tf_op jit(solution)/shard_map/ppermute | solution.py:310
  57.6 0.6 pad_add_fusion.2._.scalars
  58.2 16.6 %all-to-all-done = bf16[64,8,1792]{2,1,0:T(8,128)(2,1)} async-done(((bf16[64,8,1792]{2,1,0:T(8,128)(2,1)}), bf16[64,8,1792]{2,1,0:T(8,128)(2,1)}, u32[]{:S(2)}, u32[]{:S(2)}) %all-to-all-start) | async-done | bytes 1835040 | tf_op jit(solution)/shard_map/all_to_all | solution.py:347
  74.8 4.6 %up_project.2 = (f32[2,512,256]{2,1,0:T(8,128)}, bf16[2,512,256]{2,1,0:T(8,128)(2,1)}) custom-call(s32[2]{0:T(128)} %pad_add_fusion.2._.scalars, bf16[512,1792]{1,0:T(8,128)(2,1)} %bitcast.19.rows, bf16[3584,256]{1,0:T(8,128)(2,1)} %bitcast.54, bf16[1792,256]{1,0:T(8,128)(2,1)} %copy-done.8), custom_call_target="tpu_custom_call" | custom-call | flops 939524096 | bytes 5000000 | tf_op jit(solution)/shard_map/up_project/pallas_call | solution.py:160
  79.4 1.7 %collective-permute-start.11 = (bf16[2,512,256]{2,1,0:T(8,128)(2,1)}, bf16[2,512,256]{2,1,0:T(8,128)(2,1)S(1)}, u32[]{:S(2)}, u32[]{:S(2)}) collective-permute-start(bf16[2,512,256]{2,1,0:T(8,128)(2,1)} %get-tuple-element.26), channel_id=1, source_target_pairs={{1,2},{2,1},{3,0},{0,3},{6,7},{7,6},{4,5},{5,4},{9,10},{10,9},{11,... | collective-permute-start | bytes 1572872 | tf_op jit(solution)/shard_map/ppermute | solution.py:388
  81.1 4.6 %up_project.3 = (f32[2,512,256]{2,1,0:T(8,128)}, bf16[2,512,256]{2,1,0:T(8,128)(2,1)}) custom-call(s32[2]{0:T(128)} %pad_add_fusion.2._.scalars, bf16[512,1792]{1,0:T(8,128)(2,1)} %bitcast.19.rows, bf16[1792,256]{1,0:T(8,128)(2,1)} %collective-permute-done.10.refs_0_, bf16[1792,256]{1,0:T(8,128)(2,1)} %collective-permute-done.9.first.refs_1_), custom_call_target="tpu_custom_call" | custom-call | flops 939524096 | bytes 5000000 | tf_op jit(solution)/shard_map/up_project/pallas_call | solution.py:160
  85.7 0.4 collective-permute-start.15
  86.0 2.1 %collective-permute-done.11.theirs_a = bf16[2,512,256]{2,1,0:T(8,128)(2,1)S(1)} collective-permute-done((bf16[2,512,256]{2,1,0:T(8,128)(2,1)}, bf16[2,512,256]{2,1,0:T(8,128)(2,1)S(1)}, u32[]{:S(2)}, u32[]{:S(2)}) %collective-permute-start.11) | collective-permute-done | bytes 524320 | tf_op jit(solution)/shard_map/ppermute | solution.py:388
  88.1 6.3 %collective-permute-done.15.theirs_b = bf16[2,512,256]{2,1,0:T(8,128)(2,1)S(1)} collective-permute-done((bf16[2,512,256]{2,1,0:T(8,128)(2,1)}, bf16[2,512,256]{2,1,0:T(8,128)(2,1)S(1)}, u32[]{:S(2)}, u32[]{:S(2)}) %collective-permute-start.15) | collective-permute-done | bytes 524320 | tf_op jit(solution)/shard_map/ppermute | solution.py:391
  94.4 1.2 copy-done.2
  95.7 6.1 %down_project.1 = bf16[512,1792]{1,0:T(8,128)(2,1)} custom-call(s32[2]{0:T(128)S(1)} %copy-done.4, f32[2,512,256]{2,1,0:T(8,128)S(1)} %copy-done.1, f32[2,512,256]{2,1,0:T(8,128)S(1)} %copy-done.2, bf16[2,512,256]{2,1,0:T(8,128)(2,1)S(1)} %collective-permute-done.11.theirs_a, bf16[2,512,256]{2,1,0:T(8,128)(2,1)S(1)} %collective-permute-done.15.theirs_b, ...), custom_call_target="tpu_custom_call" | custom-call | flops 1879048192 | bytes 9000000 | tf_op jit(solution)/shard_map/down_project/pallas_call | solution.py:210
  101.8 10.0 %all-to-all-start.1 = ((bf16[64,8,1792]{2,1,0:T(8,128)(2,1)}), bf16[64,8,1792]{2,1,0:T(8,128)(2,1)}, u32[]{:S(2)}, u32[]{:S(2)}) async-start(bf16[64,8,1792]{2,1,0:T(8,128)(2,1)} %bitcast.27), calls=%async_computation.1 | async-start | bytes 3670016 | tf_op jit(solution)/shard_map/all_to_all | solution.py:399
  113.1 0.1 select_reduce_fusion.2
  113.3 0.1 min.15
  113.6 0.1 select_reduce_fusion.1.pages
  113.7 0.1 maximum_maximum_fusion
  113.8 0.8 collective-permute-start.4
  114.6 0.8 collective-permute-start.2
  115.4 2.5 %collective-permute-done.4 = bf16[80,576]{1,0:T(8,128)(2,1)S(1)} collective-permute-done((bf16[80,576]{1,0:T(8,128)(2,1)S(1)}, bf16[80,576]{1,0:T(8,128)(2,1)S(1)}, u32[]{:S(2)}, u32[]{:S(2)}) %collective-permute-start.4) | collective-permute-done | bytes 92192 | tf_op jit(solution)/shard_map/ppermute | solution.py:18
  117.9 2.1 %collective-permute-done.3 = bf16[80,576]{1,0:T(8,128)(2,1)S(1)} collective-permute-done((bf16[80,576]{1,0:T(8,128)(2,1)S(1)}, bf16[80,576]{1,0:T(8,128)(2,1)S(1)}, u32[]{:S(2)}, u32[]{:S(2)}) %collective-permute-start.3) | collective-permute-done | bytes 92192 | tf_op jit(solution)/shard_map/ppermute | solution.py:18
  120.0 3.1 %collective-permute-done.2 = bf16[80,576]{1,0:T(8,128)(2,1)S(1)} collective-permute-done((bf16[80,576]{1,0:T(8,128)(2,1)S(1)}, bf16[80,576]{1,0:T(8,128)(2,1)S(1)}, u32[]{:S(2)}, u32[]{:S(2)}) %collective-permute-start.2) | collective-permute-done | bytes 92192 | tf_op jit(solution)/shard_map/ppermute | solution.py:18
  123.0 0.1 select_select_fusion
  123.2 1.7 %copy-done.5 = bf16[32,64,576]{2,1,0:T(8,128)(2,1)S(1)} copy-done((bf16[32,64,576]{2,1,0:T(8,128)(2,1)S(1)}, bf16[32,64,576]{2,1,0:T(8,128)(2,1)}, u32[]{:S(2)}) %copy-start.5) | copy-done | bytes 2359320
  125.0 18.9 %attention.1 = (bf16[16,64,512]{2,1,0:T(8,128)(2,1)}, bf16[16,64,512]{2,1,0:T(8,128)(2,1)}, bf16[64,512]{1,0:T(8,128)(2,1)S(1)}) custom-call(s32[16]{0:T(128)S(1)} %bitcast.53, s32[128]{0:T(128)S(1)} %select_reduce_fusion.1.pages, s32[1]{0:T(128)} %bitcast.47.moved, bf16[16,64,576]{2,1,0:T(8,128)(2,1)S(1)} %copy-done.6, bf16[16,64,576]{2,1,0:T(8,128)(2,1)S(1)} %copy-done.3, ...), custom_call_target="tpu_custom_call" | custom-call | flops 12000000000 | bytes 8000000 | tf_op jit(solution)/shard_map/attention/pallas_call | solution.py:89
  143.9 0.1 collective-permute-start.5
  144.0 2.7 %collective-permute-start.7 = (bf16[64,512]{1,0:T(8,128)(2,1)S(1)}, bf16[64,512]{1,0:T(8,128)(2,1)S(1)}, u32[]{:S(2)}, u32[]{:S(2)}) collective-permute-start(bf16[64,512]{1,0:T(8,128)(2,1)S(1)} %get-tuple-element.48), channel_id=1, source_target_pairs={{0,3},{1,0},{2,1},{3,2},{4,7},{5,4},{6,5},{7,6},{8,11},{9,8},{10,9... | collective-permute-start | bytes 196616 | tf_op jit(solution)/shard_map/ppermute | solution.py:18
  146.6 9.3 %all-to-all-done.1 = bf16[64,8,1792]{2,1,0:T(8,128)(2,1)} async-done(((bf16[64,8,1792]{2,1,0:T(8,128)(2,1)}), bf16[64,8,1792]{2,1,0:T(8,128)(2,1)}, u32[]{:S(2)}, u32[]{:S(2)}) %all-to-all-start.1) | async-done | bytes 1835040 | tf_op jit(solution)/shard_map/all_to_all | solution.py:399
  156.0 1.9 %fusion = f32[128,1792]{1,0:T(8,128)S(1)} fusion(bf16[64,8,1792]{2,1,0:T(8,128)(2,1)} %all-to-all-done.1, bf16[64,512]{1,0:T(8,128)(2,1)S(1)} %get-tuple-element.42, bf16[64,512]{1,0:T(8,128)(2,1)S(1)} %get-tuple-element.41), kind=kOutput, calls=%fused_computation.1 | convolution fusion | flops 235143168 | bytes 2883584 | tf_op jit(solution)/shard_map/dot_general | solution.py:410
  158.0 0.8 collective-permute-start.16
  158.8 0.7 bitcast_dynamic-update-slice_fusion
  159.5 3.5 %collective-permute-done.16 = f32[16,1792]{1,0:T(8,128)S(1)} collective-permute-done((f32[16,1792]{1,0:T(8,128)S(1)}, f32[16,1792]{1,0:T(8,128)S(1)}, u32[]{:S(2)}, u32[]{:S(2)}) %collective-permute-start.16) | collective-permute-done | bytes 114720 | tf_op jit(solution)/shard_map/ppermute | solution.py:415
  163.0 0.7 pad_maximum_fusion.1
  (67 shorter events, 0.7 us)
Async XLA Ops:
  3.1 9.5 %collective-permute-start = (bf16[16,1920]{1,0:T(8,128)(2,1)S(1)}, bf16[16,1920]{1,0:T(8,128)(2,1)S(1)}, u32[]{:S(2)}, u32[]{:S(2)}) collective-permute-start(bf16[16,1920]{1,0:T(8,128)(2,1)S(1)} %get-tuple-element.58), channel_id=1, source_target_pairs={{1,2},{2,1},{3,0},{0,3},{5,6},{6,5},{7,4},{4,7},{9,10},{10,9},{11,... | collective-permute-start | bytes 184328 | tf_op jit(solution)/shard_map/ppermute | solution.py:295
  6.8 5.9 %collective-permute-start.1 = (bf16[16,1920]{1,0:T(8,128)(2,1)S(1)}, bf16[16,1920]{1,0:T(8,128)(2,1)S(1)}, u32[]{:S(2)}, u32[]{:S(2)}) collective-permute-start(bf16[16,1920]{1,0:T(8,128)(2,1)S(1)} %get-tuple-element.59), channel_id=1, source_target_pairs={{2,3},{3,2},{0,1},{1,0},{6,7},{7,6},{4,5},{5,4},{10,11},{11,10},{8... | collective-permute-start | bytes 184328 | tf_op jit(solution)/shard_map/ppermute | solution.py:295
  6.8 4.4 %copy-start = (bf16[1,3584,256]{2,1,0:T(8,128)(2,1)S(1)}, bf16[1,3584,256]{2,1,0:T(8,128)(2,1)}, u32[]{:S(2)}) copy-start(bf16[1,3584,256]{2,1,0:T(8,128)(2,1)} %param.18) | copy-start | bytes 5505028
  9.7 21.1 %collective-permute-start.8 = (bf16[1792,256]{1,0:T(8,128)(2,1)}, bf16[1792,256]{1,0:T(8,128)(2,1)S(1)}, u32[]{:S(2)}, u32[]{:S(2)}) collective-permute-start(bf16[1792,256]{1,0:T(8,128)(2,1)} %get-tuple-element.22), channel_id=1, source_target_pairs={{0,3},{1,0},{2,1},{3,2},{4,7},{5,4},{6,5},{7,6},{8,11},{9,8},{10,9... | collective-permute-start | bytes 2752520 | tf_op jit(solution)/shard_map/ppermute | solution.py:18
  10.4 21.1 %collective-permute-start.9 = (bf16[1792,256]{1,0:T(8,128)(2,1)}, bf16[1792,256]{1,0:T(8,128)(2,1)}, u32[]{:S(2)}, u32[]{:S(2)}) collective-permute-start(bf16[1792,256]{1,0:T(8,128)(2,1)} %get-tuple-element.24), channel_id=1, source_target_pairs={{0,1},{1,2},{2,3},{3,0},{4,5},{5,6},{6,7},{7,4},{8,9},{9,10},{10,1... | collective-permute-start | bytes 2752520 | tf_op jit(solution)/shard_map/ppermute | solution.py:18
  11.2 1.6 copy-start.10
  11.2 2.7 %copy-start.13 = (f32[16,8]{0,1:T(8,128)S(1)}, f32[16,8]{0,1:T(8,128)}, u32[]{:S(2)}) copy-start(f32[16,8]{0,1:T(8,128)} %param.16) | copy-start | bytes 1540
  17.2 57.5 %all-to-all-start = ((bf16[64,8,1792]{2,1,0:T(8,128)(2,1)}), bf16[64,8,1792]{2,1,0:T(8,128)(2,1)}, u32[]{:S(2)}, u32[]{:S(2)}) async-start(bf16[64,8,1792]{2,1,0:T(8,128)(2,1)} %bitcast.55), calls=%async_computation | async-start | bytes 3670016 | tf_op jit(solution)/shard_map/all_to_all | solution.py:347
  30.8 3.3 %copy-start.8 = (bf16[1792,256]{1,0:T(8,128)(2,1)}, bf16[1792,256]{1,0:T(8,128)(2,1)S(1)}, u32[]{:S(2)}) copy-start(bf16[1792,256]{1,0:T(8,128)(2,1)S(1)} %collective-permute-done.8.refs_1_.second) | copy-start | bytes 2752516
  31.4 20.2 %collective-permute-start.12 = (bf16[1792,256]{1,0:T(8,128)(2,1)}, bf16[1792,256]{1,0:T(8,128)(2,1)}, u32[]{:S(2)}, u32[]{:S(2)}) collective-permute-start(bf16[1792,256]{1,0:T(8,128)(2,1)} %get-tuple-element.27), channel_id=1, source_target_pairs={{0,1},{1,2},{2,3},{3,0},{4,5},{5,6},{6,7},{7,4},{8,9},{9,10},{10,1... | collective-permute-start | bytes 2752520 | tf_op jit(solution)/shard_map/ppermute | solution.py:18
  32.3 19.8 %collective-permute-start.13 = (bf16[1792,256]{1,0:T(8,128)(2,1)}, bf16[1792,256]{1,0:T(8,128)(2,1)}, u32[]{:S(2)}, u32[]{:S(2)}) collective-permute-start(bf16[1792,256]{1,0:T(8,128)(2,1)} %get-tuple-element.28), channel_id=1, source_target_pairs={{0,3},{1,0},{2,1},{3,2},{4,7},{5,4},{6,5},{7,6},{8,11},{9,8},{10,9... | collective-permute-start | bytes 2752520 | tf_op jit(solution)/shard_map/ppermute | solution.py:18
  37.7 43.4 %collective-permute-start.10 = (bf16[1792,256]{1,0:T(8,128)(2,1)}, bf16[1792,256]{1,0:T(8,128)(2,1)}, u32[]{:S(2)}, u32[]{:S(2)}) collective-permute-start(bf16[1792,256]{1,0:T(8,128)(2,1)} %choose.2), channel_id=1, source_target_pairs={{0,1},{1,0},{2,3},{3,2},{5,6},{6,5},{7,4},{4,7},{8,9},{9,8},{10,11... | collective-permute-start | bytes 2752520 | tf_op jit(solution)/shard_map/ppermute | solution.py:310
  55.6 30.1 %collective-permute-start.14 = (bf16[1792,256]{1,0:T(8,128)(2,1)}, bf16[1792,256]{1,0:T(8,128)(2,1)S(1)}, u32[]{:S(2)}, u32[]{:S(2)}) collective-permute-start(bf16[1792,256]{1,0:T(8,128)(2,1)} %choose.3), channel_id=1, source_target_pairs={{0,1},{1,0},{2,3},{3,2},{5,6},{6,5},{7,4},{4,7},{8,9},{9,8},{10,11... | collective-permute-start | bytes 2752520 | tf_op jit(solution)/shard_map/ppermute | solution.py:310
  79.4 15.1 %copy-start.1 = (f32[2,512,256]{2,1,0:T(8,128)S(1)}, f32[2,512,256]{2,1,0:T(8,128)}, u32[]{:S(2)}) copy-start(f32[2,512,256]{2,1,0:T(8,128)} %get-tuple-element.23.mine_a) | copy-start | bytes 3145732
  79.4 15.1 %copy-start.4 = (s32[2]{0:T(128)S(1)}, s32[2]{0:T(128)}, u32[]{:S(2)}) copy-start(s32[2]{0:T(128)} %pad_add_fusion.2._.scalars) | copy-start | bytes 28
  79.4 8.8 %collective-permute-start.11 = (bf16[2,512,256]{2,1,0:T(8,128)(2,1)}, bf16[2,512,256]{2,1,0:T(8,128)(2,1)S(1)}, u32[]{:S(2)}, u32[]{:S(2)}) collective-permute-start(bf16[2,512,256]{2,1,0:T(8,128)(2,1)} %get-tuple-element.26), channel_id=1, source_target_pairs={{1,2},{2,1},{3,0},{0,3},{6,7},{7,6},{4,5},{5,4},{9,10},{10,9},{11,... | collective-permute-start | bytes 1572872 | tf_op jit(solution)/shard_map/ppermute | solution.py:388
  85.7 8.7 %collective-permute-start.15 = (bf16[2,512,256]{2,1,0:T(8,128)(2,1)}, bf16[2,512,256]{2,1,0:T(8,128)(2,1)S(1)}, u32[]{:S(2)}, u32[]{:S(2)}) collective-permute-start(bf16[2,512,256]{2,1,0:T(8,128)(2,1)} %get-tuple-element.30), channel_id=1, source_target_pairs={{1,2},{2,1},{3,0},{0,3},{6,7},{7,6},{4,5},{5,4},{9,10},{10,9},{11,... | collective-permute-start | bytes 1572872 | tf_op jit(solution)/shard_map/ppermute | solution.py:391
  94.4 1.2 copy-start.2
  101.7 11.4 %copy-start.7 = (s32[1,16]{1,0:T(1,128)S(1)}, s32[1,16]{1,0:T(1,128)}, u32[]{:S(2)}) copy-start(s32[1,16]{1,0:T(1,128)} %param.24) | copy-start | bytes 196
  101.7 11.7 %copy-start.12 = (bf16[16,576]{1,0:T(8,128)(2,1)S(1)}, bf16[16,576]{1,0:T(8,128)(2,1)}, u32[]{:S(2)}) copy-start(bf16[16,576]{1,0:T(8,128)(2,1)} %param.20) | copy-start | bytes 55300
  101.7 11.8 %copy-start.14 = (s32[1,32]{1,0:T(1,128)S(1)}, s32[1,32]{1,0:T(1,128)}, u32[]{:S(2)}) copy-start(s32[1,32]{1,0:T(1,128)} %param.25) | copy-start | bytes 388
  101.7 11.9 %copy-start.11 = (bf16[16,576]{1,0:T(8,128)(2,1)S(1)}, bf16[16,576]{1,0:T(8,128)(2,1)}, u32[]{:S(2)}) copy-start(bf16[16,576]{1,0:T(8,128)(2,1)} %param.22) | copy-start | bytes 55300
  101.8 11.9 %copy-start.3 = (bf16[16,64,576]{2,1,0:T(8,128)(2,1)S(1)}, bf16[16,64,576]{2,1,0:T(8,128)(2,1)}, u32[]{:S(2)}) copy-start(bf16[16,64,576]{2,1,0:T(8,128)(2,1)} %q_two) | copy-start | bytes 3538948
  101.8 13.6 %copy-start.9 = (f32[64,512]{1,0:T(8,128)S(1)}, f32[64,512]{1,0:T(8,128)}, u32[]{:S(2)}) copy-start(f32[64,512]{1,0:T(8,128)} %get-tuple-element.31) | copy-start | bytes 393220
  101.8 21.4 %copy-start.6 = (bf16[16,64,576]{2,1,0:T(8,128)(2,1)S(1)}, bf16[16,64,576]{2,1,0:T(8,128)(2,1)}, u32[]{:S(2)}) copy-start(bf16[16,64,576]{2,1,0:T(8,128)(2,1)} %q_one.1) | copy-start | bytes 3538948
  101.8 54.2 %all-to-all-start.1 = ((bf16[64,8,1792]{2,1,0:T(8,128)(2,1)}), bf16[64,8,1792]{2,1,0:T(8,128)(2,1)}, u32[]{:S(2)}, u32[]{:S(2)}) async-start(bf16[64,8,1792]{2,1,0:T(8,128)(2,1)} %bitcast.27), calls=%async_computation.1 | async-start | bytes 3670016 | tf_op jit(solution)/shard_map/all_to_all | solution.py:399
  113.8 4.1 %collective-permute-start.4 = (bf16[80,576]{1,0:T(8,128)(2,1)S(1)}, bf16[80,576]{1,0:T(8,128)(2,1)S(1)}, u32[]{:S(2)}, u32[]{:S(2)}) collective-permute-start(bf16[80,576]{1,0:T(8,128)(2,1)S(1)} %maximum_maximum_fusion), channel_id=1, source_target_pairs={{0,3},{1,0},{2,1},{3,2},{4,7},{5,4},{6,5},{7,6},{8,11},{9,8},{10,9... | collective-permute-start | bytes 276488 | tf_op jit(solution)/shard_map/ppermute | solution.py:18
  114.5 5.4 %collective-permute-start.3 = (bf16[80,576]{1,0:T(8,128)(2,1)S(1)}, bf16[80,576]{1,0:T(8,128)(2,1)S(1)}, u32[]{:S(2)}, u32[]{:S(2)}) collective-permute-start(bf16[80,576]{1,0:T(8,128)(2,1)S(1)} %maximum_maximum_fusion), channel_id=1, source_target_pairs={{0,2},{1,3},{2,0},{3,1},{4,6},{5,7},{6,4},{7,5},{8,10},{9,11},{10,... | collective-permute-start | bytes 276488 | tf_op jit(solution)/shard_map/ppermute | solution.py:18
  114.6 8.5 %collective-permute-start.2 = (bf16[80,576]{1,0:T(8,128)(2,1)S(1)}, bf16[80,576]{1,0:T(8,128)(2,1)S(1)}, u32[]{:S(2)}, u32[]{:S(2)}) collective-permute-start(bf16[80,576]{1,0:T(8,128)(2,1)S(1)} %maximum_maximum_fusion), channel_id=1, source_target_pairs={{0,1},{1,2},{2,3},{3,0},{4,5},{5,6},{6,7},{7,4},{8,9},{9,10},{10,1... | collective-permute-start | bytes 276488 | tf_op jit(solution)/shard_map/ppermute | solution.py:18
  123.2 1.7 %copy-start.5 = (bf16[32,64,576]{2,1,0:T(8,128)(2,1)S(1)}, bf16[32,64,576]{2,1,0:T(8,128)(2,1)}, u32[]{:S(2)}) copy-start(bf16[32,64,576]{2,1,0:T(8,128)(2,1)} %pool.1) | copy-start | bytes 7077892
  143.9 14.9 %collective-permute-start.5 = (bf16[64,512]{1,0:T(8,128)(2,1)S(1)}, bf16[64,512]{1,0:T(8,128)(2,1)S(1)}, u32[]{:S(2)}, u32[]{:S(2)}) collective-permute-start(bf16[64,512]{1,0:T(8,128)(2,1)S(1)} %get-tuple-element.47), channel_id=1, source_target_pairs={{0,1},{1,2},{2,3},{3,0},{4,5},{5,6},{6,7},{7,4},{8,9},{9,10},{10,1... | collective-permute-start | bytes 196616 | tf_op jit(solution)/shard_map/ppermute | solution.py:18
  144.0 14.8 %collective-permute-start.7 = (bf16[64,512]{1,0:T(8,128)(2,1)S(1)}, bf16[64,512]{1,0:T(8,128)(2,1)S(1)}, u32[]{:S(2)}, u32[]{:S(2)}) collective-permute-start(bf16[64,512]{1,0:T(8,128)(2,1)S(1)} %get-tuple-element.48), channel_id=1, source_target_pairs={{0,3},{1,0},{2,1},{3,2},{4,7},{5,4},{6,5},{7,6},{8,11},{9,8},{10,9... | collective-permute-start | bytes 196616 | tf_op jit(solution)/shard_map/ppermute | solution.py:18
  146.6 12.1 %collective-permute-start.6 = (bf16[64,512]{1,0:T(8,128)(2,1)S(1)}, bf16[64,512]{1,0:T(8,128)(2,1)S(1)}, u32[]{:S(2)}, u32[]{:S(2)}) collective-permute-start(bf16[64,512]{1,0:T(8,128)(2,1)S(1)} %get-tuple-element.49), channel_id=1, source_target_pairs={{0,2},{1,3},{2,0},{3,1},{4,6},{5,7},{6,4},{7,5},{8,10},{9,11},{10,... | collective-permute-start | bytes 196616 | tf_op jit(solution)/shard_map/ppermute | solution.py:18
  158.0 4.9 %collective-permute-start.16 = (f32[16,1792]{1,0:T(8,128)S(1)}, f32[16,1792]{1,0:T(8,128)S(1)}, u32[]{:S(2)}, u32[]{:S(2)}) collective-permute-start(f32[16,1792]{1,0:T(8,128)S(1)} %get-tuple-element.39), channel_id=1, source_target_pairs={{1,2},{2,1},{3,0},{0,3},{5,6},{6,5},{7,4},{4,7},{9,10},{10,9},{11,... | collective-permute-start | bytes 344072 | tf_op jit(solution)/shard_map/ppermute | solution.py:415
  158.8 4.2 %collective-permute-start.17 = (f32[16,1792]{1,0:T(8,128)S(1)}, f32[16,1792]{1,0:T(8,128)S(1)}, u32[]{:S(2)}, u32[]{:S(2)}) collective-permute-start(f32[16,1792]{1,0:T(8,128)S(1)} %get-tuple-element.40), channel_id=1, source_target_pairs={{2,3},{3,2},{0,1},{1,0},{6,7},{7,6},{4,5},{5,4},{10,11},{11,10},{8... | collective-permute-start | bytes 344072 | tf_op jit(solution)/shard_map/ppermute | solution.py:415

commit v12 on v11

--- a/solution.py
+++ b/solution.py
@@ -170,7 +170,7 @@
             jax.ShapeDtypeStruct(shape, jnp.float32),
             jax.ShapeDtypeStruct(shape, jnp.bfloat16),
         ],
-        compiler_params=pltpu.CompilerParams(vmem_limit_bytes=58 * 1024 * 1024),
+        compiler_params=pltpu.CompilerParams(vmem_limit_bytes=24 * 1024 * 1024),
         cost_estimate=pl.CostEstimate(
             flops=2 * len(weights) * count * depth * units,
             bytes_accessed=5_000_000,

time: 166 us -> 165 us (level)
  Pallas kernels: 41.3 us -> 38.9 us
    pallas_call x2, Pallas kernels: 9.22 us -> 6.86 us  [up_project(): pl.pallas_call(up_kernel, grid_spec=pltpu.PrefetchScalarGridSpec(num_scal...]
    unnamed x31 -> x29, local copies, waits for them, and re-layouts: 3.1 us -> 4.54 us
  transfers between devices with their start and end apart: 20 -> 20, of which waited for: 12 -> 13; matrix products, arithmetic and copies ran while one was open for 8% -> 8% of each run, Pallas kernels for 22% -> 20%
where the time goes in v12:
time: 165 us; the launch traced here: 163 us
  waiting for transfers between devices  60.3 us (37%)
  starting transfers between devices  41 us (25%)
  Pallas kernels  38.9 us (24%)
  local copies, waits for them, and re-layouts  10.8 us (7%)
  other arithmetic  5.18 us (3%)
  matrix products  4.1 us (2%)
  between operations  2.39 us (1%)
    ppermute x10, waiting for transfers between devices, hop(): lax.ppermute(value, axis, [(i, (i + step) % size) for i in range(size)])  22.7 us
    pallas_call x1, Pallas kernels, attention(): pl.pallas_call(attention_kernel, grid_spec=pltpu.PrefetchScalarGridSpec(n...  18.9 us
    all_to_all x1, waiting for transfers between devices, shards(): lax.all_to_all(outgoing.reshape(ep_size, rank, half), 'ep', split_axis=0,...  17.2 us
    all_to_all x1, starting transfers between devices, shards(): lax.all_to_all(outgoing.reshape(ep_size, rank, half), 'ep', split_axis=0,...  13.3 us
    all_to_all x1, starting transfers between devices, shards(): lax.all_to_all(produced.reshape(ep_size, rank, half), 'ep', split_axis=0,...  9.81 us
    all_to_all x1, waiting for transfers between devices, shards(): lax.all_to_all(produced.reshape(ep_size, rank, half), 'ep', split_axis=0,...  9.02 us
    ppermute x10, starting transfers between devices, hop(): lax.ppermute(value, axis, [(i, (i + step) % size) for i in range(size)])  8.98 us
    pallas_call x2, Pallas kernels, choose(): pl.pallas_call(choose_kernel, grid_spec=pltpu.PrefetchScalarGridSpec(num_...  7.13 us
  transfers between devices with their start and end apart: 20, of which 13 were waited for; matrix products, arithmetic and copies ran while one was open for 8% of the time, Pallas kernels for 20%

profile of v12, /device:TPU:1, one launch (start us, length us, event | category | flops | bytes accessed | tf_op | source)
XLA Modules:
  0.0 162.7 jit_solution(17432022079462727992)
XLA Ops:
  0.7 0.7 convert_convert_fusion
  1.4 0.7 reduce-precision_convert_fusion.2
  2.1 0.1 copy.43
  2.2 0.9 constant_dynamic-slice_fusion.2
  3.2 3.7 %collective-permute-start = (bf16[16,1920]{1,0:T(8,128)(2,1)S(1)}, bf16[16,1920]{1,0:T(8,128)(2,1)S(1)}, u32[]{:S(2)}, u32[]{:S(2)}) collective-permute-start(bf16[16,1920]{1,0:T(8,128)(2,1)S(1)} %get-tuple-element.58), channel_id=1, source_target_pairs={{1,2},{2,1},{3,0},{0,3},{5,6},{6,5},{7,4},{4,7},{9,10},{10,9},{11,... | collective-permute-start | bytes 184328 | tf_op jit(solution)/shard_map/ppermute | solution.py:295
  6.8 2.9 %dynamic-slice_bitcast_fusion.2 = (bf16[1792,256]{1,0:T(8,128)(2,1)}, bf16[1792,256]{1,0:T(8,128)(2,1)}) fusion(bf16[1,3584,256]{2,1,0:T(8,128)(2,1)} %param.17, s32[]{:T(128)S(6)} %select_n.252, s32[]{:T(128)S(6)} %select_n.251), kind=kLoop, calls=%fused_computation.10 | loop fusion | bytes 3670024 | tf_op jit(solution)/shard_map/dynamic_slice | solution.py:283
  9.7 0.6 collective-permute-start.8
  10.4 0.8 collective-permute-start.9
  11.2 1.5 dynamic-slice_bitcast_fusion
  12.9 0.1 copy.37
  13.0 0.1 eq.111
  13.1 0.3 fusion.2
  13.4 0.1 convert_element_type.48
  13.6 0.1 multiply_add_fusion
  13.7 0.1 add_select_fusion.6
  13.8 0.1 pad_add_fusion.1
  13.8 0.1 copy.39
  13.9 0.1 pad_maximum_fusion.3
  14.0 0.1 copy.42
  14.1 1.3 select_reduce_fusion
  15.5 1.9 %convolution_convert_fusion = bf16[512,1792]{1,0:T(8,128)(2,1)} fusion(bf16[64,512]{1,0:T(8,128)(2,1)S(1)} %get-tuple-element.32, bf16[16,1792]{1,0:T(8,128)(2,1)S(1)} %slice.107, bf16[16,1792]{1,0:T(8,128)(2,1)S(1)} %get-tuple-element.46, bf16[16,1792]{1,0:T(8,128)(2,1)S(1)} %slice.106, bf16[16,1792]{1,0:T(8,128)(2,1)S(1)} %get-tuple-element.43), kind=kOutput, calls=%fused_computation | convolution fusion | flops 119275520 | bytes 2129920 | tf_op jit(solution)/shard_map/dot_general | solution.py:344
  17.3 13.3 %all-to-all-start = ((bf16[64,8,1792]{2,1,0:T(8,128)(2,1)}), bf16[64,8,1792]{2,1,0:T(8,128)(2,1)}, u32[]{:S(2)}, u32[]{:S(2)}) async-start(bf16[64,8,1792]{2,1,0:T(8,128)(2,1)} %bitcast.55), calls=%async_computation | async-start | bytes 3670016 | tf_op jit(solution)/shard_map/all_to_all | solution.py:347
  30.6 0.2 collective-permute-done.8.refs_1_.second
  30.8 0.6 collective-permute-done.9.first.refs_1_
  31.5 0.9 collective-permute-start.12
  32.4 1.8 %collective-permute-start.13 = (bf16[1792,256]{1,0:T(8,128)(2,1)}, bf16[1792,256]{1,0:T(8,128)(2,1)}, u32[]{:S(2)}, u32[]{:S(2)}) collective-permute-start(bf16[1792,256]{1,0:T(8,128)(2,1)} %get-tuple-element.28), channel_id=1, source_target_pairs={{0,3},{1,0},{2,1},{3,2},{4,7},{5,4},{6,5},{7,6},{8,11},{9,8},{10,9... | collective-permute-start | bytes 2752520 | tf_op jit(solution)/shard_map/ppermute | solution.py:18
  34.1 3.5 %choose.2 = bf16[1792,256]{1,0:T(8,128)(2,1)} custom-call(s32[1]{0:T(128)} %bitcast.23.which, bf16[1792,256]{1,0:T(8,128)(2,1)} %collective-permute-done.9.first.refs_1_, bf16[1792,256]{1,0:T(8,128)(2,1)} %copy-done.2), custom_call_target="tpu_custom_call" | custom-call | flops 199999995904 | bytes 2752512 | tf_op jit(solution)/shard_map/choose/pallas_call | solution.py:132
  37.8 13.9 %collective-permute-done.12.first.refs_3_ = bf16[1792,256]{1,0:T(8,128)(2,1)} collective-permute-done((bf16[1792,256]{1,0:T(8,128)(2,1)}, bf16[1792,256]{1,0:T(8,128)(2,1)}, u32[]{:S(2)}, u32[]{:S(2)}) %collective-permute-start.12) | collective-permute-done | bytes 917536 | tf_op jit(solution)/shard_map/ppermute | solution.py:18
  51.6 0.6 collective-permute-done.13.second.refs_1_
  52.2 3.6 %choose.3 = bf16[1792,256]{1,0:T(8,128)(2,1)} custom-call(s32[1]{0:T(128)} %bitcast.23.which, bf16[1792,256]{1,0:T(8,128)(2,1)} %collective-permute-done.12.first.refs_3_, bf16[1792,256]{1,0:T(8,128)(2,1)} %collective-permute-done.13.second.refs_1_), custom_call_target="tpu_custom_call" | custom-call | bytes 2752512 | tf_op jit(solution)/shard_map/choose/pallas_call | solution.py:132
  55.8 1.8 %collective-permute-start.14 = (bf16[1792,256]{1,0:T(8,128)(2,1)}, bf16[1792,256]{1,0:T(8,128)(2,1)S(1)}, u32[]{:S(2)}, u32[]{:S(2)}) collective-permute-start(bf16[1792,256]{1,0:T(8,128)(2,1)} %choose.3), channel_id=1, source_target_pairs={{0,1},{1,0},{2,3},{3,2},{5,6},{6,5},{7,4},{4,7},{8,9},{9,8},{10,11... | collective-permute-start | bytes 2752520 | tf_op jit(solution)/shard_map/ppermute | solution.py:310
  57.7 17.2 %all-to-all-done = bf16[64,8,1792]{2,1,0:T(8,128)(2,1)} async-done(((bf16[64,8,1792]{2,1,0:T(8,128)(2,1)}), bf16[64,8,1792]{2,1,0:T(8,128)(2,1)}, u32[]{:S(2)}, u32[]{:S(2)}) %all-to-all-start) | async-done | bytes 1835040 | tf_op jit(solution)/shard_map/all_to_all | solution.py:347
  74.9 1.5 copy-done.1
  76.4 1.2 copy-done.3
  77.5 3.1 %up_project.2 = (f32[2,512,256]{2,1,0:T(8,128)S(1)}, bf16[2,512,256]{2,1,0:T(8,128)(2,1)S(1)}) custom-call(s32[2]{0:T(128)S(1)} %pad_add_fusion.2._.scalars, bf16[512,1792]{1,0:T(8,128)(2,1)} %bitcast.19.rows, bf16[3584,256]{1,0:T(8,128)(2,1)S(1)} %bitcast.53, bf16[1792,256]{1,0:T(8,128)(2,1)S(1)} %copy-done.3), custom_call_target="tpu_custom_call" | custom-call | flops 939524096 | bytes 5000000 | tf_op jit(solution)/shard_map/up_project/pallas_call | solution.py:160
  80.7 1.7 %collective-permute-start.11 = (bf16[2,512,256]{2,1,0:T(8,128)(2,1)S(1)}, bf16[2,512,256]{2,1,0:T(8,128)(2,1)S(1)}, u32[]{:S(2)}, u32[]{:S(2)}) collective-permute-start(bf16[2,512,256]{2,1,0:T(8,128)(2,1)S(1)} %get-tuple-element.26), channel_id=1, source_target_pairs={{1,2},{2,1},{3,0},{0,3},{6,7},{7,6},{4,5},{5,4},{9,10},{10,9},{11,... | collective-permute-start | bytes 1572872 | tf_op jit(solution)/shard_map/ppermute | solution.py:388
  82.4 3.7 %up_project.3 = (f32[2,512,256]{2,1,0:T(8,128)S(1)}, bf16[2,512,256]{2,1,0:T(8,128)(2,1)S(1)}) custom-call(s32[2]{0:T(128)S(1)} %pad_add_fusion.2._.scalars, bf16[512,1792]{1,0:T(8,128)(2,1)} %bitcast.19.rows, bf16[1792,256]{1,0:T(8,128)(2,1)} %collective-permute-done.10.refs_0_, bf16[1792,256]{1,0:T(8,128)(2,1)} %collective-permute-done.9.first.refs_1_), custom_call_target="tpu_custom_call" | custom-call | flops 939524096 | bytes 5000000 | tf_op jit(solution)/shard_map/up_project/pallas_call | solution.py:160
  86.1 0.3 collective-permute-start.15
  86.4 2.8 %collective-permute-done.11.theirs_a = bf16[2,512,256]{2,1,0:T(8,128)(2,1)S(1)} collective-permute-done((bf16[2,512,256]{2,1,0:T(8,128)(2,1)S(1)}, bf16[2,512,256]{2,1,0:T(8,128)(2,1)S(1)}, u32[]{:S(2)}, u32[]{:S(2)}) %collective-permute-start.11) | collective-permute-done | bytes 524320 | tf_op jit(solution)/shard_map/ppermute | solution.py:388
  89.2 5.6 %collective-permute-done.15.theirs_b = bf16[2,512,256]{2,1,0:T(8,128)(2,1)S(1)} collective-permute-done((bf16[2,512,256]{2,1,0:T(8,128)(2,1)S(1)}, bf16[2,512,256]{2,1,0:T(8,128)(2,1)S(1)}, u32[]{:S(2)}, u32[]{:S(2)}) %collective-permute-start.15) | collective-permute-done | bytes 524320 | tf_op jit(solution)/shard_map/ppermute | solution.py:391
  94.9 6.0 %down_project.1 = bf16[512,1792]{1,0:T(8,128)(2,1)} custom-call(s32[2]{0:T(128)S(1)} %pad_add_fusion.2._.scalars, f32[2,512,256]{2,1,0:T(8,128)S(1)} %get-tuple-element.23.mine_a, f32[2,512,256]{2,1,0:T(8,128)S(1)} %get-tuple-element.25.mine_b, bf16[2,512,256]{2,1,0:T(8,128)(2,1)S(1)} %collective-permute-done.11.theirs_a, ...), custom_call_target="tpu_custom_call" | custom-call | flops 1879048192 | bytes 9000000 | tf_op jit(solution)/shard_map/down_project/pallas_call | solution.py:210
  100.9 9.8 %all-to-all-start.1 = ((bf16[64,8,1792]{2,1,0:T(8,128)(2,1)}), bf16[64,8,1792]{2,1,0:T(8,128)(2,1)}, u32[]{:S(2)}, u32[]{:S(2)}) async-start(bf16[64,8,1792]{2,1,0:T(8,128)(2,1)} %bitcast.27), calls=%async_computation.1 | async-start | bytes 3670016 | tf_op jit(solution)/shard_map/all_to_all | solution.py:399
  112.1 0.1 select_reduce_fusion.2
  112.3 0.1 min.15
  112.5 0.1 select_reduce_fusion.1.pages
  112.6 0.1 maximum_maximum_fusion
  112.7 1.4 collective-permute-start.4
  114.1 0.2 collective-permute-start.3
  114.3 0.5 collective-permute-start.2
  114.9 2.0 %collective-permute-done.4 = bf16[80,576]{1,0:T(8,128)(2,1)S(1)} collective-permute-done((bf16[80,576]{1,0:T(8,128)(2,1)S(1)}, bf16[80,576]{1,0:T(8,128)(2,1)S(1)}, u32[]{:S(2)}, u32[]{:S(2)}) %collective-permute-start.4) | collective-permute-done | bytes 92192 | tf_op jit(solution)/shard_map/ppermute | solution.py:18
  116.8 2.8 %collective-permute-done.3 = bf16[80,576]{1,0:T(8,128)(2,1)S(1)} collective-permute-done((bf16[80,576]{1,0:T(8,128)(2,1)S(1)}, bf16[80,576]{1,0:T(8,128)(2,1)S(1)}, u32[]{:S(2)}, u32[]{:S(2)}) %collective-permute-start.3) | collective-permute-done | bytes 92192 | tf_op jit(solution)/shard_map/ppermute | solution.py:18
  119.6 2.7 %collective-permute-done.2 = bf16[80,576]{1,0:T(8,128)(2,1)S(1)} collective-permute-done((bf16[80,576]{1,0:T(8,128)(2,1)S(1)}, bf16[80,576]{1,0:T(8,128)(2,1)S(1)}, u32[]{:S(2)}, u32[]{:S(2)}) %collective-permute-start.2) | collective-permute-done | bytes 92192 | tf_op jit(solution)/shard_map/ppermute | solution.py:18
  122.3 0.1 select_select_fusion
  122.5 1.7 %copy-done.5 = bf16[32,64,576]{2,1,0:T(8,128)(2,1)S(1)} copy-done((bf16[32,64,576]{2,1,0:T(8,128)(2,1)S(1)}, bf16[32,64,576]{2,1,0:T(8,128)(2,1)}, u32[]{:S(2)}) %copy-start.5) | copy-done | bytes 2359320
  124.2 18.9 %attention.1 = (bf16[16,64,512]{2,1,0:T(8,128)(2,1)}, bf16[16,64,512]{2,1,0:T(8,128)(2,1)}, bf16[64,512]{1,0:T(8,128)(2,1)S(1)}) custom-call(s32[16]{0:T(128)S(1)} %bitcast.54, s32[128]{0:T(128)S(1)} %select_reduce_fusion.1.pages, s32[1]{0:T(128)} %bitcast.47.moved, bf16[16,64,576]{2,1,0:T(8,128)(2,1)S(1)} %copy-done.6, bf16[16,64,576]{2,1,0:T(8,128)(2,1)S(1)} %copy-done.4, ...), custom_call_target="tpu_custom_call" | custom-call | flops 12000000000 | bytes 8000000 | tf_op jit(solution)/shard_map/attention/pallas_call | solution.py:89
  143.2 0.1 collective-permute-start.5
  143.2 2.7 %collective-permute-start.7 = (bf16[64,512]{1,0:T(8,128)(2,1)S(1)}, bf16[64,512]{1,0:T(8,128)(2,1)S(1)}, u32[]{:S(2)}, u32[]{:S(2)}) collective-permute-start(bf16[64,512]{1,0:T(8,128)(2,1)S(1)} %get-tuple-element.48), channel_id=1, source_target_pairs={{0,3},{1,0},{2,1},{3,2},{4,7},{5,4},{6,5},{7,6},{8,11},{9,8},{10,9... | collective-permute-start | bytes 196616 | tf_op jit(solution)/shard_map/ppermute | solution.py:18
  145.9 9.0 %all-to-all-done.1 = bf16[64,8,1792]{2,1,0:T(8,128)(2,1)} async-done(((bf16[64,8,1792]{2,1,0:T(8,128)(2,1)}), bf16[64,8,1792]{2,1,0:T(8,128)(2,1)}, u32[]{:S(2)}, u32[]{:S(2)}) %all-to-all-start.1) | async-done | bytes 1835040 | tf_op jit(solution)/shard_map/all_to_all | solution.py:399
  154.9 1.9 %fusion = f32[128,1792]{1,0:T(8,128)S(1)} fusion(bf16[64,8,1792]{2,1,0:T(8,128)(2,1)} %all-to-all-done.1, bf16[64,512]{1,0:T(8,128)(2,1)S(1)} %get-tuple-element.42, bf16[64,512]{1,0:T(8,128)(2,1)S(1)} %get-tuple-element.41), kind=kOutput, calls=%fused_computation.1 | convolution fusion | flops 235143168 | bytes 2883584 | tf_op jit(solution)/shard_map/dot_general | solution.py:410
  156.9 1.4 collective-permute-start.16
  158.4 0.7 bitcast_dynamic-update-slice_fusion
  159.0 2.8 %collective-permute-done.16 = f32[16,1792]{1,0:T(8,128)S(1)} collective-permute-done((f32[16,1792]{1,0:T(8,128)S(1)}, f32[16,1792]{1,0:T(8,128)S(1)}, u32[]{:S(2)}, u32[]{:S(2)}) %collective-permute-start.16) | collective-permute-done | bytes 114720 | tf_op jit(solution)/shard_map/ppermute | solution.py:415
  161.9 0.1 collective-permute-done.17
  162.0 0.7 pad_maximum_fusion.1
  (65 shorter events, 1.0 us)
Async XLA Ops:
  3.2 9.5 %collective-permute-start = (bf16[16,1920]{1,0:T(8,128)(2,1)S(1)}, bf16[16,1920]{1,0:T(8,128)(2,1)S(1)}, u32[]{:S(2)}, u32[]{:S(2)}) collective-permute-start(bf16[16,1920]{1,0:T(8,128)(2,1)S(1)} %get-tuple-element.58), channel_id=1, source_target_pairs={{1,2},{2,1},{3,0},{0,3},{5,6},{6,5},{7,4},{4,7},{9,10},{10,9},{11,... | collective-permute-start | bytes 184328 | tf_op jit(solution)/shard_map/ppermute | solution.py:295
  6.8 6.0 %collective-permute-start.1 = (bf16[16,1920]{1,0:T(8,128)(2,1)S(1)}, bf16[16,1920]{1,0:T(8,128)(2,1)S(1)}, u32[]{:S(2)}, u32[]{:S(2)}) collective-permute-start(bf16[16,1920]{1,0:T(8,128)(2,1)S(1)} %get-tuple-element.59), channel_id=1, source_target_pairs={{2,3},{3,2},{0,1},{1,0},{6,7},{7,6},{4,5},{5,4},{10,11},{11,10},{8... | collective-permute-start | bytes 184328 | tf_op jit(solution)/shard_map/ppermute | solution.py:295
  6.8 4.4 %copy-start = (bf16[1,3584,256]{2,1,0:T(8,128)(2,1)S(1)}, bf16[1,3584,256]{2,1,0:T(8,128)(2,1)}, u32[]{:S(2)}) copy-start(bf16[1,3584,256]{2,1,0:T(8,128)(2,1)} %param.18) | copy-start | bytes 5505028
  9.7 21.1 %collective-permute-start.8 = (bf16[1792,256]{1,0:T(8,128)(2,1)}, bf16[1792,256]{1,0:T(8,128)(2,1)S(1)}, u32[]{:S(2)}, u32[]{:S(2)}) collective-permute-start(bf16[1792,256]{1,0:T(8,128)(2,1)} %get-tuple-element.22), channel_id=1, source_target_pairs={{0,3},{1,0},{2,1},{3,2},{4,7},{5,4},{6,5},{7,6},{8,11},{9,8},{10,9... | collective-permute-start | bytes 2752520 | tf_op jit(solution)/shard_map/ppermute | solution.py:18
  10.4 21.1 %collective-permute-start.9 = (bf16[1792,256]{1,0:T(8,128)(2,1)}, bf16[1792,256]{1,0:T(8,128)(2,1)}, u32[]{:S(2)}, u32[]{:S(2)}) collective-permute-start(bf16[1792,256]{1,0:T(8,128)(2,1)} %get-tuple-element.24), channel_id=1, source_target_pairs={{0,1},{1,2},{2,3},{3,0},{4,5},{5,6},{6,7},{7,4},{8,9},{9,10},{10,1... | collective-permute-start | bytes 2752520 | tf_op jit(solution)/shard_map/ppermute | solution.py:18
  11.2 1.6 %copy-start.9 = (s32[16,8]{0,1:T(8,128)S(1)}, s32[16,8]{0,1:T(8,128)}, u32[]{:S(2)}) copy-start(s32[16,8]{0,1:T(8,128)} %param.15) | copy-start | bytes 1540
  11.2 2.7 %copy-start.12 = (f32[16,8]{0,1:T(8,128)S(1)}, f32[16,8]{0,1:T(8,128)}, u32[]{:S(2)}) copy-start(f32[16,8]{0,1:T(8,128)} %param.16) | copy-start | bytes 1540
  17.3 57.5 %all-to-all-start = ((bf16[64,8,1792]{2,1,0:T(8,128)(2,1)}), bf16[64,8,1792]{2,1,0:T(8,128)(2,1)}, u32[]{:S(2)}, u32[]{:S(2)}) async-start(bf16[64,8,1792]{2,1,0:T(8,128)(2,1)} %bitcast.55), calls=%async_computation | async-start | bytes 3670016 | tf_op jit(solution)/shard_map/all_to_all | solution.py:347
  30.8 3.3 %copy-start.2 = (bf16[1792,256]{1,0:T(8,128)(2,1)}, bf16[1792,256]{1,0:T(8,128)(2,1)S(1)}, u32[]{:S(2)}) copy-start(bf16[1792,256]{1,0:T(8,128)(2,1)S(1)} %collective-permute-done.8.refs_1_.second) | copy-start | bytes 2752516
  31.5 20.2 %collective-permute-start.12 = (bf16[1792,256]{1,0:T(8,128)(2,1)}, bf16[1792,256]{1,0:T(8,128)(2,1)}, u32[]{:S(2)}, u32[]{:S(2)}) collective-permute-start(bf16[1792,256]{1,0:T(8,128)(2,1)} %get-tuple-element.27), channel_id=1, source_target_pairs={{0,1},{1,2},{2,3},{3,0},{4,5},{5,6},{6,7},{7,4},{8,9},{9,10},{10,1... | collective-permute-start | bytes 2752520 | tf_op jit(solution)/shard_map/ppermute | solution.py:18
  32.4 19.8 %collective-permute-start.13 = (bf16[1792,256]{1,0:T(8,128)(2,1)}, bf16[1792,256]{1,0:T(8,128)(2,1)}, u32[]{:S(2)}, u32[]{:S(2)}) collective-permute-start(bf16[1792,256]{1,0:T(8,128)(2,1)} %get-tuple-element.28), channel_id=1, source_target_pairs={{0,3},{1,0},{2,1},{3,2},{4,7},{5,4},{6,5},{7,6},{8,11},{9,8},{10,9... | collective-permute-start | bytes 2752520 | tf_op jit(solution)/shard_map/ppermute | solution.py:18
  37.7 44.7 %collective-permute-start.10 = (bf16[1792,256]{1,0:T(8,128)(2,1)}, bf16[1792,256]{1,0:T(8,128)(2,1)}, u32[]{:S(2)}, u32[]{:S(2)}) collective-permute-start(bf16[1792,256]{1,0:T(8,128)(2,1)} %choose.2), channel_id=1, source_target_pairs={{0,1},{1,0},{2,3},{3,2},{5,6},{6,5},{7,4},{4,7},{8,9},{9,8},{10,11... | collective-permute-start | bytes 2752520 | tf_op jit(solution)/shard_map/ppermute | solution.py:310
  55.8 30.3 %collective-permute-start.14 = (bf16[1792,256]{1,0:T(8,128)(2,1)}, bf16[1792,256]{1,0:T(8,128)(2,1)S(1)}, u32[]{:S(2)}, u32[]{:S(2)}) collective-permute-start(bf16[1792,256]{1,0:T(8,128)(2,1)} %choose.3), channel_id=1, source_target_pairs={{0,1},{1,0},{2,3},{3,2},{5,6},{6,5},{7,4},{4,7},{8,9},{9,8},{10,11... | collective-permute-start | bytes 2752520 | tf_op jit(solution)/shard_map/ppermute | solution.py:310
  74.9 1.5 copy-start.1
  76.4 1.2 copy-start.3
  80.7 8.6 %collective-permute-start.11 = (bf16[2,512,256]{2,1,0:T(8,128)(2,1)S(1)}, bf16[2,512,256]{2,1,0:T(8,128)(2,1)S(1)}, u32[]{:S(2)}, u32[]{:S(2)}) collective-permute-start(bf16[2,512,256]{2,1,0:T(8,128)(2,1)S(1)} %get-tuple-element.26), channel_id=1, source_target_pairs={{1,2},{2,1},{3,0},{0,3},{6,7},{7,6},{4,5},{5,4},{9,10},{10,9},{11,... | collective-permute-start | bytes 1572872 | tf_op jit(solution)/shard_map/ppermute | solution.py:388
  86.1 8.7 %collective-permute-start.15 = (bf16[2,512,256]{2,1,0:T(8,128)(2,1)S(1)}, bf16[2,512,256]{2,1,0:T(8,128)(2,1)S(1)}, u32[]{:S(2)}, u32[]{:S(2)}) collective-permute-start(bf16[2,512,256]{2,1,0:T(8,128)(2,1)S(1)} %get-tuple-element.30), channel_id=1, source_target_pairs={{1,2},{2,1},{3,0},{0,3},{6,7},{7,6},{4,5},{5,4},{9,10},{10,9},{11,... | collective-permute-start | bytes 1572872 | tf_op jit(solution)/shard_map/ppermute | solution.py:391
  100.8 11.2 %copy-start.7 = (s32[1,16]{1,0:T(1,128)S(1)}, s32[1,16]{1,0:T(1,128)}, u32[]{:S(2)}) copy-start(s32[1,16]{1,0:T(1,128)} %param.24) | copy-start | bytes 196
  100.8 11.5 %copy-start.11 = (bf16[16,576]{1,0:T(8,128)(2,1)S(1)}, bf16[16,576]{1,0:T(8,128)(2,1)}, u32[]{:S(2)}) copy-start(bf16[16,576]{1,0:T(8,128)(2,1)} %param.20) | copy-start | bytes 55300
  100.8 11.7 %copy-start.13 = (s32[1,32]{1,0:T(1,128)S(1)}, s32[1,32]{1,0:T(1,128)}, u32[]{:S(2)}) copy-start(s32[1,32]{1,0:T(1,128)} %param.25) | copy-start | bytes 388
  100.8 11.7 %copy-start.10 = (bf16[16,576]{1,0:T(8,128)(2,1)S(1)}, bf16[16,576]{1,0:T(8,128)(2,1)}, u32[]{:S(2)}) copy-start(bf16[16,576]{1,0:T(8,128)(2,1)} %param.22) | copy-start | bytes 55300
  100.9 11.7 %copy-start.4 = (bf16[16,64,576]{2,1,0:T(8,128)(2,1)S(1)}, bf16[16,64,576]{2,1,0:T(8,128)(2,1)}, u32[]{:S(2)}) copy-start(bf16[16,64,576]{2,1,0:T(8,128)(2,1)} %q_two) | copy-start | bytes 3538948
  100.9 13.9 %copy-start.8 = (f32[64,512]{1,0:T(8,128)S(1)}, f32[64,512]{1,0:T(8,128)}, u32[]{:S(2)}) copy-start(f32[64,512]{1,0:T(8,128)} %get-tuple-element.31) | copy-start | bytes 393220
  100.9 21.6 %copy-start.6 = (bf16[16,64,576]{2,1,0:T(8,128)(2,1)S(1)}, bf16[16,64,576]{2,1,0:T(8,128)(2,1)}, u32[]{:S(2)}) copy-start(bf16[16,64,576]{2,1,0:T(8,128)(2,1)} %q_one.1) | copy-start | bytes 3538948
  100.9 54.0 %all-to-all-start.1 = ((bf16[64,8,1792]{2,1,0:T(8,128)(2,1)}), bf16[64,8,1792]{2,1,0:T(8,128)(2,1)}, u32[]{:S(2)}, u32[]{:S(2)}) async-start(bf16[64,8,1792]{2,1,0:T(8,128)(2,1)} %bitcast.27), calls=%async_computation.1 | async-start | bytes 3670016 | tf_op jit(solution)/shard_map/all_to_all | solution.py:399
  112.7 4.1 %collective-permute-start.4 = (bf16[80,576]{1,0:T(8,128)(2,1)S(1)}, bf16[80,576]{1,0:T(8,128)(2,1)S(1)}, u32[]{:S(2)}, u32[]{:S(2)}) collective-permute-start(bf16[80,576]{1,0:T(8,128)(2,1)S(1)} %maximum_maximum_fusion), channel_id=1, source_target_pairs={{0,3},{1,0},{2,1},{3,2},{4,7},{5,4},{6,5},{7,6},{8,11},{9,8},{10,9... | collective-permute-start | bytes 276488 | tf_op jit(solution)/shard_map/ppermute | solution.py:18
  114.1 5.5 %collective-permute-start.3 = (bf16[80,576]{1,0:T(8,128)(2,1)S(1)}, bf16[80,576]{1,0:T(8,128)(2,1)S(1)}, u32[]{:S(2)}, u32[]{:S(2)}) collective-permute-start(bf16[80,576]{1,0:T(8,128)(2,1)S(1)} %maximum_maximum_fusion), channel_id=1, source_target_pairs={{0,2},{1,3},{2,0},{3,1},{4,6},{5,7},{6,4},{7,5},{8,10},{9,11},{10,... | collective-permute-start | bytes 276488 | tf_op jit(solution)/shard_map/ppermute | solution.py:18
  114.3 8.0 %collective-permute-start.2 = (bf16[80,576]{1,0:T(8,128)(2,1)S(1)}, bf16[80,576]{1,0:T(8,128)(2,1)S(1)}, u32[]{:S(2)}, u32[]{:S(2)}) collective-permute-start(bf16[80,576]{1,0:T(8,128)(2,1)S(1)} %maximum_maximum_fusion), channel_id=1, source_target_pairs={{0,1},{1,2},{2,3},{3,0},{4,5},{5,6},{6,7},{7,4},{8,9},{9,10},{10,1... | collective-permute-start | bytes 276488 | tf_op jit(solution)/shard_map/ppermute | solution.py:18
  122.5 1.7 %copy-start.5 = (bf16[32,64,576]{2,1,0:T(8,128)(2,1)S(1)}, bf16[32,64,576]{2,1,0:T(8,128)(2,1)}, u32[]{:S(2)}) copy-start(bf16[32,64,576]{2,1,0:T(8,128)(2,1)} %pool.1) | copy-start | bytes 7077892
  143.2 15.2 %collective-permute-start.5 = (bf16[64,512]{1,0:T(8,128)(2,1)S(1)}, bf16[64,512]{1,0:T(8,128)(2,1)S(1)}, u32[]{:S(2)}, u32[]{:S(2)}) collective-permute-start(bf16[64,512]{1,0:T(8,128)(2,1)S(1)} %get-tuple-element.47), channel_id=1, source_target_pairs={{0,1},{1,2},{2,3},{3,0},{4,5},{5,6},{6,7},{7,4},{8,9},{9,10},{10,1... | collective-permute-start | bytes 196616 | tf_op jit(solution)/shard_map/ppermute | solution.py:18
  143.2 15.1 %collective-permute-start.7 = (bf16[64,512]{1,0:T(8,128)(2,1)S(1)}, bf16[64,512]{1,0:T(8,128)(2,1)S(1)}, u32[]{:S(2)}, u32[]{:S(2)}) collective-permute-start(bf16[64,512]{1,0:T(8,128)(2,1)S(1)} %get-tuple-element.48), channel_id=1, source_target_pairs={{0,3},{1,0},{2,1},{3,2},{4,7},{5,4},{6,5},{7,6},{8,11},{9,8},{10,9... | collective-permute-start | bytes 196616 | tf_op jit(solution)/shard_map/ppermute | solution.py:18
  145.9 12.5 %collective-permute-start.6 = (bf16[64,512]{1,0:T(8,128)(2,1)S(1)}, bf16[64,512]{1,0:T(8,128)(2,1)S(1)}, u32[]{:S(2)}, u32[]{:S(2)}) collective-permute-start(bf16[64,512]{1,0:T(8,128)(2,1)S(1)} %get-tuple-element.49), channel_id=1, source_target_pairs={{0,2},{1,3},{2,0},{3,1},{4,6},{5,7},{6,4},{7,5},{8,10},{9,11},{10,... | collective-permute-start | bytes 196616 | tf_op jit(solution)/shard_map/ppermute | solution.py:18
  156.9 4.9 %collective-permute-start.16 = (f32[16,1792]{1,0:T(8,128)S(1)}, f32[16,1792]{1,0:T(8,128)S(1)}, u32[]{:S(2)}, u32[]{:S(2)}) collective-permute-start(f32[16,1792]{1,0:T(8,128)S(1)} %get-tuple-element.39), channel_id=1, source_target_pairs={{1,2},{2,1},{3,0},{0,3},{5,6},{6,5},{7,4},{4,7},{9,10},{10,9},{11,... | collective-permute-start | bytes 344072 | tf_op jit(solution)/shard_map/ppermute | solution.py:415
  158.3 3.6 %collective-permute-start.17 = (f32[16,1792]{1,0:T(8,128)S(1)}, f32[16,1792]{1,0:T(8,128)S(1)}, u32[]{:S(2)}, u32[]{:S(2)}) collective-permute-start(f32[16,1792]{1,0:T(8,128)S(1)} %get-tuple-element.40), channel_id=1, source_target_pairs={{2,3},{3,2},{0,1},{1,0},{6,7},{7,6},{4,5},{5,4},{10,11},{11,10},{8... | collective-permute-start | bytes 344072 | tf_op jit(solution)/shard_map/ppermute | solution.py:415

commit v13 on v12

--- a/solution.py
+++ b/solution.py
@@ -185,13 +185,16 @@
 
     @pl.when(pl.program_id(0) == 0)
     def _():
-        mine = [mine_a[0], mine_a[1], mine_b[0], mine_b[1]]
+        mine = [mine_a.at[0], mine_a.at[1], mine_b.at[0], mine_b.at[1]]
         theirs = [theirs_a.at[0], theirs_a.at[1], theirs_b.at[0], theirs_b.at[1]]
-        for i in range(4):
-            up, down = theirs[(i + 1) % 4][...], theirs[(i - 1) % 4][...]
-            other = jnp.where(scalars[1] == 1, up.astype(jnp.float32), down.astype(jnp.float32))
-            value = mine[i] + other
-            held[i] = (value / (1.0 + jnp.exp(-value))).astype(jnp.bfloat16)
+
+        def fill(turn):
+            for i in range(4):
+                value = mine[i][...] + theirs[(i + turn) % 4][...].astype(jnp.float32)
+                held[i] = (value / (1.0 + jnp.exp(-value))).astype(jnp.bfloat16)
+
+        pl.when(scalars[1] == 1)(lambda: fill(1))
+        pl.when(scalars[1] != 1)(lambda: fill(3))
 
     total = None
     for i, weight in enumerate(weights):
@@ -299,9 +302,9 @@
         rows += [part(hidden, side[c], 1), theirs[:, :half]]
     rows = jnp.concatenate(rows, axis=0)
 
-    ahead = jnp.where((here == 0) | (here == 3), 0, 1)
-
-    def spread(weight, *first):
+    lead = jnp.where((here == 0) | (here == 3), 0, 1)
+
+    def spread(weight, ahead, *first):
         to_next, to_prev = after(first, part(weight, ahead, 0), part(weight, 1 - ahead, 0))
         return hop(to_next, "grp", 1), hop(to_prev, "grp", -1)
 
@@ -310,10 +313,8 @@
         far = lax.ppermute(picked, ("ep", "grp"), by_core([(0, 1), (1, 0), (2, 3), (3, 2)]))
         return far
 
-    up_prev, up_next = spread(w_up[0], rows)
+    up_prev, up_next = spread(w_up[0], lead, rows)
     up_far = pass_on(up_prev, up_next, 200_000_000_000)
-    down_prev, down_next = spread(w_down[0], up_prev, up_next)
-    down_far = pass_on(down_prev, down_next, 0)
 
     rank = 2 * capacity
     lanes_all = ep_size * rank
@@ -344,6 +345,9 @@
     outgoing = lax.dot_general(
         placing, rows, (((0,), (0,)), ((), ())), preferred_element_type=jnp.float32
     ).astype(jnp.bfloat16)
+    late = jnp.minimum(placing[0, 0].astype(jnp.float32), 0.0).astype(jnp.int32)
+    down_prev, down_next = spread(w_down[0], lead + late, up_prev, up_next)
+    down_far = pass_on(down_prev, down_next, 0)
     arrived = lax.all_to_all(
         outgoing.reshape(ep_size, rank, half), "ep", split_axis=0, concat_axis=0, tiled=True
     ).reshape(lanes_all, half)

time: 165 us -> 165 us (level)
  transfers between devices with their start and end apart: 20 -> 20, of which waited for: 13 -> 11; matrix products, arithmetic and copies ran while one was open for 8% -> 8% of each run, Pallas kernels for 20% -> 20%
where the time goes in v13:
time: 165 us; the launch traced here: 162 us
  waiting for transfers between devices  59.7 us (36%)
  starting transfers between devices  40.7 us (25%)
  Pallas kernels  38.3 us (23%)
  local copies, waits for them, and re-layouts  11.3 us (7%)
  other arithmetic  5.18 us (3%)
  matrix products  4.11 us (2%)
  between operations  3.11 us (2%)
    ppermute x10, waiting for transfers between devices, hop(): lax.ppermute(value, axis, [(i, (i + step) % size) for i in range(size)])  23.3 us
    pallas_call x1, Pallas kernels, attention(): pl.pallas_call(attention_kernel, grid_spec=pltpu.PrefetchScalarGridSpec(n...  18.4 us
    all_to_all x1, waiting for transfers between devices, shards(): lax.all_to_all(outgoing.reshape(ep_size, rank, half), 'ep', split_axis=0,...  15.5 us
    all_to_all x1, starting transfers between devices, shards(): lax.all_to_all(outgoing.reshape(ep_size, rank, half), 'ep', split_axis=0,...  13.4 us
    all_to_all x1, starting transfers between devices, shards(): lax.all_to_all(produced.reshape(ep_size, rank, half), 'ep', split_axis=0,...  9.81 us
    all_to_all x1, waiting for transfers between devices, shards(): lax.all_to_all(produced.reshape(ep_size, rank, half), 'ep', split_axis=0,...  9.49 us
    ppermute x10, starting transfers between devices, hop(): lax.ppermute(value, axis, [(i, (i + step) % size) for i in range(size)])  9.05 us
    pallas_call x2, Pallas kernels, choose(): pl.pallas_call(choose_kernel, grid_spec=pltpu.PrefetchScalarGridSpec(num_...  7.13 us
  transfers between devices with their start and end apart: 20, of which 11 were waited for; matrix products, arithmetic and copies ran while one was open for 8% of the time, Pallas kernels for 20%

profile of v13, /device:TPU:1, one launch (start us, length us, event | category | flops | bytes accessed | tf_op | source)
XLA Modules:
  0.0 162.4 jit_solution(12767092575056330009)
XLA Ops:
  0.7 0.7 convert_convert_fusion
  1.4 0.7 reduce-precision_convert_fusion.2
  2.1 0.1 copy.43
  2.2 0.9 constant_dynamic-slice_fusion.2
  3.1 3.7 %collective-permute-start = (bf16[16,1920]{1,0:T(8,128)(2,1)S(1)}, bf16[16,1920]{1,0:T(8,128)(2,1)S(1)}, u32[]{:S(2)}, u32[]{:S(2)}) collective-permute-start(bf16[16,1920]{1,0:T(8,128)(2,1)S(1)} %get-tuple-element.58), channel_id=1, source_target_pairs={{1,2},{2,1},{3,0},{0,3},{5,6},{6,5},{7,4},{4,7},{9,10},{10,9},{11,... | collective-permute-start | bytes 184328 | tf_op jit(solution)/shard_map/ppermute | solution.py:298
  6.8 2.8 %dynamic-slice_bitcast_fusion.2 = (bf16[1792,256]{1,0:T(8,128)(2,1)}, bf16[1792,256]{1,0:T(8,128)(2,1)}) fusion(bf16[1,3584,256]{2,1,0:T(8,128)(2,1)} %param.17, s32[]{:T(128)S(6)} %select_n.256, s32[]{:T(128)S(6)} %select_n.255), kind=kLoop, calls=%fused_computation.10 | loop fusion | bytes 3670024 | tf_op jit(solution)/shard_map/dynamic_slice | solution.py:286
  9.6 0.6 collective-permute-start.8
  10.3 0.8 collective-permute-start.9
  11.4 0.1 copy.37
  11.4 0.1 eq.111
  11.5 0.3 fusion.2
  11.9 0.1 convert_element_type.58
  12.0 0.1 multiply_add_fusion
  12.1 0.1 add_select_fusion.6
  12.2 0.1 pad_add_fusion.1
  12.3 0.1 copy.39
  12.4 0.1 pad_maximum_fusion.3
  12.4 0.1 copy.42
  12.5 1.3 select_reduce_fusion
  13.9 0.6 slice.120
  15.2 1.9 %convolution_convert_fusion = bf16[512,1792]{1,0:T(8,128)(2,1)} fusion(bf16[64,512]{1,0:T(8,128)(2,1)S(1)} %get-tuple-element.32, bf16[16,1792]{1,0:T(8,128)(2,1)S(1)} %slice.111, bf16[16,1792]{1,0:T(8,128)(2,1)S(1)} %get-tuple-element.46, bf16[16,1792]{1,0:T(8,128)(2,1)S(1)} %slice.110, bf16[16,1792]{1,0:T(8,128)(2,1)S(1)} %get-tuple-element.43), kind=kOutput, calls=%fused_computation | convolution fusion | flops 119275520 | bytes 2129920 | tf_op jit(solution)/shard_map/dot_general | solution.py:345
  17.0 13.4 %all-to-all-start = ((bf16[64,8,1792]{2,1,0:T(8,128)(2,1)}), bf16[64,8,1792]{2,1,0:T(8,128)(2,1)}, u32[]{:S(2)}, u32[]{:S(2)}) async-start(bf16[64,8,1792]{2,1,0:T(8,128)(2,1)} %bitcast.56), calls=%async_computation | async-start | bytes 3670016 | tf_op jit(solution)/shard_map/all_to_all | solution.py:351
  30.5 1.5 dynamic-slice_bitcast_fusion
  32.0 1.7 %collective-permute-start.12 = (bf16[1792,256]{1,0:T(8,128)(2,1)}, bf16[1792,256]{1,0:T(8,128)(2,1)}, u32[]{:S(2)}, u32[]{:S(2)}) collective-permute-start(bf16[1792,256]{1,0:T(8,128)(2,1)} %get-tuple-element.27), channel_id=1, source_target_pairs={{0,1},{1,2},{2,3},{3,0},{4,5},{5,6},{6,7},{7,4},{8,9},{9,10},{10,1... | collective-permute-start | bytes 2752520 | tf_op jit(solution)/shard_map/ppermute | solution.py:18
  33.7 1.1 collective-permute-start.13
  34.7 3.5 %choose.2 = bf16[1792,256]{1,0:T(8,128)(2,1)} custom-call(s32[1]{0:T(128)} %bitcast.23.which, bf16[1792,256]{1,0:T(8,128)(2,1)} %collective-permute-done.9.first.refs_1_, bf16[1792,256]{1,0:T(8,128)(2,1)} %copy-done.2), custom_call_target="tpu_custom_call" | custom-call | flops 199999995904 | bytes 2752512 | tf_op jit(solution)/shard_map/choose/pallas_call | solution.py:132
  38.3 0.8 collective-permute-start.10
  39.1 14.0 %collective-permute-done.12.first.refs_3_ = bf16[1792,256]{1,0:T(8,128)(2,1)} collective-permute-done((bf16[1792,256]{1,0:T(8,128)(2,1)}, bf16[1792,256]{1,0:T(8,128)(2,1)}, u32[]{:S(2)}, u32[]{:S(2)}) %collective-permute-start.12) | collective-permute-done | bytes 917536 | tf_op jit(solution)/shard_map/ppermute | solution.py:18
  53.1 1.9 %collective-permute-done.13.second.refs_1_ = bf16[1792,256]{1,0:T(8,128)(2,1)} collective-permute-done((bf16[1792,256]{1,0:T(8,128)(2,1)}, bf16[1792,256]{1,0:T(8,128)(2,1)}, u32[]{:S(2)}, u32[]{:S(2)}) %collective-permute-start.13) | collective-permute-done | bytes 917536 | tf_op jit(solution)/shard_map/ppermute | solution.py:18
  54.9 3.6 %choose.3 = bf16[1792,256]{1,0:T(8,128)(2,1)} custom-call(s32[1]{0:T(128)} %bitcast.23.which, bf16[1792,256]{1,0:T(8,128)(2,1)} %collective-permute-done.12.first.refs_3_, bf16[1792,256]{1,0:T(8,128)(2,1)} %collective-permute-done.13.second.refs_1_), custom_call_target="tpu_custom_call" | custom-call | bytes 2752512 | tf_op jit(solution)/shard_map/choose/pallas_call | solution.py:132
  58.5 0.6 collective-permute-start.14
  59.2 15.5 %all-to-all-done = bf16[64,8,1792]{2,1,0:T(8,128)(2,1)} async-done(((bf16[64,8,1792]{2,1,0:T(8,128)(2,1)}), bf16[64,8,1792]{2,1,0:T(8,128)(2,1)}, u32[]{:S(2)}, u32[]{:S(2)}) %all-to-all-start) | async-done | bytes 1835040 | tf_op jit(solution)/shard_map/all_to_all | solution.py:351
  74.7 1.5 copy-done.1
  76.2 1.2 copy-done.3
  77.4 3.1 %up_project.2 = (f32[2,512,256]{2,1,0:T(8,128)S(1)}, bf16[2,512,256]{2,1,0:T(8,128)(2,1)S(1)}) custom-call(s32[2]{0:T(128)S(1)} %pad_add_fusion.2._.scalars, bf16[512,1792]{1,0:T(8,128)(2,1)} %bitcast.19.rows, bf16[3584,256]{1,0:T(8,128)(2,1)S(1)} %bitcast.54, bf16[1792,256]{1,0:T(8,128)(2,1)S(1)} %copy-done.3), custom_call_target="tpu_custom_call" | custom-call | flops 939524096 | bytes 5000000 | tf_op jit(solution)/shard_map/up_project/pallas_call | solution.py:160
  80.5 1.7 %collective-permute-start.11 = (bf16[2,512,256]{2,1,0:T(8,128)(2,1)S(1)}, bf16[2,512,256]{2,1,0:T(8,128)(2,1)S(1)}, u32[]{:S(2)}, u32[]{:S(2)}) collective-permute-start(bf16[2,512,256]{2,1,0:T(8,128)(2,1)S(1)} %get-tuple-element.26), channel_id=1, source_target_pairs={{1,2},{2,1},{3,0},{0,3},{6,7},{7,6},{4,5},{5,4},{9,10},{10,9},{11,... | collective-permute-start | bytes 1572872 | tf_op jit(solution)/shard_map/ppermute | solution.py:392
  82.2 3.7 %up_project.3 = (f32[2,512,256]{2,1,0:T(8,128)S(1)}, bf16[2,512,256]{2,1,0:T(8,128)(2,1)S(1)}) custom-call(s32[2]{0:T(128)S(1)} %pad_add_fusion.2._.scalars, bf16[512,1792]{1,0:T(8,128)(2,1)} %bitcast.19.rows, bf16[1792,256]{1,0:T(8,128)(2,1)} %collective-permute-done.10.refs_0_, bf16[1792,256]{1,0:T(8,128)(2,1)} %collective-permute-done.9.first.refs_1_), custom_call_target="tpu_custom_call" | custom-call | flops 939524096 | bytes 5000000 | tf_op jit(solution)/shard_map/up_project/pallas_call | solution.py:160
  86.0 0.3 collective-permute-start.15
  86.3 2.8 %collective-permute-done.11.theirs_a = bf16[2,512,256]{2,1,0:T(8,128)(2,1)S(1)} collective-permute-done((bf16[2,512,256]{2,1,0:T(8,128)(2,1)S(1)}, bf16[2,512,256]{2,1,0:T(8,128)(2,1)S(1)}, u32[]{:S(2)}, u32[]{:S(2)}) %collective-permute-start.11) | collective-permute-done | bytes 524320 | tf_op jit(solution)/shard_map/ppermute | solution.py:392
  89.1 5.6 %collective-permute-done.15.theirs_b = bf16[2,512,256]{2,1,0:T(8,128)(2,1)S(1)} collective-permute-done((bf16[2,512,256]{2,1,0:T(8,128)(2,1)S(1)}, bf16[2,512,256]{2,1,0:T(8,128)(2,1)S(1)}, u32[]{:S(2)}, u32[]{:S(2)}) %collective-permute-start.15) | collective-permute-done | bytes 524320 | tf_op jit(solution)/shard_map/ppermute | solution.py:395
  94.7 5.8 %down_project.1 = bf16[512,1792]{1,0:T(8,128)(2,1)} custom-call(s32[2]{0:T(128)S(1)} %pad_add_fusion.2._.scalars, f32[2,512,256]{2,1,0:T(8,128)S(1)} %get-tuple-element.23.mine_a, f32[2,512,256]{2,1,0:T(8,128)S(1)} %get-tuple-element.25.mine_b, bf16[2,512,256]{2,1,0:T(8,128)(2,1)S(1)} %collective-permute-done.11.theirs_a, ...), custom_call_target="tpu_custom_call" | custom-call | flops 1879048192 | bytes 9000000 | tf_op jit(solution)/shard_map/down_project/pallas_call | solution.py:213
  100.6 9.8 %all-to-all-start.1 = ((bf16[64,8,1792]{2,1,0:T(8,128)(2,1)}), bf16[64,8,1792]{2,1,0:T(8,128)(2,1)}, u32[]{:S(2)}, u32[]{:S(2)}) async-start(bf16[64,8,1792]{2,1,0:T(8,128)(2,1)} %bitcast.28), calls=%async_computation.1 | async-start | bytes 3670016 | tf_op jit(solution)/shard_map/all_to_all | solution.py:403
  111.8 0.1 select_reduce_fusion.2
  112.0 0.1 min.19
  112.2 0.1 select_reduce_fusion.1.pages
  112.3 0.1 maximum_maximum_fusion
  112.4 1.4 collective-permute-start.4
  113.8 0.2 collective-permute-start.3
  114.0 0.5 collective-permute-start.2
  114.6 2.0 %collective-permute-done.4 = bf16[80,576]{1,0:T(8,128)(2,1)S(1)} collective-permute-done((bf16[80,576]{1,0:T(8,128)(2,1)S(1)}, bf16[80,576]{1,0:T(8,128)(2,1)S(1)}, u32[]{:S(2)}, u32[]{:S(2)}) %collective-permute-start.4) | collective-permute-done | bytes 92192 | tf_op jit(solution)/shard_map/ppermute | solution.py:18
  116.5 2.8 %collective-permute-done.3 = bf16[80,576]{1,0:T(8,128)(2,1)S(1)} collective-permute-done((bf16[80,576]{1,0:T(8,128)(2,1)S(1)}, bf16[80,576]{1,0:T(8,128)(2,1)S(1)}, u32[]{:S(2)}, u32[]{:S(2)}) %collective-permute-start.3) | collective-permute-done | bytes 92192 | tf_op jit(solution)/shard_map/ppermute | solution.py:18
  119.3 2.7 %collective-permute-done.2 = bf16[80,576]{1,0:T(8,128)(2,1)S(1)} collective-permute-done((bf16[80,576]{1,0:T(8,128)(2,1)S(1)}, bf16[80,576]{1,0:T(8,128)(2,1)S(1)}, u32[]{:S(2)}, u32[]{:S(2)}) %collective-permute-start.2) | collective-permute-done | bytes 92192 | tf_op jit(solution)/shard_map/ppermute | solution.py:18
  122.0 0.1 select_select_fusion
  122.2 1.7 %copy-done.5 = bf16[32,64,576]{2,1,0:T(8,128)(2,1)S(1)} copy-done((bf16[32,64,576]{2,1,0:T(8,128)(2,1)S(1)}, bf16[32,64,576]{2,1,0:T(8,128)(2,1)}, u32[]{:S(2)}) %copy-start.5) | copy-done | bytes 2359320
  123.9 18.4 %attention.1 = (bf16[16,64,512]{2,1,0:T(8,128)(2,1)}, bf16[16,64,512]{2,1,0:T(8,128)(2,1)}, bf16[64,512]{1,0:T(8,128)(2,1)S(1)}) custom-call(s32[16]{0:T(128)S(1)} %bitcast.55, s32[128]{0:T(128)S(1)} %select_reduce_fusion.1.pages, s32[1]{0:T(128)} %bitcast.48.moved, bf16[16,64,576]{2,1,0:T(8,128)(2,1)S(1)} %copy-done.6, bf16[16,64,576]{2,1,0:T(8,128)(2,1)S(1)} %copy-done.4, ...), custom_call_target="tpu_custom_call" | custom-call | flops 12000000000 | bytes 8000000 | tf_op jit(solution)/shard_map/attention/pallas_call | solution.py:89
  142.4 0.1 collective-permute-start.5
  142.5 2.7 %collective-permute-start.7 = (bf16[64,512]{1,0:T(8,128)(2,1)S(1)}, bf16[64,512]{1,0:T(8,128)(2,1)S(1)}, u32[]{:S(2)}, u32[]{:S(2)}) collective-permute-start(bf16[64,512]{1,0:T(8,128)(2,1)S(1)} %get-tuple-element.48), channel_id=1, source_target_pairs={{0,3},{1,0},{2,1},{3,2},{4,7},{5,4},{6,5},{7,6},{8,11},{9,8},{10,9... | collective-permute-start | bytes 196616 | tf_op jit(solution)/shard_map/ppermute | solution.py:18
  145.1 9.5 %all-to-all-done.1 = bf16[64,8,1792]{2,1,0:T(8,128)(2,1)} async-done(((bf16[64,8,1792]{2,1,0:T(8,128)(2,1)}), bf16[64,8,1792]{2,1,0:T(8,128)(2,1)}, u32[]{:S(2)}, u32[]{:S(2)}) %all-to-all-start.1) | async-done | bytes 1835040 | tf_op jit(solution)/shard_map/all_to_all | solution.py:403
  154.6 1.9 %fusion = f32[128,1792]{1,0:T(8,128)S(1)} fusion(bf16[64,8,1792]{2,1,0:T(8,128)(2,1)} %all-to-all-done.1, bf16[64,512]{1,0:T(8,128)(2,1)S(1)} %get-tuple-element.42, bf16[64,512]{1,0:T(8,128)(2,1)S(1)} %get-tuple-element.41), kind=kOutput, calls=%fused_computation.1 | convolution fusion | flops 235143168 | bytes 2883584 | tf_op jit(solution)/shard_map/dot_general | solution.py:414
  156.6 1.4 collective-permute-start.16
  158.1 0.7 bitcast_dynamic-update-slice_fusion
  158.8 2.8 %collective-permute-done.16 = f32[16,1792]{1,0:T(8,128)S(1)} collective-permute-done((f32[16,1792]{1,0:T(8,128)S(1)}, f32[16,1792]{1,0:T(8,128)S(1)}, u32[]{:S(2)}, u32[]{:S(2)}) %collective-permute-start.16) | collective-permute-done | bytes 114720 | tf_op jit(solution)/shard_map/ppermute | solution.py:419
  161.6 0.1 collective-permute-done.17
  161.7 0.7 pad_maximum_fusion.1
  (66 shorter events, 0.9 us)
Async XLA Ops:
  3.1 8.0 %collective-permute-start = (bf16[16,1920]{1,0:T(8,128)(2,1)S(1)}, bf16[16,1920]{1,0:T(8,128)(2,1)S(1)}, u32[]{:S(2)}, u32[]{:S(2)}) collective-permute-start(bf16[16,1920]{1,0:T(8,128)(2,1)S(1)} %get-tuple-element.58), channel_id=1, source_target_pairs={{1,2},{2,1},{3,0},{0,3},{5,6},{6,5},{7,4},{4,7},{9,10},{10,9},{11,... | collective-permute-start | bytes 184328 | tf_op jit(solution)/shard_map/ppermute | solution.py:298
  6.8 4.4 %collective-permute-start.1 = (bf16[16,1920]{1,0:T(8,128)(2,1)S(1)}, bf16[16,1920]{1,0:T(8,128)(2,1)S(1)}, u32[]{:S(2)}, u32[]{:S(2)}) collective-permute-start(bf16[16,1920]{1,0:T(8,128)(2,1)S(1)} %get-tuple-element.59), channel_id=1, source_target_pairs={{2,3},{3,2},{0,1},{1,0},{6,7},{7,6},{4,5},{5,4},{10,11},{11,10},{8... | collective-permute-start | bytes 184328 | tf_op jit(solution)/shard_map/ppermute | solution.py:298
  6.8 4.5 %copy-start.9 = (s32[16,8]{0,1:T(8,128)S(1)}, s32[16,8]{0,1:T(8,128)}, u32[]{:S(2)}) copy-start(s32[16,8]{0,1:T(8,128)} %param.15) | copy-start | bytes 1540
  6.8 5.6 %copy-start.12 = (f32[16,8]{0,1:T(8,128)S(1)}, f32[16,8]{0,1:T(8,128)}, u32[]{:S(2)}) copy-start(f32[16,8]{0,1:T(8,128)} %param.16) | copy-start | bytes 1540
  9.6 22.3 %collective-permute-start.8 = (bf16[1792,256]{1,0:T(8,128)(2,1)}, bf16[1792,256]{1,0:T(8,128)(2,1)S(1)}, u32[]{:S(2)}, u32[]{:S(2)}) collective-permute-start(bf16[1792,256]{1,0:T(8,128)(2,1)} %get-tuple-element.22), channel_id=1, source_target_pairs={{0,3},{1,0},{2,1},{3,2},{4,7},{5,4},{6,5},{7,6},{8,11},{9,8},{10,9... | collective-permute-start | bytes 2752520 | tf_op jit(solution)/shard_map/ppermute | solution.py:18
  10.3 21.7 %collective-permute-start.9 = (bf16[1792,256]{1,0:T(8,128)(2,1)}, bf16[1792,256]{1,0:T(8,128)(2,1)}, u32[]{:S(2)}, u32[]{:S(2)}) collective-permute-start(bf16[1792,256]{1,0:T(8,128)(2,1)} %get-tuple-element.24), channel_id=1, source_target_pairs={{0,1},{1,2},{2,3},{3,0},{4,5},{5,6},{6,7},{7,4},{8,9},{9,10},{10,1... | collective-permute-start | bytes 2752520 | tf_op jit(solution)/shard_map/ppermute | solution.py:18
  17.0 13.5 %copy-start = (bf16[1,3584,256]{2,1,0:T(8,128)(2,1)S(1)}, bf16[1,3584,256]{2,1,0:T(8,128)(2,1)}, u32[]{:S(2)}) copy-start(bf16[1,3584,256]{2,1,0:T(8,128)(2,1)} %param.18) | copy-start | bytes 5505028
  17.0 57.7 %all-to-all-start = ((bf16[64,8,1792]{2,1,0:T(8,128)(2,1)}), bf16[64,8,1792]{2,1,0:T(8,128)(2,1)}, u32[]{:S(2)}, u32[]{:S(2)}) async-start(bf16[64,8,1792]{2,1,0:T(8,128)(2,1)} %bitcast.56), calls=%async_computation | async-start | bytes 3670016 | tf_op jit(solution)/shard_map/all_to_all | solution.py:351
  32.0 2.8 %copy-start.2 = (bf16[1792,256]{1,0:T(8,128)(2,1)}, bf16[1792,256]{1,0:T(8,128)(2,1)S(1)}, u32[]{:S(2)}) copy-start(bf16[1792,256]{1,0:T(8,128)(2,1)S(1)} %collective-permute-done.8.refs_1_.second) | copy-start | bytes 2752516
  32.0 21.1 %collective-permute-start.12 = (bf16[1792,256]{1,0:T(8,128)(2,1)}, bf16[1792,256]{1,0:T(8,128)(2,1)}, u32[]{:S(2)}, u32[]{:S(2)}) collective-permute-start(bf16[1792,256]{1,0:T(8,128)(2,1)} %get-tuple-element.27), channel_id=1, source_target_pairs={{0,1},{1,2},{2,3},{3,0},{4,5},{5,6},{6,7},{7,4},{8,9},{9,10},{10,1... | collective-permute-start | bytes 2752520 | tf_op jit(solution)/shard_map/ppermute | solution.py:18
  33.7 21.3 %collective-permute-start.13 = (bf16[1792,256]{1,0:T(8,128)(2,1)}, bf16[1792,256]{1,0:T(8,128)(2,1)}, u32[]{:S(2)}, u32[]{:S(2)}) collective-permute-start(bf16[1792,256]{1,0:T(8,128)(2,1)} %get-tuple-element.28), channel_id=1, source_target_pairs={{0,3},{1,0},{2,1},{3,2},{4,7},{5,4},{6,5},{7,6},{8,11},{9,8},{10,9... | collective-permute-start | bytes 2752520 | tf_op jit(solution)/shard_map/ppermute | solution.py:18
  38.3 44.0 %collective-permute-start.10 = (bf16[1792,256]{1,0:T(8,128)(2,1)}, bf16[1792,256]{1,0:T(8,128)(2,1)}, u32[]{:S(2)}, u32[]{:S(2)}) collective-permute-start(bf16[1792,256]{1,0:T(8,128)(2,1)} %choose.2), channel_id=1, source_target_pairs={{0,1},{1,0},{2,3},{3,2},{5,6},{6,5},{7,4},{4,7},{8,9},{9,8},{10,11... | collective-permute-start | bytes 2752520 | tf_op jit(solution)/shard_map/ppermute | solution.py:313
  58.5 27.4 %collective-permute-start.14 = (bf16[1792,256]{1,0:T(8,128)(2,1)}, bf16[1792,256]{1,0:T(8,128)(2,1)S(1)}, u32[]{:S(2)}, u32[]{:S(2)}) collective-permute-start(bf16[1792,256]{1,0:T(8,128)(2,1)} %choose.3), channel_id=1, source_target_pairs={{0,1},{1,0},{2,3},{3,2},{5,6},{6,5},{7,4},{4,7},{8,9},{9,8},{10,11... | collective-permute-start | bytes 2752520 | tf_op jit(solution)/shard_map/ppermute | solution.py:313
  74.7 1.5 copy-start.1
  76.2 1.2 copy-start.3
  80.5 8.6 %collective-permute-start.11 = (bf16[2,512,256]{2,1,0:T(8,128)(2,1)S(1)}, bf16[2,512,256]{2,1,0:T(8,128)(2,1)S(1)}, u32[]{:S(2)}, u32[]{:S(2)}) collective-permute-start(bf16[2,512,256]{2,1,0:T(8,128)(2,1)S(1)} %get-tuple-element.26), channel_id=1, source_target_pairs={{1,2},{2,1},{3,0},{0,3},{6,7},{7,6},{4,5},{5,4},{9,10},{10,9},{11,... | collective-permute-start | bytes 1572872 | tf_op jit(solution)/shard_map/ppermute | solution.py:392
  86.0 8.7 %collective-permute-start.15 = (bf16[2,512,256]{2,1,0:T(8,128)(2,1)S(1)}, bf16[2,512,256]{2,1,0:T(8,128)(2,1)S(1)}, u32[]{:S(2)}, u32[]{:S(2)}) collective-permute-start(bf16[2,512,256]{2,1,0:T(8,128)(2,1)S(1)} %get-tuple-element.30), channel_id=1, source_target_pairs={{1,2},{2,1},{3,0},{0,3},{6,7},{7,6},{4,5},{5,4},{9,10},{10,9},{11,... | collective-permute-start | bytes 1572872 | tf_op jit(solution)/shard_map/ppermute | solution.py:395
  100.5 11.2 %copy-start.7 = (s32[1,16]{1,0:T(1,128)S(1)}, s32[1,16]{1,0:T(1,128)}, u32[]{:S(2)}) copy-start(s32[1,16]{1,0:T(1,128)} %param.24) | copy-start | bytes 196
  100.5 11.5 %copy-start.11 = (bf16[16,576]{1,0:T(8,128)(2,1)S(1)}, bf16[16,576]{1,0:T(8,128)(2,1)}, u32[]{:S(2)}) copy-start(bf16[16,576]{1,0:T(8,128)(2,1)} %param.20) | copy-start | bytes 55300
  100.5 11.7 %copy-start.13 = (s32[1,32]{1,0:T(1,128)S(1)}, s32[1,32]{1,0:T(1,128)}, u32[]{:S(2)}) copy-start(s32[1,32]{1,0:T(1,128)} %param.25) | copy-start | bytes 388
  100.6 11.7 %copy-start.10 = (bf16[16,576]{1,0:T(8,128)(2,1)S(1)}, bf16[16,576]{1,0:T(8,128)(2,1)}, u32[]{:S(2)}) copy-start(bf16[16,576]{1,0:T(8,128)(2,1)} %param.22) | copy-start | bytes 55300
  100.6 11.8 %copy-start.4 = (bf16[16,64,576]{2,1,0:T(8,128)(2,1)S(1)}, bf16[16,64,576]{2,1,0:T(8,128)(2,1)}, u32[]{:S(2)}) copy-start(bf16[16,64,576]{2,1,0:T(8,128)(2,1)} %q_two) | copy-start | bytes 3538948
  100.6 13.9 %copy-start.8 = (f32[64,512]{1,0:T(8,128)S(1)}, f32[64,512]{1,0:T(8,128)}, u32[]{:S(2)}) copy-start(f32[64,512]{1,0:T(8,128)} %get-tuple-element.31) | copy-start | bytes 393220
  100.6 21.6 %copy-start.6 = (bf16[16,64,576]{2,1,0:T(8,128)(2,1)S(1)}, bf16[16,64,576]{2,1,0:T(8,128)(2,1)}, u32[]{:S(2)}) copy-start(bf16[16,64,576]{2,1,0:T(8,128)(2,1)} %q_one.1) | copy-start | bytes 3538948
  100.6 54.0 %all-to-all-start.1 = ((bf16[64,8,1792]{2,1,0:T(8,128)(2,1)}), bf16[64,8,1792]{2,1,0:T(8,128)(2,1)}, u32[]{:S(2)}, u32[]{:S(2)}) async-start(bf16[64,8,1792]{2,1,0:T(8,128)(2,1)} %bitcast.28), calls=%async_computation.1 | async-start | bytes 3670016 | tf_op jit(solution)/shard_map/all_to_all | solution.py:403
  112.4 4.1 %collective-permute-start.4 = (bf16[80,576]{1,0:T(8,128)(2,1)S(1)}, bf16[80,576]{1,0:T(8,128)(2,1)S(1)}, u32[]{:S(2)}, u32[]{:S(2)}) collective-permute-start(bf16[80,576]{1,0:T(8,128)(2,1)S(1)} %maximum_maximum_fusion), channel_id=1, source_target_pairs={{0,3},{1,0},{2,1},{3,2},{4,7},{5,4},{6,5},{7,6},{8,11},{9,8},{10,9... | collective-permute-start | bytes 276488 | tf_op jit(solution)/shard_map/ppermute | solution.py:18
  113.8 5.5 %collective-permute-start.3 = (bf16[80,576]{1,0:T(8,128)(2,1)S(1)}, bf16[80,576]{1,0:T(8,128)(2,1)S(1)}, u32[]{:S(2)}, u32[]{:S(2)}) collective-permute-start(bf16[80,576]{1,0:T(8,128)(2,1)S(1)} %maximum_maximum_fusion), channel_id=1, source_target_pairs={{0,2},{1,3},{2,0},{3,1},{4,6},{5,7},{6,4},{7,5},{8,10},{9,11},{10,... | collective-permute-start | bytes 276488 | tf_op jit(solution)/shard_map/ppermute | solution.py:18
  114.0 8.0 %collective-permute-start.2 = (bf16[80,576]{1,0:T(8,128)(2,1)S(1)}, bf16[80,576]{1,0:T(8,128)(2,1)S(1)}, u32[]{:S(2)}, u32[]{:S(2)}) collective-permute-start(bf16[80,576]{1,0:T(8,128)(2,1)S(1)} %maximum_maximum_fusion), channel_id=1, source_target_pairs={{0,1},{1,2},{2,3},{3,0},{4,5},{5,6},{6,7},{7,4},{8,9},{9,10},{10,1... | collective-permute-start | bytes 276488 | tf_op jit(solution)/shard_map/ppermute | solution.py:18
  122.2 1.7 %copy-start.5 = (bf16[32,64,576]{2,1,0:T(8,128)(2,1)S(1)}, bf16[32,64,576]{2,1,0:T(8,128)(2,1)}, u32[]{:S(2)}) copy-start(bf16[32,64,576]{2,1,0:T(8,128)(2,1)} %pool.1) | copy-start | bytes 7077892
  142.4 15.7 %collective-permute-start.5 = (bf16[64,512]{1,0:T(8,128)(2,1)S(1)}, bf16[64,512]{1,0:T(8,128)(2,1)S(1)}, u32[]{:S(2)}, u32[]{:S(2)}) collective-permute-start(bf16[64,512]{1,0:T(8,128)(2,1)S(1)} %get-tuple-element.47), channel_id=1, source_target_pairs={{0,1},{1,2},{2,3},{3,0},{4,5},{5,6},{6,7},{7,4},{8,9},{9,10},{10,1... | collective-permute-start | bytes 196616 | tf_op jit(solution)/shard_map/ppermute | solution.py:18
  142.5 15.6 %collective-permute-start.7 = (bf16[64,512]{1,0:T(8,128)(2,1)S(1)}, bf16[64,512]{1,0:T(8,128)(2,1)S(1)}, u32[]{:S(2)}, u32[]{:S(2)}) collective-permute-start(bf16[64,512]{1,0:T(8,128)(2,1)S(1)} %get-tuple-element.48), channel_id=1, source_target_pairs={{0,3},{1,0},{2,1},{3,2},{4,7},{5,4},{6,5},{7,6},{8,11},{9,8},{10,9... | collective-permute-start | bytes 196616 | tf_op jit(solution)/shard_map/ppermute | solution.py:18
  145.1 12.9 %collective-permute-start.6 = (bf16[64,512]{1,0:T(8,128)(2,1)S(1)}, bf16[64,512]{1,0:T(8,128)(2,1)S(1)}, u32[]{:S(2)}, u32[]{:S(2)}) collective-permute-start(bf16[64,512]{1,0:T(8,128)(2,1)S(1)} %get-tuple-element.49), channel_id=1, source_target_pairs={{0,2},{1,3},{2,0},{3,1},{4,6},{5,7},{6,4},{7,5},{8,10},{9,11},{10,... | collective-permute-start | bytes 196616 | tf_op jit(solution)/shard_map/ppermute | solution.py:18
  156.6 4.9 %collective-permute-start.16 = (f32[16,1792]{1,0:T(8,128)S(1)}, f32[16,1792]{1,0:T(8,128)S(1)}, u32[]{:S(2)}, u32[]{:S(2)}) collective-permute-start(f32[16,1792]{1,0:T(8,128)S(1)} %get-tuple-element.39), channel_id=1, source_target_pairs={{1,2},{2,1},{3,0},{0,3},{5,6},{6,5},{7,4},{4,7},{9,10},{10,9},{11,... | collective-permute-start | bytes 344072 | tf_op jit(solution)/shard_map/ppermute | solution.py:419
  158.1 3.6 %collective-permute-start.17 = (f32[16,1792]{1,0:T(8,128)S(1)}, f32[16,1792]{1,0:T(8,128)S(1)}, u32[]{:S(2)}, u32[]{:S(2)}) collective-permute-start(f32[16,1792]{1,0:T(8,128)S(1)} %get-tuple-element.40), channel_id=1, source_target_pairs={{2,3},{3,2},{0,1},{1,0},{6,7},{7,6},{4,5},{5,4},{10,11},{11,10},{8... | collective-permute-start | bytes 344072 | tf_op jit(solution)/shard_map/ppermute | solution.py:419

commit v14 on v13

--- a/solution.py
+++ b/solution.py
@@ -150,7 +150,7 @@
         sent[i] = part.astype(jnp.bfloat16)
 
 
-def up_project(which, rows, weights, steps):
+def up_project(which, rows, weights, steps, room):
     count, depth = rows.shape
     units = weights[0].shape[1]
     shape = (len(weights), count, units)
@@ -170,7 +170,7 @@
             jax.ShapeDtypeStruct(shape, jnp.float32),
             jax.ShapeDtypeStruct(shape, jnp.bfloat16),
         ],
-        compiler_params=pltpu.CompilerParams(vmem_limit_bytes=24 * 1024 * 1024),
+        compiler_params=pltpu.CompilerParams(vmem_limit_bytes=room * 1024 * 1024),
         cost_estimate=pl.CostEstimate(
             flops=2 * len(weights) * count * depth * units,
             bytes_accessed=5_000_000,
@@ -388,9 +388,9 @@
     attn_second = lax.dynamic_update_index_in_dim(attn_second, arrived_out, moved_slot, 0)
 
     scalars = jnp.stack([here // 2, 1 - here % 2]).astype(jnp.int32)
-    mine_a, sent_a = up_project(scalars, arrived, [w_up[0], up_next], 2)
+    mine_a, sent_a = up_project(scalars, arrived, [w_up[0], up_next], 2, 58)
     theirs_a = lax.ppermute(sent_a, ("ep", "grp"), by_core(PAIRS))
-    mine_b, sent_b = up_project(scalars, arrived, [up_far, up_prev], 2)
+    mine_b, sent_b = up_project(scalars, arrived, [up_far, up_prev], 2, 24)
     (sent_b,) = after(down_far, sent_b)
     theirs_b = lax.ppermute(sent_b, ("ep", "grp"), by_core(PAIRS))
     produced = down_project(

time: 165 us -> 164 us (level)
  local copies, waits for them, and re-layouts: 11.3 us -> 8.55 us
    unnamed x29 -> x31, local copies, waits for them, and re-layouts: 4.54 us -> 1.88 us
  transfers between devices with their start and end apart: 20 -> 20, of which waited for: 11 -> 11; matrix products, arithmetic and copies ran while one was open for 8% -> 8% of each run, Pallas kernels for 20% -> 21%
where the time goes in v14:
time: 164 us; the launch traced here: 161 us
  waiting for transfers between devices  59.3 us (36%)
  starting transfers between devices  41.1 us (25%)
  Pallas kernels  39.6 us (24%)
  local copies, waits for them, and re-layouts  8.55 us (5%)
  other arithmetic  5.72 us (3%)
  matrix products  4.1 us (2%)
  between operations  3.11 us (2%)
    ppermute x10, waiting for transfers between devices, hop(): lax.ppermute(value, axis, [(i, (i + step) % size) for i in range(size)])  23.3 us
    pallas_call x1, Pallas kernels, attention(): pl.pallas_call(attention_kernel, grid_spec=pltpu.PrefetchScalarGridSpec(n...  18.4 us
    all_to_all x1, waiting for transfers between devices, shards(): lax.all_to_all(outgoing.reshape(ep_size, rank, half), 'ep', split_axis=0,...  15 us
    all_to_all x1, starting transfers between devices, shards(): lax.all_to_all(outgoing.reshape(ep_size, rank, half), 'ep', split_axis=0,...  13.4 us
    ppermute x10, starting transfers between devices, hop(): lax.ppermute(value, axis, [(i, (i + step) % size) for i in range(size)])  9.54 us
    all_to_all x1, starting transfers between devices, shards(): lax.all_to_all(produced.reshape(ep_size, rank, half), 'ep', split_axis=0,...  9.33 us
    all_to_all x1, waiting for transfers between devices, shards(): lax.all_to_all(produced.reshape(ep_size, rank, half), 'ep', split_axis=0,...  9.02 us
    pallas_call x2, Pallas kernels, up_project(): pl.pallas_call(up_kernel, grid_spec=pltpu.PrefetchScalarGridSpec(num_scal...  8.15 us
  transfers between devices with their start and end apart: 20, of which 11 were waited for; matrix products, arithmetic and copies ran while one was open for 8% of the time, Pallas kernels for 21%

profile of v14, /device:TPU:1, one launch (start us, length us, event | category | flops | bytes accessed | tf_op | source)
XLA Modules:
  0.0 161.5 jit_solution(9060278668662318667)
XLA Ops:
  0.7 0.7 convert_convert_fusion
  1.4 0.7 reduce-precision_convert_fusion.2
  2.1 0.1 copy.43
  2.2 0.9 constant_dynamic-slice_fusion.2
  3.1 3.7 %collective-permute-start = (bf16[16,1920]{1,0:T(8,128)(2,1)S(1)}, bf16[16,1920]{1,0:T(8,128)(2,1)S(1)}, u32[]{:S(2)}, u32[]{:S(2)}) collective-permute-start(bf16[16,1920]{1,0:T(8,128)(2,1)S(1)} %get-tuple-element.58), channel_id=1, source_target_pairs={{1,2},{2,1},{3,0},{0,3},{5,6},{6,5},{7,4},{4,7},{9,10},{10,9},{11,... | collective-permute-start | bytes 184328 | tf_op jit(solution)/shard_map/ppermute | solution.py:298
  6.8 2.8 %dynamic-slice_bitcast_fusion.2 = (bf16[1792,256]{1,0:T(8,128)(2,1)}, bf16[1792,256]{1,0:T(8,128)(2,1)}) fusion(bf16[1,3584,256]{2,1,0:T(8,128)(2,1)} %param.17, s32[]{:T(128)S(6)} %select_n.256, s32[]{:T(128)S(6)} %select_n.255), kind=kLoop, calls=%fused_computation.10 | loop fusion | bytes 3670024 | tf_op jit(solution)/shard_map/dynamic_slice | solution.py:286
  9.6 0.6 collective-permute-start.8
  10.3 0.8 collective-permute-start.9
  11.1 0.1 copy.34
  11.4 0.1 copy.37
  11.4 0.1 eq.111
  11.5 0.3 fusion.2
  11.9 0.1 convert_element_type.58
  12.0 0.1 multiply_add_fusion
  12.1 0.1 add_select_fusion.6
  12.2 0.1 pad_add_fusion.1
  12.3 0.1 copy.39
  12.4 0.1 pad_maximum_fusion.3
  12.4 0.1 copy.42
  12.5 1.3 select_reduce_fusion
  13.9 0.6 slice.120
  15.2 1.9 %convolution_convert_fusion = bf16[512,1792]{1,0:T(8,128)(2,1)} fusion(bf16[64,512]{1,0:T(8,128)(2,1)S(1)} %get-tuple-element.32, bf16[16,1792]{1,0:T(8,128)(2,1)S(1)} %slice.111, bf16[16,1792]{1,0:T(8,128)(2,1)S(1)} %get-tuple-element.46, bf16[16,1792]{1,0:T(8,128)(2,1)S(1)} %slice.110, bf16[16,1792]{1,0:T(8,128)(2,1)S(1)} %get-tuple-element.43), kind=kOutput, calls=%fused_computation | convolution fusion | flops 119275520 | bytes 2129920 | tf_op jit(solution)/shard_map/dot_general | solution.py:345
  17.0 13.4 %all-to-all-start = ((bf16[64,8,1792]{2,1,0:T(8,128)(2,1)}), bf16[64,8,1792]{2,1,0:T(8,128)(2,1)}, u32[]{:S(2)}, u32[]{:S(2)}) async-start(bf16[64,8,1792]{2,1,0:T(8,128)(2,1)} %bitcast.56), calls=%async_computation | async-start | bytes 3670016 | tf_op jit(solution)/shard_map/all_to_all | solution.py:351
  30.5 1.4 dynamic-slice_bitcast_fusion
  31.9 1.7 %collective-permute-start.12 = (bf16[1792,256]{1,0:T(8,128)(2,1)}, bf16[1792,256]{1,0:T(8,128)(2,1)}, u32[]{:S(2)}, u32[]{:S(2)}) collective-permute-start(bf16[1792,256]{1,0:T(8,128)(2,1)} %get-tuple-element.27), channel_id=1, source_target_pairs={{0,1},{1,2},{2,3},{3,0},{4,5},{5,6},{6,7},{7,4},{8,9},{9,10},{10,1... | collective-permute-start | bytes 2752520 | tf_op jit(solution)/shard_map/ppermute | solution.py:18
  33.6 1.1 collective-permute-start.13
  34.7 3.6 %choose.2 = bf16[1792,256]{1,0:T(8,128)(2,1)} custom-call(s32[1]{0:T(128)} %bitcast.23.which, bf16[1792,256]{1,0:T(8,128)(2,1)} %copy-done.2, bf16[1792,256]{1,0:T(8,128)(2,1)} %collective-permute-done.8.refs_1_.second), custom_call_target="tpu_custom_call" | custom-call | flops 199999995904 | bytes 2752512 | tf_op jit(solution)/shard_map/choose/pallas_call | solution.py:132
  38.2 0.8 collective-permute-start.10
  39.0 14.0 %collective-permute-done.12.first.refs_3_ = bf16[1792,256]{1,0:T(8,128)(2,1)} collective-permute-done((bf16[1792,256]{1,0:T(8,128)(2,1)}, bf16[1792,256]{1,0:T(8,128)(2,1)}, u32[]{:S(2)}, u32[]{:S(2)}) %collective-permute-start.12) | collective-permute-done | bytes 917536 | tf_op jit(solution)/shard_map/ppermute | solution.py:18
  53.0 1.9 %collective-permute-done.13.second.refs_1_ = bf16[1792,256]{1,0:T(8,128)(2,1)} collective-permute-done((bf16[1792,256]{1,0:T(8,128)(2,1)}, bf16[1792,256]{1,0:T(8,128)(2,1)}, u32[]{:S(2)}, u32[]{:S(2)}) %collective-permute-start.13) | collective-permute-done | bytes 917536 | tf_op jit(solution)/shard_map/ppermute | solution.py:18
  54.9 3.6 %choose.3 = bf16[1792,256]{1,0:T(8,128)(2,1)} custom-call(s32[1]{0:T(128)} %bitcast.23.which, bf16[1792,256]{1,0:T(8,128)(2,1)} %collective-permute-done.12.first.refs_3_, bf16[1792,256]{1,0:T(8,128)(2,1)} %collective-permute-done.13.second.refs_1_), custom_call_target="tpu_custom_call" | custom-call | bytes 2752512 | tf_op jit(solution)/shard_map/choose/pallas_call | solution.py:132
  58.4 0.6 collective-permute-start.14
  59.0 0.6 pad_add_fusion.2._.scalars
  59.6 15.0 %all-to-all-done = bf16[64,8,1792]{2,1,0:T(8,128)(2,1)} async-done(((bf16[64,8,1792]{2,1,0:T(8,128)(2,1)}), bf16[64,8,1792]{2,1,0:T(8,128)(2,1)}, u32[]{:S(2)}, u32[]{:S(2)}) %all-to-all-start) | async-done | bytes 1835040 | tf_op jit(solution)/shard_map/all_to_all | solution.py:351
  74.7 4.7 %up_project.2 = (f32[2,512,256]{2,1,0:T(8,128)}, bf16[2,512,256]{2,1,0:T(8,128)(2,1)}) custom-call(s32[2]{0:T(128)} %pad_add_fusion.2._.scalars, bf16[512,1792]{1,0:T(8,128)(2,1)} %bitcast.19.rows, bf16[3584,256]{1,0:T(8,128)(2,1)} %bitcast.55, bf16[1792,256]{1,0:T(8,128)(2,1)} %collective-permute-done.8.refs_1_.second), custom_call_target="tpu_custom_call" | custom-call | flops 939524096 | bytes 5000000 | tf_op jit(solution)/shard_map/up_project/pallas_call | solution.py:160
  79.4 1.6 collective-permute-start.11
  81.0 3.4 %up_project.3 = (f32[2,512,256]{2,1,0:T(8,128)S(1)}, bf16[2,512,256]{2,1,0:T(8,128)(2,1)S(1)}) custom-call(s32[2]{0:T(128)S(1)} %copy-done.5, bf16[512,1792]{1,0:T(8,128)(2,1)} %bitcast.19.rows, bf16[1792,256]{1,0:T(8,128)(2,1)} %collective-permute-done.10.refs_0_, bf16[1792,256]{1,0:T(8,128)(2,1)S(1)} %copy-done.3), custom_call_target="tpu_custom_call" | custom-call | flops 939524096 | bytes 5000000 | tf_op jit(solution)/shard_map/up_project/pallas_call | solution.py:160
  84.5 0.3 collective-permute-start.15
  84.8 3.3 %collective-permute-done.11.theirs_a = bf16[2,512,256]{2,1,0:T(8,128)(2,1)S(1)} collective-permute-done((bf16[2,512,256]{2,1,0:T(8,128)(2,1)}, bf16[2,512,256]{2,1,0:T(8,128)(2,1)S(1)}, u32[]{:S(2)}, u32[]{:S(2)}) %collective-permute-start.11) | collective-permute-done | bytes 524320 | tf_op jit(solution)/shard_map/ppermute | solution.py:392
  88.1 5.6 %collective-permute-done.15.theirs_b = bf16[2,512,256]{2,1,0:T(8,128)(2,1)S(1)} collective-permute-done((bf16[2,512,256]{2,1,0:T(8,128)(2,1)S(1)}, bf16[2,512,256]{2,1,0:T(8,128)(2,1)S(1)}, u32[]{:S(2)}, u32[]{:S(2)}) %collective-permute-start.15) | collective-permute-done | bytes 524320 | tf_op jit(solution)/shard_map/ppermute | solution.py:395
  93.7 5.9 %down_project.1 = bf16[512,1792]{1,0:T(8,128)(2,1)} custom-call(s32[2]{0:T(128)S(1)} %copy-done.5, f32[2,512,256]{2,1,0:T(8,128)S(1)} %copy-done.1, f32[2,512,256]{2,1,0:T(8,128)S(1)} %get-tuple-element.25.mine_b, bf16[2,512,256]{2,1,0:T(8,128)(2,1)S(1)} %collective-permute-done.11.theirs_a, bf16[2,512,256]{2,1,0:T(8,128)(2,1)S(1)} %collective-permute-done.15.theirs_b, ...), custom_call_target="tpu_custom_call" | custom-call | flops 1879048192 | bytes 9000000 | tf_op jit(solution)/shard_map/down_project/pallas_call | solution.py:213
  99.7 9.3 %all-to-all-start.1 = ((bf16[64,8,1792]{2,1,0:T(8,128)(2,1)}), bf16[64,8,1792]{2,1,0:T(8,128)(2,1)}, u32[]{:S(2)}, u32[]{:S(2)}) async-start(bf16[64,8,1792]{2,1,0:T(8,128)(2,1)} %bitcast.28), calls=%async_computation.1 | async-start | bytes 3670016 | tf_op jit(solution)/shard_map/all_to_all | solution.py:403
  110.4 0.1 select_reduce_fusion.2
  110.6 0.1 min.19
  110.8 0.1 select_reduce_fusion.1.pages
  111.0 0.1 maximum_maximum_fusion
  111.0 1.9 %collective-permute-start.4 = (bf16[80,576]{1,0:T(8,128)(2,1)S(1)}, bf16[80,576]{1,0:T(8,128)(2,1)S(1)}, u32[]{:S(2)}, u32[]{:S(2)}) collective-permute-start(bf16[80,576]{1,0:T(8,128)(2,1)S(1)} %maximum_maximum_fusion), channel_id=1, source_target_pairs={{0,3},{1,0},{2,1},{3,2},{4,7},{5,4},{6,5},{7,6},{8,11},{9,8},{10,9... | collective-permute-start | bytes 276488 | tf_op jit(solution)/shard_map/ppermute | solution.py:18
  112.9 0.2 collective-permute-start.3
  113.1 0.5 collective-permute-start.2
  113.7 1.5 collective-permute-done.4
  115.2 3.2 %collective-permute-done.3 = bf16[80,576]{1,0:T(8,128)(2,1)S(1)} collective-permute-done((bf16[80,576]{1,0:T(8,128)(2,1)S(1)}, bf16[80,576]{1,0:T(8,128)(2,1)S(1)}, u32[]{:S(2)}, u32[]{:S(2)}) %collective-permute-start.3) | collective-permute-done | bytes 92192 | tf_op jit(solution)/shard_map/ppermute | solution.py:18
  118.4 2.7 %collective-permute-done.2 = bf16[80,576]{1,0:T(8,128)(2,1)S(1)} collective-permute-done((bf16[80,576]{1,0:T(8,128)(2,1)S(1)}, bf16[80,576]{1,0:T(8,128)(2,1)S(1)}, u32[]{:S(2)}, u32[]{:S(2)}) %collective-permute-start.2) | collective-permute-done | bytes 92192 | tf_op jit(solution)/shard_map/ppermute | solution.py:18
  121.1 0.1 select_select_fusion
  121.3 1.7 %copy-done.6 = bf16[32,64,576]{2,1,0:T(8,128)(2,1)S(1)} copy-done((bf16[32,64,576]{2,1,0:T(8,128)(2,1)S(1)}, bf16[32,64,576]{2,1,0:T(8,128)(2,1)}, u32[]{:S(2)}) %copy-start.6) | copy-done | bytes 2359320
  123.0 18.4 %attention.1 = (bf16[16,64,512]{2,1,0:T(8,128)(2,1)}, bf16[16,64,512]{2,1,0:T(8,128)(2,1)}, bf16[64,512]{1,0:T(8,128)(2,1)S(1)}) custom-call(s32[16]{0:T(128)S(1)} %bitcast.54, s32[128]{0:T(128)S(1)} %select_reduce_fusion.1.pages, s32[1]{0:T(128)} %bitcast.48.moved, bf16[16,64,576]{2,1,0:T(8,128)(2,1)S(1)} %copy-done.7, bf16[16,64,576]{2,1,0:T(8,128)(2,1)S(1)} %copy-done.4, ...), custom_call_target="tpu_custom_call" | custom-call | flops 12000000000 | bytes 8000000 | tf_op jit(solution)/shard_map/attention/pallas_call | solution.py:89
  141.5 0.1 collective-permute-start.5
  141.6 2.7 %collective-permute-start.7 = (bf16[64,512]{1,0:T(8,128)(2,1)S(1)}, bf16[64,512]{1,0:T(8,128)(2,1)S(1)}, u32[]{:S(2)}, u32[]{:S(2)}) collective-permute-start(bf16[64,512]{1,0:T(8,128)(2,1)S(1)} %get-tuple-element.48), channel_id=1, source_target_pairs={{0,3},{1,0},{2,1},{3,2},{4,7},{5,4},{6,5},{7,6},{8,11},{9,8},{10,9... | collective-permute-start | bytes 196616 | tf_op jit(solution)/shard_map/ppermute | solution.py:18
  144.2 9.0 %all-to-all-done.1 = bf16[64,8,1792]{2,1,0:T(8,128)(2,1)} async-done(((bf16[64,8,1792]{2,1,0:T(8,128)(2,1)}), bf16[64,8,1792]{2,1,0:T(8,128)(2,1)}, u32[]{:S(2)}, u32[]{:S(2)}) %all-to-all-start.1) | async-done | bytes 1835040 | tf_op jit(solution)/shard_map/all_to_all | solution.py:403
  153.2 1.9 %fusion = f32[128,1792]{1,0:T(8,128)S(1)} fusion(bf16[64,8,1792]{2,1,0:T(8,128)(2,1)} %all-to-all-done.1, bf16[64,512]{1,0:T(8,128)(2,1)S(1)} %get-tuple-element.42, bf16[64,512]{1,0:T(8,128)(2,1)S(1)} %get-tuple-element.41), kind=kOutput, calls=%fused_computation.1 | convolution fusion | flops 235143168 | bytes 2883584 | tf_op jit(solution)/shard_map/dot_general | solution.py:414
  155.2 1.9 %collective-permute-start.16 = (f32[16,1792]{1,0:T(8,128)S(1)}, f32[16,1792]{1,0:T(8,128)S(1)}, u32[]{:S(2)}, u32[]{:S(2)}) collective-permute-start(f32[16,1792]{1,0:T(8,128)S(1)} %get-tuple-element.39), channel_id=1, source_target_pairs={{1,2},{2,1},{3,0},{0,3},{5,6},{6,5},{7,4},{4,7},{9,10},{10,9},{11,... | collective-permute-start | bytes 344072 | tf_op jit(solution)/shard_map/ppermute | solution.py:419
  157.2 0.7 bitcast_dynamic-update-slice_fusion
  157.9 2.3 %collective-permute-done.16 = f32[16,1792]{1,0:T(8,128)S(1)} collective-permute-done((f32[16,1792]{1,0:T(8,128)S(1)}, f32[16,1792]{1,0:T(8,128)S(1)}, u32[]{:S(2)}, u32[]{:S(2)}) %collective-permute-start.16) | collective-permute-done | bytes 114720 | tf_op jit(solution)/shard_map/ppermute | solution.py:419
  160.2 0.6 collective-permute-done.17
  160.8 0.7 pad_maximum_fusion.1
  (68 shorter events, 0.8 us)
Async XLA Ops:
  3.1 8.0 %collective-permute-start = (bf16[16,1920]{1,0:T(8,128)(2,1)S(1)}, bf16[16,1920]{1,0:T(8,128)(2,1)S(1)}, u32[]{:S(2)}, u32[]{:S(2)}) collective-permute-start(bf16[16,1920]{1,0:T(8,128)(2,1)S(1)} %get-tuple-element.58), channel_id=1, source_target_pairs={{1,2},{2,1},{3,0},{0,3},{5,6},{6,5},{7,4},{4,7},{9,10},{10,9},{11,... | collective-permute-start | bytes 184328 | tf_op jit(solution)/shard_map/ppermute | solution.py:298
  6.8 4.4 %collective-permute-start.1 = (bf16[16,1920]{1,0:T(8,128)(2,1)S(1)}, bf16[16,1920]{1,0:T(8,128)(2,1)S(1)}, u32[]{:S(2)}, u32[]{:S(2)}) collective-permute-start(bf16[16,1920]{1,0:T(8,128)(2,1)S(1)} %get-tuple-element.59), channel_id=1, source_target_pairs={{2,3},{3,2},{0,1},{1,0},{6,7},{7,6},{4,5},{5,4},{10,11},{11,10},{8... | collective-permute-start | bytes 184328 | tf_op jit(solution)/shard_map/ppermute | solution.py:298
  6.8 4.5 %copy-start.10 = (s32[16,8]{0,1:T(8,128)S(1)}, s32[16,8]{0,1:T(8,128)}, u32[]{:S(2)}) copy-start(s32[16,8]{0,1:T(8,128)} %param.15) | copy-start | bytes 1540
  6.8 5.6 %copy-start.13 = (f32[16,8]{0,1:T(8,128)S(1)}, f32[16,8]{0,1:T(8,128)}, u32[]{:S(2)}) copy-start(f32[16,8]{0,1:T(8,128)} %param.16) | copy-start | bytes 1540
  9.6 22.3 %collective-permute-start.8 = (bf16[1792,256]{1,0:T(8,128)(2,1)}, bf16[1792,256]{1,0:T(8,128)(2,1)}, u32[]{:S(2)}, u32[]{:S(2)}) collective-permute-start(bf16[1792,256]{1,0:T(8,128)(2,1)} %get-tuple-element.22), channel_id=1, source_target_pairs={{0,3},{1,0},{2,1},{3,2},{4,7},{5,4},{6,5},{7,6},{8,11},{9,8},{10,9... | collective-permute-start | bytes 2752520 | tf_op jit(solution)/shard_map/ppermute | solution.py:18
  10.3 21.6 %collective-permute-start.9 = (bf16[1792,256]{1,0:T(8,128)(2,1)}, bf16[1792,256]{1,0:T(8,128)(2,1)S(1)}, u32[]{:S(2)}, u32[]{:S(2)}) collective-permute-start(bf16[1792,256]{1,0:T(8,128)(2,1)} %get-tuple-element.24), channel_id=1, source_target_pairs={{0,1},{1,2},{2,3},{3,0},{4,5},{5,6},{6,7},{7,4},{8,9},{9,10},{10,1... | collective-permute-start | bytes 2752520 | tf_op jit(solution)/shard_map/ppermute | solution.py:18
  17.0 13.5 %copy-start = (bf16[1,3584,256]{2,1,0:T(8,128)(2,1)S(1)}, bf16[1,3584,256]{2,1,0:T(8,128)(2,1)}, u32[]{:S(2)}) copy-start(bf16[1,3584,256]{2,1,0:T(8,128)(2,1)} %param.18) | copy-start | bytes 5505028
  17.0 57.7 %all-to-all-start = ((bf16[64,8,1792]{2,1,0:T(8,128)(2,1)}), bf16[64,8,1792]{2,1,0:T(8,128)(2,1)}, u32[]{:S(2)}, u32[]{:S(2)}) async-start(bf16[64,8,1792]{2,1,0:T(8,128)(2,1)} %bitcast.56), calls=%async_computation | async-start | bytes 3670016 | tf_op jit(solution)/shard_map/all_to_all | solution.py:351
  31.9 2.8 %copy-start.2 = (bf16[1792,256]{1,0:T(8,128)(2,1)}, bf16[1792,256]{1,0:T(8,128)(2,1)S(1)}, u32[]{:S(2)}) copy-start(bf16[1792,256]{1,0:T(8,128)(2,1)S(1)} %collective-permute-done.9.first.refs_1_) | copy-start | bytes 2752516
  31.9 21.1 %collective-permute-start.12 = (bf16[1792,256]{1,0:T(8,128)(2,1)}, bf16[1792,256]{1,0:T(8,128)(2,1)}, u32[]{:S(2)}, u32[]{:S(2)}) collective-permute-start(bf16[1792,256]{1,0:T(8,128)(2,1)} %get-tuple-element.27), channel_id=1, source_target_pairs={{0,1},{1,2},{2,3},{3,0},{4,5},{5,6},{6,7},{7,4},{8,9},{9,10},{10,1... | collective-permute-start | bytes 2752520 | tf_op jit(solution)/shard_map/ppermute | solution.py:18
  33.6 21.3 %collective-permute-start.13 = (bf16[1792,256]{1,0:T(8,128)(2,1)}, bf16[1792,256]{1,0:T(8,128)(2,1)}, u32[]{:S(2)}, u32[]{:S(2)}) collective-permute-start(bf16[1792,256]{1,0:T(8,128)(2,1)} %get-tuple-element.28), channel_id=1, source_target_pairs={{0,3},{1,0},{2,1},{3,2},{4,7},{5,4},{6,5},{7,6},{8,11},{9,8},{10,9... | collective-permute-start | bytes 2752520 | tf_op jit(solution)/shard_map/ppermute | solution.py:18
  38.2 42.8 %collective-permute-start.10 = (bf16[1792,256]{1,0:T(8,128)(2,1)}, bf16[1792,256]{1,0:T(8,128)(2,1)}, u32[]{:S(2)}, u32[]{:S(2)}) collective-permute-start(bf16[1792,256]{1,0:T(8,128)(2,1)} %choose.2), channel_id=1, source_target_pairs={{0,1},{1,0},{2,3},{3,2},{5,6},{6,5},{7,4},{4,7},{8,9},{9,8},{10,11... | collective-permute-start | bytes 2752520 | tf_op jit(solution)/shard_map/ppermute | solution.py:313
  58.4 26.0 %collective-permute-start.14 = (bf16[1792,256]{1,0:T(8,128)(2,1)}, bf16[1792,256]{1,0:T(8,128)(2,1)S(1)}, u32[]{:S(2)}, u32[]{:S(2)}) collective-permute-start(bf16[1792,256]{1,0:T(8,128)(2,1)} %choose.3), channel_id=1, source_target_pairs={{0,1},{1,0},{2,3},{3,2},{5,6},{6,5},{7,4},{4,7},{8,9},{9,8},{10,11... | collective-permute-start | bytes 2752520 | tf_op jit(solution)/shard_map/ppermute | solution.py:313
  74.7 6.3 %copy-start.3 = (bf16[1792,256]{1,0:T(8,128)(2,1)S(1)}, bf16[1792,256]{1,0:T(8,128)(2,1)}, u32[]{:S(2)}) copy-start(bf16[1792,256]{1,0:T(8,128)(2,1)} %copy-done.2) | copy-start | bytes 2752516
  74.7 6.3 %copy-start.5 = (s32[2]{0:T(128)S(1)}, s32[2]{0:T(128)}, u32[]{:S(2)}) copy-start(s32[2]{0:T(128)} %pad_add_fusion.2._.scalars) | copy-start | bytes 28
  79.4 14.3 %copy-start.1 = (f32[2,512,256]{2,1,0:T(8,128)S(1)}, f32[2,512,256]{2,1,0:T(8,128)}, u32[]{:S(2)}) copy-start(f32[2,512,256]{2,1,0:T(8,128)} %get-tuple-element.23.mine_a) | copy-start | bytes 3145732
  79.4 8.7 %collective-permute-start.11 = (bf16[2,512,256]{2,1,0:T(8,128)(2,1)}, bf16[2,512,256]{2,1,0:T(8,128)(2,1)S(1)}, u32[]{:S(2)}, u32[]{:S(2)}) collective-permute-start(bf16[2,512,256]{2,1,0:T(8,128)(2,1)} %get-tuple-element.26), channel_id=1, source_target_pairs={{1,2},{2,1},{3,0},{0,3},{6,7},{7,6},{4,5},{5,4},{9,10},{10,9},{11,... | collective-permute-start | bytes 1572872 | tf_op jit(solution)/shard_map/ppermute | solution.py:392
  84.5 9.2 %collective-permute-start.15 = (bf16[2,512,256]{2,1,0:T(8,128)(2,1)S(1)}, bf16[2,512,256]{2,1,0:T(8,128)(2,1)S(1)}, u32[]{:S(2)}, u32[]{:S(2)}) collective-permute-start(bf16[2,512,256]{2,1,0:T(8,128)(2,1)S(1)} %get-tuple-element.30), channel_id=1, source_target_pairs={{1,2},{2,1},{3,0},{0,3},{6,7},{7,6},{4,5},{5,4},{9,10},{10,9},{11,... | collective-permute-start | bytes 1572872 | tf_op jit(solution)/shard_map/ppermute | solution.py:395
  99.6 10.7 %copy-start.8 = (s32[1,16]{1,0:T(1,128)S(1)}, s32[1,16]{1,0:T(1,128)}, u32[]{:S(2)}) copy-start(s32[1,16]{1,0:T(1,128)} %param.24) | copy-start | bytes 196
  99.6 11.0 %copy-start.12 = (bf16[16,576]{1,0:T(8,128)(2,1)S(1)}, bf16[16,576]{1,0:T(8,128)(2,1)}, u32[]{:S(2)}) copy-start(bf16[16,576]{1,0:T(8,128)(2,1)} %param.20) | copy-start | bytes 55300
  99.6 11.2 %copy-start.14 = (s32[1,32]{1,0:T(1,128)S(1)}, s32[1,32]{1,0:T(1,128)}, u32[]{:S(2)}) copy-start(s32[1,32]{1,0:T(1,128)} %param.25) | copy-start | bytes 388
  99.6 11.3 %copy-start.11 = (bf16[16,576]{1,0:T(8,128)(2,1)S(1)}, bf16[16,576]{1,0:T(8,128)(2,1)}, u32[]{:S(2)}) copy-start(bf16[16,576]{1,0:T(8,128)(2,1)} %param.22) | copy-start | bytes 55300
  99.7 11.3 %copy-start.4 = (bf16[16,64,576]{2,1,0:T(8,128)(2,1)S(1)}, bf16[16,64,576]{2,1,0:T(8,128)(2,1)}, u32[]{:S(2)}) copy-start(bf16[16,64,576]{2,1,0:T(8,128)(2,1)} %q_two) | copy-start | bytes 3538948
  99.7 14.0 %copy-start.9 = (f32[64,512]{1,0:T(8,128)S(1)}, f32[64,512]{1,0:T(8,128)}, u32[]{:S(2)}) copy-start(f32[64,512]{1,0:T(8,128)} %get-tuple-element.31) | copy-start | bytes 393220
  99.7 21.6 %copy-start.7 = (bf16[16,64,576]{2,1,0:T(8,128)(2,1)S(1)}, bf16[16,64,576]{2,1,0:T(8,128)(2,1)}, u32[]{:S(2)}) copy-start(bf16[16,64,576]{2,1,0:T(8,128)(2,1)} %q_one.1) | copy-start | bytes 3538948
  99.7 53.6 %all-to-all-start.1 = ((bf16[64,8,1792]{2,1,0:T(8,128)(2,1)}), bf16[64,8,1792]{2,1,0:T(8,128)(2,1)}, u32[]{:S(2)}, u32[]{:S(2)}) async-start(bf16[64,8,1792]{2,1,0:T(8,128)(2,1)} %bitcast.28), calls=%async_computation.1 | async-start | bytes 3670016 | tf_op jit(solution)/shard_map/all_to_all | solution.py:403
  111.0 4.2 %collective-permute-start.4 = (bf16[80,576]{1,0:T(8,128)(2,1)S(1)}, bf16[80,576]{1,0:T(8,128)(2,1)S(1)}, u32[]{:S(2)}, u32[]{:S(2)}) collective-permute-start(bf16[80,576]{1,0:T(8,128)(2,1)S(1)} %maximum_maximum_fusion), channel_id=1, source_target_pairs={{0,3},{1,0},{2,1},{3,2},{4,7},{5,4},{6,5},{7,6},{8,11},{9,8},{10,9... | collective-permute-start | bytes 276488 | tf_op jit(solution)/shard_map/ppermute | solution.py:18
  112.9 5.5 %collective-permute-start.3 = (bf16[80,576]{1,0:T(8,128)(2,1)S(1)}, bf16[80,576]{1,0:T(8,128)(2,1)S(1)}, u32[]{:S(2)}, u32[]{:S(2)}) collective-permute-start(bf16[80,576]{1,0:T(8,128)(2,1)S(1)} %maximum_maximum_fusion), channel_id=1, source_target_pairs={{0,2},{1,3},{2,0},{3,1},{4,6},{5,7},{6,4},{7,5},{8,10},{9,11},{10,... | collective-permute-start | bytes 276488 | tf_op jit(solution)/shard_map/ppermute | solution.py:18
  113.1 8.0 %collective-permute-start.2 = (bf16[80,576]{1,0:T(8,128)(2,1)S(1)}, bf16[80,576]{1,0:T(8,128)(2,1)S(1)}, u32[]{:S(2)}, u32[]{:S(2)}) collective-permute-start(bf16[80,576]{1,0:T(8,128)(2,1)S(1)} %maximum_maximum_fusion), channel_id=1, source_target_pairs={{0,1},{1,2},{2,3},{3,0},{4,5},{5,6},{6,7},{7,4},{8,9},{9,10},{10,1... | collective-permute-start | bytes 276488 | tf_op jit(solution)/shard_map/ppermute | solution.py:18
  121.3 1.7 %copy-start.6 = (bf16[32,64,576]{2,1,0:T(8,128)(2,1)S(1)}, bf16[32,64,576]{2,1,0:T(8,128)(2,1)}, u32[]{:S(2)}) copy-start(bf16[32,64,576]{2,1,0:T(8,128)(2,1)} %pool.1) | copy-start | bytes 7077892
  141.5 15.7 %collective-permute-start.5 = (bf16[64,512]{1,0:T(8,128)(2,1)S(1)}, bf16[64,512]{1,0:T(8,128)(2,1)S(1)}, u32[]{:S(2)}, u32[]{:S(2)}) collective-permute-start(bf16[64,512]{1,0:T(8,128)(2,1)S(1)} %get-tuple-element.47), channel_id=1, source_target_pairs={{0,1},{1,2},{2,3},{3,0},{4,5},{5,6},{6,7},{7,4},{8,9},{9,10},{10,1... | collective-permute-start | bytes 196616 | tf_op jit(solution)/shard_map/ppermute | solution.py:18
  141.6 15.6 %collective-permute-start.7 = (bf16[64,512]{1,0:T(8,128)(2,1)S(1)}, bf16[64,512]{1,0:T(8,128)(2,1)S(1)}, u32[]{:S(2)}, u32[]{:S(2)}) collective-permute-start(bf16[64,512]{1,0:T(8,128)(2,1)S(1)} %get-tuple-element.48), channel_id=1, source_target_pairs={{0,3},{1,0},{2,1},{3,2},{4,7},{5,4},{6,5},{7,6},{8,11},{9,8},{10,9... | collective-permute-start | bytes 196616 | tf_op jit(solution)/shard_map/ppermute | solution.py:18
  144.2 12.9 %collective-permute-start.6 = (bf16[64,512]{1,0:T(8,128)(2,1)S(1)}, bf16[64,512]{1,0:T(8,128)(2,1)S(1)}, u32[]{:S(2)}, u32[]{:S(2)}) collective-permute-start(bf16[64,512]{1,0:T(8,128)(2,1)S(1)} %get-tuple-element.49), channel_id=1, source_target_pairs={{0,2},{1,3},{2,0},{3,1},{4,6},{5,7},{6,4},{7,5},{8,10},{9,11},{10,... | collective-permute-start | bytes 196616 | tf_op jit(solution)/shard_map/ppermute | solution.py:18
  155.2 4.9 %collective-permute-start.16 = (f32[16,1792]{1,0:T(8,128)S(1)}, f32[16,1792]{1,0:T(8,128)S(1)}, u32[]{:S(2)}, u32[]{:S(2)}) collective-permute-start(f32[16,1792]{1,0:T(8,128)S(1)} %get-tuple-element.39), channel_id=1, source_target_pairs={{1,2},{2,1},{3,0},{0,3},{5,6},{6,5},{7,4},{4,7},{9,10},{10,9},{11,... | collective-permute-start | bytes 344072 | tf_op jit(solution)/shard_map/ppermute | solution.py:419
  157.2 3.6 %collective-permute-start.17 = (f32[16,1792]{1,0:T(8,128)S(1)}, f32[16,1792]{1,0:T(8,128)S(1)}, u32[]{:S(2)}, u32[]{:S(2)}) collective-permute-start(f32[16,1792]{1,0:T(8,128)S(1)} %get-tuple-element.40), channel_id=1, source_target_pairs={{2,3},{3,2},{0,1},{1,0},{6,7},{7,6},{4,5},{5,4},{10,11},{11,10},{8... | collective-permute-start | bytes 344072 | tf_op jit(solution)/shard_map/ppermute | solution.py:419
